TPU v7x, 512 devices: a whole 4x8x8 slice. The times are simulated.
512 devices in a mesh: section: 8 (over y), dp: 32 (over z_lo, x, core), tensor: 2 (over z_hi).
Axes of the slice: x: 4, y: 8, z: 8 (z_hi: 2, z_lo: 4; z = z_hi * 4 + z_lo), core: 2. Of those that a mesh axis runs over, the one named last changes fastest.
Arguments:
- context: bfloat16 [16384, 6144], P('dp', 'section'), may hold values from -64 to 64
- out_weight: bfloat16 [6144, 6144], P('section', ('tensor', 'dp')), may hold values from -0.078125 to 0.078125
- previous: bfloat16 [16384, 6144], P('dp', ('tensor', 'section')), may hold values from -64 to 64
- section_act: bfloat16 [8, 6144, 6144], P('section', 'dp', 'tensor'), may hold values from -6 to 6
- fresh_batch: bfloat16 [6144, 6144], P('dp', 'tensor'), may hold values from -6 to 6
- section_gains: float32 [8, 6144], P('section', 'tensor'), may hold values from 0.1 to 1.9
- mask_blocks: int32 [32, 12], P('dp'), may hold values from 0 to 15, all different within a row
Outputs:
- targets: bfloat16 [16384, 6144], P('dp', ('tensor', 'section'))
- section_out: bfloat16 [8, 6144, 6144], P('section', 'dp', 'tensor')
- target_error: float32 [6144, 6144], P('dp', ('tensor', 'section'))
Inputs may be any that keep to these rules, and one draw needn't show every extreme that they name: `mask_blocks`: each row names 12 different blocks.
All inputs are finite; a program needn't handle non-finite values.
Results may differ from a plain program's by a relative error of at most 0.015.
Values may be sent and summed in bfloat16 or wider, within the bound.
No kernel may reach another device: no remote copies, remote signals or barrier semaphores. Data moves between devices by JAX's collectives and lax.ppermute only.
A program may use at most 64 MiB of HBM per device.

v0:
```python
import jax
import jax.numpy as jnp
from jax import lax
from jax.sharding import PartitionSpec as P

GRID_SIDE = 16
BLOCK_SIDE = 4
PATCHES = 256


def shifted(value, axis, steps):
    count = lax.axis_size(axis)
    leading, last = (max(0, -steps), min(count, count - steps))
    return lax.ppermute(value, axis, [(source, source + steps) for source in range(leading, last)])


def spread_2(x, axis, root):
    mine = lax.axis_index(axis) == root
    return lax.psum(jnp.where(mine, x, jnp.zeros_like(x)), axis)


def instance_norm(values, images):
    shaped = values.reshape(images, -1, values.shape[-1])
    center = jnp.mean(shaped, axis=1, keepdims=True)
    spread = jnp.mean(jnp.square(shaped - center), axis=1, keepdims=True)
    return ((shaped - center) * lax.rsqrt(spread + 1e-05)).reshape(values.shape)


def masked_patches(mask_blocks):
    per_side = GRID_SIDE // BLOCK_SIDE
    within = jnp.arange(BLOCK_SIDE * BLOCK_SIDE, dtype=jnp.int32)
    chosen = mask_blocks[..., None]
    grid_row = chosen // per_side * BLOCK_SIDE + within // BLOCK_SIDE
    grid_col = chosen % per_side * BLOCK_SIDE + within % BLOCK_SIDE
    return grid_row * GRID_SIDE + grid_col


def on_device(context, out_weight, previous, section_act, fresh_batch, section_gains, mask_blocks):
    partial_sum = jnp.dot(
        context,
        lax.all_gather(out_weight, "dp", axis=1, tiled=True),
        preferred_element_type=jnp.float32,
    ).astype(jnp.bfloat16)
    width = previous.shape[1]
    position = lax.axis_index("section")
    sections = lax.axis_size("section")
    summed = lax.psum(partial_sum, "section").astype(jnp.float32)
    share = lax.dynamic_slice_in_dim(summed, position * width, width, 1)
    images = context.shape[0] // PATCHES
    normed_new = instance_norm(share, images)
    normed_old = instance_norm(previous.astype(jnp.float32), images)
    targets = (0.5 * (normed_new + normed_old)).astype(jnp.bfloat16)
    incoming = shifted(section_act, "section", 1)
    current = jnp.where(position == 0, fresh_batch[None], incoming).astype(jnp.float32)
    squares = lax.psum(jnp.sum(current * current, axis=-1), "tensor")
    features = current.shape[-1] * lax.axis_size("tensor")
    scaling = lax.rsqrt(squares[..., None] / features + 1e-06)
    section_out = (current * scaling * section_gains[:, None, :]).astype(jnp.bfloat16)
    predicted = spread_2(section_act[0], "section", sections - 1)
    own_columns = lax.dynamic_slice_in_dim(predicted, position * width, width, 1)
    patch_ids = masked_patches(mask_blocks[0]).reshape(-1)
    picked = jnp.take(targets, patch_ids, axis=0).astype(jnp.float32)
    target_error = own_columns.astype(jnp.float32) - picked
    return (targets, section_out, target_error)


def solution(mesh):
    in_specs = (
        P("dp", "section"),
        P("section", ("tensor", "dp")),
        P("dp", ("tensor", "section")),
        P("section", "dp", "tensor"),
        P("dp", "tensor"),
        P("section", "tensor"),
        P("dp", None),
    )
    out_specs = (
        P("dp", ("tensor", "section")),
        P("section", "dp", "tensor"),
        P("dp", ("tensor", "section")),
    )
    return jax.shard_map(
        on_device, mesh=mesh, in_specs=in_specs, out_specs=out_specs, check_vma=False
    )
```

profile of v0, /device:TPU:1, one launch (start us, length us, event | category | flops | bytes accessed | tf_op | source)
XLA Modules:
  0.0 233.4 jit_solution(17504914805390724261)
XLA Ops:
  7.2 0.0 copy-start
  7.2 0.0 all-gather.2.cloned.1.call-start
  7.2 0.7 all-gather.2.cloned.1.call-update
  7.9 0.0 all-reduce.3.cloned.1.call-start
  8.0 1.2 select_bitcast_fusion
  9.2 73.9 %all-gather.2.cloned.1.call-done = bf16[768,3072]{0,1:T(8,128)(2,1)} async-done(((bf16[768,96]{0,1:T(8,128)(2,1)}), bf16[768,3072]{0,1:T(8,128)(2,1)}) %all-gather.2.cloned.1.call-update) | async-done | bytes 4718608 | tf_op jit(solution)/shard_map/all_gather | solution.py:41
  83.1 0.0 copy-done
  83.1 6.3 %convolution_convert_fusion = bf16[512,3072]{1,0:T(8,128)(2,1)} fusion(bf16[512,768]{1,0:T(8,128)(2,1)S(1)} %copy-done, bf16[768,3072]{0,1:T(8,128)(2,1)} %all-gather.2.cloned.1.call-done), kind=kOutput, calls=%fused_computation.1 | convolution fusion | flops 2417491968 | bytes 8650752 | tf_op jit(solution)/shard_map/dot_general | solution.py:39
  89.4 0.0 copy-start.6
  89.4 0.0 copy-start.3
  89.4 0.0 copy-start.2
  89.4 0.0 all-reduce.3.cloned.1.call-update
  89.4 3.3 %collective-permute-start = (bf16[1,192,3072]{2,1,0:T(8,128)(2,1)}, bf16[1,192,3072]{2,1,0:T(8,128)(2,1)S(1)}, u32[]{:S(2)}, u32[]{:S(2)}) collective-permute-start(bf16[1,192,3072]{2,1,0:T(8,128)(2,1)} %param.10), channel_id=1, source_target_pairs={{0,64},{64,128},{128,192},{192,256},{256,320},{320,384},{384,448},... | collective-permute-start | bytes 3538952 | tf_op jit(solution)/shard_map/ppermute | solution.py:14
  92.8 0.0 copy-done.6
  92.8 0.1 add_add_fusion
  92.9 0.1 add.181
  92.9 0.6 add.178
  93.6 0.0 copy-start.4
  93.6 0.6 pad_clamp_fusion
  94.2 0.0 copy-done.3
  94.2 0.1 bitcast_reduce_fusion
  94.3 0.1 fusion.7
  94.4 1.2 compare_and_fusion
  95.6 0.6 add_rsqrt_fusion
  96.2 38.2 %collective-permute-done = bf16[1,192,3072]{2,1,0:T(8,128)(2,1)S(1)} collective-permute-done((bf16[1,192,3072]{2,1,0:T(8,128)(2,1)}, bf16[1,192,3072]{2,1,0:T(8,128)(2,1)S(1)}, u32[]{:S(2)}, u32[]{:S(2)}) %collective-permute-start) | collective-permute-done | bytes 1179680 | tf_op jit(solution)/shard_map/ppermute | solution.py:14
  134.4 0.0 copy-done.2
  134.4 1.0 fusion
  135.5 8.4 %psum.22 = f32[1,192]{1,0:T(1,128)} all-reduce(f32[1,192]{1,0:T(1,128)} %bitcast.67), channel_id=1, replica_groups=mesh['section'=8,'dp'=32,'tensor'=2] {'tensor'}, use_global_device_ids=true, to_apply=%region_6.7 | all-reduce | flops 192 | bytes 1536 | tf_op jit(solution)/shard_map/psum | solution.py:55
  143.8 0.7 add_rsqrt_fusion.2
  144.5 0.0 copy-done.4
  144.5 1.5 fusion.2
  146.0 0.0 copy-start.5
  146.0 74.2 %all-reduce.3.cloned.1.call-done = (bf16[512,3072]{1,0:T(8,128)(2,1)}, bf16[192,3072]{1,0:T(8,128)(2,1)}) async-done(((bf16[512,3072]{1,0:T(8,128)(2,1)}, bf16[192,3072]{1,0:T(8,128)(2,1)}), (bf16[512,3072]{1,0:T(8,128)(2,1)}, bf16[192,3072]{1,0:T(8,128)(2,1)})) %all-reduce.3.cloned.1.call-update) | async-done | bytes 4325392 | tf_op jit(solution)/shard_map/psum | solution.py:47
  220.2 1.1 bitcast_reduce_fusion.1
  221.3 1.1 fusion.9
  222.4 1.2 fusion.5
  223.7 0.0 copy-start.1
  223.7 1.2 gather_fusion
  224.8 0.0 copy-done.5
  224.8 1.7 convert_subtract_fusion
  226.6 0.0 copy-done.1
  (6 shorter events, 0.0 us)
Async XLA Ops:
  7.2 75.9 %copy-start = (bf16[512,768]{1,0:T(8,128)(2,1)S(1)}, bf16[512,768]{1,0:T(8,128)(2,1)}, u32[]{:S(2)}) copy-start(bf16[512,768]{1,0:T(8,128)(2,1)} %param.7) | copy-start | bytes 2359300
  7.2 75.9 %all-gather.2.cloned.1.call-start = ((), (), s32[]{:S(2)}) async-start(), calls=%async_computation | async-start | bytes 4866048 | tf_op jit(solution)/shard_map/all_gather | solution.py:41
  7.9 212.3 %all-reduce.3.cloned.1.call-start = ((), (), s32[]{:S(2)}) async-start(), calls=%async_computation.1 | async-start | bytes 8650752 | tf_op jit(solution)/shard_map/psum | solution.py:47
  89.4 3.4 %copy-start.6 = (s32[1,12]{1,0:T(1,128)S(1)}, s32[1,12]{1,0:T(1,128)}, u32[]{:S(2)}) copy-start(s32[1,12]{1,0:T(1,128)} %param.13) | copy-start | bytes 148
  89.4 4.8 %copy-start.3 = (bf16[512,384]{1,0:T(8,128)(2,1)S(1)}, bf16[512,384]{1,0:T(8,128)(2,1)}, u32[]{:S(2)}) copy-start(bf16[512,384]{1,0:T(8,128)(2,1)} %param.9) | copy-start | bytes 1179652
  89.4 45.0 %copy-start.2 = (bf16[192,3072]{1,0:T(8,128)(2,1)S(1)}, bf16[192,3072]{1,0:T(8,128)(2,1)}, u32[]{:S(2)}) copy-start(bf16[192,3072]{1,0:T(8,128)(2,1)} %param.11) | copy-start | bytes 3538948
  89.4 45.0 %collective-permute-start = (bf16[1,192,3072]{2,1,0:T(8,128)(2,1)}, bf16[1,192,3072]{2,1,0:T(8,128)(2,1)S(1)}, u32[]{:S(2)}, u32[]{:S(2)}) collective-permute-start(bf16[1,192,3072]{2,1,0:T(8,128)(2,1)} %param.10), channel_id=1, source_target_pairs={{0,64},{64,128},{128,192},{192,256},{256,320},{320,384},{384,448},... | collective-permute-start | bytes 3538952 | tf_op jit(solution)/shard_map/ppermute | solution.py:14
  93.6 50.9 %copy-start.4 = (f32[1,3072]{1,0:T(1,128)S(1)}, f32[1,3072]{1,0:T(1,128)}, u32[]{:S(2)}) copy-start(f32[1,3072]{1,0:T(1,128)} %param.12) | copy-start | bytes 36868
  146.0 78.8 %copy-start.5 = (pred[192]{0:T(512)(128)(4,1)S(1)}, pred[192]{0:T(512)(128)(4,1)}, u32[]{:S(2)}) copy-start(pred[192]{0:T(512)(128)(4,1)} %compare_and_fusion) | copy-start | bytes 580
  223.7 2.9 %copy-start.1 = (bf16[512,384]{1,0:T(8,128)(2,1)}, bf16[512,384]{1,0:T(8,128)(2,1)S(1)}, u32[]{:S(2)}) copy-start(bf16[512,384]{1,0:T(8,128)(2,1)S(1)} %fusion.5) | copy-start | bytes 1179652
Sparse Core Ops, SparseCore 0:
  10.2 72.8 all-gather.1
  89.5 130.6 all-reduce.2
where the time goes:
time: 234 us; the launch traced here: 233 us
  waiting for transfers between devices  187 us (80%)
  between operations  14.1 us (6%)
  other arithmetic  12.4 us (5%)
  blocking collectives  8.36 us (4%)
  matrix products  6.33 us (3%)
  starting transfers between devices  3.39 us (1%)
    psum x1, waiting for transfers between devices, on_device(): summed = lax.psum(partial_sum, 'section').astype(jnp.float32)  74.2 us
    all_gather x1, waiting for transfers between devices, on_device(): lax.all_gather(out_weight, 'dp', axis=1, tiled=True)  73.9 us
    ppermute x1, waiting for transfers between devices, shifted(): lax.ppermute(value, axis, [(source, source + steps) for source in range(l...  38.2 us
    psum x1, blocking collectives, on_device(): squares = lax.psum(jnp.sum(current * current, axis=-1), 'tensor')  8.36 us
    dot_general x1, matrix products, on_device(): jnp.dot(context, lax.all_gather(out_weight, 'dp', axis=1, tiled=True), pr...  6.33 us
  transfers between devices with their start and end apart: 3, of which 3 were waited for; matrix products, arithmetic and copies ran while one was open for 3% of the time, Pallas kernels for 0%

commit v1 on v0

v1 whole, which is shorter than its diff:
```python
import jax
import jax.numpy as jnp
from jax import lax
from jax.experimental import pallas as pl
from jax.experimental.pallas import tpu as pltpu
from jax.sharding import Mesh, PartitionSpec as P

GRID_SIDE = 16
BLOCK_SIDE = 4
PATCHES = 256
AXES = ("section", "zlo", "x", "core", "tensor")
DP = ("zlo", "x", "core")


def masked_patches(mask_blocks):
    per_side = GRID_SIDE // BLOCK_SIDE
    within = jnp.arange(BLOCK_SIDE * BLOCK_SIDE, dtype=jnp.int32)
    chosen = mask_blocks[..., None]
    grid_row = chosen // per_side * BLOCK_SIDE + within // BLOCK_SIDE
    grid_col = chosen % per_side * BLOCK_SIDE + within % BLOCK_SIDE
    return grid_row * GRID_SIDE + grid_col


def normed(values, images):
    shaped = values.reshape(images, -1, values.shape[-1])
    center = jnp.mean(shaped, axis=1, keepdims=True)
    off = shaped - center
    spread = jnp.mean(jnp.square(off), axis=1, keepdims=True)
    return (off * lax.rsqrt(spread + 1e-05)).reshape(values.shape)


def product_kernel(context, weight, out):
    rows = weight[...].reshape(-1, weight.shape[-1])
    out[0] = lax.dot_general(
        context[...], rows, (((1,), (1,)), ((), ())), preferred_element_type=jnp.float32
    ).astype(out.dtype)


def products(context, gathered):
    halves, pair, lines, shard, depth = gathered.shape
    rows, count, width = context.shape[0], halves * lines, pair * shard
    return pl.pallas_call(
        product_kernel,
        grid=(count,),
        in_specs=[
            pl.BlockSpec((rows, depth), lambda d: (0, 0)),
            pl.BlockSpec((1, pair, 1, shard, depth), lambda d: (d % 2, 0, d // 2, 0, 0)),
        ],
        out_specs=pl.BlockSpec((1, rows, width), lambda d: (d, 0, 0)),
        out_shape=jax.ShapeDtypeStruct((count, rows, width), jnp.bfloat16),
        compiler_params=pltpu.CompilerParams(vmem_limit_bytes=24 << 20),
        cost_estimate=pl.CostEstimate(
            flops=2 * rows * depth * count * width,
            bytes_accessed=2 * (rows * depth + count * width * (rows + depth)),
            transcendentals=0,
        ),
    )(context, gathered)


def old_kernel(previous, ids, out, hot):
    images = previous.shape[0] // PATCHES
    out[...] = 0.5 * normed(previous[...].astype(jnp.float32), images)
    lane = lax.broadcasted_iota(jnp.int32, hot.shape, 1)
    hot[...] = jnp.where(lane == ids[...], 1.0, 0.0).astype(hot.dtype)


def final_kernel(summed, old, hot, predicted, targets, error):
    images = summed.shape[0] // PATCHES
    new = normed(summed[...].astype(jnp.float32), images)
    made = (0.5 * new + old[...]).astype(targets.dtype)
    targets[...] = made
    picked = jnp.dot(hot[...], made[:PATCHES], preferred_element_type=jnp.float32)
    error[...] = predicted[...].astype(jnp.float32) - picked


def on_device(context, out_weight, previous, section_act, fresh_batch, section_gains, mask_blocks):
    sections = lax.axis_size("section")
    position = lax.axis_index("section")
    rows, width = previous.shape
    act = section_act[0]
    incoming = lax.ppermute(act, "section", [(s, s + 1) for s in range(sections - 1)])
    shards = lax.all_gather(out_weight.T, "zlo", axis=0, tiled=False)
    gathered = lax.all_gather(shards, ("x", "core"), axis=0, tiled=False)
    predicted = lax.dynamic_slice_in_dim(act, (sections - 1) * width, width, 1)
    for s in range(sections - 1):
        piece = lax.ppermute(act[:, s * width:(s + 1) * width], "section", [(sections - 1, s)])
        predicted = jnp.where(position == s, piece, predicted)

    current = jnp.where(position == 0, fresh_batch, incoming)
    wide = current.astype(jnp.float32)
    own = jnp.sum(wide * wide, axis=-1)
    squares = own + lax.ppermute(own, "tensor", [(0, 1), (1, 0)])
    features = act.shape[-1] * lax.axis_size("tensor")
    scaling = lax.rsqrt(squares[:, None] / features + 1e-06)
    section_out = (wide * scaling * section_gains).astype(jnp.bfloat16)[None]

    gathered, section_out, predicted = lax.optimization_barrier((gathered, section_out, predicted))
    gathered = gathered.reshape(2, 4, *shards.shape)
    partial = products(context, gathered)
    summed = lax.psum_scatter(partial, "section", scatter_dimension=0, tiled=False)

    ids = masked_patches(mask_blocks[0]).reshape(-1, 1)
    old, hot = pl.pallas_call(
        old_kernel,
        out_shape=(
            jax.ShapeDtypeStruct((rows, width), jnp.float32),
            jax.ShapeDtypeStruct((ids.shape[0], PATCHES), jnp.bfloat16),
        ),
    )(previous, ids)
    targets, target_error = pl.pallas_call(
        final_kernel,
        out_shape=(
            jax.ShapeDtypeStruct((rows, width), jnp.bfloat16),
            jax.ShapeDtypeStruct((ids.shape[0], width), jnp.float32),
        ),
    )(summed, old, hot, predicted)
    return (targets, section_out, target_error)


def solution(mesh):
    fine = Mesh(mesh.devices.reshape(8, 4, 4, 2, 2), AXES)
    in_specs = (
        P(DP, "section"),
        P("section", ("tensor",) + DP),
        P(DP, ("tensor", "section")),
        P("section", DP, "tensor"),
        P(DP, "tensor"),
        P("section", "tensor"),
        P(DP, None),
    )
    out_specs = (
        P(DP, ("tensor", "section")),
        P("section", DP, "tensor"),
        P(DP, ("tensor", "section")),
    )
    return jax.shard_map(
        on_device, mesh=fine, in_specs=in_specs, out_specs=out_specs, check_vma=False
    )
```

time: 234 us -> 141 us (0.60)
  waiting for transfers between devices: 187 us -> 67.4 us
  starting transfers between devices: 3.39 us -> 19 us
  blocking collectives: 8.36 us -> 19.6 us
  Pallas kernels: 0 us -> 11 us
  other arithmetic: 12.4 us -> 2.86 us
  matrix products: 6.33 us -> 0 us
  local copies, waits for them, and re-layouts: 1.91 us -> 4.69 us
    psum x1 -> x0, waiting for transfers between devices: 74.2 us -> none  [on_device(): summed = lax.psum(partial_sum, 'section').astype(jnp.float32)]
    all_gather x1, waiting for transfers between devices: 73.9 us -> 1.2 us  [on_device(): gathered = lax.all_gather(shards, ('x', 'core'), axis=0, tiled=False)]
    reduce_scatter x0 -> x1, waiting for transfers between devices: none -> 45.7 us  [on_device(): lax.psum_scatter(partial, 'section', scatter_dimension=0, tiled=False)]
    all_gather x0 -> x1, blocking collectives: none -> 19.6 us  [on_device(): shards = lax.all_gather(out_weight.T, 'zlo', axis=0, tiled=False)]
    ppermute x1 -> x9, waiting for transfers between devices: 38.2 us -> 20.5 us  [the longest x1 20.4 us: on_device(): lax.ppermute(act, 'section', [(s, s + 1) for s in range(sections - 1)])]
    ppermute x1 -> x9, starting transfers between devices: 3.32 us -> 18.9 us  [the longest x1 7.96 us: on_device(): squares = own + lax.ppermute(own, 'tensor', [(0, 1), (1, 0)])]
    pallas_call x0 -> x3, Pallas kernels: none -> 11 us  [the longest x1 6.26 us: products(): pl.pallas_call(product_kernel, grid=(count,), in_specs=[pl.BlockSpec((row...]
    psum x1 -> x0, blocking collectives: 8.36 us -> none  [on_device(): squares = lax.psum(jnp.sum(current * current, axis=-1), 'tensor')]
  transfers between devices with their start and end apart: 3 -> 11, of which waited for: 3 -> 4; matrix products, arithmetic and copies ran while one was open for 3% -> 3% of each run, Pallas kernels for 0% -> 2%
where the time goes in v1:
time: 141 us; the launch traced here: 139 us
  waiting for transfers between devices  67.4 us (48%)
  blocking collectives  19.6 us (14%)
  starting transfers between devices  19 us (13%)
  between operations  14.2 us (10%)
  Pallas kernels  11 us (8%)
  local copies, waits for them, and re-layouts  4.69 us (3%)
  other arithmetic  2.86 us (2%)
    reduce_scatter x1, waiting for transfers between devices, on_device(): lax.psum_scatter(partial, 'section', scatter_dimension=0, tiled=False)  45.7 us
    ppermute x1, waiting for transfers between devices, on_device(): lax.ppermute(act, 'section', [(s, s + 1) for s in range(sections - 1)])  20.4 us
    all_gather x1, blocking collectives, on_device(): shards = lax.all_gather(out_weight.T, 'zlo', axis=0, tiled=False)  19.6 us
    ppermute x1, starting transfers between devices, on_device(): squares = own + lax.ppermute(own, 'tensor', [(0, 1), (1, 0)])  7.96 us
    ppermute x7, starting transfers between devices, on_device(): lax.ppermute(act[:, s * width:(s + 1) * width], 'section', [(sections - 1...  7.91 us
    pallas_call x1, Pallas kernels, products(): pl.pallas_call(product_kernel, grid=(count,), in_specs=[pl.BlockSpec((row...  6.26 us
    ppermute x1, starting transfers between devices, on_device(): lax.ppermute(act, 'section', [(s, s + 1) for s in range(sections - 1)])  3.06 us
    unnamed x12, local copies, waits for them, and re-layouts  2.98 us
  transfers between devices with their start and end apart: 11, of which 4 were waited for; matrix products, arithmetic and copies ran while one was open for 3% of the time, Pallas kernels for 2%

profile of v1, /device:TPU:1, one launch (start us, length us, event | category | flops | bytes accessed | tf_op | source)
XLA Modules:
  0.0 138.8 jit_solution(16138804924249262113)
XLA Ops:
  7.2 0.0 copy-start.3
  7.2 0.0 all-gather.4.cloned.1.call-start
  7.2 19.6 %all-gather = bf16[384,768]{1,0:T(8,128)(2,1)} all-gather(bf16[96,768]{1,0:T(8,128)(2,1)} %bitcast.32), channel_id=2, replica_groups=mesh['section'=8,'zlo'=4,'x'=4,'core'=2,'tensor'=2] {'zlo'}, dimensions={0}, use_global_device_ids=true | all-gather | bytes 737280 | tf_op jit(solution)/shard_map/all_gather | solution.py:82
  26.8 0.0 all-gather.4.cloned.1.call-update
  26.8 0.0 copy-start.2
  26.8 0.0 reduce-scatter.2.cloned.1.call-start
  26.9 0.0 copy-done.3
  26.9 3.1 %collective-permute-start = (bf16[192,3072]{1,0:T(8,128)(2,1)S(1)}, bf16[192,3072]{1,0:T(8,128)(2,1)S(1)}, u32[]{:S(2)}, u32[]{:S(2)}) collective-permute-start(bf16[192,3072]{1,0:T(8,128)(2,1)S(1)} %bitcast.28), channel_id=1, source_target_pairs={{0,64},{64,128},{128,192},{192,256},{256,320},{320,384},{384,448},... | collective-permute-start | bytes 3538952 | tf_op jit(solution)/shard_map/ppermute | solution.py:81
  30.0 1.0 fusion.12
  30.9 1.3 collective-permute-start.2
  32.3 1.3 collective-permute-start.3
  33.6 1.3 collective-permute-start.4
  34.9 1.3 collective-permute-start.5
  36.2 0.0 collective-permute-done.2
  36.2 0.7 collective-permute-start.6
  36.9 0.0 collective-permute-done.3
  36.9 0.7 collective-permute-start.7
  37.6 20.4 %collective-permute-done = bf16[192,3072]{1,0:T(8,128)(2,1)S(1)} collective-permute-done((bf16[192,3072]{1,0:T(8,128)(2,1)S(1)}, bf16[192,3072]{1,0:T(8,128)(2,1)S(1)}, u32[]{:S(2)}, u32[]{:S(2)}) %collective-permute-start) | collective-permute-done | bytes 1179680 | tf_op jit(solution)/shard_map/ppermute | solution.py:81
  58.0 1.3 collective-permute-start.8
  59.2 0.0 copy-done.2
  59.3 0.5 fusion
  59.7 0.0 copy-start.4
  59.7 0.0 collective-permute-done.4
  59.7 8.0 %collective-permute-start.1 = (f32[192]{0:T(256)S(1)}, f32[192]{0:T(256)S(1)}, u32[]{:S(2)}, u32[]{:S(2)}) collective-permute-start(f32[192]{0:T(256)S(1)} %fusion), channel_id=1, source_target_pairs={{0,1},{1,0},{2,3},{3,2},{4,5},{5,4},{6,7},{7,6},{8,9},{9,8},{10,11... | collective-permute-start | bytes 2312 | tf_op jit(solution)/shard_map/ppermute | solution.py:92
  67.7 0.0 collective-permute-done.5
  67.7 0.0 collective-permute-done.6
  67.7 0.0 collective-permute-done.7
  67.7 0.0 collective-permute-done.8
  67.8 0.8 fusion.9.predicted
  68.5 0.1 collective-permute-done.1
  68.7 0.0 copy-done.4
  68.7 0.0 copy-start.1
  68.7 1.5 %fusion.3 = bf16[1,192,3072]{2,1,0:T(8,128)(2,1)} fusion(f32[3072]{0:T(1024)S(1)} %bitcast.33, f32[192]{0:T(256)S(1)} %add_rsqrt_fusion, bf16[192,3072]{1,0:T(8,128)(2,1)S(1)} %copy-done.2, bf16[192,3072]{1,0:T(8,128)(2,1)S(1)} %collective-permute-done, pred[]{:T(512)S(6)} %eq.26), kind=kLoop, calls=%fused_computation.5 | loop fusion | flops 2949120 | bytes 3552001 | tf_op jit(solution)/shard_map/broadcast_in_dim | solution.py:95
  70.2 1.2 all-gather.4.cloned.1.call-done
  71.4 0.0 copy-done.1
  71.4 0.0 copy-start
  71.4 2.3 %copy-done = bf16[32,96,768]{2,1,0:T(8,128)(2,1)S(1)} copy-done((bf16[32,96,768]{2,1,0:T(8,128)(2,1)S(1)}, bf16[32,96,768]{2,1,0:T(8,128)(2,1)}, u32[]{:S(2)}) %copy-start) | copy-done | bytes 4718616
  73.7 6.3 %shard_map.94 = bf16[8,512,384]{2,1,0:T(8,128)(2,1)} custom-call(bf16[512,768]{1,0:T(8,128)(2,1)S(1)} %copy-done.1, bf16[2,4,4,96,768]{4,3,2,1,0:T(8,128)(2,1)S(1)} %bitcast.26), custom_call_target="tpu_custom_call" | custom-call | flops 2415919104 | bytes 8650752 | tf_op jit(solution)/shard_map/pallas_call | solution.py:42
  80.0 0.0 copy-start.5
  80.0 0.0 reduce-scatter.2.cloned.1.call-update
  80.0 0.6 copy-done.5
  80.7 0.1 add_add_fusion
  80.7 0.7 add.112.ids
  81.5 2.3 %shard_map.95 = (f32[512,384]{1,0:T(8,128)}, bf16[192,256]{1,0:T(8,128)(2,1)}) custom-call(bf16[512,384]{1,0:T(8,128)(2,1)} %previous.1, s32[192,1]{1,0:T(8,128)} %add.112.ids), custom_call_target="tpu_custom_call" | custom-call | tf_op jit(solution)/shard_map/pallas_call | solution.py:103
  83.7 45.7 %reduce-scatter.2.cloned.1.call-done = bf16[1,512,384]{2,1,0:T(8,128)(2,1)} async-done(((bf16[8,512,384]{2,1,0:T(8,128)(2,1)}), bf16[1,512,384]{2,1,0:T(8,128)(2,1)}) %reduce-scatter.2.cloned.1.call-update) | async-done | bytes 393232 | tf_op jit(solution)/shard_map/reduce_scatter | solution.py:100
  129.4 2.5 %shard_map.96 = (bf16[512,384]{1,0:T(8,128)(2,1)}, f32[192,384]{1,0:T(8,128)}) custom-call(bf16[512,384]{1,0:T(8,128)(2,1)} %bitcast.31, f32[512,384]{1,0:T(8,128)} %get-tuple-element.11.old, bf16[192,256]{1,0:T(8,128)(2,1)} %get-tuple-element.12.hot, bf16[192,384]{1,0:T(8,128)(2,1)} %fusion.9.predicted), custom_call_target="tpu_custom_call" | custom-call | tf_op jit(solution)/shard_map/pallas_call | solution.py:110
  (3 shorter events, 0.0 us)
Async XLA Ops:
  7.2 19.7 %copy-start.3 = (bf16[1,192,3072]{2,1,0:T(8,128)(2,1)S(1)}, bf16[1,192,3072]{2,1,0:T(8,128)(2,1)}, u32[]{:S(2)}) copy-start(bf16[1,192,3072]{2,1,0:T(8,128)(2,1)} %param.10) | copy-start | bytes 3538948
  7.2 64.2 %all-gather.4.cloned.1.call-start = ((), (), s32[]{:S(2)}) async-start(), calls=%async_computation.2 | async-start | bytes 5308416 | tf_op jit(solution)/shard_map/all_gather | solution.py:83
  26.8 32.4 %copy-start.2 = (bf16[192,3072]{1,0:T(8,128)(2,1)S(1)}, bf16[192,3072]{1,0:T(8,128)(2,1)}, u32[]{:S(2)}) copy-start(bf16[192,3072]{1,0:T(8,128)(2,1)} %param.11) | copy-start | bytes 3538948
  26.8 102.6 %reduce-scatter.2.cloned.1.call-start = ((), (), s32[]{:S(2)}) async-start(), calls=%async_computation.1 | async-start | bytes 3538944 | tf_op jit(solution)/shard_map/reduce_scatter | solution.py:100
  26.9 31.1 %collective-permute-start = (bf16[192,3072]{1,0:T(8,128)(2,1)S(1)}, bf16[192,3072]{1,0:T(8,128)(2,1)S(1)}, u32[]{:S(2)}, u32[]{:S(2)}) collective-permute-start(bf16[192,3072]{1,0:T(8,128)(2,1)S(1)} %bitcast.28), channel_id=1, source_target_pairs={{0,64},{64,128},{128,192},{192,256},{256,320},{320,384},{384,448},... | collective-permute-start | bytes 3538952 | tf_op jit(solution)/shard_map/ppermute | solution.py:81
  30.9 5.3 %collective-permute-start.2 = (bf16[192,384]{1,0:T(8,128)(2,1)}, bf16[192,384]{1,0:T(8,128)(2,1)}, u32[]{:S(2)}, u32[]{:S(2)}) collective-permute-start(bf16[192,384]{1,0:T(8,128)(2,1)} %get-tuple-element.23), channel_id=1, source_target_pairs={{448,384},{449,385},{450,386},{451,387},{452,388},{453,389},{454,3... | collective-permute-start | bytes 442376 | tf_op jit(solution)/shard_map/ppermute | solution.py:86
  32.3 4.6 %collective-permute-start.3 = (bf16[192,384]{1,0:T(8,128)(2,1)}, bf16[192,384]{1,0:T(8,128)(2,1)}, u32[]{:S(2)}, u32[]{:S(2)}) collective-permute-start(bf16[192,384]{1,0:T(8,128)(2,1)} %get-tuple-element.22), channel_id=1, source_target_pairs={{448,320},{449,321},{450,322},{451,323},{452,324},{453,325},{454,3... | collective-permute-start | bytes 442376 | tf_op jit(solution)/shard_map/ppermute | solution.py:86
  33.6 26.1 %collective-permute-start.4 = (bf16[192,384]{1,0:T(8,128)(2,1)}, bf16[192,384]{1,0:T(8,128)(2,1)}, u32[]{:S(2)}, u32[]{:S(2)}) collective-permute-start(bf16[192,384]{1,0:T(8,128)(2,1)} %get-tuple-element.21), channel_id=1, source_target_pairs={{448,256},{449,257},{450,258},{451,259},{452,260},{453,261},{454,2... | collective-permute-start | bytes 442376 | tf_op jit(solution)/shard_map/ppermute | solution.py:86
  34.9 32.8 %collective-permute-start.5 = (bf16[192,384]{1,0:T(8,128)(2,1)}, bf16[192,384]{1,0:T(8,128)(2,1)}, u32[]{:S(2)}, u32[]{:S(2)}) collective-permute-start(bf16[192,384]{1,0:T(8,128)(2,1)} %get-tuple-element.20), channel_id=1, source_target_pairs={{448,192},{449,193},{450,194},{451,195},{452,196},{453,197},{454,1... | collective-permute-start | bytes 442376 | tf_op jit(solution)/shard_map/ppermute | solution.py:86
  36.2 31.5 %collective-permute-start.6 = (bf16[192,384]{1,0:T(8,128)(2,1)}, bf16[192,384]{1,0:T(8,128)(2,1)S(1)}, u32[]{:S(2)}, u32[]{:S(2)}) collective-permute-start(bf16[192,384]{1,0:T(8,128)(2,1)} %get-tuple-element.19), channel_id=1, source_target_pairs={{448,128},{449,129},{450,130},{451,131},{452,132},{453,133},{454,1... | collective-permute-start | bytes 442376 | tf_op jit(solution)/shard_map/ppermute | solution.py:86
  36.9 30.8 %collective-permute-start.7 = (bf16[192,384]{1,0:T(8,128)(2,1)}, bf16[192,384]{1,0:T(8,128)(2,1)S(1)}, u32[]{:S(2)}, u32[]{:S(2)}) collective-permute-start(bf16[192,384]{1,0:T(8,128)(2,1)} %get-tuple-element.18), channel_id=1, source_target_pairs={{448,64},{449,65},{450,66},{451,67},{452,68},{453,69},{454,70},{45... | collective-permute-start | bytes 442376 | tf_op jit(solution)/shard_map/ppermute | solution.py:86
  58.0 9.8 %collective-permute-start.8 = (bf16[192,384]{1,0:T(8,128)(2,1)}, bf16[192,384]{1,0:T(8,128)(2,1)S(1)}, u32[]{:S(2)}, u32[]{:S(2)}) collective-permute-start(bf16[192,384]{1,0:T(8,128)(2,1)} %get-tuple-element.17), channel_id=1, source_target_pairs={{448,0},{449,1},{450,2},{451,3},{452,4},{453,5},{454,6},{455,7},{4... | collective-permute-start | bytes 442376 | tf_op jit(solution)/shard_map/ppermute | solution.py:86
  59.7 8.9 %copy-start.4 = (f32[1,3072]{1,0:T(1,128)S(1)}, f32[1,3072]{1,0:T(1,128)}, u32[]{:S(2)}) copy-start(f32[1,3072]{1,0:T(1,128)} %param.12) | copy-start | bytes 36868
  59.7 8.9 %collective-permute-start.1 = (f32[192]{0:T(256)S(1)}, f32[192]{0:T(256)S(1)}, u32[]{:S(2)}, u32[]{:S(2)}) collective-permute-start(f32[192]{0:T(256)S(1)} %fusion), channel_id=1, source_target_pairs={{0,1},{1,0},{2,3},{3,2},{4,5},{5,4},{6,7},{7,6},{8,9},{9,8},{10,11... | collective-permute-start | bytes 2312 | tf_op jit(solution)/shard_map/ppermute | solution.py:92
  68.7 2.7 %copy-start.1 = (bf16[512,768]{1,0:T(8,128)(2,1)S(1)}, bf16[512,768]{1,0:T(8,128)(2,1)}, u32[]{:S(2)}) copy-start(bf16[512,768]{1,0:T(8,128)(2,1)} %context.1) | copy-start | bytes 2359300
  71.4 2.3 %copy-start = (bf16[32,96,768]{2,1,0:T(8,128)(2,1)S(1)}, bf16[32,96,768]{2,1,0:T(8,128)(2,1)}, u32[]{:S(2)}) copy-start(bf16[32,96,768]{2,1,0:T(8,128)(2,1)} %all-gather.4.cloned.1.call-done) | copy-start | bytes 14155780
  80.0 0.7 copy-start.5
Sparse Core Ops, SparseCore 0:
  27.0 44.3 all-gather.3
  80.1 49.2 reduce-scatter.1

commit v2 on v1

v2 whole, which is shorter than its diff:
```python
import jax
import jax.numpy as jnp
from jax import lax
from jax.experimental import pallas as pl
from jax.experimental.pallas import tpu as pltpu
from jax.sharding import Mesh, PartitionSpec as P

GRID_SIDE = 16
BLOCK_SIDE = 4
PATCHES = 256
AXES = ("section", "zlo", "x", "core", "tensor")
DP = ("zlo", "x", "core")
FIRST = 40


def masked_patches(mask_blocks):
    per_side = GRID_SIDE // BLOCK_SIDE
    within = jnp.arange(BLOCK_SIDE * BLOCK_SIDE, dtype=jnp.int32)
    chosen = mask_blocks[..., None]
    grid_row = chosen // per_side * BLOCK_SIDE + within // BLOCK_SIDE
    grid_col = chosen % per_side * BLOCK_SIDE + within % BLOCK_SIDE
    return grid_row * GRID_SIDE + grid_col


def normed(values, images):
    shaped = values.reshape(images, -1, values.shape[-1])
    center = jnp.mean(shaped, axis=1, keepdims=True)
    off = shaped - center
    spread = jnp.mean(jnp.square(off), axis=1, keepdims=True)
    return (off * lax.rsqrt(spread + 1e-05)).reshape(values.shape)


def product_kernel(context, mine, other, rest, out):
    pieces = []
    for half in range(2):
        small, large = mine.shape[1] // 2, rest.shape[2] // 2
        pieces.append(mine[0, half * small:(half + 1) * small])
        pieces.append(other[0, half * small:(half + 1) * small])
        pieces.append(rest[0, 0, half * large:(half + 1) * large])
        pieces.append(rest[0, 1, half * large:(half + 1) * large])
    made = lax.dot_general(
        context[...],
        jnp.concatenate(pieces, axis=0),
        (((1,), (1,)), ((), ())),
        preferred_element_type=jnp.float32,
    ).astype(out.dtype)
    width = out.shape[-1]
    out[0] = made[:, :width]
    out[1] = made[:, width:]


def products(context, mine, other, rest):
    rows, depth = context.shape
    lines, small, _ = mine.shape
    large = rest.shape[2]
    width = small + large
    return pl.pallas_call(
        product_kernel,
        grid=(lines,),
        in_specs=[
            pl.BlockSpec((rows, depth), lambda z: (0, 0)),
            pl.BlockSpec((1, small, depth), lambda z: (z, 0, 0)),
            pl.BlockSpec((1, small, depth), lambda z: (z, 0, 0)),
            pl.BlockSpec((1, 2, large, depth), lambda z: (z, 0, 0, 0)),
        ],
        out_specs=pl.BlockSpec((2, rows, width), lambda z: (z, 0, 0)),
        out_shape=jax.ShapeDtypeStruct((2 * lines, rows, width), jnp.bfloat16),
        compiler_params=pltpu.CompilerParams(vmem_limit_bytes=56 << 20),
        cost_estimate=pl.CostEstimate(
            flops=4 * rows * depth * lines * width,
            bytes_accessed=2 * (rows * depth + 2 * lines * width * (rows + depth)),
            transcendentals=0,
        ),
    )(context, mine, other, rest)


def column_order(core, shard):
    pair = jnp.arange(2)[:, None]
    early, late = jnp.arange(FIRST), jnp.arange(FIRST, shard)
    place = lambda held, columns: (pair * 2 * shard + held * shard + columns).reshape(-1)
    return jnp.concatenate(
        [place(core, early), place(1 - core, early), place(0, late), place(1, late)]
    ).astype(jnp.int32)


def ready_kernel(previous, ids, order, out, hot, moved):
    images = previous.shape[0] // PATCHES
    out[...] = 0.5 * normed(previous[...].astype(jnp.float32), images)
    for table, index in ((hot, ids), (moved, order)):
        lane = lax.broadcasted_iota(jnp.int32, table.shape, 1)
        table[...] = jnp.where(lane == index[...], 1.0, 0.0).astype(table.dtype)


def final_kernel(summed, old, hot, moved, predicted, targets, error):
    images = summed.shape[0] // PATCHES
    ordered = jnp.dot(summed[...], moved[...], preferred_element_type=jnp.float32)
    made = (0.5 * normed(ordered, images) + old[...]).astype(targets.dtype)
    targets[...] = made
    picked = jnp.dot(hot[...], made[:PATCHES], preferred_element_type=jnp.float32)
    error[...] = predicted[...].astype(jnp.float32) - picked


def on_device(context, out_weight, previous, section_act, fresh_batch, section_gains, mask_blocks):
    sections = lax.axis_size("section")
    position = lax.axis_index("section")
    rows, width = previous.shape
    act = section_act[0]
    depth, shard = out_weight.shape
    incoming = lax.ppermute(act, "section", [(s, (s + 1) % sections) for s in range(sections)])

    group = lax.all_gather(out_weight.T, "x", axis=0, tiled=False)
    early = group[:, :FIRST].reshape(-1, depth)
    late = group[:, FIRST:].reshape(-1, depth)
    rest = lax.all_gather(late, ("zlo", "core"), axis=0, tiled=False)
    mine = lax.all_gather(early, "zlo", axis=0, tiled=False)
    other = lax.ppermute(mine, "core", [(0, 1), (1, 0)])
    rest, other, incoming = lax.optimization_barrier((rest, other, incoming))
    rest = rest.reshape(-1, 2, *late.shape)
    partial = products(context, mine, other, rest)
    summed = lax.psum_scatter(partial, "section", scatter_dimension=0, tiled=False)

    held = jnp.where(position == 0, incoming, act)
    share = lambda s: lax.dynamic_slice_in_dim(held, s * width, width, 1)
    predicted = share(position)
    for hop in range(1, sections // 2):
        last = sections - 1
        piece = lax.ppermute(
            share(jnp.where(position == 0, hop, last - hop)),
            "section",
            [(0, hop), (last, last - hop)],
        )
        here = (position == hop) | (position == last - hop)
        predicted = jnp.where(here, piece, predicted)

    current = jnp.where(position == 0, fresh_batch, incoming)
    wide = current.astype(jnp.float32)
    own = jnp.sum(wide * wide, axis=-1)
    squares = own + lax.ppermute(own, "tensor", [(0, 1), (1, 0)])
    features = act.shape[-1] * lax.axis_size("tensor")
    scaling = lax.rsqrt(squares[:, None] / features + 1e-06)
    section_out = (wide * scaling * section_gains).astype(jnp.bfloat16)[None]

    ids = masked_patches(mask_blocks[0]).reshape(-1, 1)
    order = column_order(lax.axis_index("core"), shard).reshape(-1, 1)
    old, hot, moved = pl.pallas_call(
        ready_kernel,
        out_shape=(
            jax.ShapeDtypeStruct((rows, width), jnp.float32),
            jax.ShapeDtypeStruct((ids.shape[0], PATCHES), jnp.bfloat16),
            jax.ShapeDtypeStruct((width, width), jnp.bfloat16),
        ),
    )(previous, ids, order)
    targets, target_error = pl.pallas_call(
        final_kernel,
        out_shape=(
            jax.ShapeDtypeStruct((rows, width), jnp.bfloat16),
            jax.ShapeDtypeStruct((ids.shape[0], width), jnp.float32),
        ),
    )(summed, old, hot, moved, predicted)
    return (targets, section_out, target_error)


def solution(mesh):
    fine = Mesh(mesh.devices.reshape(8, 4, 4, 2, 2), AXES)
    in_specs = (
        P(DP, "section"),
        P("section", ("tensor",) + DP),
        P(DP, ("tensor", "section")),
        P("section", DP, "tensor"),
        P(DP, "tensor"),
        P("section", "tensor"),
        P(DP, None),
    )
    out_specs = (
        P(DP, ("tensor", "section")),
        P("section", DP, "tensor"),
        P(DP, ("tensor", "section")),
    )
    return jax.shard_map(
        on_device, mesh=fine, in_specs=in_specs, out_specs=out_specs, check_vma=False
    )
```

time: 141 us -> 148 us (1.050)
  waiting for transfers between devices: 67.4 us -> 45.9 us
  starting transfers between devices: 19 us -> 34 us
  blocking collectives: 19.6 us -> 32.9 us
    reduce_scatter x1, waiting for transfers between devices: 45.7 us -> 14.7 us  [on_device(): lax.psum_scatter(partial, 'section', scatter_dimension=0, tiled=False)]
    ppermute x8 -> x5, starting transfers between devices: 11 us -> 25 us  [the longest x1 11.6 us: on_device(): other = lax.ppermute(mine, 'core', [(0, 1), (1, 0)])]
    all_gather x1 -> x2, blocking collectives: 19.6 us -> 32.9 us  [the longest x1 21.4 us: on_device(): mine = lax.all_gather(early, 'zlo', axis=0, tiled=False)]
    all_gather x1, waiting for transfers between devices: 1.2 us -> 14.5 us  [on_device(): rest = lax.all_gather(late, ('zlo', 'core'), axis=0, tiled=False)]
    ppermute x8 -> x5, waiting for transfers between devices: 20.4 us -> 16.7 us  [the longest x3 14.6 us: on_device(): lax.ppermute(share(jnp.where(position == 0, hop, last - hop)), 'section',...]
    unnamed x12, local copies, waits for them, and re-layouts: 2.98 us -> 0.6 us
  transfers between devices with their start and end apart: 11 -> 8, of which waited for: 4 -> 6; matrix products, arithmetic and copies ran while one was open for 3% -> 4% of each run, Pallas kernels for 2% -> 2%
where the time goes in v2:
time: 148 us; the launch traced here: 147 us
  waiting for transfers between devices  45.9 us (31%)
  starting transfers between devices  34 us (23%)
  blocking collectives  32.9 us (22%)
  between operations  14.2 us (10%)
  Pallas kernels  12.1 us (8%)
  local copies, waits for them, and re-layouts  3.98 us (3%)
  other arithmetic  3.83 us (3%)
    all_gather x1, blocking collectives, on_device(): mine = lax.all_gather(early, 'zlo', axis=0, tiled=False)  21.4 us
    reduce_scatter x1, waiting for transfers between devices, on_device(): lax.psum_scatter(partial, 'section', scatter_dimension=0, tiled=False)  14.7 us
    ppermute x3, waiting for transfers between devices, on_device(): lax.ppermute(share(jnp.where(position == 0, hop, last - hop)), 'section',...  14.6 us
    all_gather x1, waiting for transfers between devices, on_device(): rest = lax.all_gather(late, ('zlo', 'core'), axis=0, tiled=False)  14.5 us
    ppermute x1, starting transfers between devices, on_device(): other = lax.ppermute(mine, 'core', [(0, 1), (1, 0)])  11.6 us
    all_gather x1, blocking collectives, on_device(): group = lax.all_gather(out_weight.T, 'x', axis=0, tiled=False)  11.6 us
    ppermute x1, starting transfers between devices, on_device(): squares = own + lax.ppermute(own, 'tensor', [(0, 1), (1, 0)])  8.96 us
    ppermute x3, starting transfers between devices, on_device(): lax.ppermute(share(jnp.where(position == 0, hop, last - hop)), 'section',...  8.92 us
  transfers between devices with their start and end apart: 8, of which 6 were waited for; matrix products, arithmetic and copies ran while one was open for 4% of the time, Pallas kernels for 2%

profile of v2, /device:TPU:1, one launch (start us, length us, event | category | flops | bytes accessed | tf_op | source)
XLA Modules:
  0.0 146.9 jit_solution(706365807305729275)
XLA Ops:
  7.2 0.0 copy-start.1
  7.2 0.0 all-gather.3.cloned.1.call-start
  7.2 11.6 %all-gather = bf16[384,768]{1,0:T(8,128)(2,1)S(1)} all-gather(bf16[96,768]{1,0:T(8,128)(2,1)} %bitcast.34), channel_id=2, replica_groups=mesh['section'=8,'zlo'=4,'x'=4,'core'=2,'tensor'=2] {'x'}, dimensions={0}, use_global_device_ids=true | all-gather | bytes 737280 | tf_op jit(solution)/shard_map/all_gather | solution.py:111
  18.8 0.8 slice.9
  19.5 0.0 all-gather.3.cloned.1.call-update
  19.6 0.0 reduce-scatter.2.cloned.1.call-start
  19.6 0.0 copy-done.1
  19.6 4.5 %collective-permute-start.1 = (bf16[192,3072]{1,0:T(8,128)(2,1)S(1)}, bf16[192,3072]{1,0:T(8,128)(2,1)S(1)}, u32[]{:S(2)}, u32[]{:S(2)}) collective-permute-start(bf16[192,3072]{1,0:T(8,128)(2,1)S(1)} %bitcast.31), channel_id=1, source_target_pairs={{0,64},{64,128},{128,192},{192,256},{256,320},{320,384},{384,448},... | collective-permute-start | bytes 3538952 | tf_op jit(solution)/shard_map/ppermute | solution.py:109
  24.1 21.4 %all_gather.14.mine = bf16[4,160,768]{2,1,0:T(8,128)(2,1)S(1)} all-gather(bf16[1,160,768]{2,1,0:T(8,128)(2,1)S(1)} %bitcast.32), channel_id=1, replica_groups=mesh['section'=8,'zlo'=4,'x'=4,'core'=2,'tensor'=2] {'zlo'}, dimensions={0}, use_global_device_ids=true | all-gather | bytes 1228800 | tf_op jit(solution)/shard_map/all_gather | solution.py:115
  45.5 0.0 copy-start.2
  45.5 11.6 %collective-permute-start = (bf16[4,160,768]{2,1,0:T(8,128)(2,1)S(1)}, bf16[4,160,768]{2,1,0:T(8,128)(2,1)S(1)}, u32[]{:S(2)}, u32[]{:S(2)}) collective-permute-start(bf16[4,160,768]{2,1,0:T(8,128)(2,1)S(1)} %all_gather.14.mine), channel_id=1, source_target_pairs={{0,2},{2,0},{1,3},{3,1},{4,6},{6,4},{5,7},{7,5},{8,10},{10,8},{9,1... | collective-permute-start | bytes 2949128 | tf_op jit(solution)/shard_map/ppermute | solution.py:116
  57.1 0.0 copy-done.2
  57.1 2.2 %collective-permute-done.other = bf16[4,160,768]{2,1,0:T(8,128)(2,1)S(1)} collective-permute-done((bf16[4,160,768]{2,1,0:T(8,128)(2,1)S(1)}, bf16[4,160,768]{2,1,0:T(8,128)(2,1)S(1)}, u32[]{:S(2)}, u32[]{:S(2)}) %collective-permute-start) | collective-permute-done | bytes 983072 | tf_op jit(solution)/shard_map/ppermute | solution.py:116
  59.3 0.0 copy-start.4
  59.3 0.0 collective-permute-done.1
  59.3 14.5 %all-gather.3.cloned.1.call-done = bf16[8,224,768]{2,1,0:T(8,128)(2,1)} async-done(((bf16[1,224,768]{2,1,0:T(8,128)(2,1)}), bf16[8,224,768]{2,1,0:T(8,128)(2,1)}) %all-gather.3.cloned.1.call-update) | async-done | bytes 2752528 | tf_op jit(solution)/shard_map/all_gather | solution.py:114
  73.8 0.0 copy-done.4
  73.8 6.7 %shard_map.94 = bf16[8,512,384]{2,1,0:T(8,128)(2,1)} custom-call(bf16[512,768]{1,0:T(8,128)(2,1)} %context.1, bf16[4,160,768]{2,1,0:T(8,128)(2,1)} %copy-done.2, bf16[4,160,768]{2,1,0:T(8,128)(2,1)} %copy-done.4, bf16[4,2,224,768]{3,2,1,0:T(8,128)(2,1)} %bitcast.36), custom_call_target="tpu_custom_call" | custom-call | flops 2415919104 | bytes 8650752 | tf_op jit(solution)/shard_map/pallas_call | solution.py:57
  80.5 0.0 copy-start.5
  80.5 0.0 copy-start
  80.5 0.0 reduce-scatter.2.cloned.1.call-update
  80.6 0.6 copy-done.5
  81.2 0.1 add_add_fusion
  81.2 0.7 add.260.ids
  82.0 0.1 broadcast_add_fusion.1
  82.1 0.1 add.252
  82.2 0.1 add.248
  82.2 0.1 iota_add_fusion
  82.3 0.1 add.242
  82.4 0.6 iota_add_fusion.1
  83.0 0.8 add.236
  83.8 0.1 pad_add_fusion
  83.9 0.8 reshape.220.order
  84.7 2.4 %shard_map.95 = (f32[512,384]{1,0:T(8,128)}, bf16[192,256]{1,0:T(8,128)(2,1)}, bf16[384,384]{1,0:T(8,128)(2,1)}) custom-call(bf16[512,384]{1,0:T(8,128)(2,1)} %previous.1, s32[192,1]{1,0:T(8,128)} %add.260.ids, s32[384,1]{1,0:T(8,128)} %reshape.220.order), custom_call_target="tpu_custom_call" | custom-call | tf_op jit(solution)/shard_map/pallas_call | solution.py:145
  87.1 0.0 copy-done
  87.1 0.5 fusion
  87.6 0.0 copy-start.3
  87.6 9.0 %collective-permute-start.5 = (f32[192]{0:T(256)S(1)}, f32[192]{0:T(256)S(1)}, u32[]{:S(2)}, u32[]{:S(2)}) collective-permute-start(f32[192]{0:T(256)S(1)} %fusion), channel_id=1, source_target_pairs={{0,1},{1,0},{2,3},{3,2},{4,5},{5,4},{6,7},{7,6},{8,9},{9,8},{10,11... | collective-permute-start | bytes 2312 | tf_op jit(solution)/shard_map/ppermute | solution.py:138
  96.5 0.1 broadcast_select_fusion.1
  96.7 0.1 constant_dynamic-slice_fusion
  96.7 6.3 %collective-permute-start.2 = (bf16[192,384]{1,0:T(8,128)(2,1)S(1)}, bf16[192,384]{1,0:T(8,128)(2,1)S(1)}, u32[]{:S(2)}, u32[]{:S(2)}) collective-permute-start(bf16[192,384]{1,0:T(8,128)(2,1)S(1)} %get-tuple-element.21), channel_id=1, source_target_pairs={{0,192},{448,256},{1,193},{449,257},{2,194},{450,258},{3,195},{451... | collective-permute-start | bytes 442376 | tf_op jit(solution)/shard_map/ppermute | solution.py:127
  103.1 1.3 collective-permute-start.3
  104.4 1.3 collective-permute-start.4
  105.7 0.0 collective-permute-done.5
  105.7 0.0 copy-done.3
  105.7 1.5 %fusion.3 = bf16[1,192,3072]{2,1,0:T(8,128)(2,1)} fusion(f32[3072]{0:T(1024)S(1)} %bitcast.35, f32[192]{0:T(256)S(1)} %add_rsqrt_fusion, bf16[192,3072]{1,0:T(8,128)(2,1)S(1)} %copy-done, bf16[192,3072]{1,0:T(8,128)(2,1)S(1)} %collective-permute-done.1, pred[]{:T(512)S(6)} %eq.31), kind=kLoop, calls=%fused_computation.5 | loop fusion | flops 2949120 | bytes 3552001 | tf_op jit(solution)/shard_map/broadcast_in_dim | solution.py:141
  107.2 1.9 %collective-permute-done.2 = bf16[192,384]{1,0:T(8,128)(2,1)S(1)} collective-permute-done((bf16[192,384]{1,0:T(8,128)(2,1)S(1)}, bf16[192,384]{1,0:T(8,128)(2,1)S(1)}, u32[]{:S(2)}, u32[]{:S(2)}) %collective-permute-start.2) | collective-permute-done | bytes 147488 | tf_op jit(solution)/shard_map/ppermute | solution.py:127
  109.1 6.3 %collective-permute-done.3 = bf16[192,384]{1,0:T(8,128)(2,1)S(1)} collective-permute-done((bf16[192,384]{1,0:T(8,128)(2,1)S(1)}, bf16[192,384]{1,0:T(8,128)(2,1)S(1)}, u32[]{:S(2)}, u32[]{:S(2)}) %collective-permute-start.3) | collective-permute-done | bytes 147488 | tf_op jit(solution)/shard_map/ppermute | solution.py:127
  115.5 6.3 %collective-permute-done.4 = bf16[192,384]{1,0:T(8,128)(2,1)S(1)} collective-permute-done((bf16[192,384]{1,0:T(8,128)(2,1)S(1)}, bf16[192,384]{1,0:T(8,128)(2,1)S(1)}, u32[]{:S(2)}, u32[]{:S(2)}) %collective-permute-start.4) | collective-permute-done | bytes 147488 | tf_op jit(solution)/shard_map/ppermute | solution.py:127
  121.8 0.8 select_select_fusion.predicted
  122.5 14.7 %reduce-scatter.2.cloned.1.call-done = bf16[1,512,384]{2,1,0:T(8,128)(2,1)} async-done(((bf16[8,512,384]{2,1,0:T(8,128)(2,1)}), bf16[1,512,384]{2,1,0:T(8,128)(2,1)}) %reduce-scatter.2.cloned.1.call-update) | async-done | bytes 393232 | tf_op jit(solution)/shard_map/reduce_scatter | solution.py:120
  137.2 2.9 %shard_map.96 = (bf16[512,384]{1,0:T(8,128)(2,1)}, f32[192,384]{1,0:T(8,128)}) custom-call(bf16[512,384]{1,0:T(8,128)(2,1)} %bitcast.33, f32[512,384]{1,0:T(8,128)} %get-tuple-element.13.old, bf16[192,256]{1,0:T(8,128)(2,1)} %get-tuple-element.14.hot, bf16[384,384]{1,0:T(8,128)(2,1)} %get-tuple-element.15.moved, bf16[192,384]{1,0:T(8,128)(2,1)} %select_select_fusion.predicted), custom_call_target="tpu_custom_call" | custom-call | tf_op jit(solution)/shard_map/pallas_call | solution.py:153
  (8 shorter events, 0.1 us)
Async XLA Ops:
  7.2 12.4 %copy-start.1 = (bf16[1,192,3072]{2,1,0:T(8,128)(2,1)S(1)}, bf16[1,192,3072]{2,1,0:T(8,128)(2,1)}, u32[]{:S(2)}) copy-start(bf16[1,192,3072]{2,1,0:T(8,128)(2,1)} %param.10) | copy-start | bytes 3538948
  7.2 66.6 %all-gather.3.cloned.1.call-start = ((), (), s32[]{:S(2)}) async-start(), calls=%async_computation.1 | async-start | bytes 3096576 | tf_op jit(solution)/shard_map/all_gather | solution.py:114
  19.6 117.6 %reduce-scatter.2.cloned.1.call-start = ((), (), s32[]{:S(2)}) async-start(), calls=%async_computation.2 | async-start | bytes 3538944 | tf_op jit(solution)/shard_map/reduce_scatter | solution.py:120
  19.6 39.7 %collective-permute-start.1 = (bf16[192,3072]{1,0:T(8,128)(2,1)S(1)}, bf16[192,3072]{1,0:T(8,128)(2,1)S(1)}, u32[]{:S(2)}, u32[]{:S(2)}) collective-permute-start(bf16[192,3072]{1,0:T(8,128)(2,1)S(1)} %bitcast.31), channel_id=1, source_target_pairs={{0,64},{64,128},{128,192},{192,256},{256,320},{320,384},{384,448},... | collective-permute-start | bytes 3538952 | tf_op jit(solution)/shard_map/ppermute | solution.py:109
  45.5 11.6 %copy-start.2 = (bf16[4,160,768]{2,1,0:T(8,128)(2,1)}, bf16[4,160,768]{2,1,0:T(8,128)(2,1)S(1)}, u32[]{:S(2)}) copy-start(bf16[4,160,768]{2,1,0:T(8,128)(2,1)S(1)} %all_gather.14.mine) | copy-start | bytes 2949124
  45.5 13.7 %collective-permute-start = (bf16[4,160,768]{2,1,0:T(8,128)(2,1)S(1)}, bf16[4,160,768]{2,1,0:T(8,128)(2,1)S(1)}, u32[]{:S(2)}, u32[]{:S(2)}) collective-permute-start(bf16[4,160,768]{2,1,0:T(8,128)(2,1)S(1)} %all_gather.14.mine), channel_id=1, source_target_pairs={{0,2},{2,0},{1,3},{3,1},{4,6},{6,4},{5,7},{7,5},{8,10},{10,8},{9,1... | collective-permute-start | bytes 2949128 | tf_op jit(solution)/shard_map/ppermute | solution.py:116
  59.3 14.5 %copy-start.4 = (bf16[4,160,768]{2,1,0:T(8,128)(2,1)}, bf16[4,160,768]{2,1,0:T(8,128)(2,1)S(1)}, u32[]{:S(2)}) copy-start(bf16[4,160,768]{2,1,0:T(8,128)(2,1)S(1)} %collective-permute-done.other) | copy-start | bytes 2949124
  80.5 0.7 copy-start.5
  80.5 6.6 %copy-start = (bf16[192,3072]{1,0:T(8,128)(2,1)S(1)}, bf16[192,3072]{1,0:T(8,128)(2,1)}, u32[]{:S(2)}) copy-start(bf16[192,3072]{1,0:T(8,128)(2,1)} %param.11) | copy-start | bytes 3538948
  87.6 18.1 %copy-start.3 = (f32[1,3072]{1,0:T(1,128)S(1)}, f32[1,3072]{1,0:T(1,128)}, u32[]{:S(2)}) copy-start(f32[1,3072]{1,0:T(1,128)} %param.12) | copy-start | bytes 36868
  87.6 18.1 %collective-permute-start.5 = (f32[192]{0:T(256)S(1)}, f32[192]{0:T(256)S(1)}, u32[]{:S(2)}, u32[]{:S(2)}) collective-permute-start(f32[192]{0:T(256)S(1)} %fusion), channel_id=1, source_target_pairs={{0,1},{1,0},{2,3},{3,2},{4,5},{5,4},{6,7},{7,6},{8,9},{9,8},{10,11... | collective-permute-start | bytes 2312 | tf_op jit(solution)/shard_map/ppermute | solution.py:138
  96.7 12.4 %collective-permute-start.2 = (bf16[192,384]{1,0:T(8,128)(2,1)S(1)}, bf16[192,384]{1,0:T(8,128)(2,1)S(1)}, u32[]{:S(2)}, u32[]{:S(2)}) collective-permute-start(bf16[192,384]{1,0:T(8,128)(2,1)S(1)} %get-tuple-element.21), channel_id=1, source_target_pairs={{0,192},{448,256},{1,193},{449,257},{2,194},{450,258},{3,195},{451... | collective-permute-start | bytes 442376 | tf_op jit(solution)/shard_map/ppermute | solution.py:127
  103.1 12.4 %collective-permute-start.3 = (bf16[192,384]{1,0:T(8,128)(2,1)S(1)}, bf16[192,384]{1,0:T(8,128)(2,1)S(1)}, u32[]{:S(2)}, u32[]{:S(2)}) collective-permute-start(bf16[192,384]{1,0:T(8,128)(2,1)S(1)} %get-tuple-element.20), channel_id=1, source_target_pairs={{0,128},{448,320},{1,129},{449,321},{2,130},{450,322},{3,131},{451... | collective-permute-start | bytes 442376 | tf_op jit(solution)/shard_map/ppermute | solution.py:127
  104.4 17.4 %collective-permute-start.4 = (bf16[192,384]{1,0:T(8,128)(2,1)S(1)}, bf16[192,384]{1,0:T(8,128)(2,1)S(1)}, u32[]{:S(2)}, u32[]{:S(2)}) collective-permute-start(bf16[192,384]{1,0:T(8,128)(2,1)S(1)} %get-tuple-element.19), channel_id=1, source_target_pairs={{0,64},{448,384},{1,65},{449,385},{2,66},{450,386},{3,67},{451,387... | collective-permute-start | bytes 442376 | tf_op jit(solution)/shard_map/ppermute | solution.py:127
Sparse Core Ops, SparseCore 0:
  19.7 54.0 all-gather.2
  80.6 56.4 reduce-scatter.1

commit v3 on v1

v3 whole, which is shorter than its diff:
```python
import jax
import jax.numpy as jnp
from jax import lax
from jax.experimental import pallas as pl
from jax.experimental.pallas import tpu as pltpu
from jax.sharding import Mesh, PartitionSpec as P

GRID_SIDE = 16
BLOCK_SIDE = 4
PATCHES = 256
AXES = ("section", "zlo", "x", "core", "tensor")
DP = ("zlo", "x", "core")
LATE = 3


def around(value, axis, steps):
    count = lax.axis_size(axis)
    return lax.ppermute(value, axis, [(i, (i + steps) % count) for i in range(count)])


def tied(value, *others):
    return lax.optimization_barrier((value, *others))[0]


def masked_patches(mask_blocks):
    per_side = GRID_SIDE // BLOCK_SIDE
    within = jnp.arange(BLOCK_SIDE * BLOCK_SIDE, dtype=jnp.int32)
    chosen = mask_blocks[..., None]
    grid_row = chosen // per_side * BLOCK_SIDE + within // BLOCK_SIDE
    grid_col = chosen % per_side * BLOCK_SIDE + within % BLOCK_SIDE
    return grid_row * GRID_SIDE + grid_col


def normed(values, images):
    shaped = values.reshape(images, -1, values.shape[-1])
    center = jnp.mean(shaped, axis=1, keepdims=True)
    off = shaped - center
    spread = jnp.mean(jnp.square(off), axis=1, keepdims=True)
    return (off * lax.rsqrt(spread + 1e-05)).reshape(values.shape)


def transpose_kernel(first, second, out):
    rows = first.shape[0]
    out[:, :rows] = first[...].T
    out[:, rows:] = second[...].T


def transposed(first, second):
    rows, depth = first.shape
    return pl.pallas_call(
        transpose_kernel,
        out_shape=jax.ShapeDtypeStruct((depth, 2 * rows), first.dtype),
        compiler_params=pltpu.CompilerParams(vmem_limit_bytes=24 << 20),
    )(first, second)


def ready_kernel(previous, ids, out, hot, same):
    images = previous.shape[0] // PATCHES
    out[...] = 0.5 * normed(previous[...].astype(jnp.float32), images)
    lane = lax.broadcasted_iota(jnp.int32, hot.shape, 1)
    hot[...] = jnp.where(lane == ids[...], 1.0, 0.0).astype(hot.dtype)
    row = lax.broadcasted_iota(jnp.int32, same.shape, 0)
    lane = lax.broadcasted_iota(jnp.int32, same.shape, 1)
    same[...] = jnp.where(lane == row, 1.0, 0.0).astype(same.dtype)


def final_kernel(core, mine, other, old, hot, same, predicted, targets, error):
    images = targets.shape[0] // PATCHES
    shard = mine.shape[0] // 2
    first = core[0] == 0
    pieces = []
    for pair in range(2):
        a, b = (part[pair * shard:(pair + 1) * shard] for part in (mine, other))
        pieces += [jnp.where(first, a, b), jnp.where(first, b, a)]
    ordered = lax.dot_general(
        same[...],
        jnp.concatenate(pieces, axis=0),
        (((1,), (1,)), ((), ())),
        preferred_element_type=jnp.float32,
    )
    made = (0.5 * normed(ordered, images) + old[...]).astype(targets.dtype)
    targets[...] = made
    picked = jnp.dot(hot[...], made[:PATCHES], preferred_element_type=jnp.float32)
    error[...] = predicted[...].astype(jnp.float32) - picked


def on_device(context, out_weight, previous, section_act, fresh_batch, section_gains, mask_blocks):
    f32, bf16 = jnp.float32, jnp.bfloat16
    sections = lax.axis_size("section")
    position, x, core = (lax.axis_index(name) for name in ("section", "x", "core"))
    rows, width = previous.shape
    act = section_act[0]
    depth, shard = out_weight.shape
    far = sections // 2

    held = lax.all_gather(out_weight.T, "zlo", axis=0, tiled=False)
    below = around(held, "x", 1)
    above = around(held, "x", -1)
    incoming = around(act, "section", 1)
    both = transposed(context, around(context, "core", 1))
    opposite = around(below[:LATE], "x", 1)
    opposite_rest = around(above[LATE:], "x", -1)

    def product(weight):
        return jnp.dot(weight, both, preferred_element_type=f32)

    def early_half(dest):
        return (x % 2) ^ (dest % 2 != x // 2).astype(jnp.int32)

    def up(value):
        return around(value.astype(bf16), "section", 1)

    def down(value):
        return around(value.astype(bf16), "section", -1)

    dest = (position + far) % sections
    plane = lambda part: lax.dynamic_index_in_dim(part, dest // 2, 0, keepdims=False)
    near = jnp.where(x % 2 == 0, plane(below), plane(above))
    rising = up(product(jnp.where(dest % 2 == x // 2, plane(held), near)))

    count = lax.axis_size("x")
    weight = jnp.zeros((held.shape[0], count, shard, depth), bf16)
    for part, at, line in (
        (held, x, 0), (below, x + 3, 0), (above, x + 1, 0), (opposite, x + 2, 0), (opposite_rest, x + 2, LATE),
    ):
        weight = lax.dynamic_update_slice(weight, part[:, None], (line, at % count, 0, 0))
    weight = weight.reshape(sections, 2 * shard, depth)

    def block(steps, after=()):
        place = tied(position, *after)
        return lax.dynamic_index_in_dim(weight, (place + steps) % sections, 0, keepdims=False)

    rest = lax.dynamic_slice(weight, (dest, (1 - early_half(dest)) * shard, 0), (1, shard, depth))
    falling = down(product(rest.reshape(shard, depth)))

    def spread(value, half):
        empty = jnp.zeros_like(value)
        return jnp.concatenate([jnp.where(half == 0, value, empty), jnp.where(half == 0, empty, value)])

    half = early_half((position + far - 1) % sections)
    rising = spread(rising, half)
    half = early_half((position + far + 1) % sections)
    falling = spread(falling, 1 - half)
    def round_of(steps, after):
        upward = product(block(steps, after)) + rising.astype(f32)
        downward = product(block(sections - steps, after)) + falling.astype(f32)
        return upward.astype(bf16), downward.astype(bf16)

    sent = round_of(3, ())
    rising, falling = up(sent[0]), down(sent[1])

    ids = masked_patches(mask_blocks[0]).reshape(-1, 1)
    old, hot, same = pl.pallas_call(
        ready_kernel,
        out_shape=(
            jax.ShapeDtypeStruct((rows, width), f32),
            jax.ShapeDtypeStruct((ids.shape[0], PATCHES), bf16),
            jax.ShapeDtypeStruct((rows, rows), bf16),
        ),
        cost_estimate=pl.CostEstimate(flops=0, bytes_accessed=8 << 20, transcendentals=0),
    )(tied(previous, *sent), ids)

    sent = round_of(2, (old,))
    rising, falling = up(sent[0]), down(sent[1])

    last = sections - 1
    source = jnp.where(position == 0, tied(incoming, *sent), act)
    share = lambda s: lax.dynamic_slice_in_dim(source, s * width, width, 1)
    predicted = share(position)
    given = [share(jnp.where(position == 0, hop, last - hop)) for hop in range(1, far)]
    sent = round_of(1, given)
    rising, falling = up(sent[0]), down(sent[1])

    for hop, piece in zip(range(1, far), given):
        piece = lax.ppermute(piece, "section", [(0, hop), (last, last - hop)])
        here = (position == hop) | (position == last - hop)
        predicted = jnp.where(here, piece, predicted)
    current = jnp.where(position == 0, fresh_batch, incoming)
    wide = current.astype(f32)
    own = tied(jnp.sum(wide * wide, axis=-1), *sent)
    squares = own + around(own, "tensor", 1)
    features = act.shape[-1] * lax.axis_size("tensor")
    scaling = lax.rsqrt(squares[:, None] / features + 1e-06)

    summed = (product(block(0, (scaling,))) + rising.astype(f32) + falling.astype(f32)).astype(bf16)
    other = around(summed[:, rows:], "core", 1)
    section_out = (wide * scaling * section_gains).astype(bf16)[None]

    vmem = pl.BlockSpec(memory_space=pltpu.VMEM)
    targets, target_error = pl.pallas_call(
        final_kernel,
        in_specs=[pl.BlockSpec(memory_space=pltpu.SMEM)] + [vmem] * 6,
        out_specs=(vmem, vmem),
        out_shape=(
            jax.ShapeDtypeStruct((rows, width), bf16),
            jax.ShapeDtypeStruct((ids.shape[0], width), f32),
        ),
    )(core.astype(jnp.int32).reshape(1), summed[:, :rows], other, old, hot, same, predicted)
    return (targets, section_out, target_error)


def solution(mesh):
    fine = Mesh(mesh.devices.reshape(8, 4, 4, 2, 2), AXES)
    in_specs = (
        P(DP, "section"),
        P("section", ("tensor",) + DP),
        P(DP, ("tensor", "section")),
        P("section", DP, "tensor"),
        P(DP, "tensor"),
        P("section", "tensor"),
        P(DP, None),
    )
    out_specs = (
        P(DP, ("tensor", "section")),
        P("section", DP, "tensor"),
        P(DP, ("tensor", "section")),
    )
    return jax.shard_map(
        on_device, mesh=fine, in_specs=in_specs, out_specs=out_specs, check_vma=False
    )
```

time: 141 us -> 138 us (0.979); the launches traced: 139 us -> 137 us
  starting transfers between devices: 19 us -> 67.4 us
  waiting for transfers between devices: 67.4 us -> 20.3 us
  between operations: 14.2 us -> 1.34 us
  matrix products: 0 us -> 12.6 us
  Pallas kernels: 11 us -> 5.96 us
  other arithmetic: 2.86 us -> 4.65 us
  local copies, waits for them, and re-layouts: 4.69 us -> 6.38 us
    ppermute x9 -> x19, starting transfers between devices: 18.9 us -> 67.4 us  [the longest x16 60.1 us: around(): lax.ppermute(value, axis, [(i, (i + steps) % count) for i in range(count)])]
    reduce_scatter x1 -> x0, waiting for transfers between devices: 45.7 us -> none  [on_device(): lax.psum_scatter(partial, 'section', scatter_dimension=0, tiled=False)]
    dot_general x0 -> x9, matrix products: none -> 12.6 us  [product(): return jnp.dot(weight, both, preferred_element_type=f32)]
    pallas_call x3, Pallas kernels: 11 us -> 5.96 us  [the longest x1 3.05 us: on_device(): pl.pallas_call(final_kernel, in_specs=[pl.BlockSpec(memory_space=pltpu.SM...]
    unnamed x12 -> x20, local copies, waits for them, and re-layouts: 2.98 us -> 1.72 us
    ppermute x9 -> x19, waiting for transfers between devices: 20.5 us -> 20.3 us  [the longest x16 20.3 us: around(): lax.ppermute(value, axis, [(i, (i + steps) % count) for i in range(count)])]
  transfers between devices with their start and end apart: 11 -> 19, of which waited for: 4 -> 3; matrix products, arithmetic and copies ran while one was open for 3% -> 14% of each run, Pallas kernels for 2% -> 2%
where the time goes in v3:
time: 138 us; the launch traced here: 137 us
  starting transfers between devices  67.4 us (49%)
  waiting for transfers between devices  20.3 us (15%)
  blocking collectives  18.5 us (13%)
  matrix products  12.6 us (9%)
  local copies, waits for them, and re-layouts  6.38 us (5%)
  Pallas kernels  5.96 us (4%)
  other arithmetic  4.65 us (3%)
    ppermute x16, starting transfers between devices, around(): lax.ppermute(value, axis, [(i, (i + steps) % count) for i in range(count)])  60.1 us
    ppermute x16, waiting for transfers between devices, around(): lax.ppermute(value, axis, [(i, (i + steps) % count) for i in range(count)])  20.3 us
    all_gather x1, blocking collectives, on_device(): held = lax.all_gather(out_weight.T, 'zlo', axis=0, tiled=False)  18.5 us
    dot_general x9, matrix products, product(): return jnp.dot(weight, both, preferred_element_type=f32)  12.6 us
    ppermute x3, starting transfers between devices, on_device(): piece = lax.ppermute(piece, 'section', [(0, hop), (last, last - hop)])  7.31 us
    pallas_call x1, Pallas kernels, on_device(): pl.pallas_call(final_kernel, in_specs=[pl.BlockSpec(memory_space=pltpu.SM...  3.05 us
  transfers between devices with their start and end apart: 19, of which 3 were waited for; matrix products, arithmetic and copies ran while one was open for 14% of the time, Pallas kernels for 2%

profile of v3, /device:TPU:1, one launch (start us, length us, event | category | flops | bytes accessed | tf_op | source)
XLA Modules:
  0.0 137.2 jit_solution(86274319316237102)
XLA Ops:
  0.6 18.5 %all-gather = bf16[384,768]{1,0:T(8,128)(2,1)S(1)} all-gather(bf16[96,768]{1,0:T(8,128)(2,1)} %bitcast.90), channel_id=2, replica_groups=mesh['section'=8,'zlo'=4,'x'=4,'core'=2,'tensor'=2] {'zlo'}, dimensions={0}, use_global_device_ids=true | all-gather | bytes 737280 | tf_op jit(solution)/shard_map/all_gather | solution.py:96
  19.1 2.9 %collective-permute-start = (bf16[4,96,768]{2,1,0:T(8,128)(2,1)S(1)}, bf16[4,96,768]{2,1,0:T(8,128)(2,1)S(1)}, u32[]{:S(2)}, u32[]{:S(2)}) collective-permute-start(bf16[4,96,768]{2,1,0:T(8,128)(2,1)S(1)} %bitcast.85), channel_id=1, source_target_pairs={{0,4},{4,8},{8,12},{12,0},{1,5},{5,9},{9,13},{13,1},{2,6},{6,10},{... | collective-permute-start | bytes 1769480 | tf_op jit(solution)/shard_map/ppermute | solution.py:18
  22.1 3.5 %collective-permute-start.1 = (bf16[4,96,768]{2,1,0:T(8,128)(2,1)S(1)}, bf16[4,96,768]{2,1,0:T(8,128)(2,1)}, u32[]{:S(2)}, u32[]{:S(2)}) collective-permute-start(bf16[4,96,768]{2,1,0:T(8,128)(2,1)S(1)} %bitcast.86), channel_id=1, source_target_pairs={{0,12},{4,0},{8,4},{12,8},{1,13},{5,1},{9,5},{13,9},{2,14},{6,2},{... | collective-permute-start | bytes 1769480 | tf_op jit(solution)/shard_map/ppermute | solution.py:18
  25.6 7.3 %collective-permute-start.4 = (bf16[512,768]{1,0:T(8,128)(2,1)}, bf16[512,768]{1,0:T(8,128)(2,1)S(1)}, u32[]{:S(2)}, u32[]{:S(2)}) collective-permute-start(bf16[512,768]{1,0:T(8,128)(2,1)} %first.1), channel_id=1, source_target_pairs={{0,2},{2,0},{1,3},{3,1},{4,6},{6,4},{5,7},{7,5},{8,10},{10,8},{9,1... | collective-permute-start | bytes 2359304 | tf_op jit(solution)/shard_map/ppermute | solution.py:18
  32.9 1.9 %collective-permute-start.5 = (bf16[192,3072]{1,0:T(8,128)(2,1)}, bf16[192,3072]{1,0:T(8,128)(2,1)S(1)}, u32[]{:S(2)}, u32[]{:S(2)}) collective-permute-start(bf16[192,3072]{1,0:T(8,128)(2,1)} %bitcast.89), channel_id=1, source_target_pairs={{0,64},{64,128},{128,192},{192,256},{256,320},{320,384},{384,448},... | collective-permute-start | bytes 3538952 | tf_op jit(solution)/shard_map/ppermute | solution.py:18
  35.1 0.7 fusion.46
  35.8 0.1 add_add_fusion
  35.9 0.7 add.351.ids
  36.6 0.2 broadcast_in_dim.24
  36.8 0.0 copy-start
  36.9 0.0 collective-permute-done
  36.9 0.0 copy-start.6
  37.0 2.1 %collective-permute-start.2 = (bf16[3,96,768]{2,1,0:T(8,128)(2,1)S(1)}, bf16[3,96,768]{2,1,0:T(8,128)(2,1)S(1)}, u32[]{:S(2)}, u32[]{:S(2)}) collective-permute-start(bf16[3,96,768]{2,1,0:T(8,128)(2,1)S(1)} %slice.16), channel_id=1, source_target_pairs={{0,4},{4,8},{8,12},{12,0},{1,5},{5,9},{9,13},{13,1},{2,6},{6,10},{... | collective-permute-start | bytes 1327112 | tf_op jit(solution)/shard_map/ppermute | solution.py:18
  39.0 0.9 slice.17
  40.0 4.6 %collective-permute-start.3 = (bf16[1,96,768]{2,1,0:T(8,128)(2,1)S(1)}, bf16[1,96,768]{2,1,0:T(8,128)(2,1)S(1)}, u32[]{:S(2)}, u32[]{:S(2)}) collective-permute-start(bf16[1,96,768]{2,1,0:T(8,128)(2,1)S(1)} %slice.17), channel_id=1, source_target_pairs={{0,12},{4,0},{8,4},{12,8},{1,13},{5,1},{9,5},{13,9},{2,14},{6,2},{... | collective-permute-start | bytes 442376 | tf_op jit(solution)/shard_map/ppermute | solution.py:18
  44.6 0.0 collective-permute-done.4.second
  44.6 0.5 shard_map.94
  45.1 1.4 %convolution_convert_fusion.1 = bf16[96,1024]{1,0:T(8,128)(2,1)S(1)} fusion(bf16[768,1024]{1,0:T(8,128)(2,1)S(1)} %shard_map.94, bf16[4,96,768]{2,1,0:T(8,128)(2,1)} %collective-permute-done.1, s32[]{:T(128)S(6)} %select_n.300, bf16[4,96,768]{2,1,0:T(8,128)(2,1)} %copy-done.6, bf16[4,96,768]{2,1,0:T(8,128)(2,1)} %bitcast.88, pred[]{:T(512)S(6)} %eq.70, ...), kind=kOutput, calls=%fused_computation.24 | convolution fusion | flops 151240704 | bytes 2211846 | tf_op jit(solution)/shard_map/dot_general | solution.py:105
  46.6 2.2 %collective-permute-start.6 = (bf16[96,1024]{1,0:T(8,128)(2,1)S(1)}, bf16[96,1024]{1,0:T(8,128)(2,1)S(1)}, u32[]{:S(2)}, u32[]{:S(2)}) collective-permute-start(bf16[96,1024]{1,0:T(8,128)(2,1)S(1)} %convolution_convert_fusion.1), channel_id=1, source_target_pairs={{0,64},{64,128},{128,192},{192,256},{256,320},{320,384},{384,448},... | collective-permute-start | bytes 589832 | tf_op jit(solution)/shard_map/ppermute | solution.py:18
  48.7 1.1 bitcast_dynamic-update-slice_fusion
  49.9 18.2 %collective-permute-done.6 = bf16[96,1024]{1,0:T(8,128)(2,1)S(1)} collective-permute-done((bf16[96,1024]{1,0:T(8,128)(2,1)S(1)}, bf16[96,1024]{1,0:T(8,128)(2,1)S(1)}, u32[]{:S(2)}, u32[]{:S(2)}) %collective-permute-start.6) | collective-permute-done | bytes 196640 | tf_op jit(solution)/shard_map/ppermute | solution.py:18
  68.1 0.0 collective-permute-done.2
  68.1 0.0 collective-permute-done.3
  68.2 0.4 convolution_convert_fusion
  68.6 1.9 %collective-permute-start.7 = (bf16[96,1024]{1,0:T(8,128)(2,1)S(1)}, bf16[96,1024]{1,0:T(8,128)(2,1)S(1)}, u32[]{:S(2)}, u32[]{:S(2)}) collective-permute-start(bf16[96,1024]{1,0:T(8,128)(2,1)S(1)} %convolution_convert_fusion), channel_id=1, source_target_pairs={{0,448},{64,0},{128,64},{192,128},{256,192},{320,256},{384,320},{4... | collective-permute-start | bytes 589832 | tf_op jit(solution)/shard_map/ppermute | solution.py:18
  70.5 1.2 fusion.5
  71.7 3.5 %collective-permute-start.8 = (bf16[192,1024]{1,0:T(8,128)(2,1)}, bf16[192,1024]{1,0:T(8,128)(2,1)S(1)}, u32[]{:S(2)}, u32[]{:S(2)}) collective-permute-start(bf16[192,1024]{1,0:T(8,128)(2,1)} %fusion.5), channel_id=1, source_target_pairs={{0,64},{64,128},{128,192},{192,256},{256,320},{320,384},{384,448},... | collective-permute-start | bytes 1179656 | tf_op jit(solution)/shard_map/ppermute | solution.py:18
  75.2 0.9 collective-permute-done.7
  76.1 1.2 fusion.6
  77.4 3.4 %collective-permute-start.9 = (bf16[192,1024]{1,0:T(8,128)(2,1)}, bf16[192,1024]{1,0:T(8,128)(2,1)}, u32[]{:S(2)}, u32[]{:S(2)}) collective-permute-start(bf16[192,1024]{1,0:T(8,128)(2,1)} %fusion.6), channel_id=1, source_target_pairs={{0,448},{64,0},{128,64},{192,128},{256,192},{320,256},{384,320},{4... | collective-permute-start | bytes 1179656 | tf_op jit(solution)/shard_map/ppermute | solution.py:18
  80.8 0.5 fusion
  81.3 2.4 %shard_map.95 = (f32[512,384]{1,0:T(8,128)}, bf16[192,256]{1,0:T(8,128)(2,1)}, bf16[512,512]{1,0:T(8,128)(2,1)}) custom-call(bf16[512,384]{1,0:T(8,128)(2,1)} %previous, s32[192,1]{1,0:T(8,128)} %add.351.ids), custom_call_target="tpu_custom_call" | custom-call | bytes 8388608 | tf_op jit(solution)/shard_map/pallas_call | solution.py:153
  83.8 1.2 collective-permute-done.8
  85.0 1.4 %fusion.7 = bf16[192,1024]{1,0:T(8,128)(2,1)S(1)} fusion(bf16[768,1024]{1,0:T(8,128)(2,1)S(1)} %shard_map.94, bf16[192,1024]{1,0:T(8,128)(2,1)S(1)} %collective-permute-done.8, bf16[8,192,768]{2,1,0:T(8,128)(2,1)} %bitcast.80, s32[]{:T(128)S(6)} %select_n.321), kind=kOutput, calls=%fused_computation.16 | convolution fusion | flops 302579712 | bytes 2654212 | tf_op jit(solution)/shard_map/dot_general | solution.py:105
  86.5 0.0 copy-start.7
  86.5 2.1 %collective-permute-start.10 = (bf16[192,1024]{1,0:T(8,128)(2,1)S(1)}, bf16[192,1024]{1,0:T(8,128)(2,1)S(1)}, u32[]{:S(2)}, u32[]{:S(2)}) collective-permute-start(bf16[192,1024]{1,0:T(8,128)(2,1)S(1)} %fusion.7), channel_id=1, source_target_pairs={{0,64},{64,128},{128,192},{192,256},{256,320},{320,384},{384,448},... | collective-permute-start | bytes 1179656 | tf_op jit(solution)/shard_map/ppermute | solution.py:18
  88.6 0.0 collective-permute-done.9
  88.6 2.3 %fusion.8 = bf16[192,1024]{1,0:T(8,128)(2,1)} fusion(bf16[768,1024]{1,0:T(8,128)(2,1)S(1)} %shard_map.94, bf16[192,1024]{1,0:T(8,128)(2,1)} %collective-permute-done.9, bf16[8,192,768]{2,1,0:T(8,128)(2,1)} %bitcast.81, s32[]{:T(128)S(6)} %select_n.323), kind=kOutput, calls=%fused_computation.17 | convolution fusion | flops 302579712 | bytes 2654212 | tf_op jit(solution)/shard_map/dot_general | solution.py:105
  90.9 4.9 %collective-permute-start.12 = (bf16[192,1024]{1,0:T(8,128)(2,1)}, bf16[192,1024]{1,0:T(8,128)(2,1)}, u32[]{:S(2)}, u32[]{:S(2)}) collective-permute-start(bf16[192,1024]{1,0:T(8,128)(2,1)} %fusion.8), channel_id=1, source_target_pairs={{0,448},{64,0},{128,64},{192,128},{256,192},{320,256},{384,320},{4... | collective-permute-start | bytes 1179656 | tf_op jit(solution)/shard_map/ppermute | solution.py:18
  95.8 0.2 broadcast_select_fusion.1
  96.0 0.0 copy-start.5
  96.0 1.0 copy-done.5
  97.0 0.8 constant_dynamic-slice_fusion
  97.8 3.4 %collective-permute-start.15 = (bf16[192,384]{1,0:T(8,128)(2,1)}, bf16[192,384]{1,0:T(8,128)(2,1)}, u32[]{:S(2)}, u32[]{:S(2)}) collective-permute-start(bf16[192,384]{1,0:T(8,128)(2,1)} %get-tuple-element.23), channel_id=1, source_target_pairs={{0,192},{448,256},{1,193},{449,257},{2,194},{450,258},{3,195},{451... | collective-permute-start | bytes 442376 | tf_op jit(solution)/shard_map/ppermute | solution.py:175
  101.2 1.9 %collective-permute-start.16 = (bf16[192,384]{1,0:T(8,128)(2,1)}, bf16[192,384]{1,0:T(8,128)(2,1)}, u32[]{:S(2)}, u32[]{:S(2)}) collective-permute-start(bf16[192,384]{1,0:T(8,128)(2,1)} %get-tuple-element.24), channel_id=1, source_target_pairs={{0,128},{448,320},{1,129},{449,321},{2,130},{450,322},{3,131},{451... | collective-permute-start | bytes 442376 | tf_op jit(solution)/shard_map/ppermute | solution.py:175
  103.1 2.0 %collective-permute-start.17 = (bf16[192,384]{1,0:T(8,128)(2,1)}, bf16[192,384]{1,0:T(8,128)(2,1)}, u32[]{:S(2)}, u32[]{:S(2)}) collective-permute-start(bf16[192,384]{1,0:T(8,128)(2,1)} %get-tuple-element.25), channel_id=1, source_target_pairs={{0,64},{448,384},{1,65},{449,385},{2,66},{450,386},{3,67},{451,387... | collective-permute-start | bytes 442376 | tf_op jit(solution)/shard_map/ppermute | solution.py:175
  105.1 1.4 %fusion.9 = bf16[192,1024]{1,0:T(8,128)(2,1)S(1)} fusion(bf16[768,1024]{1,0:T(8,128)(2,1)S(1)} %shard_map.94, bf16[192,1024]{1,0:T(8,128)(2,1)S(1)} %collective-permute-done.10, bf16[8,192,768]{2,1,0:T(8,128)(2,1)} %bitcast.82, s32[]{:T(128)S(6)} %select_n.332), kind=kOutput, calls=%fused_computation.18 | convolution fusion | flops 302579712 | bytes 2654212 | tf_op jit(solution)/shard_map/dot_general | solution.py:105
  106.5 1.9 %collective-permute-start.11 = (bf16[192,1024]{1,0:T(8,128)(2,1)S(1)}, bf16[192,1024]{1,0:T(8,128)(2,1)S(1)}, u32[]{:S(2)}, u32[]{:S(2)}) collective-permute-start(bf16[192,1024]{1,0:T(8,128)(2,1)S(1)} %fusion.9), channel_id=1, source_target_pairs={{0,64},{64,128},{128,192},{192,256},{256,320},{320,384},{384,448},... | collective-permute-start | bytes 1179656 | tf_op jit(solution)/shard_map/ppermute | solution.py:18
  108.5 1.6 %fusion.10 = bf16[192,1024]{1,0:T(8,128)(2,1)S(1)} fusion(bf16[768,1024]{1,0:T(8,128)(2,1)S(1)} %shard_map.94, bf16[192,1024]{1,0:T(8,128)(2,1)} %collective-permute-done.12, bf16[8,192,768]{2,1,0:T(8,128)(2,1)} %bitcast.83, s32[]{:T(128)S(6)} %select_n.334), kind=kOutput, calls=%fused_computation.19 | convolution fusion | flops 302579712 | bytes 2654212 | tf_op jit(solution)/shard_map/dot_general | solution.py:105
  110.0 4.6 %collective-permute-start.13 = (bf16[192,1024]{1,0:T(8,128)(2,1)S(1)}, bf16[192,1024]{1,0:T(8,128)(2,1)S(1)}, u32[]{:S(2)}, u32[]{:S(2)}) collective-permute-start(bf16[192,1024]{1,0:T(8,128)(2,1)S(1)} %fusion.10), channel_id=1, source_target_pairs={{0,448},{64,0},{128,64},{192,128},{256,192},{320,256},{384,320},{4... | collective-permute-start | bytes 1179656 | tf_op jit(solution)/shard_map/ppermute | solution.py:18
  114.6 8.0 %collective-permute-start.18 = (f32[192]{0:T(256)S(1)}, f32[192]{0:T(256)S(1)}, u32[]{:S(2)}, u32[]{:S(2)}) collective-permute-start(f32[192]{0:T(256)S(1)} %fusion), channel_id=1, source_target_pairs={{0,1},{1,0},{2,3},{3,2},{4,5},{5,4},{6,7},{7,6},{8,9},{9,8},{10,11... | collective-permute-start | bytes 2312 | tf_op jit(solution)/shard_map/ppermute | solution.py:18
  122.6 0.0 collective-permute-done.16
  122.6 0.0 collective-permute-done.17
  122.6 1.7 %select_select_fusion.predicted = bf16[192,384]{1,0:T(8,128)(2,1)} fusion(bf16[192,384]{1,0:T(8,128)(2,1)} %collective-permute-done.15, bf16[192,384]{1,0:T(8,128)(2,1)} %collective-permute-done.16, bf16[192,384]{1,0:T(8,128)(2,1)} %collective-permute-done.17, bf16[192,3072]{1,0:T(8,128)(2,1)} %copy-done.5, s32[]{:T(128)S(6)} %select_n.338, pred[]{:T(512)S(6)} %or.11, ...), kind=kLoop, calls=%fused_computation.49 | loop fusion | flops 221184 | bytes 737287 | tf_op jit(solution)/shard_map/jit(_where)/select_n | solution.py:177
  124.3 0.0 collective-permute-done.18
  124.3 0.0 copy-start.3
  124.3 0.0 copy-start.9
  124.4 0.0 collective-permute-done.13
  124.4 1.6 %fusion.4 = bf16[192,1024]{1,0:T(8,128)(2,1)S(1)} fusion(bf16[768,1024]{1,0:T(8,128)(2,1)S(1)} %shard_map.94, bf16[192,1024]{1,0:T(8,128)(2,1)S(1)} %collective-permute-done.13, bf16[192,1024]{1,0:T(8,128)(2,1)S(1)} %collective-permute-done.11, bf16[8,192,768]{2,1,0:T(8,128)(2,1)} %bitcast.84, s32[]{:T(128)S(6)} %select_n.287), kind=kOutput, calls=%fused_computation.13 | convolution fusion | flops 302972928 | bytes 3047428 | tf_op jit(solution)/shard_map/dot_general | solution.py:105
  125.9 0.7 fusion.47
  126.6 5.3 %collective-permute-start.14 = (bf16[192,512]{1,0:T(8,128)(2,1)S(1)}, bf16[192,512]{1,0:T(8,128)(2,1)S(1)}, u32[]{:S(2)}, u32[]{:S(2)}) collective-permute-start(bf16[192,512]{1,0:T(8,128)(2,1)S(1)} %get-tuple-element.26), channel_id=1, source_target_pairs={{0,2},{2,0},{1,3},{3,1},{4,6},{6,4},{5,7},{7,5},{8,10},{10,8},{9,1... | collective-permute-start | bytes 589832 | tf_op jit(solution)/shard_map/ppermute | solution.py:18
  132.0 1.5 %fusion.11 = bf16[1,192,3072]{2,1,0:T(8,128)(2,1)} fusion(f32[3072]{0:T(1024)S(1)} %bitcast.91, f32[192]{0:T(256)S(1)} %add_rsqrt_fusion, bf16[192,3072]{1,0:T(8,128)(2,1)S(1)} %copy-done.3, bf16[192,3072]{1,0:T(8,128)(2,1)S(1)} %collective-permute-done.5, pred[]{:T(512)S(6)} %eq.67), kind=kLoop, calls=%fused_computation.20 | loop fusion | flops 2949120 | bytes 3552001 | tf_op jit(solution)/shard_map/broadcast_in_dim | solution.py:187
  133.5 0.7 copy-done.8
  134.2 3.0 %shard_map.96 = (bf16[512,384]{1,0:T(8,128)(2,1)}, f32[192,384]{1,0:T(8,128)}) custom-call(s32[1]{0:T(128)} %bitcast.core, bf16[192,512]{1,0:T(8,128)(2,1)} %get-tuple-element.27.mine, bf16[192,512]{1,0:T(8,128)(2,1)} %copy-done.8, f32[512,384]{1,0:T(8,128)} %get-tuple-element.14.old, bf16[192,256]{1,0:T(8,128)(2,1)} %get-tuple-element.18.hot, ...), custom_call_target="tpu_custom_call" | custom-call | tf_op jit(solution)/shard_map/pallas_call | solution.py:190
  (28 shorter events, 0.3 us)
Async XLA Ops:
  19.1 17.8 %copy-start.4 = (bf16[384,768]{1,0:T(8,128)(2,1)}, bf16[384,768]{1,0:T(8,128)(2,1)S(1)}, u32[]{:S(2)}) copy-start(bf16[384,768]{1,0:T(8,128)(2,1)S(1)} %all-gather) | copy-start | bytes 1769476
  19.1 17.8 %collective-permute-start = (bf16[4,96,768]{2,1,0:T(8,128)(2,1)S(1)}, bf16[4,96,768]{2,1,0:T(8,128)(2,1)S(1)}, u32[]{:S(2)}, u32[]{:S(2)}) collective-permute-start(bf16[4,96,768]{2,1,0:T(8,128)(2,1)S(1)} %bitcast.85), channel_id=1, source_target_pairs={{0,4},{4,8},{8,12},{12,0},{1,5},{5,9},{9,13},{13,1},{2,6},{6,10},{... | collective-permute-start | bytes 1769480 | tf_op jit(solution)/shard_map/ppermute | solution.py:18
  22.1 16.9 %collective-permute-start.1 = (bf16[4,96,768]{2,1,0:T(8,128)(2,1)S(1)}, bf16[4,96,768]{2,1,0:T(8,128)(2,1)}, u32[]{:S(2)}, u32[]{:S(2)}) collective-permute-start(bf16[4,96,768]{2,1,0:T(8,128)(2,1)S(1)} %bitcast.86), channel_id=1, source_target_pairs={{0,12},{4,0},{8,4},{12,8},{1,13},{5,1},{9,5},{13,9},{2,14},{6,2},{... | collective-permute-start | bytes 1769480 | tf_op jit(solution)/shard_map/ppermute | solution.py:18
  25.6 19.0 %collective-permute-start.4 = (bf16[512,768]{1,0:T(8,128)(2,1)}, bf16[512,768]{1,0:T(8,128)(2,1)S(1)}, u32[]{:S(2)}, u32[]{:S(2)}) collective-permute-start(bf16[512,768]{1,0:T(8,128)(2,1)} %first.1), channel_id=1, source_target_pairs={{0,2},{2,0},{1,3},{3,1},{4,6},{6,4},{5,7},{7,5},{8,10},{10,8},{9,1... | collective-permute-start | bytes 2359304 | tf_op jit(solution)/shard_map/ppermute | solution.py:18
  32.9 47.9 %collective-permute-start.5 = (bf16[192,3072]{1,0:T(8,128)(2,1)}, bf16[192,3072]{1,0:T(8,128)(2,1)S(1)}, u32[]{:S(2)}, u32[]{:S(2)}) collective-permute-start(bf16[192,3072]{1,0:T(8,128)(2,1)} %bitcast.89), channel_id=1, source_target_pairs={{0,64},{64,128},{128,192},{192,256},{256,320},{320,384},{384,448},... | collective-permute-start | bytes 3538952 | tf_op jit(solution)/shard_map/ppermute | solution.py:18
  36.8 7.8 %copy-start = (bf16[512,768]{1,0:T(8,128)(2,1)S(1)}, bf16[512,768]{1,0:T(8,128)(2,1)}, u32[]{:S(2)}) copy-start(bf16[512,768]{1,0:T(8,128)(2,1)} %first.1) | copy-start | bytes 2359300
  36.9 7.7 %copy-start.6 = (bf16[4,96,768]{2,1,0:T(8,128)(2,1)}, bf16[4,96,768]{2,1,0:T(8,128)(2,1)S(1)}, u32[]{:S(2)}) copy-start(bf16[4,96,768]{2,1,0:T(8,128)(2,1)S(1)} %collective-permute-done) | copy-start | bytes 1769476
  37.0 31.1 %collective-permute-start.2 = (bf16[3,96,768]{2,1,0:T(8,128)(2,1)S(1)}, bf16[3,96,768]{2,1,0:T(8,128)(2,1)S(1)}, u32[]{:S(2)}, u32[]{:S(2)}) collective-permute-start(bf16[3,96,768]{2,1,0:T(8,128)(2,1)S(1)} %slice.16), channel_id=1, source_target_pairs={{0,4},{4,8},{8,12},{12,0},{1,5},{5,9},{9,13},{13,1},{2,6},{6,10},{... | collective-permute-start | bytes 1327112 | tf_op jit(solution)/shard_map/ppermute | solution.py:18
  40.0 28.2 %collective-permute-start.3 = (bf16[1,96,768]{2,1,0:T(8,128)(2,1)S(1)}, bf16[1,96,768]{2,1,0:T(8,128)(2,1)S(1)}, u32[]{:S(2)}, u32[]{:S(2)}) collective-permute-start(bf16[1,96,768]{2,1,0:T(8,128)(2,1)S(1)} %slice.17), channel_id=1, source_target_pairs={{0,12},{4,0},{8,4},{12,8},{1,13},{5,1},{9,5},{13,9},{2,14},{6,2},{... | collective-permute-start | bytes 442376 | tf_op jit(solution)/shard_map/ppermute | solution.py:18
  46.6 21.5 %collective-permute-start.6 = (bf16[96,1024]{1,0:T(8,128)(2,1)S(1)}, bf16[96,1024]{1,0:T(8,128)(2,1)S(1)}, u32[]{:S(2)}, u32[]{:S(2)}) collective-permute-start(bf16[96,1024]{1,0:T(8,128)(2,1)S(1)} %convolution_convert_fusion.1), channel_id=1, source_target_pairs={{0,64},{64,128},{128,192},{192,256},{256,320},{320,384},{384,448},... | collective-permute-start | bytes 589832 | tf_op jit(solution)/shard_map/ppermute | solution.py:18
  68.2 8.0 %copy-start.1 = (bf16[4,4,96,768]{3,2,1,0:T(8,128)(2,1)}, bf16[4,4,96,768]{3,2,1,0:T(8,128)(2,1)S(1)}, u32[]{:S(2)}) copy-start(bf16[4,4,96,768]{3,2,1,0:T(8,128)(2,1)S(1)} %bitcast_dynamic-update-slice_fusion.3) | copy-start | bytes 7077892
  68.6 7.5 %collective-permute-start.7 = (bf16[96,1024]{1,0:T(8,128)(2,1)S(1)}, bf16[96,1024]{1,0:T(8,128)(2,1)S(1)}, u32[]{:S(2)}, u32[]{:S(2)}) collective-permute-start(bf16[96,1024]{1,0:T(8,128)(2,1)S(1)} %convolution_convert_fusion), channel_id=1, source_target_pairs={{0,448},{64,0},{128,64},{192,128},{256,192},{320,256},{384,320},{4... | collective-permute-start | bytes 589832 | tf_op jit(solution)/shard_map/ppermute | solution.py:18
  71.7 9.1 %copy-start.2 = (bf16[192,3072]{1,0:T(8,128)(2,1)S(1)}, bf16[192,3072]{1,0:T(8,128)(2,1)}, u32[]{:S(2)}) copy-start(bf16[192,3072]{1,0:T(8,128)(2,1)} %param.11) | copy-start | bytes 3538948
  71.7 13.3 %collective-permute-start.8 = (bf16[192,1024]{1,0:T(8,128)(2,1)}, bf16[192,1024]{1,0:T(8,128)(2,1)S(1)}, u32[]{:S(2)}, u32[]{:S(2)}) collective-permute-start(bf16[192,1024]{1,0:T(8,128)(2,1)} %fusion.5), channel_id=1, source_target_pairs={{0,64},{64,128},{128,192},{192,256},{256,320},{320,384},{384,448},... | collective-permute-start | bytes 1179656 | tf_op jit(solution)/shard_map/ppermute | solution.py:18
  77.4 11.2 %collective-permute-start.9 = (bf16[192,1024]{1,0:T(8,128)(2,1)}, bf16[192,1024]{1,0:T(8,128)(2,1)}, u32[]{:S(2)}, u32[]{:S(2)}) collective-permute-start(bf16[192,1024]{1,0:T(8,128)(2,1)} %fusion.6), channel_id=1, source_target_pairs={{0,448},{64,0},{128,64},{192,128},{256,192},{320,256},{384,320},{4... | collective-permute-start | bytes 1179656 | tf_op jit(solution)/shard_map/ppermute | solution.py:18
  86.5 9.3 %copy-start.7 = (bf16[1,192,3072]{2,1,0:T(8,128)(2,1)S(1)}, bf16[1,192,3072]{2,1,0:T(8,128)(2,1)}, u32[]{:S(2)}) copy-start(bf16[1,192,3072]{2,1,0:T(8,128)(2,1)} %param.10) | copy-start | bytes 3538948
  86.5 18.6 %collective-permute-start.10 = (bf16[192,1024]{1,0:T(8,128)(2,1)S(1)}, bf16[192,1024]{1,0:T(8,128)(2,1)S(1)}, u32[]{:S(2)}, u32[]{:S(2)}) collective-permute-start(bf16[192,1024]{1,0:T(8,128)(2,1)S(1)} %fusion.7), channel_id=1, source_target_pairs={{0,64},{64,128},{128,192},{192,256},{256,320},{320,384},{384,448},... | collective-permute-start | bytes 1179656 | tf_op jit(solution)/shard_map/ppermute | solution.py:18
  90.9 17.5 %collective-permute-start.12 = (bf16[192,1024]{1,0:T(8,128)(2,1)}, bf16[192,1024]{1,0:T(8,128)(2,1)}, u32[]{:S(2)}, u32[]{:S(2)}) collective-permute-start(bf16[192,1024]{1,0:T(8,128)(2,1)} %fusion.8), channel_id=1, source_target_pairs={{0,448},{64,0},{128,64},{192,128},{256,192},{320,256},{384,320},{4... | collective-permute-start | bytes 1179656 | tf_op jit(solution)/shard_map/ppermute | solution.py:18
  96.0 1.0 copy-start.5
  97.8 16.9 %collective-permute-start.15 = (bf16[192,384]{1,0:T(8,128)(2,1)}, bf16[192,384]{1,0:T(8,128)(2,1)}, u32[]{:S(2)}, u32[]{:S(2)}) collective-permute-start(bf16[192,384]{1,0:T(8,128)(2,1)} %get-tuple-element.23), channel_id=1, source_target_pairs={{0,192},{448,256},{1,193},{449,257},{2,194},{450,258},{3,195},{451... | collective-permute-start | bytes 442376 | tf_op jit(solution)/shard_map/ppermute | solution.py:175
  101.2 21.4 %collective-permute-start.16 = (bf16[192,384]{1,0:T(8,128)(2,1)}, bf16[192,384]{1,0:T(8,128)(2,1)}, u32[]{:S(2)}, u32[]{:S(2)}) collective-permute-start(bf16[192,384]{1,0:T(8,128)(2,1)} %get-tuple-element.24), channel_id=1, source_target_pairs={{0,128},{448,320},{1,129},{449,321},{2,130},{450,322},{3,131},{451... | collective-permute-start | bytes 442376 | tf_op jit(solution)/shard_map/ppermute | solution.py:175
  103.1 19.5 %collective-permute-start.17 = (bf16[192,384]{1,0:T(8,128)(2,1)}, bf16[192,384]{1,0:T(8,128)(2,1)}, u32[]{:S(2)}, u32[]{:S(2)}) collective-permute-start(bf16[192,384]{1,0:T(8,128)(2,1)} %get-tuple-element.25), channel_id=1, source_target_pairs={{0,64},{448,384},{1,65},{449,385},{2,66},{450,386},{3,67},{451,387... | collective-permute-start | bytes 442376 | tf_op jit(solution)/shard_map/ppermute | solution.py:175
  106.5 17.8 %collective-permute-start.11 = (bf16[192,1024]{1,0:T(8,128)(2,1)S(1)}, bf16[192,1024]{1,0:T(8,128)(2,1)S(1)}, u32[]{:S(2)}, u32[]{:S(2)}) collective-permute-start(bf16[192,1024]{1,0:T(8,128)(2,1)S(1)} %fusion.9), channel_id=1, source_target_pairs={{0,64},{64,128},{128,192},{192,256},{256,320},{320,384},{384,448},... | collective-permute-start | bytes 1179656 | tf_op jit(solution)/shard_map/ppermute | solution.py:18
  110.0 14.3 %collective-permute-start.13 = (bf16[192,1024]{1,0:T(8,128)(2,1)S(1)}, bf16[192,1024]{1,0:T(8,128)(2,1)S(1)}, u32[]{:S(2)}, u32[]{:S(2)}) collective-permute-start(bf16[192,1024]{1,0:T(8,128)(2,1)S(1)} %fusion.10), channel_id=1, source_target_pairs={{0,448},{64,0},{128,64},{192,128},{256,192},{320,256},{384,320},{4... | collective-permute-start | bytes 1179656 | tf_op jit(solution)/shard_map/ppermute | solution.py:18
  114.6 9.7 %collective-permute-start.18 = (f32[192]{0:T(256)S(1)}, f32[192]{0:T(256)S(1)}, u32[]{:S(2)}, u32[]{:S(2)}) collective-permute-start(f32[192]{0:T(256)S(1)} %fusion), channel_id=1, source_target_pairs={{0,1},{1,0},{2,3},{3,2},{4,5},{5,4},{6,7},{7,6},{8,9},{9,8},{10,11... | collective-permute-start | bytes 2312 | tf_op jit(solution)/shard_map/ppermute | solution.py:18
  124.3 7.6 %copy-start.3 = (bf16[192,3072]{1,0:T(8,128)(2,1)S(1)}, bf16[192,3072]{1,0:T(8,128)(2,1)}, u32[]{:S(2)}) copy-start(bf16[192,3072]{1,0:T(8,128)(2,1)} %param.11) | copy-start | bytes 3538948
  124.3 7.6 %copy-start.9 = (f32[1,3072]{1,0:T(1,128)S(1)}, f32[1,3072]{1,0:T(1,128)}, u32[]{:S(2)}) copy-start(f32[1,3072]{1,0:T(1,128)} %param.12) | copy-start | bytes 36868
  126.6 6.8 %collective-permute-start.14 = (bf16[192,512]{1,0:T(8,128)(2,1)S(1)}, bf16[192,512]{1,0:T(8,128)(2,1)S(1)}, u32[]{:S(2)}, u32[]{:S(2)}) collective-permute-start(bf16[192,512]{1,0:T(8,128)(2,1)S(1)} %get-tuple-element.26), channel_id=1, source_target_pairs={{0,2},{2,0},{1,3},{3,1},{4,6},{6,4},{5,7},{7,5},{8,10},{10,8},{9,1... | collective-permute-start | bytes 589832 | tf_op jit(solution)/shard_map/ppermute | solution.py:18
  133.5 0.7 copy-start.8

commit v4 on v3

--- a/solution.py
+++ b/solution.py
@@ -10,7 +10,6 @@
 PATCHES = 256
 AXES = ("section", "zlo", "x", "core", "tensor")
 DP = ("zlo", "x", "core")
-LATE = 3
 
 
 def around(value, axis, steps):
@@ -50,7 +49,6 @@
     return pl.pallas_call(
         transpose_kernel,
         out_shape=jax.ShapeDtypeStruct((depth, 2 * rows), first.dtype),
-        compiler_params=pltpu.CompilerParams(vmem_limit_bytes=24 << 20),
     )(first, second)
 
 
@@ -97,58 +95,6 @@
     below = around(held, "x", 1)
     above = around(held, "x", -1)
     incoming = around(act, "section", 1)
-    both = transposed(context, around(context, "core", 1))
-    opposite = around(below[:LATE], "x", 1)
-    opposite_rest = around(above[LATE:], "x", -1)
-
-    def product(weight):
-        return jnp.dot(weight, both, preferred_element_type=f32)
-
-    def early_half(dest):
-        return (x % 2) ^ (dest % 2 != x // 2).astype(jnp.int32)
-
-    def up(value):
-        return around(value.astype(bf16), "section", 1)
-
-    def down(value):
-        return around(value.astype(bf16), "section", -1)
-
-    dest = (position + far) % sections
-    plane = lambda part: lax.dynamic_index_in_dim(part, dest // 2, 0, keepdims=False)
-    near = jnp.where(x % 2 == 0, plane(below), plane(above))
-    rising = up(product(jnp.where(dest % 2 == x // 2, plane(held), near)))
-
-    count = lax.axis_size("x")
-    weight = jnp.zeros((held.shape[0], count, shard, depth), bf16)
-    for part, at, line in (
-        (held, x, 0), (below, x + 3, 0), (above, x + 1, 0), (opposite, x + 2, 0), (opposite_rest, x + 2, LATE),
-    ):
-        weight = lax.dynamic_update_slice(weight, part[:, None], (line, at % count, 0, 0))
-    weight = weight.reshape(sections, 2 * shard, depth)
-
-    def block(steps, after=()):
-        place = tied(position, *after)
-        return lax.dynamic_index_in_dim(weight, (place + steps) % sections, 0, keepdims=False)
-
-    rest = lax.dynamic_slice(weight, (dest, (1 - early_half(dest)) * shard, 0), (1, shard, depth))
-    falling = down(product(rest.reshape(shard, depth)))
-
-    def spread(value, half):
-        empty = jnp.zeros_like(value)
-        return jnp.concatenate([jnp.where(half == 0, value, empty), jnp.where(half == 0, empty, value)])
-
-    half = early_half((position + far - 1) % sections)
-    rising = spread(rising, half)
-    half = early_half((position + far + 1) % sections)
-    falling = spread(falling, 1 - half)
-    def round_of(steps, after):
-        upward = product(block(steps, after)) + rising.astype(f32)
-        downward = product(block(sections - steps, after)) + falling.astype(f32)
-        return upward.astype(bf16), downward.astype(bf16)
-
-    sent = round_of(3, ())
-    rising, falling = up(sent[0]), down(sent[1])
-
     ids = masked_patches(mask_blocks[0]).reshape(-1, 1)
     old, hot, same = pl.pallas_call(
         ready_kernel,
@@ -158,23 +104,82 @@
             jax.ShapeDtypeStruct((rows, rows), bf16),
         ),
         cost_estimate=pl.CostEstimate(flops=0, bytes_accessed=8 << 20, transcendentals=0),
-    )(tied(previous, *sent), ids)
-
-    sent = round_of(2, (old,))
+    )(previous, ids)
+
+    below, incoming, old = lax.optimization_barrier((below, incoming, old))
+    opposite = around(below, "x", 1)
+    both = transposed(context, around(tied(context, below), "core", 1))
+
+    def product(weight):
+        return jnp.dot(weight, both, preferred_element_type=f32)
+
+    def early_half(dest):
+        return (x % 2) ^ (dest % 2 != x // 2).astype(jnp.int32)
+
+    def up(value):
+        return around(value.astype(bf16), "section", 1)
+
+    def down(value):
+        return around(value.astype(bf16), "section", -1)
+
+    dest = (position + far) % sections
+    plane = lambda part: lax.dynamic_index_in_dim(part, dest // 2, 0, keepdims=False)
+    near = jnp.where(x % 2 == 0, plane(below), plane(above))
+    begun = product(jnp.where(dest % 2 == x // 2, plane(held), near)).astype(bf16)
+    rising = up(begun)
+    last = sections - 1
+    cut = lambda value, s, count=1: value[:, s * width:(s + count) * width]
+    arrived = tied(incoming, begun)
+    given = jnp.where(position == 0, cut(arrived, 2, 2), cut(act, last - 3, 2))
+    passed = lax.ppermute(given, "section", [(0, 2), (last, last - 2)])
+    opposite = tied(opposite, begun, given)
+
+    count = lax.axis_size("x")
+    weight = jnp.zeros((held.shape[0], count, shard, depth), bf16)
+    for part, at in (
+        (held, x), (below, x + 3), (above, x + 1), (opposite, x + 2),
+    ):
+        weight = lax.dynamic_update_slice(weight, part[:, None], (0, at % count, 0, 0))
+    weight = weight.reshape(sections, 2 * shard, depth)
+
+    def block(steps, after=()):
+        place = tied(position, *after)
+        return lax.dynamic_index_in_dim(weight, (place + steps) % sections, 0, keepdims=False)
+
+    rest = lax.dynamic_slice(weight, (dest, (1 - early_half(dest)) * shard, 0), (1, shard, depth))
+    falling = down(product(rest.reshape(shard, depth)))
+
+    def spread(value, half):
+        empty = jnp.zeros_like(value)
+        return jnp.concatenate([jnp.where(half == 0, value, empty), jnp.where(half == 0, empty, value)])
+
+    half = early_half((position + far - 1) % sections)
+    rising = spread(rising, half)
+    half = early_half((position + far + 1) % sections)
+    falling = spread(falling, 1 - half)
+    def round_of(steps, after):
+        upward = product(block(steps, after)) + rising.astype(f32)
+        downward = product(block(sections - steps, after)) + falling.astype(f32)
+        return upward.astype(bf16), downward.astype(bf16)
+
+    sent = round_of(3, ())
     rising, falling = up(sent[0]), down(sent[1])
 
-    last = sections - 1
-    source = jnp.where(position == 0, tied(incoming, *sent), act)
-    share = lambda s: lax.dynamic_slice_in_dim(source, s * width, width, 1)
-    predicted = share(position)
-    given = [share(jnp.where(position == 0, hop, last - hop)) for hop in range(1, far)]
-    sent = round_of(1, given)
+    sent = round_of(2, ())
     rising, falling = up(sent[0]), down(sent[1])
 
-    for hop, piece in zip(range(1, far), given):
-        piece = lax.ppermute(piece, "section", [(0, hop), (last, last - hop)])
-        here = (position == hop) | (position == last - hop)
-        predicted = jnp.where(here, piece, predicted)
+    sent = round_of(1, ())
+    rising, falling = up(sent[0]), down(sent[1])
+
+    ends = (position == 0) | (position == last)
+    low = position < far
+    first = position == 0
+    onward = jnp.where(first, cut(arrived, 1), jnp.where(ends, cut(act, last - 1), jnp.where(low, cut(passed, 1), cut(passed, 0))))
+    handed = lax.ppermute(
+        tied(onward, *sent), "section", [(0, 1), (2, 3), (last, last - 1), (last - 2, last - 3)]
+    )
+    kept = jnp.where(first, cut(arrived, 0), jnp.where(ends, cut(act, last), jnp.where(low, cut(passed, 0), cut(passed, 1))))
+    predicted = jnp.where(ends | (position == 2) | (position == last - 2), kept, handed)
     current = jnp.where(position == 0, fresh_batch, incoming)
     wide = current.astype(f32)
     own = tied(jnp.sum(wide * wide, axis=-1), *sent)
@@ -182,9 +187,11 @@
     features = act.shape[-1] * lax.axis_size("tensor")
     scaling = lax.rsqrt(squares[:, None] / features + 1e-06)
 
-    summed = (product(block(0, (scaling,))) + rising.astype(f32) + falling.astype(f32)).astype(bf16)
-    other = around(summed[:, rows:], "core", 1)
-    section_out = (wide * scaling * section_gains).astype(bf16)[None]
+    own_term = product(block(0, sent))
+    theirs = own_term[:, rows:] + rising[:, rows:].astype(f32) + falling[:, rows:].astype(f32)
+    other = around(theirs.astype(bf16), "core", 1)
+    section_out = (wide * tied(scaling, theirs) * section_gains).astype(bf16)[None]
+    mine = own_term[:, :rows] + rising[:, :rows].astype(f32) + falling[:, :rows].astype(f32)
 
     vmem = pl.BlockSpec(memory_space=pltpu.VMEM)
     targets, target_error = pl.pallas_call(
@@ -193,9 +200,9 @@
         out_specs=(vmem, vmem),
         out_shape=(
             jax.ShapeDtypeStruct((rows, width), bf16),
-            jax.ShapeDtypeStruct((ids.shape[0], width), f32),
+            jax.ShapeDtypeStruct(predicted.shape, f32),
         ),
-    )(core.astype(jnp.int32).reshape(1), summed[:, :rows], other, old, hot, same, predicted)
+    )(core.astype(jnp.int32).reshape(1), mine.astype(bf16), other, old, hot, same, predicted)
     return (targets, section_out, target_error)
 
 

time: 138 us -> 144 us (1.043)
  the two profiles are of different devices: /device:TPU:1 before, /device:TPU:25 now
where the time goes in v4:
time: 144 us; the launch traced here: 143 us
  starting transfers between devices  61 us (42%)
  waiting for transfers between devices  23.9 us (17%)
  blocking collectives  17 us (12%)
  matrix products  14 us (10%)
  other arithmetic  9.95 us (7%)
  Pallas kernels  8.49 us (6%)
  local copies, waits for them, and re-layouts  7.67 us (5%)
    ppermute x15, starting transfers between devices, around(): lax.ppermute(value, axis, [(i, (i + steps) % count) for i in range(count)])  58.9 us
    ppermute x15, waiting for transfers between devices, around(): lax.ppermute(value, axis, [(i, (i + steps) % count) for i in range(count)])  19.4 us
    all_gather x1, blocking collectives, on_device(): held = lax.all_gather(out_weight.T, 'zlo', axis=0, tiled=False)  17 us
    dot_general x9, matrix products, product(): return jnp.dot(weight, both, preferred_element_type=f32)  14 us
    ppermute x1, waiting for transfers between devices, on_device(): lax.ppermute(tied(onward, *sent), 'section', [(0, 1), (2, 3), (last, last...  4.56 us
    dynamic_update_slice x4, local copies, waits for them, and re-layouts, on_device(): lax.dynamic_update_slice(weight, part[:, None], (0, at % count, 0, 0))  4.54 us
    pallas_call x1, Pallas kernels, on_device(): pl.pallas_call(final_kernel, in_specs=[pl.BlockSpec(memory_space=pltpu.SM...  3.04 us
    pallas_call x1, Pallas kernels, transposed(): pl.pallas_call(transpose_kernel, out_shape=jax.ShapeDtypeStruct((depth, 2...  3.03 us
  transfers between devices with their start and end apart: 17, of which 7 were waited for; matrix products, arithmetic and copies ran while one was open for 19% of the time, Pallas kernels for 4%

profile of v4, /device:TPU:25, one launch (start us, length us, event | category | flops | bytes accessed | tf_op | source)
XLA Modules:
  0.0 143.3 jit_solution(9153490414847655233)
XLA Ops:
  0.6 4.4 %collective-permute-start.1 = (bf16[192,3072]{1,0:T(8,128)(2,1)}, bf16[192,3072]{1,0:T(8,128)(2,1)S(1)}, u32[]{:S(2)}, u32[]{:S(2)}) collective-permute-start(bf16[192,3072]{1,0:T(8,128)(2,1)} %bitcast.78), channel_id=1, source_target_pairs={{0,64},{64,128},{128,192},{192,256},{256,320},{320,384},{384,448},... | collective-permute-start | bytes 3538952 | tf_op jit(solution)/shard_map/ppermute | solution.py:17
  5.1 17.0 %all-gather = bf16[384,768]{1,0:T(8,128)(2,1)S(1)} all-gather(bf16[96,768]{1,0:T(8,128)(2,1)} %bitcast.82), channel_id=2, replica_groups=mesh['section'=8,'zlo'=4,'x'=4,'core'=2,'tensor'=2] {'zlo'}, dimensions={0}, use_global_device_ids=true | all-gather | bytes 737280 | tf_op jit(solution)/shard_map/all_gather | solution.py:94
  22.1 3.1 %collective-permute-start = (bf16[4,96,768]{2,1,0:T(8,128)(2,1)S(1)}, bf16[4,96,768]{2,1,0:T(8,128)(2,1)S(1)}, u32[]{:S(2)}, u32[]{:S(2)}) collective-permute-start(bf16[4,96,768]{2,1,0:T(8,128)(2,1)S(1)} %bitcast.74), channel_id=1, source_target_pairs={{0,4},{4,8},{8,12},{12,0},{1,5},{5,9},{9,13},{13,1},{2,6},{6,10},{... | collective-permute-start | bytes 1769480 | tf_op jit(solution)/shard_map/ppermute | solution.py:17
  25.2 3.4 %collective-permute-start.2 = (bf16[4,96,768]{2,1,0:T(8,128)(2,1)S(1)}, bf16[4,96,768]{2,1,0:T(8,128)(2,1)S(1)}, u32[]{:S(2)}, u32[]{:S(2)}) collective-permute-start(bf16[4,96,768]{2,1,0:T(8,128)(2,1)S(1)} %bitcast.75), channel_id=1, source_target_pairs={{0,12},{4,0},{8,4},{12,8},{1,13},{5,1},{9,5},{13,9},{2,14},{6,2},{... | collective-permute-start | bytes 1769480 | tf_op jit(solution)/shard_map/ppermute | solution.py:17
  28.6 0.7 fusion.51
  29.3 0.1 add_add_fusion
  29.3 0.7 add.340.ids
  30.1 2.4 %shard_map.94 = (f32[512,384]{1,0:T(8,128)}, bf16[192,256]{1,0:T(8,128)(2,1)}, bf16[512,512]{1,0:T(8,128)(2,1)}) custom-call(bf16[512,384]{1,0:T(8,128)(2,1)} %previous.1, s32[192,1]{1,0:T(8,128)} %add.340.ids), custom_call_target="tpu_custom_call" | custom-call | bytes 8388608 | tf_op jit(solution)/shard_map/pallas_call | solution.py:99
  32.5 4.3 %collective-permute-done = bf16[4,96,768]{2,1,0:T(8,128)(2,1)S(1)} collective-permute-done((bf16[4,96,768]{2,1,0:T(8,128)(2,1)S(1)}, bf16[4,96,768]{2,1,0:T(8,128)(2,1)S(1)}, u32[]{:S(2)}, u32[]{:S(2)}) %collective-permute-start) | collective-permute-done | bytes 589856 | tf_op jit(solution)/shard_map/ppermute | solution.py:17
  36.8 0.0 collective-permute-done.1
  36.8 6.0 %collective-permute-start.4 = (bf16[512,768]{1,0:T(8,128)(2,1)}, bf16[512,768]{1,0:T(8,128)(2,1)}, u32[]{:S(2)}, u32[]{:S(2)}) collective-permute-start(bf16[512,768]{1,0:T(8,128)(2,1)} %first.1), channel_id=1, source_target_pairs={{0,2},{2,0},{1,3},{3,1},{4,6},{6,4},{5,7},{7,5},{8,10},{10,8},{9,1... | collective-permute-start | bytes 2359304 | tf_op jit(solution)/shard_map/ppermute | solution.py:17
  43.1 1.7 %broadcast_in_dim.21 = bf16[4,4,96,768]{3,2,1,0:T(8,128)(2,1)} broadcast(bf16[]{:T(256)} %constant.213.clone.1), dimensions={} | broadcast | bytes 2359298 | tf_op jit(solution)/shard_map/broadcast_in_dim | solution.py:138
  44.8 0.9 constant_dynamic-update-slice_fusion
  45.7 1.9 %collective-permute-start.3 = (bf16[4,96,768]{2,1,0:T(8,128)(2,1)S(1)}, bf16[4,96,768]{2,1,0:T(8,128)(2,1)}, u32[]{:S(2)}, u32[]{:S(2)}) collective-permute-start(bf16[4,96,768]{2,1,0:T(8,128)(2,1)S(1)} %collective-permute-done), channel_id=1, source_target_pairs={{0,4},{4,8},{8,12},{12,0},{1,5},{5,9},{9,13},{13,1},{2,6},{6,10},{... | collective-permute-start | bytes 1769480 | tf_op jit(solution)/shard_map/ppermute | solution.py:17
  47.6 0.9 bitcast_dynamic-update-slice_fusion.1
  48.5 0.0 collective-permute-done.2
  48.5 0.9 bitcast_dynamic-update-slice_fusion
  49.3 3.0 %shard_map.95 = bf16[768,1024]{1,0:T(8,128)(2,1)} custom-call(bf16[512,768]{1,0:T(8,128)(2,1)} %first.1, bf16[512,768]{1,0:T(8,128)(2,1)} %collective-permute-done.4.second), custom_call_target="tpu_custom_call" | custom-call | tf_op jit(solution)/shard_map/pallas_call | solution.py:49
  52.4 1.8 %convolution_convert_fusion.1 = bf16[96,1024]{1,0:T(8,128)(2,1)S(1)} fusion(bf16[768,1024]{1,0:T(8,128)(2,1)} %shard_map.95, bf16[4,96,768]{2,1,0:T(8,128)(2,1)S(1)} %collective-permute-done.2, s32[]{:T(128)S(6)} %select_n.290, bf16[4,96,768]{2,1,0:T(8,128)(2,1)S(1)} %collective-permute-done, bf16[4,96,768]{2,1,0:T(8,128)(2,1)S(1)} %bitcast.77, ...), kind=kOutput, calls=%fused_computation.20 | convolution fusion | flops 151240704 | bytes 2211846 | tf_op jit(solution)/shard_map/dot_general | solution.py:114
  54.2 2.4 %collective-permute-start.5 = (bf16[96,1024]{1,0:T(8,128)(2,1)S(1)}, bf16[96,1024]{1,0:T(8,128)(2,1)S(1)}, u32[]{:S(2)}, u32[]{:S(2)}) collective-permute-start(bf16[96,1024]{1,0:T(8,128)(2,1)S(1)} %convolution_convert_fusion.1), channel_id=1, source_target_pairs={{0,64},{64,128},{128,192},{192,256},{256,320},{320,384},{384,448},... | collective-permute-start | bytes 589832 | tf_op jit(solution)/shard_map/ppermute | solution.py:17
  56.6 1.0 slice_select_fusion
  57.6 6.2 %collective-permute-done.3 = bf16[4,96,768]{2,1,0:T(8,128)(2,1)} collective-permute-done((bf16[4,96,768]{2,1,0:T(8,128)(2,1)S(1)}, bf16[4,96,768]{2,1,0:T(8,128)(2,1)}, u32[]{:S(2)}, u32[]{:S(2)}) %collective-permute-start.3) | collective-permute-done | bytes 589856 | tf_op jit(solution)/shard_map/ppermute | solution.py:17
  63.8 2.0 %bitcast_dynamic-update-slice_fusion.2 = bf16[4,4,96,768]{3,2,1,0:T(8,128)(2,1)} fusion(bf16[4,4,96,768]{3,2,1,0:T(8,128)(2,1)} %bitcast_dynamic-update-slice_fusion, s32[]{:T(128)S(6)} %select_n.299, bf16[4,96,768]{2,1,0:T(8,128)(2,1)} %collective-permute-done.3), kind=kLoop, calls=%fused_computation.23 | loop fusion | bytes 1179652 | tf_op jit(solution)/shard_map/dynamic_update_slice | solution.py:142
  65.8 1.3 convolution_convert_fusion
  67.1 1.9 %collective-permute-start.8 = (bf16[96,1024]{1,0:T(8,128)(2,1)S(1)}, bf16[96,1024]{1,0:T(8,128)(2,1)S(1)}, u32[]{:S(2)}, u32[]{:S(2)}) collective-permute-start(bf16[96,1024]{1,0:T(8,128)(2,1)S(1)} %convolution_convert_fusion), channel_id=1, source_target_pairs={{0,448},{64,0},{128,64},{192,128},{256,192},{320,256},{384,320},{4... | collective-permute-start | bytes 589832 | tf_op jit(solution)/shard_map/ppermute | solution.py:17
  69.1 1.4 %fusion.5 = bf16[192,1024]{1,0:T(8,128)(2,1)S(1)} fusion(bf16[768,1024]{1,0:T(8,128)(2,1)S(1)} %copy-done, bf16[96,1024]{1,0:T(8,128)(2,1)S(1)} %get-tuple-element.36, bf16[96,1024]{1,0:T(8,128)(2,1)S(1)} %get-tuple-element.35, bf16[8,192,768]{2,1,0:T(8,128)(2,1)} %bitcast.12, s32[]{:T(128)S(6)} %select_n.305), kind=kOutput, calls=%fused_computation.13 | convolution fusion | flops 303169536 | bytes 2654212 | tf_op jit(solution)/shard_map/dot_general | solution.py:114
  70.5 0.0 copy-start.1
  70.5 4.7 %collective-permute-start.6 = (bf16[192,1024]{1,0:T(8,128)(2,1)S(1)}, bf16[192,1024]{1,0:T(8,128)(2,1)S(1)}, u32[]{:S(2)}, u32[]{:S(2)}) collective-permute-start(bf16[192,1024]{1,0:T(8,128)(2,1)S(1)} %fusion.5), channel_id=1, source_target_pairs={{0,64},{64,128},{128,192},{192,256},{256,320},{320,384},{384,448},... | collective-permute-start | bytes 1179656 | tf_op jit(solution)/shard_map/ppermute | solution.py:17
  75.3 0.6 collective-permute-done.8
  75.9 1.4 %fusion.8 = bf16[192,1024]{1,0:T(8,128)(2,1)S(1)} fusion(bf16[768,1024]{1,0:T(8,128)(2,1)S(1)} %copy-done, bf16[96,1024]{1,0:T(8,128)(2,1)S(1)} %get-tuple-element.34, bf16[96,1024]{1,0:T(8,128)(2,1)S(1)} %get-tuple-element.33, bf16[8,192,768]{2,1,0:T(8,128)(2,1)} %bitcast.12, s32[]{:T(128)S(6)} %select_n.316), kind=kOutput, calls=%fused_computation.16 | convolution fusion | flops 303169536 | bytes 2654212 | tf_op jit(solution)/shard_map/dot_general | solution.py:114
  77.3 1.9 %collective-permute-start.9 = (bf16[192,1024]{1,0:T(8,128)(2,1)S(1)}, bf16[192,1024]{1,0:T(8,128)(2,1)S(1)}, u32[]{:S(2)}, u32[]{:S(2)}) collective-permute-start(bf16[192,1024]{1,0:T(8,128)(2,1)S(1)} %fusion.8), channel_id=1, source_target_pairs={{0,448},{64,0},{128,64},{192,128},{256,192},{320,256},{384,320},{4... | collective-permute-start | bytes 1179656 | tf_op jit(solution)/shard_map/ppermute | solution.py:17
  79.3 0.5 fusion
  79.8 0.7 collective-permute-start.14
  80.4 2.1 %collective-permute-done.6 = bf16[192,1024]{1,0:T(8,128)(2,1)S(1)} collective-permute-done((bf16[192,1024]{1,0:T(8,128)(2,1)S(1)}, bf16[192,1024]{1,0:T(8,128)(2,1)S(1)}, u32[]{:S(2)}, u32[]{:S(2)}) %collective-permute-start.6) | collective-permute-done | bytes 393248 | tf_op jit(solution)/shard_map/ppermute | solution.py:17
  82.6 1.4 %fusion.4 = bf16[192,1024]{1,0:T(8,128)(2,1)S(1)} fusion(bf16[768,1024]{1,0:T(8,128)(2,1)S(1)} %copy-done, bf16[192,1024]{1,0:T(8,128)(2,1)S(1)} %collective-permute-done.6, bf16[8,192,768]{2,1,0:T(8,128)(2,1)} %bitcast.12, s32[]{:T(128)S(6)} %select_n.303), kind=kOutput, calls=%fused_computation.12 | convolution fusion | flops 302579712 | bytes 2654212 | tf_op jit(solution)/shard_map/dot_general | solution.py:114
  84.0 5.3 %collective-permute-start.7 = (bf16[192,1024]{1,0:T(8,128)(2,1)S(1)}, bf16[192,1024]{1,0:T(8,128)(2,1)S(1)}, u32[]{:S(2)}, u32[]{:S(2)}) collective-permute-start(bf16[192,1024]{1,0:T(8,128)(2,1)S(1)} %fusion.4), channel_id=1, source_target_pairs={{0,64},{64,128},{128,192},{192,256},{256,320},{320,384},{384,448},... | collective-permute-start | bytes 1179656 | tf_op jit(solution)/shard_map/ppermute | solution.py:17
  89.3 0.0 collective-permute-done.9
  89.4 1.5 %fusion.7 = bf16[192,1024]{1,0:T(8,128)(2,1)S(1)} fusion(bf16[768,1024]{1,0:T(8,128)(2,1)S(1)} %copy-done, bf16[192,1024]{1,0:T(8,128)(2,1)S(1)} %collective-permute-done.9, bf16[8,192,768]{2,1,0:T(8,128)(2,1)} %bitcast.12, s32[]{:T(128)S(6)} %select_n.314), kind=kOutput, calls=%fused_computation.15 | convolution fusion | flops 302579712 | bytes 2654212 | tf_op jit(solution)/shard_map/dot_general | solution.py:114
  90.8 1.9 %collective-permute-start.10 = (bf16[192,1024]{1,0:T(8,128)(2,1)S(1)}, bf16[192,1024]{1,0:T(8,128)(2,1)S(1)}, u32[]{:S(2)}, u32[]{:S(2)}) collective-permute-start(bf16[192,1024]{1,0:T(8,128)(2,1)S(1)} %fusion.7), channel_id=1, source_target_pairs={{0,448},{64,0},{128,64},{192,128},{256,192},{320,256},{384,320},{4... | collective-permute-start | bytes 1179656 | tf_op jit(solution)/shard_map/ppermute | solution.py:17
  92.8 1.6 %fusion.28 = bf16[192,384]{1,0:T(8,128)(2,1)} fusion(bf16[192,3072]{1,0:T(8,128)(2,1)} %bitcast.80, bf16[192,3072]{1,0:T(8,128)(2,1)S(1)} %collective-permute-done.1, pred[]{:T(512)S(6)} %lt.174, pred[]{:T(512)S(6)} %or.9, pred[]{:T(512)S(6)} %eq.58, bf16[192,768]{1,0:T(8,128)(2,1)S(1)} %collective-permute-done.14), kind=kLoop, calls=%fused_computation.50 | loop fusion | flops 221184 | bytes 737283 | tf_op jit(solution)/shard_map/jit(_where)/select_n | solution.py:177
  94.4 1.4 collective-permute-done.7
  95.7 1.4 %fusion.3 = bf16[192,1024]{1,0:T(8,128)(2,1)S(1)} fusion(bf16[768,1024]{1,0:T(8,128)(2,1)S(1)} %copy-done, bf16[192,1024]{1,0:T(8,128)(2,1)S(1)} %collective-permute-done.7, bf16[8,192,768]{2,1,0:T(8,128)(2,1)} %bitcast.12, s32[]{:T(128)S(6)} %select_n.301), kind=kOutput, calls=%fused_computation.11 | convolution fusion | flops 302579712 | bytes 2654212 | tf_op jit(solution)/shard_map/dot_general | solution.py:114
  97.2 4.8 %collective-permute-done.10 = bf16[192,1024]{1,0:T(8,128)(2,1)S(1)} collective-permute-done((bf16[192,1024]{1,0:T(8,128)(2,1)S(1)}, bf16[192,1024]{1,0:T(8,128)(2,1)S(1)}, u32[]{:S(2)}, u32[]{:S(2)}) %collective-permute-start.10) | collective-permute-done | bytes 393248 | tf_op jit(solution)/shard_map/ppermute | solution.py:17
  101.9 2.2 %fusion.6 = bf16[192,1024]{1,0:T(8,128)(2,1)} fusion(bf16[768,1024]{1,0:T(8,128)(2,1)S(1)} %copy-done, bf16[192,1024]{1,0:T(8,128)(2,1)S(1)} %collective-permute-done.10, bf16[8,192,768]{2,1,0:T(8,128)(2,1)} %bitcast.12, s32[]{:T(128)S(6)} %select_n.312), kind=kOutput, calls=%fused_computation.14 | convolution fusion | flops 302579712 | bytes 2654212 | tf_op jit(solution)/shard_map/dot_general | solution.py:114
  104.1 1.9 %collective-permute-start.12 = (bf16[192,1024]{1,0:T(8,128)(2,1)}, bf16[192,1024]{1,0:T(8,128)(2,1)}, u32[]{:S(2)}, u32[]{:S(2)}) collective-permute-start(bf16[192,1024]{1,0:T(8,128)(2,1)} %fusion.6), channel_id=1, source_target_pairs={{0,448},{64,0},{128,64},{192,128},{256,192},{320,256},{384,320},{4... | collective-permute-start | bytes 1179656 | tf_op jit(solution)/shard_map/ppermute | solution.py:17
  106.0 4.6 %collective-permute-start.11 = (bf16[192,1024]{1,0:T(8,128)(2,1)S(1)}, bf16[192,1024]{1,0:T(8,128)(2,1)}, u32[]{:S(2)}, u32[]{:S(2)}) collective-permute-start(bf16[192,1024]{1,0:T(8,128)(2,1)S(1)} %fusion.3), channel_id=1, source_target_pairs={{0,64},{64,128},{128,192},{192,256},{256,320},{320,384},{384,448},... | collective-permute-start | bytes 1179656 | tf_op jit(solution)/shard_map/ppermute | solution.py:17
  110.6 7.9 %collective-permute-start.16 = (f32[192]{0:T(256)S(1)}, f32[192]{0:T(256)S(1)}, u32[]{:S(2)}, u32[]{:S(2)}) collective-permute-start(f32[192]{0:T(256)S(1)} %fusion), channel_id=1, source_target_pairs={{0,1},{1,0},{2,3},{3,2},{4,5},{5,4},{6,7},{7,6},{8,9},{9,8},{10,11... | collective-permute-start | bytes 2312 | tf_op jit(solution)/shard_map/ppermute | solution.py:17
  118.6 0.0 copy-start.4
  118.6 1.5 %fusion.13 = f32[192,1024]{1,0:T(8,128)S(1)} fusion(bf16[768,1024]{1,0:T(8,128)(2,1)S(1)} %copy-done, bf16[8,192,768]{2,1,0:T(8,128)(2,1)} %bitcast.12, s32[]{:T(128)S(6)} %select_n.325), kind=kOutput, calls=%fused_computation.30 | convolution fusion | flops 301989888 | bytes 2654212 | tf_op jit(solution)/shard_map/dot_general | solution.py:114
  120.1 0.0 copy-start.2
  120.1 0.0 copy-start.5
  120.1 1.4 collective-permute-start.15
  121.5 0.0 collective-permute-done.16
  121.6 4.6 %collective-permute-done.15 = bf16[192,384]{1,0:T(8,128)(2,1)S(1)} collective-permute-done((bf16[192,384]{1,0:T(8,128)(2,1)S(1)}, bf16[192,384]{1,0:T(8,128)(2,1)S(1)}, u32[]{:S(2)}, u32[]{:S(2)}) %collective-permute-start.15) | collective-permute-done | bytes 147488 | tf_op jit(solution)/shard_map/ppermute | solution.py:178
  126.1 1.6 %fusion.30.predicted = bf16[192,384]{1,0:T(8,128)(2,1)} fusion(bf16[192,384]{1,0:T(8,128)(2,1)S(1)} %collective-permute-done.15, bf16[192,3072]{1,0:T(8,128)(2,1)} %bitcast.81, bf16[192,3072]{1,0:T(8,128)(2,1)S(1)} %collective-permute-done.1, pred[]{:T(512)S(6)} %lt.174, pred[]{:T(512)S(6)} %or.9, pred[]{:T(512)S(6)} %eq.58, pred[]{:T(512)S(6)} %or.11, ...), kind=kLoop, calls=%fused_computation.53 | loop fusion | flops 294912 | bytes 884740 | tf_op jit(solution)/shard_map/jit(_where)/select_n | solution.py:182
  127.7 0.0 collective-permute-done.12
  127.7 0.0 collective-permute-done.11
  127.8 1.1 fusion.10
  128.9 7.4 %collective-permute-start.13 = (bf16[192,512]{1,0:T(8,128)(2,1)S(1)}, bf16[192,512]{1,0:T(8,128)(2,1)S(1)}, u32[]{:S(2)}, u32[]{:S(2)}) collective-permute-start(bf16[192,512]{1,0:T(8,128)(2,1)S(1)} %fusion.10), channel_id=1, source_target_pairs={{0,2},{2,0},{1,3},{3,1},{4,6},{6,4},{5,7},{7,5},{8,10},{10,8},{9,1... | collective-permute-start | bytes 589832 | tf_op jit(solution)/shard_map/ppermute | solution.py:17
  136.3 1.5 %fusion.9 = bf16[1,192,3072]{2,1,0:T(8,128)(2,1)} fusion(f32[3072]{0:T(1024)S(1)} %bitcast.83, f32[192]{0:T(256)S(1)} %add_rsqrt_fusion, bf16[192,3072]{1,0:T(8,128)(2,1)S(1)} %copy-done.2, bf16[192,3072]{1,0:T(8,128)(2,1)S(1)} %collective-permute-done.1, pred[]{:T(512)S(6)} %eq.58), kind=kLoop, calls=%fused_computation.17 | loop fusion | flops 2949120 | bytes 3552001 | tf_op jit(solution)/shard_map/broadcast_in_dim | solution.py:193
  137.8 1.8 %fusion.12.mine = bf16[192,512]{1,0:T(8,128)(2,1)} fusion(f32[192,1024]{1,0:T(8,128)S(1)} %fusion.13, bf16[192,1024]{1,0:T(8,128)(2,1)} %collective-permute-done.12, bf16[192,1024]{1,0:T(8,128)(2,1)} %collective-permute-done.11), kind=kLoop, calls=%fused_computation.28 | loop fusion | flops 491520 | bytes 983040 | tf_op jit(solution)/shard_map/convert_element_type | solution.py:205
  139.6 0.0 collective-permute-done.13.other
  139.6 0.7 copy-done.3
  140.3 3.0 %shard_map.96 = (bf16[512,384]{1,0:T(8,128)(2,1)}, f32[192,384]{1,0:T(8,128)}) custom-call(s32[1]{0:T(128)} %bitcast.core, bf16[192,512]{1,0:T(8,128)(2,1)} %fusion.12.mine, bf16[192,512]{1,0:T(8,128)(2,1)} %copy-done.3, f32[512,384]{1,0:T(8,128)} %get-tuple-element.25.old, bf16[192,256]{1,0:T(8,128)(2,1)} %get-tuple-element.26.hot, ...), custom_call_target="tpu_custom_call" | custom-call | tf_op jit(solution)/shard_map/pallas_call | solution.py:197
  (14 shorter events, 0.1 us)
Async XLA Ops:
  0.6 36.2 %collective-permute-start.1 = (bf16[192,3072]{1,0:T(8,128)(2,1)}, bf16[192,3072]{1,0:T(8,128)(2,1)S(1)}, u32[]{:S(2)}, u32[]{:S(2)}) collective-permute-start(bf16[192,3072]{1,0:T(8,128)(2,1)} %bitcast.78), channel_id=1, source_target_pairs={{0,64},{64,128},{128,192},{192,256},{256,320},{320,384},{384,448},... | collective-permute-start | bytes 3538952 | tf_op jit(solution)/shard_map/ppermute | solution.py:17
  22.1 14.7 %collective-permute-start = (bf16[4,96,768]{2,1,0:T(8,128)(2,1)S(1)}, bf16[4,96,768]{2,1,0:T(8,128)(2,1)S(1)}, u32[]{:S(2)}, u32[]{:S(2)}) collective-permute-start(bf16[4,96,768]{2,1,0:T(8,128)(2,1)S(1)} %bitcast.74), channel_id=1, source_target_pairs={{0,4},{4,8},{8,12},{12,0},{1,5},{5,9},{9,13},{13,1},{2,6},{6,10},{... | collective-permute-start | bytes 1769480 | tf_op jit(solution)/shard_map/ppermute | solution.py:17
  25.2 23.3 %collective-permute-start.2 = (bf16[4,96,768]{2,1,0:T(8,128)(2,1)S(1)}, bf16[4,96,768]{2,1,0:T(8,128)(2,1)S(1)}, u32[]{:S(2)}, u32[]{:S(2)}) collective-permute-start(bf16[4,96,768]{2,1,0:T(8,128)(2,1)S(1)} %bitcast.75), channel_id=1, source_target_pairs={{0,12},{4,0},{8,4},{12,8},{1,13},{5,1},{9,5},{13,9},{2,14},{6,2},{... | collective-permute-start | bytes 1769480 | tf_op jit(solution)/shard_map/ppermute | solution.py:17
  36.8 12.5 %collective-permute-start.4 = (bf16[512,768]{1,0:T(8,128)(2,1)}, bf16[512,768]{1,0:T(8,128)(2,1)}, u32[]{:S(2)}, u32[]{:S(2)}) collective-permute-start(bf16[512,768]{1,0:T(8,128)(2,1)} %first.1), channel_id=1, source_target_pairs={{0,2},{2,0},{1,3},{3,1},{4,6},{6,4},{5,7},{7,5},{8,10},{10,8},{9,1... | collective-permute-start | bytes 2359304 | tf_op jit(solution)/shard_map/ppermute | solution.py:17
  45.7 18.1 %collective-permute-start.3 = (bf16[4,96,768]{2,1,0:T(8,128)(2,1)S(1)}, bf16[4,96,768]{2,1,0:T(8,128)(2,1)}, u32[]{:S(2)}, u32[]{:S(2)}) collective-permute-start(bf16[4,96,768]{2,1,0:T(8,128)(2,1)S(1)} %collective-permute-done), channel_id=1, source_target_pairs={{0,4},{4,8},{8,12},{12,0},{1,5},{5,9},{9,13},{13,1},{2,6},{6,10},{... | collective-permute-start | bytes 1769480 | tf_op jit(solution)/shard_map/ppermute | solution.py:17
  54.2 11.6 %copy-start = (bf16[768,1024]{1,0:T(8,128)(2,1)S(1)}, bf16[768,1024]{1,0:T(8,128)(2,1)}, u32[]{:S(2)}) copy-start(bf16[768,1024]{1,0:T(8,128)(2,1)} %shard_map.95) | copy-start | bytes 4718596
  54.2 14.9 %collective-permute-start.5 = (bf16[96,1024]{1,0:T(8,128)(2,1)S(1)}, bf16[96,1024]{1,0:T(8,128)(2,1)S(1)}, u32[]{:S(2)}, u32[]{:S(2)}) collective-permute-start(bf16[96,1024]{1,0:T(8,128)(2,1)S(1)} %convolution_convert_fusion.1), channel_id=1, source_target_pairs={{0,64},{64,128},{128,192},{192,256},{256,320},{320,384},{384,448},... | collective-permute-start | bytes 589832 | tf_op jit(solution)/shard_map/ppermute | solution.py:17
  67.1 8.7 %collective-permute-start.8 = (bf16[96,1024]{1,0:T(8,128)(2,1)S(1)}, bf16[96,1024]{1,0:T(8,128)(2,1)S(1)}, u32[]{:S(2)}, u32[]{:S(2)}) collective-permute-start(bf16[96,1024]{1,0:T(8,128)(2,1)S(1)} %convolution_convert_fusion), channel_id=1, source_target_pairs={{0,448},{64,0},{128,64},{192,128},{256,192},{320,256},{384,320},{4... | collective-permute-start | bytes 589832 | tf_op jit(solution)/shard_map/ppermute | solution.py:17
  70.5 8.7 %copy-start.1 = (bf16[192,3072]{1,0:T(8,128)(2,1)S(1)}, bf16[192,3072]{1,0:T(8,128)(2,1)}, u32[]{:S(2)}) copy-start(bf16[192,3072]{1,0:T(8,128)(2,1)} %param.11) | copy-start | bytes 3538948
  70.5 12.0 %collective-permute-start.6 = (bf16[192,1024]{1,0:T(8,128)(2,1)S(1)}, bf16[192,1024]{1,0:T(8,128)(2,1)S(1)}, u32[]{:S(2)}, u32[]{:S(2)}) collective-permute-start(bf16[192,1024]{1,0:T(8,128)(2,1)S(1)} %fusion.5), channel_id=1, source_target_pairs={{0,64},{64,128},{128,192},{192,256},{256,320},{320,384},{384,448},... | collective-permute-start | bytes 1179656 | tf_op jit(solution)/shard_map/ppermute | solution.py:17
  77.3 12.0 %collective-permute-start.9 = (bf16[192,1024]{1,0:T(8,128)(2,1)S(1)}, bf16[192,1024]{1,0:T(8,128)(2,1)S(1)}, u32[]{:S(2)}, u32[]{:S(2)}) collective-permute-start(bf16[192,1024]{1,0:T(8,128)(2,1)S(1)} %fusion.8), channel_id=1, source_target_pairs={{0,448},{64,0},{128,64},{192,128},{256,192},{320,256},{384,320},{4... | collective-permute-start | bytes 1179656 | tf_op jit(solution)/shard_map/ppermute | solution.py:17
  79.8 13.0 %collective-permute-start.14 = (bf16[192,768]{1,0:T(8,128)(2,1)S(1)}, bf16[192,768]{1,0:T(8,128)(2,1)S(1)}, u32[]{:S(2)}, u32[]{:S(2)}) collective-permute-start(bf16[192,768]{1,0:T(8,128)(2,1)S(1)} %slice_select_fusion), channel_id=1, source_target_pairs={{0,128},{448,320},{1,129},{449,321},{2,130},{450,322},{3,131},{451... | collective-permute-start | bytes 884744 | tf_op jit(solution)/shard_map/ppermute | solution.py:134
  84.0 11.7 %collective-permute-start.7 = (bf16[192,1024]{1,0:T(8,128)(2,1)S(1)}, bf16[192,1024]{1,0:T(8,128)(2,1)S(1)}, u32[]{:S(2)}, u32[]{:S(2)}) collective-permute-start(bf16[192,1024]{1,0:T(8,128)(2,1)S(1)} %fusion.4), channel_id=1, source_target_pairs={{0,64},{64,128},{128,192},{192,256},{256,320},{320,384},{384,448},... | collective-permute-start | bytes 1179656 | tf_op jit(solution)/shard_map/ppermute | solution.py:17
  90.8 11.1 %collective-permute-start.10 = (bf16[192,1024]{1,0:T(8,128)(2,1)S(1)}, bf16[192,1024]{1,0:T(8,128)(2,1)S(1)}, u32[]{:S(2)}, u32[]{:S(2)}) collective-permute-start(bf16[192,1024]{1,0:T(8,128)(2,1)S(1)} %fusion.7), channel_id=1, source_target_pairs={{0,448},{64,0},{128,64},{192,128},{256,192},{320,256},{384,320},{4... | collective-permute-start | bytes 1179656 | tf_op jit(solution)/shard_map/ppermute | solution.py:17
  104.1 23.6 %collective-permute-start.12 = (bf16[192,1024]{1,0:T(8,128)(2,1)}, bf16[192,1024]{1,0:T(8,128)(2,1)}, u32[]{:S(2)}, u32[]{:S(2)}) collective-permute-start(bf16[192,1024]{1,0:T(8,128)(2,1)} %fusion.6), channel_id=1, source_target_pairs={{0,448},{64,0},{128,64},{192,128},{256,192},{320,256},{384,320},{4... | collective-permute-start | bytes 1179656 | tf_op jit(solution)/shard_map/ppermute | solution.py:17
  106.0 21.7 %collective-permute-start.11 = (bf16[192,1024]{1,0:T(8,128)(2,1)S(1)}, bf16[192,1024]{1,0:T(8,128)(2,1)}, u32[]{:S(2)}, u32[]{:S(2)}) collective-permute-start(bf16[192,1024]{1,0:T(8,128)(2,1)S(1)} %fusion.3), channel_id=1, source_target_pairs={{0,64},{64,128},{128,192},{192,256},{256,320},{320,384},{384,448},... | collective-permute-start | bytes 1179656 | tf_op jit(solution)/shard_map/ppermute | solution.py:17
  110.6 10.9 %collective-permute-start.16 = (f32[192]{0:T(256)S(1)}, f32[192]{0:T(256)S(1)}, u32[]{:S(2)}, u32[]{:S(2)}) collective-permute-start(f32[192]{0:T(256)S(1)} %fusion), channel_id=1, source_target_pairs={{0,1},{1,0},{2,3},{3,2},{4,5},{5,4},{6,7},{7,6},{8,9},{9,8},{10,11... | collective-permute-start | bytes 2312 | tf_op jit(solution)/shard_map/ppermute | solution.py:17
  118.6 1.5 %copy-start.4 = (bf16[192,384]{1,0:T(8,128)(2,1)S(1)}, bf16[192,384]{1,0:T(8,128)(2,1)}, u32[]{:S(2)}) copy-start(bf16[192,384]{1,0:T(8,128)(2,1)} %fusion.28) | copy-start | bytes 442372
  120.1 16.2 %copy-start.2 = (bf16[192,3072]{1,0:T(8,128)(2,1)S(1)}, bf16[192,3072]{1,0:T(8,128)(2,1)}, u32[]{:S(2)}) copy-start(bf16[192,3072]{1,0:T(8,128)(2,1)} %param.11) | copy-start | bytes 3538948
  120.1 16.2 %copy-start.5 = (f32[1,3072]{1,0:T(1,128)S(1)}, f32[1,3072]{1,0:T(1,128)}, u32[]{:S(2)}) copy-start(f32[1,3072]{1,0:T(1,128)} %param.12) | copy-start | bytes 36868
  120.1 6.0 %collective-permute-start.15 = (bf16[192,384]{1,0:T(8,128)(2,1)S(1)}, bf16[192,384]{1,0:T(8,128)(2,1)S(1)}, u32[]{:S(2)}, u32[]{:S(2)}) collective-permute-start(bf16[192,384]{1,0:T(8,128)(2,1)S(1)} %copy-done.4), channel_id=1, source_target_pairs={{0,64},{128,192},{448,384},{320,256},{1,65},{129,193},{449,385},{3... | collective-permute-start | bytes 442376 | tf_op jit(solution)/shard_map/ppermute | solution.py:178
  128.9 10.7 %collective-permute-start.13 = (bf16[192,512]{1,0:T(8,128)(2,1)S(1)}, bf16[192,512]{1,0:T(8,128)(2,1)S(1)}, u32[]{:S(2)}, u32[]{:S(2)}) collective-permute-start(bf16[192,512]{1,0:T(8,128)(2,1)S(1)} %fusion.10), channel_id=1, source_target_pairs={{0,2},{2,0},{1,3},{3,1},{4,6},{6,4},{5,7},{7,5},{8,10},{10,8},{9,1... | collective-permute-start | bytes 589832 | tf_op jit(solution)/shard_map/ppermute | solution.py:17
  139.6 0.7 copy-start.3

commit v5 on v3

v5 whole, which is shorter than its diff:
```python
import jax
import jax.numpy as jnp
from jax import lax
from jax.experimental import pallas as pl
from jax.experimental.pallas import tpu as pltpu
from jax.sharding import Mesh, PartitionSpec as P

GRID_SIDE = 16
BLOCK_SIDE = 4
PATCHES = 256
AXES = ("section", "zlo", "x", "core", "tensor")
DP = ("zlo", "x", "core")


def around(value, axis, steps):
    count = lax.axis_size(axis)
    return lax.ppermute(value, axis, [(i, (i + steps) % count) for i in range(count)])


def tied(value, *others):
    return lax.optimization_barrier((value, *others))[0]


def masked_patches(mask_blocks):
    per_side = GRID_SIDE // BLOCK_SIDE
    within = jnp.arange(BLOCK_SIDE * BLOCK_SIDE, dtype=jnp.int32)
    chosen = mask_blocks[..., None]
    grid_row = chosen // per_side * BLOCK_SIDE + within // BLOCK_SIDE
    grid_col = chosen % per_side * BLOCK_SIDE + within % BLOCK_SIDE
    return grid_row * GRID_SIDE + grid_col


def normed(values, images):
    shaped = values.reshape(images, -1, values.shape[-1])
    center = jnp.mean(shaped, axis=1, keepdims=True)
    off = shaped - center
    spread = jnp.mean(jnp.square(off), axis=1, keepdims=True)
    return (off * lax.rsqrt(spread + 1e-05)).reshape(values.shape)


def transpose_kernel(first, second, out):
    rows = first.shape[0]
    out[:, :rows] = first[...].T
    out[:, rows:] = second[...].T


def transposed(first, second):
    rows, depth = first.shape
    return pl.pallas_call(
        transpose_kernel,
        out_shape=jax.ShapeDtypeStruct((depth, 2 * rows), first.dtype),
    )(first, second)


def product_kernel(x, held, below, above, low, high, context, out):
    plane = pl.program_id(0)
    count = 4
    opposite = jnp.where(plane < count // 2, low[0], high[0])
    weight = jnp.concatenate([held[0], above[0], opposite, below[0]], axis=0)
    made = jnp.dot(weight, context[...], preferred_element_type=jnp.float32).astype(out.dtype)
    shard, rows = held.shape[1], out.shape[-1]
    for steps in range(count):
        at = (x[0] + steps) % count
        for part in range(2):
            out[0, at // 2, part, at % 2] = made[
                steps * shard:(steps + 1) * shard, part * rows:(part + 1) * rows
            ]


def products(x, held, below, above, low, high, context):
    lines, shard, depth = held.shape
    rows = context.shape[1] // 2
    block = lambda index: pl.BlockSpec((1, shard, depth), lambda z: (index(z), 0, 0))
    return pl.pallas_call(
        product_kernel,
        grid=(lines,),
        in_specs=[pl.BlockSpec(memory_space=pltpu.SMEM)]
        + [block(lambda z: z)] * 3
        + [block(lambda z: jnp.minimum(z, lines // 2 - 1)), block(lambda z: jnp.maximum(z - lines // 2, 0))]
        + [pl.BlockSpec(context.shape, lambda z: (0, 0))],
        out_specs=pl.BlockSpec((1, 2, 2, 2, shard, rows), lambda z: (z, 0, 0, 0, 0, 0)),
        out_shape=jax.ShapeDtypeStruct((lines, 2, 2, 2, shard, rows), jnp.bfloat16),
        compiler_params=pltpu.CompilerParams(vmem_limit_bytes=24 << 20),
        cost_estimate=pl.CostEstimate(
            flops=16 * lines * shard * depth * rows,
            bytes_accessed=2 * (8 * lines * shard * rows + 4 * lines * shard * depth + 2 * depth * rows),
            transcendentals=0,
        ),
    )(x, held, below, above, low, high, context)


def ready_kernel(previous, ids, out, hot, same):
    images = previous.shape[0] // PATCHES
    out[...] = 0.5 * normed(previous[...].astype(jnp.float32), images)
    lane = lax.broadcasted_iota(jnp.int32, hot.shape, 1)
    hot[...] = jnp.where(lane == ids[...], 1.0, 0.0).astype(hot.dtype)
    row = lax.broadcasted_iota(jnp.int32, same.shape, 0)
    lane = lax.broadcasted_iota(jnp.int32, same.shape, 1)
    same[...] = jnp.where(lane == row, 1.0, 0.0).astype(same.dtype)


def final_kernel(core, mine, other, old, hot, same, predicted, targets, error):
    images = targets.shape[0] // PATCHES
    shard = mine.shape[0] // 2
    first = core[0] == 0
    pieces = []
    for pair in range(2):
        a, b = (part[pair * shard:(pair + 1) * shard] for part in (mine, other))
        pieces += [jnp.where(first, a, b), jnp.where(first, b, a)]
    ordered = lax.dot_general(
        same[...],
        jnp.concatenate(pieces, axis=0),
        (((1,), (1,)), ((), ())),
        preferred_element_type=jnp.float32,
    )
    made = (0.5 * normed(ordered, images) + old[...]).astype(targets.dtype)
    targets[...] = made
    picked = jnp.dot(hot[...], made[:PATCHES], preferred_element_type=jnp.float32)
    error[...] = predicted[...].astype(jnp.float32) - picked


def on_device(context, out_weight, previous, section_act, fresh_batch, section_gains, mask_blocks):
    f32, bf16 = jnp.float32, jnp.bfloat16
    sections = lax.axis_size("section")
    position, x, core = (lax.axis_index(name) for name in ("section", "x", "core"))
    rows, width = previous.shape
    act = section_act[0]
    depth, shard = out_weight.shape
    far = sections // 2

    held = lax.all_gather(out_weight.T, "zlo", axis=0, tiled=False)
    below = around(held, "x", 1)
    above = around(held, "x", -1)
    incoming = around(act, "section", 1)
    both = transposed(context, around(context, "core", 1))
    below, incoming, both = lax.optimization_barrier((below, incoming, both))
    middle = held.shape[0] // 2
    low = around(below[:middle], "x", 1)
    high = around(above[middle:], "x", -1)
    partial = products(x.astype(jnp.int32).reshape(1), held, below, above, low, high, both)
    partial = partial.reshape(sections, 2, 2 * shard, rows)
    summed = lax.psum_scatter(partial, "section", scatter_dimension=0, tiled=False)
    mine, other = summed[0], around(summed[1], "core", 1)

    last = sections - 1
    first, ends, near = position == 0, (position == 0) | (position == last), position < far
    cut = lambda value, s, count=1: value[:, s * width:(s + count) * width]
    incoming, act, previous = lax.optimization_barrier((incoming, act, previous, partial))[:3]
    passed = lax.ppermute(
        jnp.where(first, cut(incoming, 2, 2), cut(act, last - 3, 2)), "section", [(0, 2), (last, last - 2)]
    )
    onward = jnp.where(
        ends,
        jnp.where(first, cut(incoming, 1), cut(act, last - 1)),
        jnp.where(near, cut(passed, 1), cut(passed, 0)),
    )
    handed = lax.ppermute(onward, "section", [(0, 1), (2, 3), (last, last - 1), (last - 2, last - 3)])
    kept = jnp.where(
        ends,
        jnp.where(first, cut(incoming, 0), cut(act, last)),
        jnp.where(near, cut(passed, 0), cut(passed, 1)),
    )
    predicted = jnp.where(ends | (position == 2) | (position == last - 2), kept, handed)

    current = jnp.where(first, fresh_batch, incoming)
    wide = current.astype(f32)
    own = jnp.sum(wide * wide, axis=-1)
    squares = own + around(own, "tensor", 1)
    features = act.shape[-1] * lax.axis_size("tensor")
    scaling = lax.rsqrt(squares[:, None] / features + 1e-06)
    section_out = (wide * scaling * section_gains).astype(bf16)[None]

    ids = masked_patches(mask_blocks[0]).reshape(-1, 1)
    old, hot, same = pl.pallas_call(
        ready_kernel,
        out_shape=(
            jax.ShapeDtypeStruct((rows, width), f32),
            jax.ShapeDtypeStruct((ids.shape[0], PATCHES), bf16),
            jax.ShapeDtypeStruct((rows, rows), bf16),
        ),
        cost_estimate=pl.CostEstimate(flops=0, bytes_accessed=8 << 20, transcendentals=0),
    )(previous, ids)

    vmem = pl.BlockSpec(memory_space=pltpu.VMEM)
    targets, target_error = pl.pallas_call(
        final_kernel,
        in_specs=[pl.BlockSpec(memory_space=pltpu.SMEM)] + [vmem] * 6,
        out_specs=(vmem, vmem),
        out_shape=(
            jax.ShapeDtypeStruct((rows, width), bf16),
            jax.ShapeDtypeStruct(predicted.shape, f32),
        ),
    )(core.astype(jnp.int32).reshape(1), mine, other, old, hot, same, predicted)
    return (targets, section_out, target_error)


def solution(mesh):
    fine = Mesh(mesh.devices.reshape(8, 4, 4, 2, 2), AXES)
    in_specs = (
        P(DP, "section"),
        P("section", ("tensor",) + DP),
        P(DP, ("tensor", "section")),
        P("section", DP, "tensor"),
        P(DP, "tensor"),
        P("section", "tensor"),
        P(DP, None),
    )
    out_specs = (
        P(DP, ("tensor", "section")),
        P("section", DP, "tensor"),
        P(DP, ("tensor", "section")),
    )
    return jax.shard_map(
        on_device, mesh=fine, in_specs=in_specs, out_specs=out_specs, check_vma=False
    )
```

time: 138 us -> 146 us (1.058)
  waiting for transfers between devices: 20.3 us -> 50.3 us
  starting transfers between devices: 67.4 us -> 41.6 us
  between operations: 1.34 us -> 14.2 us
  matrix products: 12.6 us -> 0 us
  Pallas kernels: 5.96 us -> 12.6 us
  blocking collectives: 18.5 us -> 14.2 us
    reduce_scatter x0 -> x1, waiting for transfers between devices: none -> 29.3 us  [on_device(): lax.psum_scatter(partial, 'section', scatter_dimension=0, tiled=False)]
    ppermute x16 -> x8, starting transfers between devices: 60.1 us -> 36 us  [around(): lax.ppermute(value, axis, [(i, (i + steps) % count) for i in range(count)])]
    dot_general x9 -> x0, matrix products: 12.6 us -> none  [product(): return jnp.dot(weight, both, preferred_element_type=f32)]
    ppermute x3 -> x2, waiting for transfers between devices: 0.01 us -> 5.18 us  [the longest x1 5.17 us: on_device(): lax.ppermute(jnp.where(first, cut(incoming, 2, 2), cut(act, last - 3, 2))...]
    ppermute x16 -> x8, waiting for transfers between devices: 20.3 us -> 15.9 us  [around(): lax.ppermute(value, axis, [(i, (i + steps) % count) for i in range(count)])]
    all_gather x1, blocking collectives: 18.5 us -> 14.2 us  [on_device(): held = lax.all_gather(out_weight.T, 'zlo', axis=0, tiled=False)]
    pallas_call x0 -> x1, Pallas kernels: none -> 4.14 us  [products(): pl.pallas_call(product_kernel, grid=(lines,), in_specs=[pl.BlockSpec(memo...]
    pallas_call x1, Pallas kernels: 0.49 us -> 3.04 us  [transposed(): pl.pallas_call(transpose_kernel, out_shape=jax.ShapeDtypeStruct((depth, 2...]
  transfers between devices with their start and end apart: 19 -> 11, of which waited for: 3 -> 4; matrix products, arithmetic and copies ran while one was open for 14% -> 7% of each run, Pallas kernels for 2% -> 4%
where the time goes in v5:
time: 146 us; the launch traced here: 145 us
  waiting for transfers between devices  50.3 us (34%)
  starting transfers between devices  41.6 us (28%)
  blocking collectives  14.2 us (10%)
  between operations  14.2 us (10%)
  Pallas kernels  12.6 us (9%)
  local copies, waits for them, and re-layouts  6.63 us (5%)
  other arithmetic  5.62 us (4%)
    ppermute x8, starting transfers between devices, around(): lax.ppermute(value, axis, [(i, (i + steps) % count) for i in range(count)])  36 us
    reduce_scatter x1, waiting for transfers between devices, on_device(): lax.psum_scatter(partial, 'section', scatter_dimension=0, tiled=False)  29.3 us
    ppermute x8, waiting for transfers between devices, around(): lax.ppermute(value, axis, [(i, (i + steps) % count) for i in range(count)])  15.9 us
    all_gather x1, blocking collectives, on_device(): held = lax.all_gather(out_weight.T, 'zlo', axis=0, tiled=False)  14.2 us
    ppermute x1, waiting for transfers between devices, on_device(): lax.ppermute(jnp.where(first, cut(incoming, 2, 2), cut(act, last - 3, 2))...  5.17 us
    ppermute x1, starting transfers between devices, on_device(): lax.ppermute(jnp.where(first, cut(incoming, 2, 2), cut(act, last - 3, 2))...  4.23 us
    pallas_call x1, Pallas kernels, products(): pl.pallas_call(product_kernel, grid=(lines,), in_specs=[pl.BlockSpec(memo...  4.14 us
    pallas_call x1, Pallas kernels, on_device(): pl.pallas_call(final_kernel, in_specs=[pl.BlockSpec(memory_space=pltpu.SM...  3.05 us
  transfers between devices with their start and end apart: 11, of which 4 were waited for; matrix products, arithmetic and copies ran while one was open for 7% of the time, Pallas kernels for 4%

profile of v5, /device:TPU:1, one launch (start us, length us, event | category | flops | bytes accessed | tf_op | source)
XLA Modules:
  0.0 145.2 jit_solution(14537212997452300126)
XLA Ops:
  7.2 0.0 reduce-scatter.2.cloned.1.call-start
  7.2 4.0 %collective-permute-start.1 = (bf16[192,3072]{1,0:T(8,128)(2,1)}, bf16[192,3072]{1,0:T(8,128)(2,1)S(1)}, u32[]{:S(2)}, u32[]{:S(2)}) collective-permute-start(bf16[192,3072]{1,0:T(8,128)(2,1)} %bitcast.33), channel_id=1, source_target_pairs={{0,64},{64,128},{128,192},{192,256},{256,320},{320,384},{384,448},... | collective-permute-start | bytes 3538952 | tf_op jit(solution)/shard_map/ppermute | solution.py:17
  11.3 6.7 %collective-permute-start.2 = (bf16[512,768]{1,0:T(8,128)(2,1)}, bf16[512,768]{1,0:T(8,128)(2,1)}, u32[]{:S(2)}, u32[]{:S(2)}) collective-permute-start(bf16[512,768]{1,0:T(8,128)(2,1)} %first.1), channel_id=1, source_target_pairs={{0,2},{2,0},{1,3},{3,1},{4,6},{6,4},{5,7},{7,5},{8,10},{10,8},{9,1... | collective-permute-start | bytes 2359304 | tf_op jit(solution)/shard_map/ppermute | solution.py:17
  17.9 14.2 %all-gather = bf16[384,768]{1,0:T(8,128)(2,1)S(1)} all-gather(bf16[96,768]{1,0:T(8,128)(2,1)} %bitcast.37), channel_id=2, replica_groups=mesh['section'=8,'zlo'=4,'x'=4,'core'=2,'tensor'=2] {'zlo'}, dimensions={0}, use_global_device_ids=true | all-gather | bytes 737280 | tf_op jit(solution)/shard_map/all_gather | solution.py:131
  32.1 4.7 %collective-permute-start.3 = (bf16[4,96,768]{2,1,0:T(8,128)(2,1)S(1)}, bf16[4,96,768]{2,1,0:T(8,128)(2,1)S(1)}, u32[]{:S(2)}, u32[]{:S(2)}) collective-permute-start(bf16[4,96,768]{2,1,0:T(8,128)(2,1)S(1)} %bitcast.30), channel_id=1, source_target_pairs={{0,12},{4,0},{8,4},{12,8},{1,13},{5,1},{9,5},{13,9},{2,14},{6,2},{... | collective-permute-start | bytes 1769480 | tf_op jit(solution)/shard_map/ppermute | solution.py:17
  36.8 1.9 %collective-permute-start = (bf16[4,96,768]{2,1,0:T(8,128)(2,1)S(1)}, bf16[4,96,768]{2,1,0:T(8,128)(2,1)S(1)}, u32[]{:S(2)}, u32[]{:S(2)}) collective-permute-start(bf16[4,96,768]{2,1,0:T(8,128)(2,1)S(1)} %bitcast.31), channel_id=1, source_target_pairs={{0,4},{4,8},{8,12},{12,0},{1,5},{5,9},{9,13},{13,1},{2,6},{6,10},{... | collective-permute-start | bytes 1769480 | tf_op jit(solution)/shard_map/ppermute | solution.py:17
  38.8 8.9 %collective-permute-done.3.above = bf16[4,96,768]{2,1,0:T(8,128)(2,1)S(1)} collective-permute-done((bf16[4,96,768]{2,1,0:T(8,128)(2,1)S(1)}, bf16[4,96,768]{2,1,0:T(8,128)(2,1)S(1)}, u32[]{:S(2)}, u32[]{:S(2)}) %collective-permute-start.3) | collective-permute-done | bytes 589856 | tf_op jit(solution)/shard_map/ppermute | solution.py:17
  47.7 0.7 slice.52
  48.4 5.3 %collective-permute-start.5 = (bf16[2,96,768]{2,1,0:T(8,128)(2,1)}, bf16[2,96,768]{2,1,0:T(8,128)(2,1)S(1)}, u32[]{:S(2)}, u32[]{:S(2)}) collective-permute-start(bf16[2,96,768]{2,1,0:T(8,128)(2,1)} %slice.52), channel_id=1, source_target_pairs={{0,12},{4,0},{8,4},{12,8},{1,13},{5,1},{9,5},{13,9},{2,14},{6,2},{... | collective-permute-start | bytes 884744 | tf_op jit(solution)/shard_map/ppermute | solution.py:17
  53.7 0.0 collective-permute-done.2.second
  53.7 3.0 %shard_map.94.context = bf16[768,1024]{1,0:T(8,128)(2,1)} custom-call(bf16[512,768]{1,0:T(8,128)(2,1)} %first.1, bf16[512,768]{1,0:T(8,128)(2,1)} %collective-permute-done.2.second), custom_call_target="tpu_custom_call" | custom-call | tf_op jit(solution)/shard_map/pallas_call | solution.py:49
  56.8 0.0 collective-permute-done.below
  56.8 0.0 collective-permute-done.1
  56.8 0.7 slice.40
  57.5 1.9 %collective-permute-start.4 = (bf16[2,96,768]{2,1,0:T(8,128)(2,1)}, bf16[2,96,768]{2,1,0:T(8,128)(2,1)S(1)}, u32[]{:S(2)}, u32[]{:S(2)}) collective-permute-start(bf16[2,96,768]{2,1,0:T(8,128)(2,1)} %slice.40), channel_id=1, source_target_pairs={{0,4},{4,8},{8,12},{12,0},{1,5},{5,9},{9,13},{13,1},{2,6},{6,10},{... | collective-permute-start | bytes 884744 | tf_op jit(solution)/shard_map/ppermute | solution.py:17
  59.4 0.0 collective-permute-done.5.high
  59.4 6.9 %collective-permute-done.4.low = bf16[2,96,768]{2,1,0:T(8,128)(2,1)S(1)} collective-permute-done((bf16[2,96,768]{2,1,0:T(8,128)(2,1)}, bf16[2,96,768]{2,1,0:T(8,128)(2,1)S(1)}, u32[]{:S(2)}, u32[]{:S(2)}) %collective-permute-start.4) | collective-permute-done | bytes 294944 | tf_op jit(solution)/shard_map/ppermute | solution.py:17
  66.4 0.0 copy-start
  66.4 1.4 copy-done
  67.8 4.1 %shard_map.95 = bf16[4,2,2,2,96,512]{5,4,3,2,1,0:T(8,128)(2,1)} custom-call(s32[1]{0:T(128)} %bitcast.1.x, bf16[4,96,768]{2,1,0:T(8,128)(2,1)S(1)} %bitcast.32, bf16[4,96,768]{2,1,0:T(8,128)(2,1)S(1)} %collective-permute-done.below, bf16[4,96,768]{2,1,0:T(8,128)(2,1)S(1)} %collective-permute-done.3.above, ...), custom_call_target="tpu_custom_call" | custom-call | flops 2415919104 | bytes 7077888 | tf_op jit(solution)/shard_map/pallas_call | solution.py:74
  71.9 0.0 copy-start.4
  71.9 0.0 copy-start.1
  71.9 0.0 reduce-scatter.2.cloned.1.call-update
  72.0 0.6 copy-done.4
  72.6 0.1 add_add_fusion
  72.7 0.7 add.112.ids
  73.4 0.0 copy-done.1
  73.4 0.5 fusion
  73.9 0.0 copy-start.3
  73.9 7.9 %collective-permute-start.9 = (f32[192]{0:T(256)S(1)}, f32[192]{0:T(256)S(1)}, u32[]{:S(2)}, u32[]{:S(2)}) collective-permute-start(f32[192]{0:T(256)S(1)} %fusion), channel_id=1, source_target_pairs={{0,1},{1,0},{2,3},{3,2},{4,5},{5,4},{6,7},{7,6},{8,9},{9,8},{10,11... | collective-permute-start | bytes 2312 | tf_op jit(solution)/shard_map/ppermute | solution.py:17
  81.8 1.0 slice_select_fusion
  82.8 4.2 %collective-permute-start.7 = (bf16[192,768]{1,0:T(8,128)(2,1)S(1)}, bf16[192,768]{1,0:T(8,128)(2,1)S(1)}, u32[]{:S(2)}, u32[]{:S(2)}) collective-permute-start(bf16[192,768]{1,0:T(8,128)(2,1)S(1)} %slice_select_fusion), channel_id=1, source_target_pairs={{0,128},{448,320},{1,129},{449,321},{2,130},{450,322},{3,131},{451... | collective-permute-start | bytes 884744 | tf_op jit(solution)/shard_map/ppermute | solution.py:149
  87.1 2.4 %shard_map.96 = (f32[512,384]{1,0:T(8,128)}, bf16[192,256]{1,0:T(8,128)(2,1)}, bf16[512,512]{1,0:T(8,128)(2,1)}) custom-call(bf16[512,384]{1,0:T(8,128)(2,1)} %previous, s32[192,1]{1,0:T(8,128)} %add.112.ids), custom_call_target="tpu_custom_call" | custom-call | bytes 8388608 | tf_op jit(solution)/shard_map/pallas_call | solution.py:174
  89.5 0.0 collective-permute-done.9
  89.5 0.0 copy-done.3
  89.5 1.5 %fusion.3 = bf16[1,192,3072]{2,1,0:T(8,128)(2,1)} fusion(f32[3072]{0:T(1024)S(1)} %bitcast.38, f32[192]{0:T(256)S(1)} %add_rsqrt_fusion, bf16[192,3072]{1,0:T(8,128)(2,1)S(1)} %copy-done.1, bf16[192,3072]{1,0:T(8,128)(2,1)S(1)} %collective-permute-done.1, pred[]{:T(512)S(6)} %eq.17), kind=kLoop, calls=%fused_computation.5 | loop fusion | flops 2949120 | bytes 3552001 | tf_op jit(solution)/shard_map/broadcast_in_dim | solution.py:171
  91.0 5.2 %collective-permute-done.7 = bf16[192,768]{1,0:T(8,128)(2,1)S(1)} collective-permute-done((bf16[192,768]{1,0:T(8,128)(2,1)S(1)}, bf16[192,768]{1,0:T(8,128)(2,1)S(1)}, u32[]{:S(2)}, u32[]{:S(2)}) %collective-permute-start.7) | collective-permute-done | bytes 294944 | tf_op jit(solution)/shard_map/ppermute | solution.py:149
  96.2 1.0 select_select_fusion
  97.2 1.3 collective-permute-start.8
  98.5 29.3 %reduce-scatter.2.cloned.1.call-done = bf16[1,2,192,512]{3,2,1,0:T(8,128)(2,1)} async-done(((bf16[8,2,192,512]{3,2,1,0:T(8,128)(2,1)}), bf16[1,2,192,512]{3,2,1,0:T(8,128)(2,1)}) %reduce-scatter.2.cloned.1.call-update) | async-done | bytes 393232 | tf_op jit(solution)/shard_map/reduce_scatter | solution.py:142
  127.7 1.7 %slice_bitcast_fusion = (bf16[192,512]{1,0:T(8,128)(2,1)S(1)}, bf16[192,512]{1,0:T(8,128)(2,1)}) fusion(bf16[1,2,192,512]{3,2,1,0:T(8,128)(2,1)} %reduce-scatter.2.cloned.1.call-done), kind=kLoop, calls=%fused_computation.8 | loop fusion | bytes 786432 | tf_op jit(solution)/shard_map/squeeze | solution.py:143
  129.5 3.5 %collective-permute-start.6 = (bf16[192,512]{1,0:T(8,128)(2,1)S(1)}, bf16[192,512]{1,0:T(8,128)(2,1)S(1)}, u32[]{:S(2)}, u32[]{:S(2)}) collective-permute-start(bf16[192,512]{1,0:T(8,128)(2,1)S(1)} %get-tuple-element.25), channel_id=1, source_target_pairs={{0,2},{2,0},{1,3},{3,1},{4,6},{6,4},{5,7},{7,5},{8,10},{10,8},{9,1... | collective-permute-start | bytes 589832 | tf_op jit(solution)/shard_map/ppermute | solution.py:17
  133.0 0.0 collective-permute-done.8
  133.0 1.6 %select_select_fusion.1.predicted = bf16[192,384]{1,0:T(8,128)(2,1)} fusion(bf16[192,384]{1,0:T(8,128)(2,1)S(1)} %collective-permute-done.8, bf16[192,3072]{1,0:T(8,128)(2,1)} %bitcast.36, bf16[192,3072]{1,0:T(8,128)(2,1)S(1)} %collective-permute-done.1, pred[]{:T(512)S(6)} %lt.17, pred[]{:T(512)S(6)} %eq.17, pred[]{:T(512)S(6)} %or.9, pred[]{:T(512)S(6)} %or.11, ...), kind=kLoop, calls=%fused_computation.11 | loop fusion | flops 294912 | bytes 884740 | tf_op jit(solution)/shard_map/jit(_where)/select_n | solution.py:163
  134.6 0.0 collective-permute-done.6.other
  134.6 0.0 copy-start.2
  134.6 0.7 copy-done.2
  135.3 3.0 %shard_map.97 = (bf16[512,384]{1,0:T(8,128)(2,1)}, f32[192,384]{1,0:T(8,128)}) custom-call(s32[1]{0:T(128)} %bitcast.core, bf16[192,512]{1,0:T(8,128)(2,1)} %get-tuple-element.26.mine, bf16[192,512]{1,0:T(8,128)(2,1)} %copy-done.2, f32[512,384]{1,0:T(8,128)} %get-tuple-element.18.old, bf16[192,256]{1,0:T(8,128)(2,1)} %get-tuple-element.19.hot, ...), custom_call_target="tpu_custom_call" | custom-call | tf_op jit(solution)/shard_map/pallas_call | solution.py:185
  (3 shorter events, 0.0 us)
Async XLA Ops:
  7.2 120.6 %reduce-scatter.2.cloned.1.call-start = ((), (), s32[]{:S(2)}) async-start(), calls=%async_computation.1 | async-start | bytes 3538944 | tf_op jit(solution)/shard_map/reduce_scatter | solution.py:142
  7.2 49.6 %collective-permute-start.1 = (bf16[192,3072]{1,0:T(8,128)(2,1)}, bf16[192,3072]{1,0:T(8,128)(2,1)S(1)}, u32[]{:S(2)}, u32[]{:S(2)}) collective-permute-start(bf16[192,3072]{1,0:T(8,128)(2,1)} %bitcast.33), channel_id=1, source_target_pairs={{0,64},{64,128},{128,192},{192,256},{256,320},{320,384},{384,448},... | collective-permute-start | bytes 3538952 | tf_op jit(solution)/shard_map/ppermute | solution.py:17
  11.3 42.5 %collective-permute-start.2 = (bf16[512,768]{1,0:T(8,128)(2,1)}, bf16[512,768]{1,0:T(8,128)(2,1)}, u32[]{:S(2)}, u32[]{:S(2)}) collective-permute-start(bf16[512,768]{1,0:T(8,128)(2,1)} %first.1), channel_id=1, source_target_pairs={{0,2},{2,0},{1,3},{3,1},{4,6},{6,4},{5,7},{7,5},{8,10},{10,8},{9,1... | collective-permute-start | bytes 2359304 | tf_op jit(solution)/shard_map/ppermute | solution.py:17
  32.1 15.6 %collective-permute-start.3 = (bf16[4,96,768]{2,1,0:T(8,128)(2,1)S(1)}, bf16[4,96,768]{2,1,0:T(8,128)(2,1)S(1)}, u32[]{:S(2)}, u32[]{:S(2)}) collective-permute-start(bf16[4,96,768]{2,1,0:T(8,128)(2,1)S(1)} %bitcast.30), channel_id=1, source_target_pairs={{0,12},{4,0},{8,4},{12,8},{1,13},{5,1},{9,5},{13,9},{2,14},{6,2},{... | collective-permute-start | bytes 1769480 | tf_op jit(solution)/shard_map/ppermute | solution.py:17
  36.8 19.9 %collective-permute-start = (bf16[4,96,768]{2,1,0:T(8,128)(2,1)S(1)}, bf16[4,96,768]{2,1,0:T(8,128)(2,1)S(1)}, u32[]{:S(2)}, u32[]{:S(2)}) collective-permute-start(bf16[4,96,768]{2,1,0:T(8,128)(2,1)S(1)} %bitcast.31), channel_id=1, source_target_pairs={{0,4},{4,8},{8,12},{12,0},{1,5},{5,9},{9,13},{13,1},{2,6},{6,10},{... | collective-permute-start | bytes 1769480 | tf_op jit(solution)/shard_map/ppermute | solution.py:17
  48.4 11.0 %collective-permute-start.5 = (bf16[2,96,768]{2,1,0:T(8,128)(2,1)}, bf16[2,96,768]{2,1,0:T(8,128)(2,1)S(1)}, u32[]{:S(2)}, u32[]{:S(2)}) collective-permute-start(bf16[2,96,768]{2,1,0:T(8,128)(2,1)} %slice.52), channel_id=1, source_target_pairs={{0,12},{4,0},{8,4},{12,8},{1,13},{5,1},{9,5},{13,9},{2,14},{6,2},{... | collective-permute-start | bytes 884744 | tf_op jit(solution)/shard_map/ppermute | solution.py:17
  57.5 8.9 %collective-permute-start.4 = (bf16[2,96,768]{2,1,0:T(8,128)(2,1)}, bf16[2,96,768]{2,1,0:T(8,128)(2,1)S(1)}, u32[]{:S(2)}, u32[]{:S(2)}) collective-permute-start(bf16[2,96,768]{2,1,0:T(8,128)(2,1)} %slice.40), channel_id=1, source_target_pairs={{0,4},{4,8},{8,12},{12,0},{1,5},{5,9},{9,13},{13,1},{2,6},{6,10},{... | collective-permute-start | bytes 884744 | tf_op jit(solution)/shard_map/ppermute | solution.py:17
  66.4 1.4 copy-start
  71.9 0.7 copy-start.4
  71.9 1.5 %copy-start.1 = (bf16[192,3072]{1,0:T(8,128)(2,1)S(1)}, bf16[192,3072]{1,0:T(8,128)(2,1)}, u32[]{:S(2)}) copy-start(bf16[192,3072]{1,0:T(8,128)(2,1)} %param.11) | copy-start | bytes 3538948
  73.9 15.6 %copy-start.3 = (f32[1,3072]{1,0:T(1,128)S(1)}, f32[1,3072]{1,0:T(1,128)}, u32[]{:S(2)}) copy-start(f32[1,3072]{1,0:T(1,128)} %param.12) | copy-start | bytes 36868
  73.9 15.6 %collective-permute-start.9 = (f32[192]{0:T(256)S(1)}, f32[192]{0:T(256)S(1)}, u32[]{:S(2)}, u32[]{:S(2)}) collective-permute-start(f32[192]{0:T(256)S(1)} %fusion), channel_id=1, source_target_pairs={{0,1},{1,0},{2,3},{3,2},{4,5},{5,4},{6,7},{7,6},{8,9},{9,8},{10,11... | collective-permute-start | bytes 2312 | tf_op jit(solution)/shard_map/ppermute | solution.py:17
  82.8 13.4 %collective-permute-start.7 = (bf16[192,768]{1,0:T(8,128)(2,1)S(1)}, bf16[192,768]{1,0:T(8,128)(2,1)S(1)}, u32[]{:S(2)}, u32[]{:S(2)}) collective-permute-start(bf16[192,768]{1,0:T(8,128)(2,1)S(1)} %slice_select_fusion), channel_id=1, source_target_pairs={{0,128},{448,320},{1,129},{449,321},{2,130},{450,322},{3,131},{451... | collective-permute-start | bytes 884744 | tf_op jit(solution)/shard_map/ppermute | solution.py:149
  97.2 35.8 %collective-permute-start.8 = (bf16[192,384]{1,0:T(8,128)(2,1)S(1)}, bf16[192,384]{1,0:T(8,128)(2,1)S(1)}, u32[]{:S(2)}, u32[]{:S(2)}) collective-permute-start(bf16[192,384]{1,0:T(8,128)(2,1)S(1)} %select_select_fusion), channel_id=1, source_target_pairs={{0,64},{128,192},{448,384},{320,256},{1,65},{129,193},{449,385},{3... | collective-permute-start | bytes 442376 | tf_op jit(solution)/shard_map/ppermute | solution.py:157
  129.5 5.1 %collective-permute-start.6 = (bf16[192,512]{1,0:T(8,128)(2,1)S(1)}, bf16[192,512]{1,0:T(8,128)(2,1)S(1)}, u32[]{:S(2)}, u32[]{:S(2)}) collective-permute-start(bf16[192,512]{1,0:T(8,128)(2,1)S(1)} %get-tuple-element.25), channel_id=1, source_target_pairs={{0,2},{2,0},{1,3},{3,1},{4,6},{6,4},{5,7},{7,5},{8,10},{10,8},{9,1... | collective-permute-start | bytes 589832 | tf_op jit(solution)/shard_map/ppermute | solution.py:17
  134.6 0.7 copy-start.2
Sparse Core Ops, SparseCore 0:
  72.1 55.6 reduce-scatter.1

commit v6 on v4

--- a/solution.py
+++ b/solution.py
@@ -10,6 +10,7 @@
 PATCHES = 256
 AXES = ("section", "zlo", "x", "core", "tensor")
 DP = ("zlo", "x", "core")
+LATE = 3
 
 
 def around(value, axis, steps):
@@ -62,10 +63,10 @@
     same[...] = jnp.where(lane == row, 1.0, 0.0).astype(same.dtype)
 
 
-def final_kernel(core, mine, other, old, hot, same, predicted, targets, error):
+def final_kernel(place, mine, other, old, hot, same, kept, handed, targets, error):
     images = targets.shape[0] // PATCHES
     shard = mine.shape[0] // 2
-    first = core[0] == 0
+    first = place[0] == 0
     pieces = []
     for pair in range(2):
         a, b = (part[pair * shard:(pair + 1) * shard] for part in (mine, other))
@@ -79,7 +80,8 @@
     made = (0.5 * normed(ordered, images) + old[...]).astype(targets.dtype)
     targets[...] = made
     picked = jnp.dot(hot[...], made[:PATCHES], preferred_element_type=jnp.float32)
-    error[...] = predicted[...].astype(jnp.float32) - picked
+    predicted = jnp.where(place[1] == 1, kept[...], handed[...])
+    error[...] = predicted.astype(jnp.float32) - picked
 
 
 def on_device(context, out_weight, previous, section_act, fresh_batch, section_gains, mask_blocks):
@@ -95,6 +97,10 @@
     below = around(held, "x", 1)
     above = around(held, "x", -1)
     incoming = around(act, "section", 1)
+    both = transposed(context, around(context, "core", 1))
+    count = lax.axis_size("x")
+    weight = jnp.broadcast_to(held[:, None], (held.shape[0], count, shard, depth))
+
     ids = masked_patches(mask_blocks[0]).reshape(-1, 1)
     old, hot, same = pl.pallas_call(
         ready_kernel,
@@ -106,9 +112,9 @@
         cost_estimate=pl.CostEstimate(flops=0, bytes_accessed=8 << 20, transcendentals=0),
     )(previous, ids)
 
-    below, incoming, old = lax.optimization_barrier((below, incoming, old))
-    opposite = around(below, "x", 1)
-    both = transposed(context, around(tied(context, below), "core", 1))
+    below, incoming, old, both, weight = lax.optimization_barrier((below, incoming, old, both, weight))
+    opposite = around(above[:LATE], "x", -1)
+    opposite_rest = around(below[LATE:], "x", 1)
 
     def product(weight):
         return jnp.dot(weight, both, preferred_element_type=f32)
@@ -122,32 +128,26 @@
     def down(value):
         return around(value.astype(bf16), "section", -1)
 
-    dest = (position + far) % sections
+    put = lambda part, at, line=0: lax.dynamic_update_slice(weight, part[:, None], (line, at % count, 0, 0))
+    weight = put(below, x + 3)
+    weight = put(above, x + 1)
+    dest, weight = lax.optimization_barrier(((position + far) % sections, weight))
     plane = lambda part: lax.dynamic_index_in_dim(part, dest // 2, 0, keepdims=False)
     near = jnp.where(x % 2 == 0, plane(below), plane(above))
     begun = product(jnp.where(dest % 2 == x // 2, plane(held), near)).astype(bf16)
     rising = up(begun)
-    last = sections - 1
-    cut = lambda value, s, count=1: value[:, s * width:(s + count) * width]
-    arrived = tied(incoming, begun)
-    given = jnp.where(position == 0, cut(arrived, 2, 2), cut(act, last - 3, 2))
-    passed = lax.ppermute(given, "section", [(0, 2), (last, last - 2)])
-    opposite = tied(opposite, begun, given)
-
-    count = lax.axis_size("x")
-    weight = jnp.zeros((held.shape[0], count, shard, depth), bf16)
-    for part, at in (
-        (held, x), (below, x + 3), (above, x + 1), (opposite, x + 2),
-    ):
-        weight = lax.dynamic_update_slice(weight, part[:, None], (0, at % count, 0, 0))
+    beside = jnp.where(x % 2 == 0, plane(above), plane(below))
+    across = jnp.where(dest // 2 < LATE, plane(opposite), opposite_rest[0])
+    ended = product(jnp.where(dest % 2 == x // 2, beside, across)).astype(bf16)
+    falling = down(ended)
+
+    weight = put(tied(opposite, ended), x + 2)
+    weight = put(tied(opposite_rest, ended), x + 2, LATE)
     weight = weight.reshape(sections, 2 * shard, depth)
 
     def block(steps, after=()):
         place = tied(position, *after)
         return lax.dynamic_index_in_dim(weight, (place + steps) % sections, 0, keepdims=False)
-
-    rest = lax.dynamic_slice(weight, (dest, (1 - early_half(dest)) * shard, 0), (1, shard, depth))
-    falling = down(product(rest.reshape(shard, depth)))
 
     def spread(value, half):
         empty = jnp.zeros_like(value)
@@ -165,6 +165,11 @@
     sent = round_of(3, ())
     rising, falling = up(sent[0]), down(sent[1])
 
+    last = sections - 1
+    cut = lambda value, s, count=1: value[:, s * width:(s + count) * width]
+    arrived = incoming
+    given = tied(jnp.where(position == 0, cut(arrived, 2, 2), cut(act, last - 3, 2)), *sent)
+    passed = lax.ppermute(given, "section", [(0, 2), (last, last - 2)])
     sent = round_of(2, ())
     rising, falling = up(sent[0]), down(sent[1])
 
@@ -176,10 +181,10 @@
     first = position == 0
     onward = jnp.where(first, cut(arrived, 1), jnp.where(ends, cut(act, last - 1), jnp.where(low, cut(passed, 1), cut(passed, 0))))
     handed = lax.ppermute(
-        tied(onward, *sent), "section", [(0, 1), (2, 3), (last, last - 1), (last - 2, last - 3)]
+        onward, "section", [(0, 1), (2, 3), (last, last - 1), (last - 2, last - 3)]
     )
     kept = jnp.where(first, cut(arrived, 0), jnp.where(ends, cut(act, last), jnp.where(low, cut(passed, 0), cut(passed, 1))))
-    predicted = jnp.where(ends | (position == 2) | (position == last - 2), kept, handed)
+    keeps = ends | (position == 2) | (position == last - 2)
     current = jnp.where(position == 0, fresh_batch, incoming)
     wide = current.astype(f32)
     own = tied(jnp.sum(wide * wide, axis=-1), *sent)
@@ -196,13 +201,13 @@
     vmem = pl.BlockSpec(memory_space=pltpu.VMEM)
     targets, target_error = pl.pallas_call(
         final_kernel,
-        in_specs=[pl.BlockSpec(memory_space=pltpu.SMEM)] + [vmem] * 6,
+        in_specs=[pl.BlockSpec(memory_space=pltpu.SMEM)] + [vmem] * 7,
         out_specs=(vmem, vmem),
         out_shape=(
             jax.ShapeDtypeStruct((rows, width), bf16),
-            jax.ShapeDtypeStruct(predicted.shape, f32),
+            jax.ShapeDtypeStruct(kept.shape, f32),
         ),
-    )(core.astype(jnp.int32).reshape(1), mine.astype(bf16), other, old, hot, same, predicted)
+    )(jnp.stack([core, keeps]).astype(jnp.int32), mine.astype(bf16), other, old, hot, same, kept, handed)
     return (targets, section_out, target_error)
 
 

time: 144 us -> 135 us (0.938)
  the two profiles are of different devices: /device:TPU:25 before, /device:TPU:1 now
where the time goes in v6:
time: 135 us; the launch traced here: 134 us
  starting transfers between devices  73.2 us (54%)
  matrix products  14.5 us (11%)
  blocking collectives  14.2 us (11%)
  local copies, waits for them, and re-layouts  11.1 us (8%)
  Pallas kernels  8.58 us (6%)
  other arithmetic  7.02 us (5%)
  waiting for transfers between devices  4.21 us (3%)
    ppermute x16, starting transfers between devices, around(): lax.ppermute(value, axis, [(i, (i + steps) % count) for i in range(count)])  69.3 us
    dot_general x9, matrix products, product(): return jnp.dot(weight, both, preferred_element_type=f32)  14.5 us
    all_gather x1, blocking collectives, on_device(): held = lax.all_gather(out_weight.T, 'zlo', axis=0, tiled=False)  14.2 us
    dynamic_update_slice x4, local copies, waits for them, and re-layouts, on_device(): lax.dynamic_update_slice(weight, part[:, None], (line, at % count, 0, 0))  5.36 us
    ppermute x16, waiting for transfers between devices, around(): lax.ppermute(value, axis, [(i, (i + steps) % count) for i in range(count)])  4.2 us
    pallas_call x1, Pallas kernels, on_device(): pl.pallas_call(final_kernel, in_specs=[pl.BlockSpec(memory_space=pltpu.SM...  3.13 us
    pallas_call x1, Pallas kernels, transposed(): pl.pallas_call(transpose_kernel, out_shape=jax.ShapeDtypeStruct((depth, 2...  3.02 us
  transfers between devices with their start and end apart: 18, of which 2 were waited for; matrix products, arithmetic and copies ran while one was open for 23% of the time, Pallas kernels for 4%

profile of v6, /device:TPU:1, one launch (start us, length us, event | category | flops | bytes accessed | tf_op | source)
XLA Modules:
  0.0 134.0 jit_solution(7363686138520773061)
XLA Ops:
  0.6 4.0 %collective-permute-start.1 = (bf16[192,3072]{1,0:T(8,128)(2,1)}, bf16[192,3072]{1,0:T(8,128)(2,1)S(1)}, u32[]{:S(2)}, u32[]{:S(2)}) collective-permute-start(bf16[192,3072]{1,0:T(8,128)(2,1)} %bitcast.82), channel_id=1, source_target_pairs={{0,64},{64,128},{128,192},{192,256},{256,320},{320,384},{384,448},... | collective-permute-start | bytes 3538952 | tf_op jit(solution)/shard_map/ppermute | solution.py:18
  4.7 6.7 %collective-permute-start.2 = (bf16[512,768]{1,0:T(8,128)(2,1)}, bf16[512,768]{1,0:T(8,128)(2,1)S(1)}, u32[]{:S(2)}, u32[]{:S(2)}) collective-permute-start(bf16[512,768]{1,0:T(8,128)(2,1)} %first.1), channel_id=1, source_target_pairs={{0,2},{2,0},{1,3},{3,1},{4,6},{6,4},{5,7},{7,5},{8,10},{10,8},{9,1... | collective-permute-start | bytes 2359304 | tf_op jit(solution)/shard_map/ppermute | solution.py:18
  11.4 14.2 %all-gather = bf16[384,768]{1,0:T(8,128)(2,1)S(1)} all-gather(bf16[96,768]{1,0:T(8,128)(2,1)} %bitcast.85), channel_id=2, replica_groups=mesh['section'=8,'zlo'=4,'x'=4,'core'=2,'tensor'=2] {'zlo'}, dimensions={0}, use_global_device_ids=true | all-gather | bytes 737280 | tf_op jit(solution)/shard_map/all_gather | solution.py:96
  25.5 4.7 %collective-permute-start.3 = (bf16[4,96,768]{2,1,0:T(8,128)(2,1)S(1)}, bf16[4,96,768]{2,1,0:T(8,128)(2,1)S(1)}, u32[]{:S(2)}, u32[]{:S(2)}) collective-permute-start(bf16[4,96,768]{2,1,0:T(8,128)(2,1)S(1)} %bitcast.78), channel_id=1, source_target_pairs={{0,12},{4,0},{8,4},{12,8},{1,13},{5,1},{9,5},{13,9},{2,14},{6,2},{... | collective-permute-start | bytes 1769480 | tf_op jit(solution)/shard_map/ppermute | solution.py:18
  30.3 1.9 %collective-permute-start = (bf16[4,96,768]{2,1,0:T(8,128)(2,1)S(1)}, bf16[4,96,768]{2,1,0:T(8,128)(2,1)}, u32[]{:S(2)}, u32[]{:S(2)}) collective-permute-start(bf16[4,96,768]{2,1,0:T(8,128)(2,1)S(1)} %bitcast.79), channel_id=1, source_target_pairs={{0,4},{4,8},{8,12},{12,0},{1,5},{5,9},{9,13},{13,1},{2,6},{6,10},{... | collective-permute-start | bytes 1769480 | tf_op jit(solution)/shard_map/ppermute | solution.py:18
  32.4 0.7 fusion.58
  33.1 0.1 add_add_fusion
  33.2 0.7 add.334.ids
  33.9 2.4 %shard_map.94 = (f32[512,384]{1,0:T(8,128)}, bf16[192,256]{1,0:T(8,128)(2,1)}, bf16[512,512]{1,0:T(8,128)(2,1)}) custom-call(bf16[512,384]{1,0:T(8,128)(2,1)} %previous.1, s32[192,1]{1,0:T(8,128)} %add.334.ids), custom_call_target="tpu_custom_call" | custom-call | bytes 8388608 | tf_op jit(solution)/shard_map/pallas_call | solution.py:105
  36.3 0.7 pad_add_fusion.place
  37.0 4.1 %collective-permute-done.3 = bf16[4,96,768]{2,1,0:T(8,128)(2,1)S(1)} collective-permute-done((bf16[4,96,768]{2,1,0:T(8,128)(2,1)S(1)}, bf16[4,96,768]{2,1,0:T(8,128)(2,1)S(1)}, u32[]{:S(2)}, u32[]{:S(2)}) %collective-permute-start.3) | collective-permute-done | bytes 589856 | tf_op jit(solution)/shard_map/ppermute | solution.py:18
  41.1 0.8 slice.66
  41.9 5.3 %collective-permute-start.4 = (bf16[3,96,768]{2,1,0:T(8,128)(2,1)}, bf16[3,96,768]{2,1,0:T(8,128)(2,1)}, u32[]{:S(2)}, u32[]{:S(2)}) collective-permute-start(bf16[3,96,768]{2,1,0:T(8,128)(2,1)} %slice.66), channel_id=1, source_target_pairs={{0,12},{4,0},{8,4},{12,8},{1,13},{5,1},{9,5},{13,9},{2,14},{6,2},{... | collective-permute-start | bytes 1327112 | tf_op jit(solution)/shard_map/ppermute | solution.py:18
  47.2 0.0 copy-start.4
  47.2 0.9 copy-done.4
  48.1 3.0 %shard_map.95 = bf16[768,1024]{1,0:T(8,128)(2,1)} custom-call(bf16[512,768]{1,0:T(8,128)(2,1)} %first.1, bf16[512,768]{1,0:T(8,128)(2,1)} %copy-done.4), custom_call_target="tpu_custom_call" | custom-call | tf_op jit(solution)/shard_map/pallas_call | solution.py:50
  51.1 1.7 %broadcast_in_dim.24 = bf16[4,4,96,768]{3,2,1,0:T(8,128)(2,1)} broadcast(bf16[4,96,768]{2,1,0:T(8,128)(2,1)S(1)} %bitcast.80), dimensions={0,2,3} | broadcast | bytes 2949120 | tf_op jit(solution)/shard_map/broadcast_in_dim | solution.py:102
  52.8 2.0 %bitcast_dynamic-update-slice_fusion.1 = bf16[4,4,96,768]{3,2,1,0:T(8,128)(2,1)} fusion(bf16[4,4,96,768]{3,2,1,0:T(8,128)(2,1)} %broadcast_in_dim.24, s32[]{:T(128)S(6)} %select_n.294, bf16[4,96,768]{2,1,0:T(8,128)(2,1)} %collective-permute-done), kind=kLoop, calls=%fused_computation.22 | loop fusion | bytes 1179652 | tf_op jit(solution)/shard_map/dynamic_update_slice | solution.py:131
  54.8 0.9 bitcast_dynamic-update-slice_fusion
  55.7 0.9 slice.51
  56.6 0.0 copy-start.1
  56.6 2.1 %collective-permute-start.5 = (bf16[1,96,768]{2,1,0:T(8,128)(2,1)S(1)}, bf16[1,96,768]{2,1,0:T(8,128)(2,1)S(1)}, u32[]{:S(2)}, u32[]{:S(2)}) collective-permute-start(bf16[1,96,768]{2,1,0:T(8,128)(2,1)S(1)} %slice.51), channel_id=1, source_target_pairs={{0,4},{4,8},{8,12},{12,0},{1,5},{5,9},{9,13},{13,1},{2,6},{6,10},{... | collective-permute-start | bytes 442376 | tf_op jit(solution)/shard_map/ppermute | solution.py:18
  58.7 1.4 %convolution_convert_fusion = bf16[96,1024]{1,0:T(8,128)(2,1)S(1)} fusion(bf16[768,1024]{1,0:T(8,128)(2,1)S(1)} %copy-done, bf16[4,96,768]{2,1,0:T(8,128)(2,1)} %bitcast.81, s32[]{:T(128)S(6)} %select_n.303, pred[]{:T(512)S(6)} %eq.63, pred[]{:T(512)S(6)} %eq.62, bf16[4,96,768]{2,1,0:T(8,128)(2,1)} %collective-permute-done, ...), kind=kOutput, calls=%fused_computation.19 | convolution fusion | flops 151240704 | bytes 2211846 | tf_op jit(solution)/shard_map/dot_general | solution.py:120
  60.1 3.2 %collective-permute-start.6 = (bf16[96,1024]{1,0:T(8,128)(2,1)S(1)}, bf16[96,1024]{1,0:T(8,128)(2,1)S(1)}, u32[]{:S(2)}, u32[]{:S(2)}) collective-permute-start(bf16[96,1024]{1,0:T(8,128)(2,1)S(1)} %convolution_convert_fusion), channel_id=1, source_target_pairs={{0,64},{64,128},{128,192},{192,256},{256,320},{320,384},{384,448},... | collective-permute-start | bytes 589832 | tf_op jit(solution)/shard_map/ppermute | solution.py:18
  63.3 0.5 fusion
  63.8 0.0 collective-permute-done.4
  63.8 0.1 collective-permute-done.5
  63.9 1.4 %convolution_convert_fusion.1 = bf16[96,1024]{1,0:T(8,128)(2,1)S(1)} fusion(bf16[768,1024]{1,0:T(8,128)(2,1)S(1)} %copy-done, bf16[1,96,768]{2,1,0:T(8,128)(2,1)S(1)} %collective-permute-done.5, bf16[3,96,768]{2,1,0:T(8,128)(2,1)} %collective-permute-done.4, s32[]{:T(128)S(6)} %select_n.306, pred[]{:T(512)S(6)} %lt.150, pred[]{:T(512)S(6)} %eq.63, ...), kind=kOutput, calls=%fused_computation.20 | convolution fusion | flops 151314432 | bytes 2359307 | tf_op jit(solution)/shard_map/dot_general | solution.py:120
  65.2 3.5 %collective-permute-start.9 = (bf16[96,1024]{1,0:T(8,128)(2,1)S(1)}, bf16[96,1024]{1,0:T(8,128)(2,1)S(1)}, u32[]{:S(2)}, u32[]{:S(2)}) collective-permute-start(bf16[96,1024]{1,0:T(8,128)(2,1)S(1)} %convolution_convert_fusion.1), channel_id=1, source_target_pairs={{0,448},{64,0},{128,64},{192,128},{256,192},{320,256},{384,320},{4... | collective-permute-start | bytes 589832 | tf_op jit(solution)/shard_map/ppermute | solution.py:18
  68.8 1.8 %bitcast_dynamic-update-slice_fusion.2 = bf16[4,4,96,768]{3,2,1,0:T(8,128)(2,1)} fusion(bf16[4,4,96,768]{3,2,1,0:T(8,128)(2,1)} %bitcast_dynamic-update-slice_fusion, s32[]{:T(128)S(6)} %select_n.311, bf16[3,96,768]{2,1,0:T(8,128)(2,1)} %collective-permute-done.4), kind=kLoop, calls=%fused_computation.23 | loop fusion | bytes 884740 | tf_op jit(solution)/shard_map/dynamic_update_slice | solution.py:131
  70.6 0.7 bitcast_dynamic-update-slice_fusion.3
  71.3 1.4 %fusion.5 = bf16[192,1024]{1,0:T(8,128)(2,1)S(1)} fusion(bf16[768,1024]{1,0:T(8,128)(2,1)S(1)} %copy-done, bf16[96,1024]{1,0:T(8,128)(2,1)S(1)} %get-tuple-element.44, bf16[96,1024]{1,0:T(8,128)(2,1)S(1)} %get-tuple-element.43, bf16[8,192,768]{2,1,0:T(8,128)(2,1)} %bitcast.14, s32[]{:T(128)S(6)} %select_n.317), kind=kOutput, calls=%fused_computation.13 | convolution fusion | flops 303169536 | bytes 2654212 | tf_op jit(solution)/shard_map/dot_general | solution.py:120
  72.7 0.0 copy-start.5
  72.8 2.1 %collective-permute-start.7 = (bf16[192,1024]{1,0:T(8,128)(2,1)S(1)}, bf16[192,1024]{1,0:T(8,128)(2,1)S(1)}, u32[]{:S(2)}, u32[]{:S(2)}) collective-permute-start(bf16[192,1024]{1,0:T(8,128)(2,1)S(1)} %fusion.5), channel_id=1, source_target_pairs={{0,64},{64,128},{128,192},{192,256},{256,320},{320,384},{384,448},... | collective-permute-start | bytes 1179656 | tf_op jit(solution)/shard_map/ppermute | solution.py:18
  74.9 1.4 %fusion.8 = bf16[192,1024]{1,0:T(8,128)(2,1)S(1)} fusion(bf16[768,1024]{1,0:T(8,128)(2,1)S(1)} %copy-done, bf16[96,1024]{1,0:T(8,128)(2,1)S(1)} %get-tuple-element.42, bf16[96,1024]{1,0:T(8,128)(2,1)S(1)} %get-tuple-element.41, bf16[8,192,768]{2,1,0:T(8,128)(2,1)} %bitcast.14, s32[]{:T(128)S(6)} %select_n.331), kind=kOutput, calls=%fused_computation.16 | convolution fusion | flops 303169536 | bytes 2654212 | tf_op jit(solution)/shard_map/dot_general | solution.py:120
  76.3 4.6 %collective-permute-start.10 = (bf16[192,1024]{1,0:T(8,128)(2,1)S(1)}, bf16[192,1024]{1,0:T(8,128)(2,1)S(1)}, u32[]{:S(2)}, u32[]{:S(2)}) collective-permute-start(bf16[192,1024]{1,0:T(8,128)(2,1)S(1)} %fusion.8), channel_id=1, source_target_pairs={{0,448},{64,0},{128,64},{192,128},{256,192},{320,256},{384,320},{4... | collective-permute-start | bytes 1179656 | tf_op jit(solution)/shard_map/ppermute | solution.py:18
  81.0 2.6 %collective-permute-start.15 = (bf16[192,768]{1,0:T(8,128)(2,1)S(1)}, bf16[192,768]{1,0:T(8,128)(2,1)S(1)}, u32[]{:S(2)}, u32[]{:S(2)}) collective-permute-start(bf16[192,768]{1,0:T(8,128)(2,1)S(1)} %slice_select_fusion), channel_id=1, source_target_pairs={{0,128},{448,320},{1,129},{449,321},{2,130},{450,322},{3,131},{451... | collective-permute-start | bytes 884744 | tf_op jit(solution)/shard_map/ppermute | solution.py:172
  83.5 1.4 %fusion.4 = bf16[192,1024]{1,0:T(8,128)(2,1)S(1)} fusion(bf16[768,1024]{1,0:T(8,128)(2,1)S(1)} %copy-done, bf16[192,1024]{1,0:T(8,128)(2,1)S(1)} %collective-permute-done.7, bf16[8,192,768]{2,1,0:T(8,128)(2,1)} %bitcast.14, s32[]{:T(128)S(6)} %select_n.315), kind=kOutput, calls=%fused_computation.12 | convolution fusion | flops 302579712 | bytes 2654212 | tf_op jit(solution)/shard_map/dot_general | solution.py:120
  85.0 1.9 %collective-permute-start.8 = (bf16[192,1024]{1,0:T(8,128)(2,1)S(1)}, bf16[192,1024]{1,0:T(8,128)(2,1)S(1)}, u32[]{:S(2)}, u32[]{:S(2)}) collective-permute-start(bf16[192,1024]{1,0:T(8,128)(2,1)S(1)} %fusion.4), channel_id=1, source_target_pairs={{0,64},{64,128},{128,192},{192,256},{256,320},{320,384},{384,448},... | collective-permute-start | bytes 1179656 | tf_op jit(solution)/shard_map/ppermute | solution.py:18
  86.9 0.0 collective-permute-done.10
  86.9 1.4 %fusion.7 = bf16[192,1024]{1,0:T(8,128)(2,1)S(1)} fusion(bf16[768,1024]{1,0:T(8,128)(2,1)S(1)} %copy-done, bf16[192,1024]{1,0:T(8,128)(2,1)S(1)} %collective-permute-done.10, bf16[8,192,768]{2,1,0:T(8,128)(2,1)} %bitcast.14, s32[]{:T(128)S(6)} %select_n.329), kind=kOutput, calls=%fused_computation.15 | convolution fusion | flops 302579712 | bytes 2654212 | tf_op jit(solution)/shard_map/dot_general | solution.py:120
  88.4 4.6 %collective-permute-start.11 = (bf16[192,1024]{1,0:T(8,128)(2,1)S(1)}, bf16[192,1024]{1,0:T(8,128)(2,1)S(1)}, u32[]{:S(2)}, u32[]{:S(2)}) collective-permute-start(bf16[192,1024]{1,0:T(8,128)(2,1)S(1)} %fusion.7), channel_id=1, source_target_pairs={{0,448},{64,0},{128,64},{192,128},{256,192},{320,256},{384,320},{4... | collective-permute-start | bytes 1179656 | tf_op jit(solution)/shard_map/ppermute | solution.py:18
  93.0 0.0 collective-permute-done.15
  93.0 0.8 fusion.28
  93.8 1.3 collective-permute-start.16
  95.1 0.0 collective-permute-done.8
  95.1 2.2 %fusion.3 = bf16[192,1024]{1,0:T(8,128)(2,1)} fusion(bf16[768,1024]{1,0:T(8,128)(2,1)S(1)} %copy-done, bf16[192,1024]{1,0:T(8,128)(2,1)S(1)} %collective-permute-done.8, bf16[8,192,768]{2,1,0:T(8,128)(2,1)} %bitcast.14, s32[]{:T(128)S(6)} %select_n.313), kind=kOutput, calls=%fused_computation.11 | convolution fusion | flops 302579712 | bytes 2654212 | tf_op jit(solution)/shard_map/dot_general | solution.py:120
  97.3 3.2 %collective-permute-start.12 = (bf16[192,1024]{1,0:T(8,128)(2,1)}, bf16[192,1024]{1,0:T(8,128)(2,1)S(1)}, u32[]{:S(2)}, u32[]{:S(2)}) collective-permute-start(bf16[192,1024]{1,0:T(8,128)(2,1)} %fusion.3), channel_id=1, source_target_pairs={{0,64},{64,128},{128,192},{192,256},{256,320},{320,384},{384,448},... | collective-permute-start | bytes 1179656 | tf_op jit(solution)/shard_map/ppermute | solution.py:18
  100.5 0.0 collective-permute-done.11
  100.5 2.2 %fusion.6 = bf16[192,1024]{1,0:T(8,128)(2,1)} fusion(bf16[768,1024]{1,0:T(8,128)(2,1)S(1)} %copy-done, bf16[192,1024]{1,0:T(8,128)(2,1)S(1)} %collective-permute-done.11, bf16[8,192,768]{2,1,0:T(8,128)(2,1)} %bitcast.14, s32[]{:T(128)S(6)} %select_n.327), kind=kOutput, calls=%fused_computation.14 | convolution fusion | flops 302579712 | bytes 2654212 | tf_op jit(solution)/shard_map/dot_general | solution.py:120
  102.7 3.3 %collective-permute-start.13 = (bf16[192,1024]{1,0:T(8,128)(2,1)}, bf16[192,1024]{1,0:T(8,128)(2,1)}, u32[]{:S(2)}, u32[]{:S(2)}) collective-permute-start(bf16[192,1024]{1,0:T(8,128)(2,1)} %fusion.6), channel_id=1, source_target_pairs={{0,448},{64,0},{128,64},{192,128},{256,192},{320,256},{384,320},{4... | collective-permute-start | bytes 1179656 | tf_op jit(solution)/shard_map/ppermute | solution.py:18
  106.0 7.8 %collective-permute-start.17 = (f32[192]{0:T(256)S(1)}, f32[192]{0:T(256)S(1)}, u32[]{:S(2)}, u32[]{:S(2)}) collective-permute-start(f32[192]{0:T(256)S(1)} %fusion), channel_id=1, source_target_pairs={{0,1},{1,0},{2,3},{3,2},{4,5},{5,4},{6,7},{7,6},{8,9},{9,8},{10,11... | collective-permute-start | bytes 2312 | tf_op jit(solution)/shard_map/ppermute | solution.py:18
  113.8 0.0 copy-start.2
  113.8 0.0 copy-start.8
  113.8 1.5 %fusion.13 = f32[192,1024]{1,0:T(8,128)S(1)} fusion(bf16[768,1024]{1,0:T(8,128)(2,1)S(1)} %copy-done, bf16[8,192,768]{2,1,0:T(8,128)(2,1)} %bitcast.14, s32[]{:T(128)S(6)} %select_n.338), kind=kOutput, calls=%fused_computation.30 | convolution fusion | flops 301989888 | bytes 2654212 | tf_op jit(solution)/shard_map/dot_general | solution.py:120
  115.4 0.0 collective-permute-done.17
  115.4 0.0 collective-permute-done.12
  115.4 1.0 fusion.10
  116.4 10.5 %collective-permute-start.14 = (bf16[192,512]{1,0:T(8,128)(2,1)S(1)}, bf16[192,512]{1,0:T(8,128)(2,1)S(1)}, u32[]{:S(2)}, u32[]{:S(2)}) collective-permute-start(bf16[192,512]{1,0:T(8,128)(2,1)S(1)} %fusion.10), channel_id=1, source_target_pairs={{0,2},{2,0},{1,3},{3,1},{4,6},{6,4},{5,7},{7,5},{8,10},{10,8},{9,1... | collective-permute-start | bytes 589832 | tf_op jit(solution)/shard_map/ppermute | solution.py:18
  126.9 1.5 %fusion.9 = bf16[1,192,3072]{2,1,0:T(8,128)(2,1)} fusion(f32[3072]{0:T(1024)S(1)} %bitcast.86, f32[192]{0:T(256)S(1)} %add_rsqrt_fusion, bf16[192,3072]{1,0:T(8,128)(2,1)S(1)} %copy-done.2, bf16[192,3072]{1,0:T(8,128)(2,1)S(1)} %collective-permute-done.1, pred[]{:T(512)S(6)} %eq.58), kind=kLoop, calls=%fused_computation.17 | loop fusion | flops 2949120 | bytes 3552001 | tf_op jit(solution)/shard_map/broadcast_in_dim | solution.py:198
  128.4 1.7 %fusion.12.mine = bf16[192,512]{1,0:T(8,128)(2,1)} fusion(f32[192,1024]{1,0:T(8,128)S(1)} %fusion.13, bf16[192,1024]{1,0:T(8,128)(2,1)} %collective-permute-done.13, bf16[192,1024]{1,0:T(8,128)(2,1)S(1)} %collective-permute-done.12), kind=kLoop, calls=%fused_computation.28 | loop fusion | flops 491520 | bytes 983040 | tf_op jit(solution)/shard_map/convert_element_type | solution.py:210
  130.2 0.6 copy-done.7
  130.8 0.1 copy-done.6
  130.9 3.1 %shard_map.96 = (bf16[512,384]{1,0:T(8,128)(2,1)}, f32[192,384]{1,0:T(8,128)}) custom-call(s32[2]{0:T(128)} %pad_add_fusion.place, bf16[192,512]{1,0:T(8,128)(2,1)} %fusion.12.mine, bf16[192,512]{1,0:T(8,128)(2,1)} %copy-done.6, f32[512,384]{1,0:T(8,128)} %get-tuple-element.30.old, bf16[192,256]{1,0:T(8,128)(2,1)} %get-tuple-element.31.hot, ...), custom_call_target="tpu_custom_call" | custom-call | tf_op jit(solution)/shard_map/pallas_call | solution.py:202
  (24 shorter events, 0.2 us)
Async XLA Ops:
  0.6 50.5 %collective-permute-start.1 = (bf16[192,3072]{1,0:T(8,128)(2,1)}, bf16[192,3072]{1,0:T(8,128)(2,1)S(1)}, u32[]{:S(2)}, u32[]{:S(2)}) collective-permute-start(bf16[192,3072]{1,0:T(8,128)(2,1)} %bitcast.82), channel_id=1, source_target_pairs={{0,64},{64,128},{128,192},{192,256},{256,320},{320,384},{384,448},... | collective-permute-start | bytes 3538952 | tf_op jit(solution)/shard_map/ppermute | solution.py:18
  4.7 42.5 %collective-permute-start.2 = (bf16[512,768]{1,0:T(8,128)(2,1)}, bf16[512,768]{1,0:T(8,128)(2,1)S(1)}, u32[]{:S(2)}, u32[]{:S(2)}) collective-permute-start(bf16[512,768]{1,0:T(8,128)(2,1)} %first.1), channel_id=1, source_target_pairs={{0,2},{2,0},{1,3},{3,1},{4,6},{6,4},{5,7},{7,5},{8,10},{10,8},{9,1... | collective-permute-start | bytes 2359304 | tf_op jit(solution)/shard_map/ppermute | solution.py:18
  25.5 25.6 %copy-start.3 = (bf16[384,768]{1,0:T(8,128)(2,1)}, bf16[384,768]{1,0:T(8,128)(2,1)S(1)}, u32[]{:S(2)}) copy-start(bf16[384,768]{1,0:T(8,128)(2,1)S(1)} %all-gather) | copy-start | bytes 1769476
  25.5 15.6 %collective-permute-start.3 = (bf16[4,96,768]{2,1,0:T(8,128)(2,1)S(1)}, bf16[4,96,768]{2,1,0:T(8,128)(2,1)S(1)}, u32[]{:S(2)}, u32[]{:S(2)}) collective-permute-start(bf16[4,96,768]{2,1,0:T(8,128)(2,1)S(1)} %bitcast.78), channel_id=1, source_target_pairs={{0,12},{4,0},{8,4},{12,8},{1,13},{5,1},{9,5},{13,9},{2,14},{6,2},{... | collective-permute-start | bytes 1769480 | tf_op jit(solution)/shard_map/ppermute | solution.py:18
  30.3 20.9 %collective-permute-start = (bf16[4,96,768]{2,1,0:T(8,128)(2,1)S(1)}, bf16[4,96,768]{2,1,0:T(8,128)(2,1)}, u32[]{:S(2)}, u32[]{:S(2)}) collective-permute-start(bf16[4,96,768]{2,1,0:T(8,128)(2,1)S(1)} %bitcast.79), channel_id=1, source_target_pairs={{0,4},{4,8},{8,12},{12,0},{1,5},{5,9},{9,13},{13,1},{2,6},{6,10},{... | collective-permute-start | bytes 1769480 | tf_op jit(solution)/shard_map/ppermute | solution.py:18
  41.9 21.9 %collective-permute-start.4 = (bf16[3,96,768]{2,1,0:T(8,128)(2,1)}, bf16[3,96,768]{2,1,0:T(8,128)(2,1)}, u32[]{:S(2)}, u32[]{:S(2)}) collective-permute-start(bf16[3,96,768]{2,1,0:T(8,128)(2,1)} %slice.66), channel_id=1, source_target_pairs={{0,12},{4,0},{8,4},{12,8},{1,13},{5,1},{9,5},{13,9},{2,14},{6,2},{... | collective-permute-start | bytes 1327112 | tf_op jit(solution)/shard_map/ppermute | solution.py:18
  47.2 0.9 copy-start.4
  52.8 5.9 %copy-start = (bf16[768,1024]{1,0:T(8,128)(2,1)S(1)}, bf16[768,1024]{1,0:T(8,128)(2,1)}, u32[]{:S(2)}) copy-start(bf16[768,1024]{1,0:T(8,128)(2,1)} %shard_map.95) | copy-start | bytes 4718596
  56.6 6.7 %copy-start.1 = (bf16[192,3072]{1,0:T(8,128)(2,1)S(1)}, bf16[192,3072]{1,0:T(8,128)(2,1)}, u32[]{:S(2)}) copy-start(bf16[192,3072]{1,0:T(8,128)(2,1)} %param.11) | copy-start | bytes 3538948
  56.6 7.2 %collective-permute-start.5 = (bf16[1,96,768]{2,1,0:T(8,128)(2,1)S(1)}, bf16[1,96,768]{2,1,0:T(8,128)(2,1)S(1)}, u32[]{:S(2)}, u32[]{:S(2)}) collective-permute-start(bf16[1,96,768]{2,1,0:T(8,128)(2,1)S(1)} %slice.51), channel_id=1, source_target_pairs={{0,4},{4,8},{8,12},{12,0},{1,5},{5,9},{9,13},{13,1},{2,6},{6,10},{... | collective-permute-start | bytes 442376 | tf_op jit(solution)/shard_map/ppermute | solution.py:18
  60.1 11.2 %collective-permute-start.6 = (bf16[96,1024]{1,0:T(8,128)(2,1)S(1)}, bf16[96,1024]{1,0:T(8,128)(2,1)S(1)}, u32[]{:S(2)}, u32[]{:S(2)}) collective-permute-start(bf16[96,1024]{1,0:T(8,128)(2,1)S(1)} %convolution_convert_fusion), channel_id=1, source_target_pairs={{0,64},{64,128},{128,192},{192,256},{256,320},{320,384},{384,448},... | collective-permute-start | bytes 589832 | tf_op jit(solution)/shard_map/ppermute | solution.py:18
  65.2 9.6 %collective-permute-start.9 = (bf16[96,1024]{1,0:T(8,128)(2,1)S(1)}, bf16[96,1024]{1,0:T(8,128)(2,1)S(1)}, u32[]{:S(2)}, u32[]{:S(2)}) collective-permute-start(bf16[96,1024]{1,0:T(8,128)(2,1)S(1)} %convolution_convert_fusion.1), channel_id=1, source_target_pairs={{0,448},{64,0},{128,64},{192,128},{256,192},{320,256},{384,320},{4... | collective-permute-start | bytes 589832 | tf_op jit(solution)/shard_map/ppermute | solution.py:18
  72.7 8.2 %copy-start.5 = (bf16[1,192,3072]{2,1,0:T(8,128)(2,1)S(1)}, bf16[1,192,3072]{2,1,0:T(8,128)(2,1)}, u32[]{:S(2)}) copy-start(bf16[1,192,3072]{2,1,0:T(8,128)(2,1)} %param.10) | copy-start | bytes 3538948
  72.8 10.8 %collective-permute-start.7 = (bf16[192,1024]{1,0:T(8,128)(2,1)S(1)}, bf16[192,1024]{1,0:T(8,128)(2,1)S(1)}, u32[]{:S(2)}, u32[]{:S(2)}) collective-permute-start(bf16[192,1024]{1,0:T(8,128)(2,1)S(1)} %fusion.5), channel_id=1, source_target_pairs={{0,64},{64,128},{128,192},{192,256},{256,320},{320,384},{384,448},... | collective-permute-start | bytes 1179656 | tf_op jit(solution)/shard_map/ppermute | solution.py:18
  76.3 10.6 %collective-permute-start.10 = (bf16[192,1024]{1,0:T(8,128)(2,1)S(1)}, bf16[192,1024]{1,0:T(8,128)(2,1)S(1)}, u32[]{:S(2)}, u32[]{:S(2)}) collective-permute-start(bf16[192,1024]{1,0:T(8,128)(2,1)S(1)} %fusion.8), channel_id=1, source_target_pairs={{0,448},{64,0},{128,64},{192,128},{256,192},{320,256},{384,320},{4... | collective-permute-start | bytes 1179656 | tf_op jit(solution)/shard_map/ppermute | solution.py:18
  81.0 12.0 %collective-permute-start.15 = (bf16[192,768]{1,0:T(8,128)(2,1)S(1)}, bf16[192,768]{1,0:T(8,128)(2,1)S(1)}, u32[]{:S(2)}, u32[]{:S(2)}) collective-permute-start(bf16[192,768]{1,0:T(8,128)(2,1)S(1)} %slice_select_fusion), channel_id=1, source_target_pairs={{0,128},{448,320},{1,129},{449,321},{2,130},{450,322},{3,131},{451... | collective-permute-start | bytes 884744 | tf_op jit(solution)/shard_map/ppermute | solution.py:172
  85.0 10.1 %collective-permute-start.8 = (bf16[192,1024]{1,0:T(8,128)(2,1)S(1)}, bf16[192,1024]{1,0:T(8,128)(2,1)S(1)}, u32[]{:S(2)}, u32[]{:S(2)}) collective-permute-start(bf16[192,1024]{1,0:T(8,128)(2,1)S(1)} %fusion.4), channel_id=1, source_target_pairs={{0,64},{64,128},{128,192},{192,256},{256,320},{320,384},{384,448},... | collective-permute-start | bytes 1179656 | tf_op jit(solution)/shard_map/ppermute | solution.py:18
  88.4 12.1 %collective-permute-start.11 = (bf16[192,1024]{1,0:T(8,128)(2,1)S(1)}, bf16[192,1024]{1,0:T(8,128)(2,1)S(1)}, u32[]{:S(2)}, u32[]{:S(2)}) collective-permute-start(bf16[192,1024]{1,0:T(8,128)(2,1)S(1)} %fusion.7), channel_id=1, source_target_pairs={{0,448},{64,0},{128,64},{192,128},{256,192},{320,256},{384,320},{4... | collective-permute-start | bytes 1179656 | tf_op jit(solution)/shard_map/ppermute | solution.py:18
  93.8 36.4 %collective-permute-start.16 = (bf16[192,384]{1,0:T(8,128)(2,1)}, bf16[192,384]{1,0:T(8,128)(2,1)S(1)}, u32[]{:S(2)}, u32[]{:S(2)}) collective-permute-start(bf16[192,384]{1,0:T(8,128)(2,1)} %get-tuple-element.39), channel_id=1, source_target_pairs={{0,64},{128,192},{448,384},{320,256},{1,65},{129,193},{449,385},{3... | collective-permute-start | bytes 442376 | tf_op jit(solution)/shard_map/ppermute | solution.py:183
  97.3 18.1 %collective-permute-start.12 = (bf16[192,1024]{1,0:T(8,128)(2,1)}, bf16[192,1024]{1,0:T(8,128)(2,1)S(1)}, u32[]{:S(2)}, u32[]{:S(2)}) collective-permute-start(bf16[192,1024]{1,0:T(8,128)(2,1)} %fusion.3), channel_id=1, source_target_pairs={{0,64},{64,128},{128,192},{192,256},{256,320},{320,384},{384,448},... | collective-permute-start | bytes 1179656 | tf_op jit(solution)/shard_map/ppermute | solution.py:18
  102.7 12.7 %collective-permute-start.13 = (bf16[192,1024]{1,0:T(8,128)(2,1)}, bf16[192,1024]{1,0:T(8,128)(2,1)}, u32[]{:S(2)}, u32[]{:S(2)}) collective-permute-start(bf16[192,1024]{1,0:T(8,128)(2,1)} %fusion.6), channel_id=1, source_target_pairs={{0,448},{64,0},{128,64},{192,128},{256,192},{320,256},{384,320},{4... | collective-permute-start | bytes 1179656 | tf_op jit(solution)/shard_map/ppermute | solution.py:18
  106.0 9.4 %collective-permute-start.17 = (f32[192]{0:T(256)S(1)}, f32[192]{0:T(256)S(1)}, u32[]{:S(2)}, u32[]{:S(2)}) collective-permute-start(f32[192]{0:T(256)S(1)} %fusion), channel_id=1, source_target_pairs={{0,1},{1,0},{2,3},{3,2},{4,5},{5,4},{6,7},{7,6},{8,9},{9,8},{10,11... | collective-permute-start | bytes 2312 | tf_op jit(solution)/shard_map/ppermute | solution.py:18
  113.8 13.1 %copy-start.2 = (bf16[192,3072]{1,0:T(8,128)(2,1)S(1)}, bf16[192,3072]{1,0:T(8,128)(2,1)}, u32[]{:S(2)}) copy-start(bf16[192,3072]{1,0:T(8,128)(2,1)} %param.11) | copy-start | bytes 3538948
  113.8 13.1 %copy-start.8 = (f32[1,3072]{1,0:T(1,128)S(1)}, f32[1,3072]{1,0:T(1,128)}, u32[]{:S(2)}) copy-start(f32[1,3072]{1,0:T(1,128)} %param.12) | copy-start | bytes 36868
  116.4 13.7 %collective-permute-start.14 = (bf16[192,512]{1,0:T(8,128)(2,1)S(1)}, bf16[192,512]{1,0:T(8,128)(2,1)S(1)}, u32[]{:S(2)}, u32[]{:S(2)}) collective-permute-start(bf16[192,512]{1,0:T(8,128)(2,1)S(1)} %fusion.10), channel_id=1, source_target_pairs={{0,2},{2,0},{1,3},{3,1},{4,6},{6,4},{5,7},{7,5},{8,10},{10,8},{9,1... | collective-permute-start | bytes 589832 | tf_op jit(solution)/shard_map/ppermute | solution.py:18
  130.1 0.6 copy-start.7
  130.1 0.7 copy-start.6

commit v7 on v6

--- a/solution.py
+++ b/solution.py
@@ -22,15 +22,6 @@
     return lax.optimization_barrier((value, *others))[0]
 
 
-def masked_patches(mask_blocks):
-    per_side = GRID_SIDE // BLOCK_SIDE
-    within = jnp.arange(BLOCK_SIDE * BLOCK_SIDE, dtype=jnp.int32)
-    chosen = mask_blocks[..., None]
-    grid_row = chosen // per_side * BLOCK_SIDE + within // BLOCK_SIDE
-    grid_col = chosen % per_side * BLOCK_SIDE + within % BLOCK_SIDE
-    return grid_row * GRID_SIDE + grid_col
-
-
 def normed(values, images):
     shaped = values.reshape(images, -1, values.shape[-1])
     center = jnp.mean(shaped, axis=1, keepdims=True)
@@ -53,34 +44,32 @@
     )(first, second)
 
 
-def ready_kernel(previous, ids, out, hot, same):
+def ready_kernel(blocks, previous, out, hot):
     images = previous.shape[0] // PATCHES
     out[...] = 0.5 * normed(previous[...].astype(jnp.float32), images)
-    lane = lax.broadcasted_iota(jnp.int32, hot.shape, 1)
-    hot[...] = jnp.where(lane == ids[...], 1.0, 0.0).astype(hot.dtype)
-    row = lax.broadcasted_iota(jnp.int32, same.shape, 0)
-    lane = lax.broadcasted_iota(jnp.int32, same.shape, 1)
-    same[...] = jnp.where(lane == row, 1.0, 0.0).astype(same.dtype)
-
-
-def final_kernel(place, mine, other, old, hot, same, kept, handed, targets, error):
+    per_side, size = GRID_SIDE // BLOCK_SIDE, BLOCK_SIDE * BLOCK_SIDE
+    within = lax.broadcasted_iota(jnp.int32, (size, PATCHES), 0)
+    lane = lax.broadcasted_iota(jnp.int32, (size, PATCHES), 1)
+    inside = within // BLOCK_SIDE * GRID_SIDE + within % BLOCK_SIDE
+    for k in range(hot.shape[0] // size):
+        chosen = blocks[0, k]
+        corner = chosen // per_side * BLOCK_SIDE * GRID_SIDE + chosen % per_side * BLOCK_SIDE
+        hot[k * size:(k + 1) * size] = jnp.where(lane == inside + corner, 1.0, 0.0).astype(hot.dtype)
+
+
+def final_kernel(core, keeps, mine, other, old, hot, kept, handed, targets, error):
     images = targets.shape[0] // PATCHES
     shard = mine.shape[0] // 2
-    first = place[0] == 0
+    first = core[0] == 0
     pieces = []
     for pair in range(2):
         a, b = (part[pair * shard:(pair + 1) * shard] for part in (mine, other))
         pieces += [jnp.where(first, a, b), jnp.where(first, b, a)]
-    ordered = lax.dot_general(
-        same[...],
-        jnp.concatenate(pieces, axis=0),
-        (((1,), (1,)), ((), ())),
-        preferred_element_type=jnp.float32,
-    )
+    ordered = jnp.concatenate(pieces, axis=0).T.astype(jnp.float32)
     made = (0.5 * normed(ordered, images) + old[...]).astype(targets.dtype)
     targets[...] = made
     picked = jnp.dot(hot[...], made[:PATCHES], preferred_element_type=jnp.float32)
-    predicted = jnp.where(place[1] == 1, kept[...], handed[...])
+    predicted = jnp.where(keeps[0] == 1, kept[...], handed[...])
     error[...] = predicted.astype(jnp.float32) - picked
 
 
@@ -101,18 +90,20 @@
     count = lax.axis_size("x")
     weight = jnp.broadcast_to(held[:, None], (held.shape[0], count, shard, depth))
 
-    ids = masked_patches(mask_blocks[0]).reshape(-1, 1)
-    old, hot, same = pl.pallas_call(
+    smem, vmem = (pl.BlockSpec(memory_space=space) for space in (pltpu.SMEM, pltpu.VMEM))
+    masked = mask_blocks.shape[1] * BLOCK_SIDE * BLOCK_SIDE
+    old, hot = pl.pallas_call(
         ready_kernel,
+        in_specs=[smem, vmem],
+        out_specs=(vmem, vmem),
         out_shape=(
             jax.ShapeDtypeStruct((rows, width), f32),
-            jax.ShapeDtypeStruct((ids.shape[0], PATCHES), bf16),
-            jax.ShapeDtypeStruct((rows, rows), bf16),
+            jax.ShapeDtypeStruct((masked, PATCHES), bf16),
         ),
         cost_estimate=pl.CostEstimate(flops=0, bytes_accessed=8 << 20, transcendentals=0),
-    )(previous, ids)
-
-    below, incoming, old, both, weight = lax.optimization_barrier((below, incoming, old, both, weight))
+    )(mask_blocks, previous)
+    above = tied(above, both, old, weight)
+    below, incoming = lax.optimization_barrier((below, incoming))
     opposite = around(above[:LATE], "x", -1)
     opposite_rest = around(below[LATE:], "x", 1)
 
@@ -158,11 +149,12 @@
     half = early_half((position + far + 1) % sections)
     falling = spread(falling, 1 - half)
     def round_of(steps, after):
-        upward = product(block(steps, after)) + rising.astype(f32)
-        downward = product(block(sections - steps, after)) + falling.astype(f32)
+        ahead, behind = lax.optimization_barrier((block(steps, after), block(sections - steps, after)))
+        upward = product(ahead) + rising.astype(f32)
+        downward = product(behind) + falling.astype(f32)
         return upward.astype(bf16), downward.astype(bf16)
 
-    sent = round_of(3, ())
+    sent = round_of(3, (ended,))
     rising, falling = up(sent[0]), down(sent[1])
 
     last = sections - 1
@@ -170,10 +162,10 @@
     arrived = incoming
     given = tied(jnp.where(position == 0, cut(arrived, 2, 2), cut(act, last - 3, 2)), *sent)
     passed = lax.ppermute(given, "section", [(0, 2), (last, last - 2)])
-    sent = round_of(2, ())
+    sent = round_of(2, sent)
     rising, falling = up(sent[0]), down(sent[1])
 
-    sent = round_of(1, ())
+    sent = round_of(1, sent)
     rising, falling = up(sent[0]), down(sent[1])
 
     ends = (position == 0) | (position == last)
@@ -192,22 +184,23 @@
     features = act.shape[-1] * lax.axis_size("tensor")
     scaling = lax.rsqrt(squares[:, None] / features + 1e-06)
 
-    own_term = product(block(0, sent))
-    theirs = own_term[:, rows:] + rising[:, rows:].astype(f32) + falling[:, rows:].astype(f32)
+    own_weight = tied(block(0, sent))
+    total = lambda part: jnp.dot(own_weight, both[:, part], preferred_element_type=f32) + (
+        rising[:, part].astype(f32) + falling[:, part].astype(f32)
+    )
+    theirs = total(slice(rows, None))
     other = around(theirs.astype(bf16), "core", 1)
     section_out = (wide * tied(scaling, theirs) * section_gains).astype(bf16)[None]
-    mine = own_term[:, :rows] + rising[:, :rows].astype(f32) + falling[:, :rows].astype(f32)
-
-    vmem = pl.BlockSpec(memory_space=pltpu.VMEM)
+    mine = total(slice(None, rows))
     targets, target_error = pl.pallas_call(
         final_kernel,
-        in_specs=[pl.BlockSpec(memory_space=pltpu.SMEM)] + [vmem] * 7,
+        in_specs=[smem] * 2 + [vmem] * 6,
         out_specs=(vmem, vmem),
         out_shape=(
             jax.ShapeDtypeStruct((rows, width), bf16),
-            jax.ShapeDtypeStruct(kept.shape, f32),
+            jax.ShapeDtypeStruct((masked, width), f32),
         ),
-    )(jnp.stack([core, keeps]).astype(jnp.int32), mine.astype(bf16), other, old, hot, same, kept, handed)
+    )(core.astype(jnp.int32).reshape(1), keeps.astype(jnp.int32).reshape(1), mine.astype(bf16), other, old, hot, kept, handed)
     return (targets, section_out, target_error)
 
 

time: 135 us -> 142 us (1.052)
  matrix products: 14.5 us -> 18.2 us
  local copies, waits for them, and re-layouts: 11.1 us -> 14.6 us
    squeeze x0 -> x4, local copies, waits for them, and re-layouts: none -> 4.36 us  [block(): lax.dynamic_index_in_dim(weight, (place + steps) % sections, 0, keepdims=...]
    ppermute x16, starting transfers between devices: 69.3 us -> 65.1 us  [around(): lax.ppermute(value, axis, [(i, (i + steps) % count) for i in range(count)])]
    dot_general x0 -> x2, matrix products: none -> 3.38 us  [on_device(): jnp.dot(own_weight, both[:, part], preferred_element_type=f32)]
    ppermute x1, starting transfers between devices: 1.29 us -> 3.69 us  [on_device(): lax.ppermute(onward, 'section', [(0, 1), (2, 3), (last, last - 1), (last...]
    select_n x2, other arithmetic: 0.07 us -> 1.92 us  [spread(): jnp.where(half == 0, value, empty)]
    convert_element_type x1 -> x0, other arithmetic: 1.7 us -> none  [on_device(): mine.astype(bf16)]
    select_n x1, other arithmetic: 0.03 us -> 1.71 us  [on_device(): jnp.where(position == 0, cut(arrived, 2, 2), cut(act, last - 3, 2))]
    dot_general x9 -> x8, matrix products: 14.5 us -> 14.8 us  [product(): return jnp.dot(weight, both, preferred_element_type=f32)]
  transfers between devices with their start and end apart: 18 -> 18, of which waited for: 2 -> 2; matrix products, arithmetic and copies ran while one was open for 23% -> 28% of each run, Pallas kernels for 4% -> 4%
where the time goes in v7:
time: 142 us; the launch traced here: 141 us
  starting transfers between devices  72.3 us (51%)
  matrix products  18.2 us (13%)
  local copies, waits for them, and re-layouts  14.6 us (10%)
  blocking collectives  14.2 us (10%)
  Pallas kernels  7.96 us (6%)
  other arithmetic  7.5 us (5%)
  waiting for transfers between devices  4.78 us (3%)
    ppermute x16, starting transfers between devices, around(): lax.ppermute(value, axis, [(i, (i + steps) % count) for i in range(count)])  65.1 us
    dot_general x8, matrix products, product(): return jnp.dot(weight, both, preferred_element_type=f32)  14.8 us
    all_gather x1, blocking collectives, on_device(): held = lax.all_gather(out_weight.T, 'zlo', axis=0, tiled=False)  14.2 us
    dynamic_update_slice x4, local copies, waits for them, and re-layouts, on_device(): lax.dynamic_update_slice(weight, part[:, None], (line, at % count, 0, 0))  5.37 us
    ppermute x16, waiting for transfers between devices, around(): lax.ppermute(value, axis, [(i, (i + steps) % count) for i in range(count)])  4.78 us
    squeeze x4, local copies, waits for them, and re-layouts, block(): lax.dynamic_index_in_dim(weight, (place + steps) % sections, 0, keepdims=...  4.36 us
    ppermute x1, starting transfers between devices, on_device(): lax.ppermute(onward, 'section', [(0, 1), (2, 3), (last, last - 1), (last...  3.69 us
    ppermute x1, starting transfers between devices, on_device(): passed = lax.ppermute(given, 'section', [(0, 2), (last, last - 2)])  3.56 us
  transfers between devices with their start and end apart: 18, of which 2 were waited for; matrix products, arithmetic and copies ran while one was open for 28% of the time, Pallas kernels for 4%

profile of v7, /device:TPU:1, one launch (start us, length us, event | category | flops | bytes accessed | tf_op | source)
XLA Modules:
  0.0 140.6 jit_solution(311930263817592206)
XLA Ops:
  0.6 4.0 %collective-permute-start.1 = (bf16[192,3072]{1,0:T(8,128)(2,1)}, bf16[192,3072]{1,0:T(8,128)(2,1)S(1)}, u32[]{:S(2)}, u32[]{:S(2)}) collective-permute-start(bf16[192,3072]{1,0:T(8,128)(2,1)} %bitcast.65), channel_id=1, source_target_pairs={{0,64},{64,128},{128,192},{192,256},{256,320},{320,384},{384,448},... | collective-permute-start | bytes 3538952 | tf_op jit(solution)/shard_map/ppermute | solution.py:18
  4.7 6.7 %collective-permute-start.3 = (bf16[512,768]{1,0:T(8,128)(2,1)}, bf16[512,768]{1,0:T(8,128)(2,1)}, u32[]{:S(2)}, u32[]{:S(2)}) collective-permute-start(bf16[512,768]{1,0:T(8,128)(2,1)} %first.1), channel_id=1, source_target_pairs={{0,2},{2,0},{1,3},{3,1},{4,6},{6,4},{5,7},{7,5},{8,10},{10,8},{9,1... | collective-permute-start | bytes 2359304 | tf_op jit(solution)/shard_map/ppermute | solution.py:18
  11.4 14.2 %all-gather = bf16[384,768]{1,0:T(8,128)(2,1)S(1)} all-gather(bf16[96,768]{1,0:T(8,128)(2,1)} %bitcast.68), channel_id=2, replica_groups=mesh['section'=8,'zlo'=4,'x'=4,'core'=2,'tensor'=2] {'zlo'}, dimensions={0}, use_global_device_ids=true | all-gather | bytes 737280 | tf_op jit(solution)/shard_map/all_gather | solution.py:85
  25.5 4.7 %collective-permute-start.2 = (bf16[4,96,768]{2,1,0:T(8,128)(2,1)S(1)}, bf16[4,96,768]{2,1,0:T(8,128)(2,1)S(1)}, u32[]{:S(2)}, u32[]{:S(2)}) collective-permute-start(bf16[4,96,768]{2,1,0:T(8,128)(2,1)S(1)} %bitcast.61), channel_id=1, source_target_pairs={{0,12},{4,0},{8,4},{12,8},{1,13},{5,1},{9,5},{13,9},{2,14},{6,2},{... | collective-permute-start | bytes 1769480 | tf_op jit(solution)/shard_map/ppermute | solution.py:18
  30.3 1.9 %collective-permute-start = (bf16[4,96,768]{2,1,0:T(8,128)(2,1)S(1)}, bf16[4,96,768]{2,1,0:T(8,128)(2,1)S(1)}, u32[]{:S(2)}, u32[]{:S(2)}) collective-permute-start(bf16[4,96,768]{2,1,0:T(8,128)(2,1)S(1)} %bitcast.62), channel_id=1, source_target_pairs={{0,4},{4,8},{8,12},{12,0},{1,5},{5,9},{9,13},{13,1},{2,6},{6,10},{... | collective-permute-start | bytes 1769480 | tf_op jit(solution)/shard_map/ppermute | solution.py:18
  32.3 2.2 %shard_map.95 = (f32[512,384]{1,0:T(8,128)}, bf16[192,256]{1,0:T(8,128)(2,1)}) custom-call(s32[1,12]{1,0:T(1,128)} %blocks.1, bf16[512,384]{1,0:T(8,128)(2,1)} %previous.1), custom_call_target="tpu_custom_call" | custom-call | bytes 8388608 | tf_op jit(solution)/shard_map/pallas_call | solution.py:95
  34.6 3.0 %shard_map.94 = bf16[768,1024]{1,0:T(8,128)(2,1)} custom-call(bf16[512,768]{1,0:T(8,128)(2,1)} %first.1, bf16[512,768]{1,0:T(8,128)(2,1)} %collective-permute-done.3.second), custom_call_target="tpu_custom_call" | custom-call | tf_op jit(solution)/shard_map/pallas_call | solution.py:41
  37.6 3.5 %collective-permute-done.2 = bf16[4,96,768]{2,1,0:T(8,128)(2,1)S(1)} collective-permute-done((bf16[4,96,768]{2,1,0:T(8,128)(2,1)S(1)}, bf16[4,96,768]{2,1,0:T(8,128)(2,1)S(1)}, u32[]{:S(2)}, u32[]{:S(2)}) %collective-permute-start.2) | collective-permute-done | bytes 589856 | tf_op jit(solution)/shard_map/ppermute | solution.py:18
  41.1 0.8 slice.50
  41.9 5.3 %collective-permute-start.4 = (bf16[3,96,768]{2,1,0:T(8,128)(2,1)}, bf16[3,96,768]{2,1,0:T(8,128)(2,1)}, u32[]{:S(2)}, u32[]{:S(2)}) collective-permute-start(bf16[3,96,768]{2,1,0:T(8,128)(2,1)} %slice.50), channel_id=1, source_target_pairs={{0,12},{4,0},{8,4},{12,8},{1,13},{5,1},{9,5},{13,9},{2,14},{6,2},{... | collective-permute-start | bytes 1327112 | tf_op jit(solution)/shard_map/ppermute | solution.py:18
  47.2 0.0 collective-permute-done
  47.2 0.0 copy-start.4
  47.3 0.8 copy-done.4
  48.1 1.7 %broadcast_in_dim.22.clone = bf16[4,4,96,768]{3,2,1,0:T(8,128)(2,1)} broadcast(bf16[4,96,768]{2,1,0:T(8,128)(2,1)S(1)} %bitcast.63), dimensions={0,2,3} | broadcast | bytes 2949120 | tf_op jit(solution)/shard_map/broadcast_in_dim | solution.py:91
  49.7 2.0 %bitcast_dynamic-update-slice_fusion.1 = bf16[4,4,96,768]{3,2,1,0:T(8,128)(2,1)} fusion(bf16[4,4,96,768]{3,2,1,0:T(8,128)(2,1)} %broadcast_in_dim.22.clone, s32[]{:T(128)S(6)} %select_n.250, bf16[4,96,768]{2,1,0:T(8,128)(2,1)} %copy-done.4), kind=kLoop, calls=%fused_computation.27 | loop fusion | bytes 1179652 | tf_op jit(solution)/shard_map/dynamic_update_slice | solution.py:122
  51.8 0.8 bitcast_dynamic-update-slice_fusion
  52.6 0.9 slice.51
  53.5 0.0 copy-start.1
  53.6 2.1 %collective-permute-start.5 = (bf16[1,96,768]{2,1,0:T(8,128)(2,1)S(1)}, bf16[1,96,768]{2,1,0:T(8,128)(2,1)S(1)}, u32[]{:S(2)}, u32[]{:S(2)}) collective-permute-start(bf16[1,96,768]{2,1,0:T(8,128)(2,1)S(1)} %slice.51), channel_id=1, source_target_pairs={{0,4},{4,8},{8,12},{12,0},{1,5},{5,9},{9,13},{13,1},{2,6},{6,10},{... | collective-permute-start | bytes 442376 | tf_op jit(solution)/shard_map/ppermute | solution.py:18
  55.6 2.0 %convolution_convert_fusion = bf16[96,1024]{1,0:T(8,128)(2,1)} fusion(bf16[768,1024]{1,0:T(8,128)(2,1)S(1)} %copy-done, bf16[4,96,768]{2,1,0:T(8,128)(2,1)} %bitcast.64, s32[]{:T(128)S(6)} %select_n.259, pred[]{:T(512)S(6)} %eq.59, pred[]{:T(512)S(6)} %eq.58, bf16[4,96,768]{2,1,0:T(8,128)(2,1)} %copy-done.4, bf16[4,96,768]{2,1,0:T(8,128)(2,1)S(1)} %collective-permute-done.2), kind=kOutput, calls=%fused_computation.22 | convolution fusion | flops 151240704 | bytes 2211846 | tf_op jit(solution)/shard_map/dot_general | solution.py:111
  57.7 3.2 %collective-permute-start.6 = (bf16[96,1024]{1,0:T(8,128)(2,1)}, bf16[96,1024]{1,0:T(8,128)(2,1)}, u32[]{:S(2)}, u32[]{:S(2)}) collective-permute-start(bf16[96,1024]{1,0:T(8,128)(2,1)} %convolution_convert_fusion), channel_id=1, source_target_pairs={{0,64},{64,128},{128,192},{192,256},{256,320},{320,384},{384,448},... | collective-permute-start | bytes 589832 | tf_op jit(solution)/shard_map/ppermute | solution.py:18
  60.9 0.5 fusion
  61.4 1.7 %slice_select_fusion = bf16[192,768]{1,0:T(8,128)(2,1)} fusion(bf16[192,3072]{1,0:T(8,128)(2,1)} %bitcast.66, bf16[192,3072]{1,0:T(8,128)(2,1)S(1)} %collective-permute-done.1, pred[]{:T(512)S(6)} %eq.54), kind=kLoop, calls=%fused_computation.29 | loop fusion | flops 147456 | bytes 884737 | tf_op jit(solution)/shard_map/jit(_where)/select_n | solution.py:163
  63.1 0.0 collective-permute-done.4
  63.1 0.0 collective-permute-done.5
  63.1 1.4 convolution_convert_fusion.1
  64.5 3.3 %collective-permute-start.7 = (bf16[96,1024]{1,0:T(8,128)(2,1)S(1)}, bf16[96,1024]{1,0:T(8,128)(2,1)}, u32[]{:S(2)}, u32[]{:S(2)}) collective-permute-start(bf16[96,1024]{1,0:T(8,128)(2,1)S(1)} %convolution_convert_fusion.1), channel_id=1, source_target_pairs={{0,448},{64,0},{128,64},{192,128},{256,192},{320,256},{384,320},{4... | collective-permute-start | bytes 589832 | tf_op jit(solution)/shard_map/ppermute | solution.py:18
  67.8 1.8 %bitcast_dynamic-update-slice_fusion.2 = bf16[4,4,96,768]{3,2,1,0:T(8,128)(2,1)} fusion(bf16[4,4,96,768]{3,2,1,0:T(8,128)(2,1)} %bitcast_dynamic-update-slice_fusion, s32[]{:T(128)S(6)} %select_n.267, bf16[3,96,768]{2,1,0:T(8,128)(2,1)} %collective-permute-done.4), kind=kLoop, calls=%fused_computation.28 | loop fusion | bytes 884740 | tf_op jit(solution)/shard_map/dynamic_update_slice | solution.py:122
  69.6 0.7 bitcast_dynamic-update-slice_fusion.3
  70.3 1.1 dynamic-slice_bitcast_fusion.5
  71.4 0.0 collective-permute-done.6
  71.4 1.0 broadcast_select_fusion.4
  72.3 1.2 fusion.3
  73.6 2.0 %collective-permute-start.8 = (bf16[192,1024]{1,0:T(8,128)(2,1)}, bf16[192,1024]{1,0:T(8,128)(2,1)}, u32[]{:S(2)}, u32[]{:S(2)}) collective-permute-start(bf16[192,1024]{1,0:T(8,128)(2,1)} %fusion.3), channel_id=1, source_target_pairs={{0,64},{64,128},{128,192},{192,256},{256,320},{320,384},{384,448},... | collective-permute-start | bytes 1179656 | tf_op jit(solution)/shard_map/ppermute | solution.py:18
  75.6 1.0 broadcast_select_fusion.2
  76.5 1.2 fusion.4
  77.8 4.5 %collective-permute-start.9 = (bf16[192,1024]{1,0:T(8,128)(2,1)}, bf16[192,1024]{1,0:T(8,128)(2,1)}, u32[]{:S(2)}, u32[]{:S(2)}) collective-permute-start(bf16[192,1024]{1,0:T(8,128)(2,1)} %fusion.4), channel_id=1, source_target_pairs={{0,448},{64,0},{128,64},{192,128},{256,192},{320,256},{384,320},{4... | collective-permute-start | bytes 1179656 | tf_op jit(solution)/shard_map/ppermute | solution.py:18
  82.3 1.1 dynamic-slice_bitcast_fusion.3
  83.4 3.6 %collective-permute-start.15 = (bf16[192,768]{1,0:T(8,128)(2,1)}, bf16[192,768]{1,0:T(8,128)(2,1)}, u32[]{:S(2)}, u32[]{:S(2)}) collective-permute-start(bf16[192,768]{1,0:T(8,128)(2,1)} %slice_select_fusion), channel_id=1, source_target_pairs={{0,128},{448,320},{1,129},{449,321},{2,130},{450,322},{3,131},{451... | collective-permute-start | bytes 884744 | tf_op jit(solution)/shard_map/ppermute | solution.py:164
  86.9 0.0 collective-permute-done.8
  86.9 2.2 %fusion.5 = bf16[192,1024]{1,0:T(8,128)(2,1)} fusion(bf16[192,768]{1,0:T(8,128)(2,1)S(1)} %get-tuple-element.38, bf16[768,1024]{1,0:T(8,128)(2,1)S(1)} %copy-done, bf16[192,1024]{1,0:T(8,128)(2,1)} %collective-permute-done.8), kind=kOutput, calls=%fused_computation.13 | convolution fusion | flops 302579712 | bytes 2654208 | tf_op jit(solution)/shard_map/dot_general | solution.py:111
  89.2 1.9 %collective-permute-start.10 = (bf16[192,1024]{1,0:T(8,128)(2,1)}, bf16[192,1024]{1,0:T(8,128)(2,1)}, u32[]{:S(2)}, u32[]{:S(2)}) collective-permute-start(bf16[192,1024]{1,0:T(8,128)(2,1)} %fusion.5), channel_id=1, source_target_pairs={{0,64},{64,128},{128,192},{192,256},{256,320},{320,384},{384,448},... | collective-permute-start | bytes 1179656 | tf_op jit(solution)/shard_map/ppermute | solution.py:18
  91.1 2.2 %fusion.6 = bf16[192,1024]{1,0:T(8,128)(2,1)} fusion(bf16[192,768]{1,0:T(8,128)(2,1)S(1)} %get-tuple-element.39, bf16[768,1024]{1,0:T(8,128)(2,1)S(1)} %copy-done, bf16[192,1024]{1,0:T(8,128)(2,1)} %collective-permute-done.9), kind=kOutput, calls=%fused_computation.14 | convolution fusion | flops 302579712 | bytes 2654208 | tf_op jit(solution)/shard_map/dot_general | solution.py:111
  93.3 4.6 %collective-permute-start.11 = (bf16[192,1024]{1,0:T(8,128)(2,1)}, bf16[192,1024]{1,0:T(8,128)(2,1)}, u32[]{:S(2)}, u32[]{:S(2)}) collective-permute-start(bf16[192,1024]{1,0:T(8,128)(2,1)} %fusion.6), channel_id=1, source_target_pairs={{0,448},{64,0},{128,64},{192,128},{256,192},{320,256},{384,320},{4... | collective-permute-start | bytes 1179656 | tf_op jit(solution)/shard_map/ppermute | solution.py:18
  97.9 1.1 dynamic-slice_bitcast_fusion.1
  99.0 1.3 collective-permute-done.10
  100.2 2.2 %fusion.7 = bf16[192,1024]{1,0:T(8,128)(2,1)} fusion(bf16[192,768]{1,0:T(8,128)(2,1)S(1)} %get-tuple-element.41, bf16[768,1024]{1,0:T(8,128)(2,1)S(1)} %copy-done, bf16[192,1024]{1,0:T(8,128)(2,1)} %collective-permute-done.10), kind=kOutput, calls=%fused_computation.15 | convolution fusion | flops 302579712 | bytes 2654208 | tf_op jit(solution)/shard_map/dot_general | solution.py:111
  102.5 4.1 %collective-permute-start.12 = (bf16[192,1024]{1,0:T(8,128)(2,1)}, bf16[192,1024]{1,0:T(8,128)(2,1)}, u32[]{:S(2)}, u32[]{:S(2)}) collective-permute-start(bf16[192,1024]{1,0:T(8,128)(2,1)} %fusion.7), channel_id=1, source_target_pairs={{0,64},{64,128},{128,192},{192,256},{256,320},{320,384},{384,448},... | collective-permute-start | bytes 1179656 | tf_op jit(solution)/shard_map/ppermute | solution.py:18
  106.6 0.0 collective-permute-done.11
  106.6 2.2 %fusion.8 = bf16[192,1024]{1,0:T(8,128)(2,1)} fusion(bf16[192,768]{1,0:T(8,128)(2,1)S(1)} %get-tuple-element.42, bf16[768,1024]{1,0:T(8,128)(2,1)S(1)} %copy-done, bf16[192,1024]{1,0:T(8,128)(2,1)} %collective-permute-done.11), kind=kOutput, calls=%fused_computation.16 | convolution fusion | flops 302579712 | bytes 2654208 | tf_op jit(solution)/shard_map/dot_general | solution.py:111
  108.8 2.4 %collective-permute-start.13 = (bf16[192,1024]{1,0:T(8,128)(2,1)}, bf16[192,1024]{1,0:T(8,128)(2,1)}, u32[]{:S(2)}, u32[]{:S(2)}) collective-permute-start(bf16[192,1024]{1,0:T(8,128)(2,1)} %fusion.8), channel_id=1, source_target_pairs={{0,448},{64,0},{128,64},{192,128},{256,192},{320,256},{384,320},{4... | collective-permute-start | bytes 1179656 | tf_op jit(solution)/shard_map/ppermute | solution.py:18
  111.2 1.9 %fusion.13 = (bf16[192,384]{1,0:T(8,128)(2,1)S(1)}, bf16[192,384]{1,0:T(8,128)(2,1)}) fusion(bf16[192,3072]{1,0:T(8,128)(2,1)} %bitcast.67, bf16[192,3072]{1,0:T(8,128)(2,1)S(1)} %collective-permute-done.1, pred[]{:T(512)S(6)} %lt.157, pred[]{:T(512)S(6)} %or.9, pred[]{:T(512)S(6)} %eq.54, bf16[192,768]{1,0:T(8,128)(2,1)} %collective-permute-done.15), kind=kLoop, calls=%fused_computation.42 | loop fusion | flops 442368 | bytes 1179651 | tf_op jit(solution)/shard_map/jit(_where)/select_n | solution.py:174
  113.0 3.7 %collective-permute-start.16 = (bf16[192,384]{1,0:T(8,128)(2,1)S(1)}, bf16[192,384]{1,0:T(8,128)(2,1)}, u32[]{:S(2)}, u32[]{:S(2)}) collective-permute-start(bf16[192,384]{1,0:T(8,128)(2,1)S(1)} %get-tuple-element.51), channel_id=1, source_target_pairs={{0,64},{128,192},{448,384},{320,256},{1,65},{129,193},{449,385},{3... | collective-permute-start | bytes 442376 | tf_op jit(solution)/shard_map/ppermute | solution.py:175
  116.7 7.8 %collective-permute-start.17 = (f32[192]{0:T(256)S(1)}, f32[192]{0:T(256)S(1)}, u32[]{:S(2)}, u32[]{:S(2)}) collective-permute-start(f32[192]{0:T(256)S(1)} %fusion), channel_id=1, source_target_pairs={{0,1},{1,0},{2,3},{3,2},{4,5},{5,4},{6,7},{7,6},{8,9},{9,8},{10,11... | collective-permute-start | bytes 2312 | tf_op jit(solution)/shard_map/ppermute | solution.py:18
  124.5 0.0 copy-start.2
  124.5 1.1 dynamic-slice_bitcast_fusion
  125.7 0.0 collective-permute-done.13
  125.7 1.4 convolution_add_fusion.6
  127.0 6.6 %collective-permute-start.14 = (bf16[192,512]{1,0:T(8,128)(2,1)S(1)}, bf16[192,512]{1,0:T(8,128)(2,1)S(1)}, u32[]{:S(2)}, u32[]{:S(2)}) collective-permute-start(bf16[192,512]{1,0:T(8,128)(2,1)S(1)} %convolution_add_fusion.6), channel_id=1, source_target_pairs={{0,2},{2,0},{1,3},{3,1},{4,6},{6,4},{5,7},{7,5},{8,10},{10,8},{9,1... | collective-permute-start | bytes 589832 | tf_op jit(solution)/shard_map/ppermute | solution.py:18
  133.7 1.5 %fusion.9 = bf16[1,192,3072]{2,1,0:T(8,128)(2,1)} fusion(f32[3072]{0:T(1024)S(1)} %bitcast.69, f32[192]{0:T(256)S(1)} %add_rsqrt_fusion, bf16[192,3072]{1,0:T(8,128)(2,1)S(1)} %copy-done.2, bf16[192,3072]{1,0:T(8,128)(2,1)S(1)} %collective-permute-done.1, pred[]{:T(512)S(6)} %eq.54), kind=kLoop, calls=%fused_computation.19 | loop fusion | flops 2949120 | bytes 3552001 | tf_op jit(solution)/shard_map/broadcast_in_dim | solution.py:193
  135.2 2.0 %fusion.10.mine = bf16[192,512]{1,0:T(8,128)(2,1)} fusion(bf16[192,768]{1,0:T(8,128)(2,1)S(1)} %dynamic-slice_bitcast_fusion, bf16[768,1024]{1,0:T(8,128)(2,1)S(1)} %copy-done, bf16[192,1024]{1,0:T(8,128)(2,1)} %collective-permute-done.13, bf16[192,1024]{1,0:T(8,128)(2,1)} %collective-permute-done.12), kind=kOutput, calls=%fused_computation.21 | convolution fusion | flops 151486464 | bytes 1671168 | tf_op jit(solution)/shard_map/dot_general | solution.py:188
  137.3 0.0 collective-permute-done.14.other
  137.3 0.7 copy-done.5
  137.9 2.7 %shard_map.96 = (bf16[512,384]{1,0:T(8,128)(2,1)}, f32[192,384]{1,0:T(8,128)}) custom-call(s32[1]{0:T(128)} %bitcast.core, s32[1]{0:T(128)} %bitcast.1.keeps, bf16[192,512]{1,0:T(8,128)(2,1)} %fusion.10.mine, bf16[192,512]{1,0:T(8,128)(2,1)} %copy-done.5, f32[512,384]{1,0:T(8,128)} %get-tuple-element.28.old, bf16[192,256]{1,0:T(8,128)(2,1)} %get-tuple-element.44.hot, ...), custom_call_target="tpu_custom_call" | custom-call | tf_op jit(solution)/shard_map/pallas_call | solution.py:195
  (18 shorter events, 0.0 us)
Async XLA Ops:
  0.6 46.6 %collective-permute-start.1 = (bf16[192,3072]{1,0:T(8,128)(2,1)}, bf16[192,3072]{1,0:T(8,128)(2,1)S(1)}, u32[]{:S(2)}, u32[]{:S(2)}) collective-permute-start(bf16[192,3072]{1,0:T(8,128)(2,1)} %bitcast.65), channel_id=1, source_target_pairs={{0,64},{64,128},{128,192},{192,256},{256,320},{320,384},{384,448},... | collective-permute-start | bytes 3538952 | tf_op jit(solution)/shard_map/ppermute | solution.py:18
  4.7 29.9 %collective-permute-start.3 = (bf16[512,768]{1,0:T(8,128)(2,1)}, bf16[512,768]{1,0:T(8,128)(2,1)}, u32[]{:S(2)}, u32[]{:S(2)}) collective-permute-start(bf16[512,768]{1,0:T(8,128)(2,1)} %first.1), channel_id=1, source_target_pairs={{0,2},{2,0},{1,3},{3,1},{4,6},{6,4},{5,7},{7,5},{8,10},{10,8},{9,1... | collective-permute-start | bytes 2359304 | tf_op jit(solution)/shard_map/ppermute | solution.py:18
  25.5 21.7 %copy-start.3 = (bf16[384,768]{1,0:T(8,128)(2,1)}, bf16[384,768]{1,0:T(8,128)(2,1)S(1)}, u32[]{:S(2)}) copy-start(bf16[384,768]{1,0:T(8,128)(2,1)S(1)} %all-gather) | copy-start | bytes 1769476
  25.5 15.6 %collective-permute-start.2 = (bf16[4,96,768]{2,1,0:T(8,128)(2,1)S(1)}, bf16[4,96,768]{2,1,0:T(8,128)(2,1)S(1)}, u32[]{:S(2)}, u32[]{:S(2)}) collective-permute-start(bf16[4,96,768]{2,1,0:T(8,128)(2,1)S(1)} %bitcast.61), channel_id=1, source_target_pairs={{0,12},{4,0},{8,4},{12,8},{1,13},{5,1},{9,5},{13,9},{2,14},{6,2},{... | collective-permute-start | bytes 1769480 | tf_op jit(solution)/shard_map/ppermute | solution.py:18
  30.3 17.0 %collective-permute-start = (bf16[4,96,768]{2,1,0:T(8,128)(2,1)S(1)}, bf16[4,96,768]{2,1,0:T(8,128)(2,1)S(1)}, u32[]{:S(2)}, u32[]{:S(2)}) collective-permute-start(bf16[4,96,768]{2,1,0:T(8,128)(2,1)S(1)} %bitcast.62), channel_id=1, source_target_pairs={{0,4},{4,8},{8,12},{12,0},{1,5},{5,9},{9,13},{13,1},{2,6},{6,10},{... | collective-permute-start | bytes 1769480 | tf_op jit(solution)/shard_map/ppermute | solution.py:18
  41.9 21.2 %collective-permute-start.4 = (bf16[3,96,768]{2,1,0:T(8,128)(2,1)}, bf16[3,96,768]{2,1,0:T(8,128)(2,1)}, u32[]{:S(2)}, u32[]{:S(2)}) collective-permute-start(bf16[3,96,768]{2,1,0:T(8,128)(2,1)} %slice.50), channel_id=1, source_target_pairs={{0,12},{4,0},{8,4},{12,8},{1,13},{5,1},{9,5},{13,9},{2,14},{6,2},{... | collective-permute-start | bytes 1327112 | tf_op jit(solution)/shard_map/ppermute | solution.py:18
  47.2 0.8 copy-start.4
  49.7 5.9 %copy-start = (bf16[768,1024]{1,0:T(8,128)(2,1)S(1)}, bf16[768,1024]{1,0:T(8,128)(2,1)}, u32[]{:S(2)}) copy-start(bf16[768,1024]{1,0:T(8,128)(2,1)} %shard_map.94) | copy-start | bytes 4718596
  53.5 7.3 %copy-start.1 = (bf16[192,3072]{1,0:T(8,128)(2,1)S(1)}, bf16[192,3072]{1,0:T(8,128)(2,1)}, u32[]{:S(2)}) copy-start(bf16[192,3072]{1,0:T(8,128)(2,1)} %param.11) | copy-start | bytes 3538948
  53.6 9.5 %collective-permute-start.5 = (bf16[1,96,768]{2,1,0:T(8,128)(2,1)S(1)}, bf16[1,96,768]{2,1,0:T(8,128)(2,1)S(1)}, u32[]{:S(2)}, u32[]{:S(2)}) collective-permute-start(bf16[1,96,768]{2,1,0:T(8,128)(2,1)S(1)} %slice.51), channel_id=1, source_target_pairs={{0,4},{4,8},{8,12},{12,0},{1,5},{5,9},{9,13},{13,1},{2,6},{6,10},{... | collective-permute-start | bytes 442376 | tf_op jit(solution)/shard_map/ppermute | solution.py:18
  57.7 13.7 %collective-permute-start.6 = (bf16[96,1024]{1,0:T(8,128)(2,1)}, bf16[96,1024]{1,0:T(8,128)(2,1)}, u32[]{:S(2)}, u32[]{:S(2)}) collective-permute-start(bf16[96,1024]{1,0:T(8,128)(2,1)} %convolution_convert_fusion), channel_id=1, source_target_pairs={{0,64},{64,128},{128,192},{192,256},{256,320},{320,384},{384,448},... | collective-permute-start | bytes 589832 | tf_op jit(solution)/shard_map/ppermute | solution.py:18
  64.5 11.1 %collective-permute-start.7 = (bf16[96,1024]{1,0:T(8,128)(2,1)S(1)}, bf16[96,1024]{1,0:T(8,128)(2,1)}, u32[]{:S(2)}, u32[]{:S(2)}) collective-permute-start(bf16[96,1024]{1,0:T(8,128)(2,1)S(1)} %convolution_convert_fusion.1), channel_id=1, source_target_pairs={{0,448},{64,0},{128,64},{192,128},{256,192},{320,256},{384,320},{4... | collective-permute-start | bytes 589832 | tf_op jit(solution)/shard_map/ppermute | solution.py:18
  73.6 13.4 %collective-permute-start.8 = (bf16[192,1024]{1,0:T(8,128)(2,1)}, bf16[192,1024]{1,0:T(8,128)(2,1)}, u32[]{:S(2)}, u32[]{:S(2)}) collective-permute-start(bf16[192,1024]{1,0:T(8,128)(2,1)} %fusion.3), channel_id=1, source_target_pairs={{0,64},{64,128},{128,192},{192,256},{256,320},{320,384},{384,448},... | collective-permute-start | bytes 1179656 | tf_op jit(solution)/shard_map/ppermute | solution.py:18
  77.8 13.3 %collective-permute-start.9 = (bf16[192,1024]{1,0:T(8,128)(2,1)}, bf16[192,1024]{1,0:T(8,128)(2,1)}, u32[]{:S(2)}, u32[]{:S(2)}) collective-permute-start(bf16[192,1024]{1,0:T(8,128)(2,1)} %fusion.4), channel_id=1, source_target_pairs={{0,448},{64,0},{128,64},{192,128},{256,192},{320,256},{384,320},{4... | collective-permute-start | bytes 1179656 | tf_op jit(solution)/shard_map/ppermute | solution.py:18
  83.4 27.8 %collective-permute-start.15 = (bf16[192,768]{1,0:T(8,128)(2,1)}, bf16[192,768]{1,0:T(8,128)(2,1)}, u32[]{:S(2)}, u32[]{:S(2)}) collective-permute-start(bf16[192,768]{1,0:T(8,128)(2,1)} %slice_select_fusion), channel_id=1, source_target_pairs={{0,128},{448,320},{1,129},{449,321},{2,130},{450,322},{3,131},{451... | collective-permute-start | bytes 884744 | tf_op jit(solution)/shard_map/ppermute | solution.py:164
  89.2 11.1 %collective-permute-start.10 = (bf16[192,1024]{1,0:T(8,128)(2,1)}, bf16[192,1024]{1,0:T(8,128)(2,1)}, u32[]{:S(2)}, u32[]{:S(2)}) collective-permute-start(bf16[192,1024]{1,0:T(8,128)(2,1)} %fusion.5), channel_id=1, source_target_pairs={{0,64},{64,128},{128,192},{192,256},{256,320},{320,384},{384,448},... | collective-permute-start | bytes 1179656 | tf_op jit(solution)/shard_map/ppermute | solution.py:18
  93.3 13.3 %collective-permute-start.11 = (bf16[192,1024]{1,0:T(8,128)(2,1)}, bf16[192,1024]{1,0:T(8,128)(2,1)}, u32[]{:S(2)}, u32[]{:S(2)}) collective-permute-start(bf16[192,1024]{1,0:T(8,128)(2,1)} %fusion.6), channel_id=1, source_target_pairs={{0,448},{64,0},{128,64},{192,128},{256,192},{320,256},{384,320},{4... | collective-permute-start | bytes 1179656 | tf_op jit(solution)/shard_map/ppermute | solution.py:18
  102.5 23.2 %collective-permute-start.12 = (bf16[192,1024]{1,0:T(8,128)(2,1)}, bf16[192,1024]{1,0:T(8,128)(2,1)}, u32[]{:S(2)}, u32[]{:S(2)}) collective-permute-start(bf16[192,1024]{1,0:T(8,128)(2,1)} %fusion.7), channel_id=1, source_target_pairs={{0,64},{64,128},{128,192},{192,256},{256,320},{320,384},{384,448},... | collective-permute-start | bytes 1179656 | tf_op jit(solution)/shard_map/ppermute | solution.py:18
  108.8 16.9 %collective-permute-start.13 = (bf16[192,1024]{1,0:T(8,128)(2,1)}, bf16[192,1024]{1,0:T(8,128)(2,1)}, u32[]{:S(2)}, u32[]{:S(2)}) collective-permute-start(bf16[192,1024]{1,0:T(8,128)(2,1)} %fusion.8), channel_id=1, source_target_pairs={{0,448},{64,0},{128,64},{192,128},{256,192},{320,256},{384,320},{4... | collective-permute-start | bytes 1179656 | tf_op jit(solution)/shard_map/ppermute | solution.py:18
  113.0 20.6 %copy-start.6 = (f32[1,3072]{1,0:T(1,128)S(1)}, f32[1,3072]{1,0:T(1,128)}, u32[]{:S(2)}) copy-start(f32[1,3072]{1,0:T(1,128)} %param.12) | copy-start | bytes 36868
  113.0 24.2 %collective-permute-start.16 = (bf16[192,384]{1,0:T(8,128)(2,1)S(1)}, bf16[192,384]{1,0:T(8,128)(2,1)}, u32[]{:S(2)}, u32[]{:S(2)}) collective-permute-start(bf16[192,384]{1,0:T(8,128)(2,1)S(1)} %get-tuple-element.51), channel_id=1, source_target_pairs={{0,64},{128,192},{448,384},{320,256},{1,65},{129,193},{449,385},{3... | collective-permute-start | bytes 442376 | tf_op jit(solution)/shard_map/ppermute | solution.py:175
  116.7 8.9 %collective-permute-start.17 = (f32[192]{0:T(256)S(1)}, f32[192]{0:T(256)S(1)}, u32[]{:S(2)}, u32[]{:S(2)}) collective-permute-start(f32[192]{0:T(256)S(1)} %fusion), channel_id=1, source_target_pairs={{0,1},{1,0},{2,3},{3,2},{4,5},{5,4},{6,7},{7,6},{8,9},{9,8},{10,11... | collective-permute-start | bytes 2312 | tf_op jit(solution)/shard_map/ppermute | solution.py:18
  124.5 9.2 %copy-start.2 = (bf16[192,3072]{1,0:T(8,128)(2,1)S(1)}, bf16[192,3072]{1,0:T(8,128)(2,1)}, u32[]{:S(2)}) copy-start(bf16[192,3072]{1,0:T(8,128)(2,1)} %param.11) | copy-start | bytes 3538948
  127.0 10.2 %collective-permute-start.14 = (bf16[192,512]{1,0:T(8,128)(2,1)S(1)}, bf16[192,512]{1,0:T(8,128)(2,1)S(1)}, u32[]{:S(2)}, u32[]{:S(2)}) collective-permute-start(bf16[192,512]{1,0:T(8,128)(2,1)S(1)} %convolution_add_fusion.6), channel_id=1, source_target_pairs={{0,2},{2,0},{1,3},{3,1},{4,6},{6,4},{5,7},{7,5},{8,10},{10,8},{9,1... | collective-permute-start | bytes 589832 | tf_op jit(solution)/shard_map/ppermute | solution.py:18
  137.3 0.7 copy-start.5

commit v8 on v7

--- a/solution.py
+++ b/solution.py
@@ -41,7 +41,26 @@
     return pl.pallas_call(
         transpose_kernel,
         out_shape=jax.ShapeDtypeStruct((depth, 2 * rows), first.dtype),
+        compiler_params=pltpu.CompilerParams(vmem_limit_bytes=8 << 20),
     )(first, second)
+
+
+def whole_kernel(x, held, above, opposite, rest, below, out):
+    lines, count = out.shape[:2]
+    for z in range(lines):
+        across = opposite[z] if z < LATE else rest[z - LATE]
+        for steps, part in enumerate((held[z], above[z], across, below[z])):
+            out[z, (x[0] + steps) % count] = part
+
+
+def whole_weight(x, *parts):
+    lines, shard, depth = parts[0].shape
+    return pl.pallas_call(
+        whole_kernel,
+        in_specs=[pl.BlockSpec(memory_space=pltpu.SMEM)] + [pl.BlockSpec(memory_space=pltpu.VMEM)] * len(parts),
+        out_shape=jax.ShapeDtypeStruct((lines, 4, shard, depth), parts[0].dtype),
+        compiler_params=pltpu.CompilerParams(vmem_limit_bytes=8 << 20),
+    )(x.astype(jnp.int32).reshape(1), *parts)
 
 
 def ready_kernel(blocks, previous, out, hot):
@@ -87,8 +106,6 @@
     above = around(held, "x", -1)
     incoming = around(act, "section", 1)
     both = transposed(context, around(context, "core", 1))
-    count = lax.axis_size("x")
-    weight = jnp.broadcast_to(held[:, None], (held.shape[0], count, shard, depth))
 
     smem, vmem = (pl.BlockSpec(memory_space=space) for space in (pltpu.SMEM, pltpu.VMEM))
     masked = mask_blocks.shape[1] * BLOCK_SIDE * BLOCK_SIDE
@@ -100,9 +117,10 @@
             jax.ShapeDtypeStruct((rows, width), f32),
             jax.ShapeDtypeStruct((masked, PATCHES), bf16),
         ),
+        compiler_params=pltpu.CompilerParams(vmem_limit_bytes=8 << 20),
         cost_estimate=pl.CostEstimate(flops=0, bytes_accessed=8 << 20, transcendentals=0),
     )(mask_blocks, previous)
-    above = tied(above, both, old, weight)
+    above = tied(above, both, old)
     below, incoming = lax.optimization_barrier((below, incoming))
     opposite = around(above[:LATE], "x", -1)
     opposite_rest = around(below[LATE:], "x", 1)
@@ -119,10 +137,7 @@
     def down(value):
         return around(value.astype(bf16), "section", -1)
 
-    put = lambda part, at, line=0: lax.dynamic_update_slice(weight, part[:, None], (line, at % count, 0, 0))
-    weight = put(below, x + 3)
-    weight = put(above, x + 1)
-    dest, weight = lax.optimization_barrier(((position + far) % sections, weight))
+    dest = (position + far) % sections
     plane = lambda part: lax.dynamic_index_in_dim(part, dest // 2, 0, keepdims=False)
     near = jnp.where(x % 2 == 0, plane(below), plane(above))
     begun = product(jnp.where(dest % 2 == x // 2, plane(held), near)).astype(bf16)
@@ -132,8 +147,7 @@
     ended = product(jnp.where(dest % 2 == x // 2, beside, across)).astype(bf16)
     falling = down(ended)
 
-    weight = put(tied(opposite, ended), x + 2)
-    weight = put(tied(opposite_rest, ended), x + 2, LATE)
+    weight = whole_weight(x, held, above, tied(opposite, ended), opposite_rest, below)
     weight = weight.reshape(sections, 2 * shard, depth)
 
     def block(steps, after=()):
@@ -149,12 +163,11 @@
     half = early_half((position + far + 1) % sections)
     falling = spread(falling, 1 - half)
     def round_of(steps, after):
-        ahead, behind = lax.optimization_barrier((block(steps, after), block(sections - steps, after)))
-        upward = product(ahead) + rising.astype(f32)
-        downward = product(behind) + falling.astype(f32)
+        upward = product(block(steps, after)) + rising.astype(f32)
+        downward = product(block(sections - steps, after)) + falling.astype(f32)
         return upward.astype(bf16), downward.astype(bf16)
 
-    sent = round_of(3, (ended,))
+    sent = round_of(3, ())
     rising, falling = up(sent[0]), down(sent[1])
 
     last = sections - 1
@@ -162,10 +175,10 @@
     arrived = incoming
     given = tied(jnp.where(position == 0, cut(arrived, 2, 2), cut(act, last - 3, 2)), *sent)
     passed = lax.ppermute(given, "section", [(0, 2), (last, last - 2)])
-    sent = round_of(2, sent)
+    sent = round_of(2, ())
     rising, falling = up(sent[0]), down(sent[1])
 
-    sent = round_of(1, sent)
+    sent = round_of(1, ())
     rising, falling = up(sent[0]), down(sent[1])
 
     ends = (position == 0) | (position == last)
@@ -184,7 +197,7 @@
     features = act.shape[-1] * lax.axis_size("tensor")
     scaling = lax.rsqrt(squares[:, None] / features + 1e-06)
 
-    own_weight = tied(block(0, sent))
+    own_weight = block(0)
     total = lambda part: jnp.dot(own_weight, both[:, part], preferred_element_type=f32) + (
         rising[:, part].astype(f32) + falling[:, part].astype(f32)
     )
@@ -200,6 +213,7 @@
             jax.ShapeDtypeStruct((rows, width), bf16),
             jax.ShapeDtypeStruct((masked, width), f32),
         ),
+        compiler_params=pltpu.CompilerParams(vmem_limit_bytes=12 << 20),
     )(core.astype(jnp.int32).reshape(1), keeps.astype(jnp.int32).reshape(1), mine.astype(bf16), other, old, hot, kept, handed)
     return (targets, section_out, target_error)
 

time: 142 us -> 117 us (0.82)
  the two profiles are of different devices: /device:TPU:1 before, /device:TPU:41 now
where the time goes in v8:
time: 117 us; the launch traced here: 116 us
  starting transfers between devices  67.5 us (58%)
  blocking collectives  18.3 us (16%)
  waiting for transfers between devices  8.68 us (7%)
  other arithmetic  6.64 us (6%)
  matrix products  5.36 us (5%)
  local copies, waits for them, and re-layouts  4.14 us (4%)
  Pallas kernels  3.75 us (3%)
  between operations  1.33 us (1%)
    ppermute x16, starting transfers between devices, around(): lax.ppermute(value, axis, [(i, (i + steps) % count) for i in range(count)])  61.6 us
    all_gather x1, blocking collectives, on_device(): held = lax.all_gather(out_weight.T, 'zlo', axis=0, tiled=False)  18.3 us
    ppermute x16, waiting for transfers between devices, around(): lax.ppermute(value, axis, [(i, (i + steps) % count) for i in range(count)])  8.68 us
    dot_general x8, matrix products, product(): return jnp.dot(weight, both, preferred_element_type=f32)  4.7 us
    ppermute x1, starting transfers between devices, on_device(): lax.ppermute(onward, 'section', [(0, 1), (2, 3), (last, last - 1), (last...  4.59 us
    unnamed x16, local copies, waits for them, and re-layouts  3.33 us
    broadcast_in_dim x1, other arithmetic, on_device(): (wide * tied(scaling, theirs) * section_gains).astype(bf16)[None]  2.78 us
  transfers between devices with their start and end apart: 18, of which 5 were waited for; matrix products, arithmetic and copies ran while one was open for 11% of the time, Pallas kernels for 2%

profile of v8, /device:TPU:41, one launch (start us, length us, event | category | flops | bytes accessed | tf_op | source)
XLA Modules:
  0.0 115.7 jit_solution(12364683565144506979)
XLA Ops:
  0.6 2.4 %collective-permute-start.4 = (bf16[192,3072]{1,0:T(8,128)(2,1)}, bf16[192,3072]{1,0:T(8,128)(2,1)}, u32[]{:S(2)}, u32[]{:S(2)}) collective-permute-start(bf16[192,3072]{1,0:T(8,128)(2,1)} %bitcast.61), channel_id=1, source_target_pairs={{0,64},{64,128},{128,192},{192,256},{256,320},{320,384},{384,448},... | collective-permute-start | bytes 3538952 | tf_op jit(solution)/shard_map/ppermute | solution.py:18
  3.1 2.9 %collective-permute-start.1 = (bf16[512,768]{1,0:T(8,128)(2,1)}, bf16[512,768]{1,0:T(8,128)(2,1)S(1)}, u32[]{:S(2)}, u32[]{:S(2)}) collective-permute-start(bf16[512,768]{1,0:T(8,128)(2,1)} %first.1), channel_id=1, source_target_pairs={{0,2},{2,0},{1,3},{3,1},{4,6},{6,4},{5,7},{7,5},{8,10},{10,8},{9,1... | collective-permute-start | bytes 2359304 | tf_op jit(solution)/shard_map/ppermute | solution.py:18
  6.0 18.3 %all-gather = bf16[384,768]{1,0:T(8,128)(2,1)S(1)} all-gather(bf16[96,768]{1,0:T(8,128)(2,1)} %bitcast.64), channel_id=2, replica_groups=mesh['section'=8,'zlo'=4,'x'=4,'core'=2,'tensor'=2] {'zlo'}, dimensions={0}, use_global_device_ids=true | all-gather | bytes 737280 | tf_op jit(solution)/shard_map/all_gather | solution.py:104
  24.3 4.4 %collective-permute-start = (bf16[4,96,768]{2,1,0:T(8,128)(2,1)S(1)}, bf16[4,96,768]{2,1,0:T(8,128)(2,1)S(1)}, u32[]{:S(2)}, u32[]{:S(2)}) collective-permute-start(bf16[4,96,768]{2,1,0:T(8,128)(2,1)S(1)} %bitcast.57), channel_id=1, source_target_pairs={{0,12},{4,0},{8,4},{12,8},{1,13},{5,1},{9,5},{13,9},{2,14},{6,2},{... | collective-permute-start | bytes 1769480 | tf_op jit(solution)/shard_map/ppermute | solution.py:18
  28.7 1.9 %collective-permute-start.3 = (bf16[4,96,768]{2,1,0:T(8,128)(2,1)S(1)}, bf16[4,96,768]{2,1,0:T(8,128)(2,1)S(1)}, u32[]{:S(2)}, u32[]{:S(2)}) collective-permute-start(bf16[4,96,768]{2,1,0:T(8,128)(2,1)S(1)} %bitcast.58), channel_id=1, source_target_pairs={{0,4},{4,8},{8,12},{12,0},{1,5},{5,9},{9,13},{13,1},{2,6},{6,10},{... | collective-permute-start | bytes 1769480 | tf_op jit(solution)/shard_map/ppermute | solution.py:18
  30.6 0.0 copy-start.3
  30.6 1.0 copy-done.3
  31.6 0.7 copy-done.4
  32.3 0.8 shard_map.95
  33.1 0.9 copy-done.1
  34.0 0.0 collective-permute-done.1.second
  34.0 0.5 shard_map.94
  34.5 4.9 %collective-permute-done.above = bf16[4,96,768]{2,1,0:T(8,128)(2,1)S(1)} collective-permute-done((bf16[4,96,768]{2,1,0:T(8,128)(2,1)S(1)}, bf16[4,96,768]{2,1,0:T(8,128)(2,1)S(1)}, u32[]{:S(2)}, u32[]{:S(2)}) %collective-permute-start) | collective-permute-done | bytes 589856 | tf_op jit(solution)/shard_map/ppermute | solution.py:18
  39.4 0.8 slice.50
  40.2 5.3 %collective-permute-start.2 = (bf16[3,96,768]{2,1,0:T(8,128)(2,1)}, bf16[3,96,768]{2,1,0:T(8,128)(2,1)}, u32[]{:S(2)}, u32[]{:S(2)}) collective-permute-start(bf16[3,96,768]{2,1,0:T(8,128)(2,1)} %slice.50), channel_id=1, source_target_pairs={{0,12},{4,0},{8,4},{12,8},{1,13},{5,1},{9,5},{13,9},{2,14},{6,2},{... | collective-permute-start | bytes 1327112 | tf_op jit(solution)/shard_map/ppermute | solution.py:18
  45.7 0.0 collective-permute-done.3.below
  45.8 0.0 collective-permute-done.4
  45.8 1.9 %collective-permute-start.5 = (bf16[1,96,768]{2,1,0:T(8,128)(2,1)S(1)}, bf16[1,96,768]{2,1,0:T(8,128)(2,1)S(1)}, u32[]{:S(2)}, u32[]{:S(2)}) collective-permute-start(bf16[1,96,768]{2,1,0:T(8,128)(2,1)S(1)} %slice.51), channel_id=1, source_target_pairs={{0,4},{4,8},{8,12},{12,0},{1,5},{5,9},{9,13},{13,1},{2,6},{6,10},{... | collective-permute-start | bytes 442376 | tf_op jit(solution)/shard_map/ppermute | solution.py:18
  47.7 0.4 convolution_convert_fusion
  48.1 2.3 %collective-permute-start.6 = (bf16[96,1024]{1,0:T(8,128)(2,1)S(1)}, bf16[96,1024]{1,0:T(8,128)(2,1)S(1)}, u32[]{:S(2)}, u32[]{:S(2)}) collective-permute-start(bf16[96,1024]{1,0:T(8,128)(2,1)S(1)} %convolution_convert_fusion), channel_id=1, source_target_pairs={{0,64},{64,128},{128,192},{192,256},{256,320},{320,384},{384,448},... | collective-permute-start | bytes 589832 | tf_op jit(solution)/shard_map/ppermute | solution.py:18
  50.4 2.0 %collective-permute-done.2.opposite = bf16[3,96,768]{2,1,0:T(8,128)(2,1)} collective-permute-done((bf16[3,96,768]{2,1,0:T(8,128)(2,1)}, bf16[3,96,768]{2,1,0:T(8,128)(2,1)}, u32[]{:S(2)}, u32[]{:S(2)}) %collective-permute-start.2) | collective-permute-done | bytes 442400 | tf_op jit(solution)/shard_map/ppermute | solution.py:18
  52.4 0.5 collective-permute-done.5.rest
  52.9 1.3 %convolution_convert_fusion.1 = bf16[96,1024]{1,0:T(8,128)(2,1)S(1)} fusion(bf16[768,1024]{1,0:T(8,128)(2,1)S(1)} %shard_map.94, bf16[1,96,768]{2,1,0:T(8,128)(2,1)S(1)} %collective-permute-done.5.rest, bf16[3,96,768]{2,1,0:T(8,128)(2,1)} %collective-permute-done.2.opposite, s32[]{:T(128)S(6)} %select_n.234, pred[]{:T(512)S(6)} %lt.108, pred[]{:T(512)S(6)} %eq.55, ...), kind=kOutput, calls=%fused_computation.23 | convolution fusion | flops 151314432 | bytes 2359307 | tf_op jit(solution)/shard_map/dot_general | solution.py:129
  54.2 3.3 %collective-permute-start.10 = (bf16[96,1024]{1,0:T(8,128)(2,1)S(1)}, bf16[96,1024]{1,0:T(8,128)(2,1)S(1)}, u32[]{:S(2)}, u32[]{:S(2)}) collective-permute-start(bf16[96,1024]{1,0:T(8,128)(2,1)S(1)} %convolution_convert_fusion.1), channel_id=1, source_target_pairs={{0,448},{64,0},{128,64},{192,128},{256,192},{320,256},{384,320},{4... | collective-permute-start | bytes 589832 | tf_op jit(solution)/shard_map/ppermute | solution.py:18
  57.5 1.2 %shard_map.96 = bf16[4,4,96,768]{3,2,1,0:T(8,128)(2,1)S(1)} custom-call(s32[1]{0:T(128)} %bitcast.2.x, bf16[4,96,768]{2,1,0:T(8,128)(2,1)S(1)} %bitcast.60, bf16[4,96,768]{2,1,0:T(8,128)(2,1)S(1)} %collective-permute-done.above, bf16[3,96,768]{2,1,0:T(8,128)(2,1)} %collective-permute-done.2.opposite, bf16[1,96,768]{2,1,0:T(8,128)(2,1)S(1)} %collective-permute-done.5.rest, ...), custom_call_target="tpu_custom_call" | custom-call | tf_op jit(solution)/shard_map/pallas_call | solution.py:58
  58.7 0.0 collective-permute-done.6
  58.7 0.5 fusion.5
  59.3 0.0 copy-start.5
  59.3 2.1 %collective-permute-start.7 = (bf16[192,1024]{1,0:T(8,128)(2,1)S(1)}, bf16[192,1024]{1,0:T(8,128)(2,1)S(1)}, u32[]{:S(2)}, u32[]{:S(2)}) collective-permute-start(bf16[192,1024]{1,0:T(8,128)(2,1)S(1)} %fusion.5), channel_id=1, source_target_pairs={{0,64},{64,128},{128,192},{192,256},{256,320},{320,384},{384,448},... | collective-permute-start | bytes 1179656 | tf_op jit(solution)/shard_map/ppermute | solution.py:18
  61.4 0.0 collective-permute-done.10
  61.4 0.5 fusion.8
  61.9 3.8 %collective-permute-start.11 = (bf16[192,1024]{1,0:T(8,128)(2,1)S(1)}, bf16[192,1024]{1,0:T(8,128)(2,1)S(1)}, u32[]{:S(2)}, u32[]{:S(2)}) collective-permute-start(bf16[192,1024]{1,0:T(8,128)(2,1)S(1)} %fusion.8), channel_id=1, source_target_pairs={{0,448},{64,0},{128,64},{192,128},{256,192},{320,256},{384,320},{4... | collective-permute-start | bytes 1179656 | tf_op jit(solution)/shard_map/ppermute | solution.py:18
  65.8 1.7 %fusion = f32[192]{0:T(256)S(1)} fusion(bf16[192,3072]{1,0:T(8,128)(2,1)S(1)} %copy-done.5, bf16[192,3072]{1,0:T(8,128)(2,1)} %collective-permute-done.4, pred[]{:T(512)S(6)} %eq.50), kind=kLoop, calls=%fused_computation.2 | loop fusion | flops 2359104 | bytes 2360065 | tf_op jit(solution)/shard_map/reduce_sum | solution.py:195
  67.5 0.9 collective-permute-done.7
  68.4 0.5 fusion.4
  68.9 0.0 copy-start.6
  68.9 2.1 %collective-permute-start.8 = (bf16[192,1024]{1,0:T(8,128)(2,1)S(1)}, bf16[192,1024]{1,0:T(8,128)(2,1)S(1)}, u32[]{:S(2)}, u32[]{:S(2)}) collective-permute-start(bf16[192,1024]{1,0:T(8,128)(2,1)S(1)} %fusion.4), channel_id=1, source_target_pairs={{0,64},{64,128},{128,192},{192,256},{256,320},{320,384},{384,448},... | collective-permute-start | bytes 1179656 | tf_op jit(solution)/shard_map/ppermute | solution.py:18
  71.0 0.0 collective-permute-done.11
  71.0 0.5 fusion.7
  71.5 4.6 %collective-permute-start.12 = (bf16[192,1024]{1,0:T(8,128)(2,1)S(1)}, bf16[192,1024]{1,0:T(8,128)(2,1)S(1)}, u32[]{:S(2)}, u32[]{:S(2)}) collective-permute-start(bf16[192,1024]{1,0:T(8,128)(2,1)S(1)} %fusion.7), channel_id=1, source_target_pairs={{0,448},{64,0},{128,64},{192,128},{256,192},{320,256},{384,320},{4... | collective-permute-start | bytes 1179656 | tf_op jit(solution)/shard_map/ppermute | solution.py:18
  76.1 1.0 slice_select_fusion
  77.1 1.3 %collective-permute-start.15 = (bf16[192,768]{1,0:T(8,128)(2,1)S(1)}, bf16[192,768]{1,0:T(8,128)(2,1)S(1)}, u32[]{:S(2)}, u32[]{:S(2)}) collective-permute-start(bf16[192,768]{1,0:T(8,128)(2,1)S(1)} %slice_select_fusion), channel_id=1, source_target_pairs={{0,128},{448,320},{1,129},{449,321},{2,130},{450,322},{3,131},{451... | collective-permute-start | bytes 884744 | tf_op jit(solution)/shard_map/ppermute | solution.py:177
  78.4 0.4 collective-permute-done.8
  78.8 0.5 fusion.3
  79.3 1.9 %collective-permute-start.9 = (bf16[192,1024]{1,0:T(8,128)(2,1)S(1)}, bf16[192,1024]{1,0:T(8,128)(2,1)S(1)}, u32[]{:S(2)}, u32[]{:S(2)}) collective-permute-start(bf16[192,1024]{1,0:T(8,128)(2,1)S(1)} %fusion.3), channel_id=1, source_target_pairs={{0,64},{64,128},{128,192},{192,256},{256,320},{320,384},{384,448},... | collective-permute-start | bytes 1179656 | tf_op jit(solution)/shard_map/ppermute | solution.py:18
  81.2 0.0 collective-permute-done.12
  81.2 0.5 fusion.6
  81.7 0.0 copy-start.7
  81.8 4.6 %collective-permute-start.13 = (bf16[192,1024]{1,0:T(8,128)(2,1)S(1)}, bf16[192,1024]{1,0:T(8,128)(2,1)S(1)}, u32[]{:S(2)}, u32[]{:S(2)}) collective-permute-start(bf16[192,1024]{1,0:T(8,128)(2,1)S(1)} %fusion.6), channel_id=1, source_target_pairs={{0,448},{64,0},{128,64},{192,128},{256,192},{320,256},{384,320},{4... | collective-permute-start | bytes 1179656 | tf_op jit(solution)/shard_map/ppermute | solution.py:18
  86.3 7.9 %collective-permute-start.17 = (f32[192]{0:T(256)S(1)}, f32[192]{0:T(256)S(1)}, u32[]{:S(2)}, u32[]{:S(2)}) collective-permute-start(f32[192]{0:T(256)S(1)} %fusion), channel_id=1, source_target_pairs={{0,1},{1,0},{2,3},{3,2},{4,5},{5,4},{6,7},{7,6},{8,9},{9,8},{10,11... | collective-permute-start | bytes 2312 | tf_op jit(solution)/shard_map/ppermute | solution.py:18
  94.3 0.0 collective-permute-done.15
  94.3 1.0 fusion.29
  95.3 4.6 %collective-permute-start.16 = (bf16[192,384]{1,0:T(8,128)(2,1)S(1)}, bf16[192,384]{1,0:T(8,128)(2,1)S(1)}, u32[]{:S(2)}, u32[]{:S(2)}) collective-permute-start(bf16[192,384]{1,0:T(8,128)(2,1)S(1)} %get-tuple-element.25), channel_id=1, source_target_pairs={{0,64},{128,192},{448,384},{320,256},{1,65},{129,193},{449,385},{3... | collective-permute-start | bytes 442376 | tf_op jit(solution)/shard_map/ppermute | solution.py:188
  99.9 0.0 collective-permute-done.17
  100.0 0.0 collective-permute-done.9
  100.0 0.0 collective-permute-done.13
  100.0 0.3 convolution_add_fusion.6
  100.3 10.2 %collective-permute-start.14 = (bf16[192,512]{1,0:T(8,128)(2,1)S(1)}, bf16[192,512]{1,0:T(8,128)(2,1)S(1)}, u32[]{:S(2)}, u32[]{:S(2)}) collective-permute-start(bf16[192,512]{1,0:T(8,128)(2,1)S(1)} %convolution_add_fusion.6), channel_id=1, source_target_pairs={{0,2},{2,0},{1,3},{3,1},{4,6},{6,4},{5,7},{7,5},{8,10},{10,8},{9,1... | collective-permute-start | bytes 589832 | tf_op jit(solution)/shard_map/ppermute | solution.py:18
  110.5 2.8 %fusion.9 = bf16[1,192,3072]{2,1,0:T(8,128)(2,1)} fusion(f32[3072]{0:T(1024)S(1)} %bitcast.65, f32[192]{0:T(256)S(1)} %add_rsqrt_fusion, bf16[192,3072]{1,0:T(8,128)(2,1)S(1)} %copy-done.5, bf16[192,3072]{1,0:T(8,128)(2,1)} %collective-permute-done.4, pred[]{:T(512)S(6)} %eq.50), kind=kLoop, calls=%fused_computation.19 | loop fusion | flops 2949120 | bytes 3552001 | tf_op jit(solution)/shard_map/broadcast_in_dim | solution.py:206
  113.3 0.3 fusion.10.mine
  113.6 0.0 collective-permute-done.16.handed
  113.6 0.0 collective-permute-done.14.other
  113.7 0.8 copy-done.2
  114.4 1.3 %shard_map.97 = (bf16[512,384]{1,0:T(8,128)(2,1)}, f32[192,384]{1,0:T(8,128)}) custom-call(s32[1]{0:T(128)} %bitcast.core, s32[1]{0:T(128)} %bitcast.1.keeps, bf16[192,512]{1,0:T(8,128)(2,1)S(1)} %fusion.10.mine, bf16[192,512]{1,0:T(8,128)(2,1)S(1)} %collective-permute-done.14.other, f32[512,384]{1,0:T(8,128)S(1)} %copy-done.2, ...), custom_call_target="tpu_custom_call" | custom-call | tf_op jit(solution)/shard_map/pallas_call | solution.py:208
  (12 shorter events, 0.1 us)
Async XLA Ops:
  0.6 33.4 %copy-start = (bf16[512,768]{1,0:T(8,128)(2,1)S(1)}, bf16[512,768]{1,0:T(8,128)(2,1)}, u32[]{:S(2)}) copy-start(bf16[512,768]{1,0:T(8,128)(2,1)} %first.1) | copy-start | bytes 2359300
  0.6 45.1 %collective-permute-start.4 = (bf16[192,3072]{1,0:T(8,128)(2,1)}, bf16[192,3072]{1,0:T(8,128)(2,1)}, u32[]{:S(2)}, u32[]{:S(2)}) collective-permute-start(bf16[192,3072]{1,0:T(8,128)(2,1)} %bitcast.61), channel_id=1, source_target_pairs={{0,64},{64,128},{128,192},{192,256},{256,320},{320,384},{384,448},... | collective-permute-start | bytes 3538952 | tf_op jit(solution)/shard_map/ppermute | solution.py:18
  3.1 30.9 %collective-permute-start.1 = (bf16[512,768]{1,0:T(8,128)(2,1)}, bf16[512,768]{1,0:T(8,128)(2,1)S(1)}, u32[]{:S(2)}, u32[]{:S(2)}) collective-permute-start(bf16[512,768]{1,0:T(8,128)(2,1)} %first.1), channel_id=1, source_target_pairs={{0,2},{2,0},{1,3},{3,1},{4,6},{6,4},{5,7},{7,5},{8,10},{10,8},{9,1... | collective-permute-start | bytes 2359304 | tf_op jit(solution)/shard_map/ppermute | solution.py:18
  24.3 15.1 %collective-permute-start = (bf16[4,96,768]{2,1,0:T(8,128)(2,1)S(1)}, bf16[4,96,768]{2,1,0:T(8,128)(2,1)S(1)}, u32[]{:S(2)}, u32[]{:S(2)}) collective-permute-start(bf16[4,96,768]{2,1,0:T(8,128)(2,1)S(1)} %bitcast.57), channel_id=1, source_target_pairs={{0,12},{4,0},{8,4},{12,8},{1,13},{5,1},{9,5},{13,9},{2,14},{6,2},{... | collective-permute-start | bytes 1769480 | tf_op jit(solution)/shard_map/ppermute | solution.py:18
  28.7 17.1 %collective-permute-start.3 = (bf16[4,96,768]{2,1,0:T(8,128)(2,1)S(1)}, bf16[4,96,768]{2,1,0:T(8,128)(2,1)S(1)}, u32[]{:S(2)}, u32[]{:S(2)}) collective-permute-start(bf16[4,96,768]{2,1,0:T(8,128)(2,1)S(1)} %bitcast.58), channel_id=1, source_target_pairs={{0,4},{4,8},{8,12},{12,0},{1,5},{5,9},{9,13},{13,1},{2,6},{6,10},{... | collective-permute-start | bytes 1769480 | tf_op jit(solution)/shard_map/ppermute | solution.py:18
  30.6 1.0 copy-start.3
  31.6 0.7 copy-start.4
  33.1 0.9 copy-start.1
  40.2 12.2 %collective-permute-start.2 = (bf16[3,96,768]{2,1,0:T(8,128)(2,1)}, bf16[3,96,768]{2,1,0:T(8,128)(2,1)}, u32[]{:S(2)}, u32[]{:S(2)}) collective-permute-start(bf16[3,96,768]{2,1,0:T(8,128)(2,1)} %slice.50), channel_id=1, source_target_pairs={{0,12},{4,0},{8,4},{12,8},{1,13},{5,1},{9,5},{13,9},{2,14},{6,2},{... | collective-permute-start | bytes 1327112 | tf_op jit(solution)/shard_map/ppermute | solution.py:18
  45.8 7.1 %collective-permute-start.5 = (bf16[1,96,768]{2,1,0:T(8,128)(2,1)S(1)}, bf16[1,96,768]{2,1,0:T(8,128)(2,1)S(1)}, u32[]{:S(2)}, u32[]{:S(2)}) collective-permute-start(bf16[1,96,768]{2,1,0:T(8,128)(2,1)S(1)} %slice.51), channel_id=1, source_target_pairs={{0,4},{4,8},{8,12},{12,0},{1,5},{5,9},{9,13},{13,1},{2,6},{6,10},{... | collective-permute-start | bytes 442376 | tf_op jit(solution)/shard_map/ppermute | solution.py:18
  48.1 10.6 %collective-permute-start.6 = (bf16[96,1024]{1,0:T(8,128)(2,1)S(1)}, bf16[96,1024]{1,0:T(8,128)(2,1)S(1)}, u32[]{:S(2)}, u32[]{:S(2)}) collective-permute-start(bf16[96,1024]{1,0:T(8,128)(2,1)S(1)} %convolution_convert_fusion), channel_id=1, source_target_pairs={{0,64},{64,128},{128,192},{192,256},{256,320},{320,384},{384,448},... | collective-permute-start | bytes 589832 | tf_op jit(solution)/shard_map/ppermute | solution.py:18
  54.2 7.2 %collective-permute-start.10 = (bf16[96,1024]{1,0:T(8,128)(2,1)S(1)}, bf16[96,1024]{1,0:T(8,128)(2,1)S(1)}, u32[]{:S(2)}, u32[]{:S(2)}) collective-permute-start(bf16[96,1024]{1,0:T(8,128)(2,1)S(1)} %convolution_convert_fusion.1), channel_id=1, source_target_pairs={{0,448},{64,0},{128,64},{192,128},{256,192},{320,256},{384,320},{4... | collective-permute-start | bytes 589832 | tf_op jit(solution)/shard_map/ppermute | solution.py:18
  59.3 6.5 %copy-start.5 = (bf16[192,3072]{1,0:T(8,128)(2,1)S(1)}, bf16[192,3072]{1,0:T(8,128)(2,1)}, u32[]{:S(2)}) copy-start(bf16[192,3072]{1,0:T(8,128)(2,1)} %param.11) | copy-start | bytes 3538948
  59.3 9.1 %collective-permute-start.7 = (bf16[192,1024]{1,0:T(8,128)(2,1)S(1)}, bf16[192,1024]{1,0:T(8,128)(2,1)S(1)}, u32[]{:S(2)}, u32[]{:S(2)}) collective-permute-start(bf16[192,1024]{1,0:T(8,128)(2,1)S(1)} %fusion.5), channel_id=1, source_target_pairs={{0,64},{64,128},{128,192},{192,256},{256,320},{320,384},{384,448},... | collective-permute-start | bytes 1179656 | tf_op jit(solution)/shard_map/ppermute | solution.py:18
  61.9 9.1 %collective-permute-start.11 = (bf16[192,1024]{1,0:T(8,128)(2,1)S(1)}, bf16[192,1024]{1,0:T(8,128)(2,1)S(1)}, u32[]{:S(2)}, u32[]{:S(2)}) collective-permute-start(bf16[192,1024]{1,0:T(8,128)(2,1)S(1)} %fusion.8), channel_id=1, source_target_pairs={{0,448},{64,0},{128,64},{192,128},{256,192},{320,256},{384,320},{4... | collective-permute-start | bytes 1179656 | tf_op jit(solution)/shard_map/ppermute | solution.py:18
  68.9 7.2 %copy-start.6 = (bf16[1,192,3072]{2,1,0:T(8,128)(2,1)S(1)}, bf16[1,192,3072]{2,1,0:T(8,128)(2,1)}, u32[]{:S(2)}) copy-start(bf16[1,192,3072]{2,1,0:T(8,128)(2,1)} %param.10) | copy-start | bytes 3538948
  68.9 9.9 %collective-permute-start.8 = (bf16[192,1024]{1,0:T(8,128)(2,1)S(1)}, bf16[192,1024]{1,0:T(8,128)(2,1)S(1)}, u32[]{:S(2)}, u32[]{:S(2)}) collective-permute-start(bf16[192,1024]{1,0:T(8,128)(2,1)S(1)} %fusion.4), channel_id=1, source_target_pairs={{0,64},{64,128},{128,192},{192,256},{256,320},{320,384},{384,448},... | collective-permute-start | bytes 1179656 | tf_op jit(solution)/shard_map/ppermute | solution.py:18
  71.5 9.7 %collective-permute-start.12 = (bf16[192,1024]{1,0:T(8,128)(2,1)S(1)}, bf16[192,1024]{1,0:T(8,128)(2,1)S(1)}, u32[]{:S(2)}, u32[]{:S(2)}) collective-permute-start(bf16[192,1024]{1,0:T(8,128)(2,1)S(1)} %fusion.7), channel_id=1, source_target_pairs={{0,448},{64,0},{128,64},{192,128},{256,192},{320,256},{384,320},{4... | collective-permute-start | bytes 1179656 | tf_op jit(solution)/shard_map/ppermute | solution.py:18
  77.1 17.2 %collective-permute-start.15 = (bf16[192,768]{1,0:T(8,128)(2,1)S(1)}, bf16[192,768]{1,0:T(8,128)(2,1)S(1)}, u32[]{:S(2)}, u32[]{:S(2)}) collective-permute-start(bf16[192,768]{1,0:T(8,128)(2,1)S(1)} %slice_select_fusion), channel_id=1, source_target_pairs={{0,128},{448,320},{1,129},{449,321},{2,130},{450,322},{3,131},{451... | collective-permute-start | bytes 884744 | tf_op jit(solution)/shard_map/ppermute | solution.py:177
  79.3 20.7 %collective-permute-start.9 = (bf16[192,1024]{1,0:T(8,128)(2,1)S(1)}, bf16[192,1024]{1,0:T(8,128)(2,1)S(1)}, u32[]{:S(2)}, u32[]{:S(2)}) collective-permute-start(bf16[192,1024]{1,0:T(8,128)(2,1)S(1)} %fusion.3), channel_id=1, source_target_pairs={{0,64},{64,128},{128,192},{192,256},{256,320},{320,384},{384,448},... | collective-permute-start | bytes 1179656 | tf_op jit(solution)/shard_map/ppermute | solution.py:18
  81.7 28.8 %copy-start.7 = (f32[1,3072]{1,0:T(1,128)S(1)}, f32[1,3072]{1,0:T(1,128)}, u32[]{:S(2)}) copy-start(f32[1,3072]{1,0:T(1,128)} %param.12) | copy-start | bytes 36868
  81.8 18.2 %collective-permute-start.13 = (bf16[192,1024]{1,0:T(8,128)(2,1)S(1)}, bf16[192,1024]{1,0:T(8,128)(2,1)S(1)}, u32[]{:S(2)}, u32[]{:S(2)}) collective-permute-start(bf16[192,1024]{1,0:T(8,128)(2,1)S(1)} %fusion.6), channel_id=1, source_target_pairs={{0,448},{64,0},{128,64},{192,128},{256,192},{320,256},{384,320},{4... | collective-permute-start | bytes 1179656 | tf_op jit(solution)/shard_map/ppermute | solution.py:18
  86.3 13.6 %collective-permute-start.17 = (f32[192]{0:T(256)S(1)}, f32[192]{0:T(256)S(1)}, u32[]{:S(2)}, u32[]{:S(2)}) collective-permute-start(f32[192]{0:T(256)S(1)} %fusion), channel_id=1, source_target_pairs={{0,1},{1,0},{2,3},{3,2},{4,5},{5,4},{6,7},{7,6},{8,9},{9,8},{10,11... | collective-permute-start | bytes 2312 | tf_op jit(solution)/shard_map/ppermute | solution.py:18
  95.3 18.3 %collective-permute-start.16 = (bf16[192,384]{1,0:T(8,128)(2,1)S(1)}, bf16[192,384]{1,0:T(8,128)(2,1)S(1)}, u32[]{:S(2)}, u32[]{:S(2)}) collective-permute-start(bf16[192,384]{1,0:T(8,128)(2,1)S(1)} %get-tuple-element.25), channel_id=1, source_target_pairs={{0,64},{128,192},{448,384},{320,256},{1,65},{129,193},{449,385},{3... | collective-permute-start | bytes 442376 | tf_op jit(solution)/shard_map/ppermute | solution.py:188
  100.3 13.3 %collective-permute-start.14 = (bf16[192,512]{1,0:T(8,128)(2,1)S(1)}, bf16[192,512]{1,0:T(8,128)(2,1)S(1)}, u32[]{:S(2)}, u32[]{:S(2)}) collective-permute-start(bf16[192,512]{1,0:T(8,128)(2,1)S(1)} %convolution_add_fusion.6), channel_id=1, source_target_pairs={{0,2},{2,0},{1,3},{3,1},{4,6},{6,4},{5,7},{7,5},{8,10},{10,8},{9,1... | collective-permute-start | bytes 589832 | tf_op jit(solution)/shard_map/ppermute | solution.py:18
  113.3 1.1 copy-start.2

commit v9 on v8

--- a/solution.py
+++ b/solution.py
@@ -120,7 +120,12 @@
         compiler_params=pltpu.CompilerParams(vmem_limit_bytes=8 << 20),
         cost_estimate=pl.CostEstimate(flops=0, bytes_accessed=8 << 20, transcendentals=0),
     )(mask_blocks, previous)
-    above = tied(above, both, old)
+    last = sections - 1
+    cut = lambda value, s, count=1: value[:, s * width:(s + count) * width]
+    arrived = incoming
+    given = jnp.where(position == 0, cut(arrived, 2, 2), cut(act, last - 3, 2))
+    passed = lax.ppermute(given, "section", [(0, 2), (last, last - 2)])
+    above = tied(above, both, old, given)
     below, incoming = lax.optimization_barrier((below, incoming))
     opposite = around(above[:LATE], "x", -1)
     opposite_rest = around(below[LATE:], "x", 1)
@@ -137,7 +142,7 @@
     def down(value):
         return around(value.astype(bf16), "section", -1)
 
-    dest = (position + far) % sections
+    dest = tied((position + far) % sections, passed)
     plane = lambda part: lax.dynamic_index_in_dim(part, dest // 2, 0, keepdims=False)
     near = jnp.where(x % 2 == 0, plane(below), plane(above))
     begun = product(jnp.where(dest % 2 == x // 2, plane(held), near)).astype(bf16)
@@ -170,15 +175,7 @@
     sent = round_of(3, ())
     rising, falling = up(sent[0]), down(sent[1])
 
-    last = sections - 1
-    cut = lambda value, s, count=1: value[:, s * width:(s + count) * width]
-    arrived = incoming
-    given = tied(jnp.where(position == 0, cut(arrived, 2, 2), cut(act, last - 3, 2)), *sent)
-    passed = lax.ppermute(given, "section", [(0, 2), (last, last - 2)])
     sent = round_of(2, ())
-    rising, falling = up(sent[0]), down(sent[1])
-
-    sent = round_of(1, ())
     rising, falling = up(sent[0]), down(sent[1])
 
     ends = (position == 0) | (position == last)
@@ -190,6 +187,9 @@
     )
     kept = jnp.where(first, cut(arrived, 0), jnp.where(ends, cut(act, last), jnp.where(low, cut(passed, 0), cut(passed, 1))))
     keeps = ends | (position == 2) | (position == last - 2)
+    sent = round_of(1, (handed,))
+    rising, falling = up(sent[0]), down(sent[1])
+
     current = jnp.where(position == 0, fresh_batch, incoming)
     wide = current.astype(f32)
     own = tied(jnp.sum(wide * wide, axis=-1), *sent)

time: 117 us -> 121 us (1.034)
  the two profiles are of different devices: /device:TPU:41 before, /device:TPU:1 now
where the time goes in v9:
time: 121 us; the launch traced here: 120 us
  starting transfers between devices  73.8 us (61%)
  blocking collectives  14.3 us (12%)
  matrix products  10.3 us (9%)
  waiting for transfers between devices  6.63 us (5%)
  other arithmetic  5.91 us (5%)
  Pallas kernels  4.89 us (4%)
  local copies, waits for them, and re-layouts  3.03 us (3%)
  between operations  1.32 us (1%)
    ppermute x16, starting transfers between devices, around(): lax.ppermute(value, axis, [(i, (i + steps) % count) for i in range(count)])  67.7 us
    all_gather x1, blocking collectives, on_device(): held = lax.all_gather(out_weight.T, 'zlo', axis=0, tiled=False)  14.3 us
    dot_general x8, matrix products, product(): return jnp.dot(weight, both, preferred_element_type=f32)  7.38 us
    ppermute x16, waiting for transfers between devices, around(): lax.ppermute(value, axis, [(i, (i + steps) % count) for i in range(count)])  6.62 us
    ppermute x1, starting transfers between devices, on_device(): passed = lax.ppermute(given, 'section', [(0, 2), (last, last - 2)])  4.83 us
    dot_general x2, matrix products, on_device(): jnp.dot(own_weight, both[:, part], preferred_element_type=f32)  2.96 us
  transfers between devices with their start and end apart: 18, of which 3 were waited for; matrix products, arithmetic and copies ran while one was open for 14% of the time, Pallas kernels for 3%

profile of v9, /device:TPU:1, one launch (start us, length us, event | category | flops | bytes accessed | tf_op | source)
XLA Modules:
  0.0 120.2 jit_solution(4534612487089757497)
XLA Ops:
  0.6 0.0 copy-start.7
  0.6 0.0 copy-start.4
  0.7 4.2 %collective-permute-start.2 = (bf16[192,3072]{1,0:T(8,128)(2,1)}, bf16[192,3072]{1,0:T(8,128)(2,1)}, u32[]{:S(2)}, u32[]{:S(2)}) collective-permute-start(bf16[192,3072]{1,0:T(8,128)(2,1)} %bitcast.61), channel_id=1, source_target_pairs={{0,64},{64,128},{128,192},{192,256},{256,320},{320,384},{384,448},... | collective-permute-start | bytes 3538952 | tf_op jit(solution)/shard_map/ppermute | solution.py:18
  4.8 6.7 %collective-permute-start.1 = (bf16[512,768]{1,0:T(8,128)(2,1)}, bf16[512,768]{1,0:T(8,128)(2,1)}, u32[]{:S(2)}, u32[]{:S(2)}) collective-permute-start(bf16[512,768]{1,0:T(8,128)(2,1)} %first.1), channel_id=1, source_target_pairs={{0,2},{2,0},{1,3},{3,1},{4,6},{6,4},{5,7},{7,5},{8,10},{10,8},{9,1... | collective-permute-start | bytes 2359304 | tf_op jit(solution)/shard_map/ppermute | solution.py:18
  11.5 14.3 %all-gather = bf16[384,768]{1,0:T(8,128)(2,1)S(1)} all-gather(bf16[96,768]{1,0:T(8,128)(2,1)} %bitcast.64), channel_id=2, replica_groups=mesh['section'=8,'zlo'=4,'x'=4,'core'=2,'tensor'=2] {'zlo'}, dimensions={0}, use_global_device_ids=true | all-gather | bytes 737280 | tf_op jit(solution)/shard_map/all_gather | solution.py:104
  25.8 4.7 %collective-permute-start = (bf16[4,96,768]{2,1,0:T(8,128)(2,1)S(1)}, bf16[4,96,768]{2,1,0:T(8,128)(2,1)S(1)}, u32[]{:S(2)}, u32[]{:S(2)}) collective-permute-start(bf16[4,96,768]{2,1,0:T(8,128)(2,1)S(1)} %bitcast.57), channel_id=1, source_target_pairs={{0,12},{4,0},{8,4},{12,8},{1,13},{5,1},{9,5},{13,9},{2,14},{6,2},{... | collective-permute-start | bytes 1769480 | tf_op jit(solution)/shard_map/ppermute | solution.py:18
  30.5 1.9 %collective-permute-start.5 = (bf16[4,96,768]{2,1,0:T(8,128)(2,1)S(1)}, bf16[4,96,768]{2,1,0:T(8,128)(2,1)S(1)}, u32[]{:S(2)}, u32[]{:S(2)}) collective-permute-start(bf16[4,96,768]{2,1,0:T(8,128)(2,1)S(1)} %bitcast.58), channel_id=1, source_target_pairs={{0,4},{4,8},{8,12},{12,0},{1,5},{5,9},{9,13},{13,1},{2,6},{6,10},{... | collective-permute-start | bytes 1769480 | tf_op jit(solution)/shard_map/ppermute | solution.py:18
  32.5 0.0 copy-start.1
  32.5 0.0 collective-permute-done.2
  32.5 1.9 %slice_select_fusion = bf16[192,768]{1,0:T(8,128)(2,1)} fusion(bf16[192,3072]{1,0:T(8,128)(2,1)} %bitcast.62, bf16[192,3072]{1,0:T(8,128)(2,1)} %collective-permute-done.2, pred[]{:T(512)S(6)} %eq.50), kind=kLoop, calls=%fused_computation.26 | loop fusion | flops 147456 | bytes 884737 | tf_op jit(solution)/shard_map/jit(_where)/select_n | solution.py:126
  34.4 4.8 %collective-permute-start.4 = (bf16[192,768]{1,0:T(8,128)(2,1)}, bf16[192,768]{1,0:T(8,128)(2,1)}, u32[]{:S(2)}, u32[]{:S(2)}) collective-permute-start(bf16[192,768]{1,0:T(8,128)(2,1)} %slice_select_fusion), channel_id=1, source_target_pairs={{0,128},{448,320},{1,129},{449,321},{2,130},{450,322},{3,131},{451... | collective-permute-start | bytes 884744 | tf_op jit(solution)/shard_map/ppermute | solution.py:127
  39.2 0.0 copy-done.4
  39.2 0.8 shard_map.95
  40.0 0.0 copy-start.2
  40.0 0.9 copy-done.2
  40.9 0.7 copy-done.5
  41.6 0.0 collective-permute-done.1.second
  41.6 1.6 %shard_map.94 = bf16[768,1024]{1,0:T(8,128)(2,1)S(1)} custom-call(bf16[512,768]{1,0:T(8,128)(2,1)S(1)} %copy-done.1, bf16[512,768]{1,0:T(8,128)(2,1)} %collective-permute-done.1.second), custom_call_target="tpu_custom_call" | custom-call | tf_op jit(solution)/shard_map/pallas_call | solution.py:41
  43.2 0.0 collective-permute-done.above
  43.2 0.8 slice.52
  44.0 4.6 %collective-permute-start.3 = (bf16[3,96,768]{2,1,0:T(8,128)(2,1)}, bf16[3,96,768]{2,1,0:T(8,128)(2,1)}, u32[]{:S(2)}, u32[]{:S(2)}) collective-permute-start(bf16[3,96,768]{2,1,0:T(8,128)(2,1)} %slice.52), channel_id=1, source_target_pairs={{0,12},{4,0},{8,4},{12,8},{1,13},{5,1},{9,5},{13,9},{2,14},{6,2},{... | collective-permute-start | bytes 1327112 | tf_op jit(solution)/shard_map/ppermute | solution.py:18
  48.7 0.0 collective-permute-done.5.below
  48.7 0.7 slice.53
  49.4 1.9 %collective-permute-start.6 = (bf16[1,96,768]{2,1,0:T(8,128)(2,1)}, bf16[1,96,768]{2,1,0:T(8,128)(2,1)S(1)}, u32[]{:S(2)}, u32[]{:S(2)}) collective-permute-start(bf16[1,96,768]{2,1,0:T(8,128)(2,1)} %slice.53), channel_id=1, source_target_pairs={{0,4},{4,8},{8,12},{12,0},{1,5},{5,9},{9,13},{13,1},{2,6},{6,10},{... | collective-permute-start | bytes 442376 | tf_op jit(solution)/shard_map/ppermute | solution.py:18
  51.3 0.0 collective-permute-done.4
  51.4 0.4 convolution_convert_fusion
  51.8 1.9 %collective-permute-start.8 = (bf16[96,1024]{1,0:T(8,128)(2,1)S(1)}, bf16[96,1024]{1,0:T(8,128)(2,1)S(1)}, u32[]{:S(2)}, u32[]{:S(2)}) collective-permute-start(bf16[96,1024]{1,0:T(8,128)(2,1)S(1)} %convolution_convert_fusion), channel_id=1, source_target_pairs={{0,64},{64,128},{128,192},{192,256},{256,320},{320,384},{384,448},... | collective-permute-start | bytes 589832 | tf_op jit(solution)/shard_map/ppermute | solution.py:18
  53.7 3.0 %collective-permute-done.6.rest = bf16[1,96,768]{2,1,0:T(8,128)(2,1)S(1)} collective-permute-done((bf16[1,96,768]{2,1,0:T(8,128)(2,1)}, bf16[1,96,768]{2,1,0:T(8,128)(2,1)S(1)}, u32[]{:S(2)}, u32[]{:S(2)}) %collective-permute-start.6) | collective-permute-done | bytes 147488 | tf_op jit(solution)/shard_map/ppermute | solution.py:18
  56.7 0.0 collective-permute-done.3.opposite
  56.7 1.3 %convolution_convert_fusion.1 = bf16[96,1024]{1,0:T(8,128)(2,1)S(1)} fusion(bf16[768,1024]{1,0:T(8,128)(2,1)S(1)} %shard_map.94, bf16[1,96,768]{2,1,0:T(8,128)(2,1)S(1)} %collective-permute-done.6.rest, bf16[3,96,768]{2,1,0:T(8,128)(2,1)} %collective-permute-done.3.opposite, s32[]{:T(128)S(6)} %select_n.236, pred[]{:T(512)S(6)} %lt.108, pred[]{:T(512)S(6)} %eq.55, ...), kind=kOutput, calls=%fused_computation.23 | convolution fusion | flops 151314432 | bytes 2359307 | tf_op jit(solution)/shard_map/dot_general | solution.py:134
  58.0 3.7 %collective-permute-start.12 = (bf16[96,1024]{1,0:T(8,128)(2,1)S(1)}, bf16[96,1024]{1,0:T(8,128)(2,1)S(1)}, u32[]{:S(2)}, u32[]{:S(2)}) collective-permute-start(bf16[96,1024]{1,0:T(8,128)(2,1)S(1)} %convolution_convert_fusion.1), channel_id=1, source_target_pairs={{0,448},{64,0},{128,64},{192,128},{256,192},{320,256},{384,320},{4... | collective-permute-start | bytes 589832 | tf_op jit(solution)/shard_map/ppermute | solution.py:18
  61.8 1.2 shard_map.96
  63.0 0.0 collective-permute-done.8
  63.0 0.5 fusion.5
  63.5 1.9 %collective-permute-start.9 = (bf16[192,1024]{1,0:T(8,128)(2,1)S(1)}, bf16[192,1024]{1,0:T(8,128)(2,1)S(1)}, u32[]{:S(2)}, u32[]{:S(2)}) collective-permute-start(bf16[192,1024]{1,0:T(8,128)(2,1)S(1)} %fusion.5), channel_id=1, source_target_pairs={{0,64},{64,128},{128,192},{192,256},{256,320},{320,384},{384,448},... | collective-permute-start | bytes 1179656 | tf_op jit(solution)/shard_map/ppermute | solution.py:18
  65.4 0.0 collective-permute-done.12
  65.5 0.5 fusion.8
  66.0 4.6 %collective-permute-start.13 = (bf16[192,1024]{1,0:T(8,128)(2,1)S(1)}, bf16[192,1024]{1,0:T(8,128)(2,1)S(1)}, u32[]{:S(2)}, u32[]{:S(2)}) collective-permute-start(bf16[192,1024]{1,0:T(8,128)(2,1)S(1)} %fusion.8), channel_id=1, source_target_pairs={{0,448},{64,0},{128,64},{192,128},{256,192},{320,256},{384,320},{4... | collective-permute-start | bytes 1179656 | tf_op jit(solution)/shard_map/ppermute | solution.py:18
  70.5 2.0 %fusion.29 = (bf16[192,384]{1,0:T(8,128)(2,1)S(1)}, bf16[192,384]{1,0:T(8,128)(2,1)}) fusion(bf16[192,3072]{1,0:T(8,128)(2,1)} %bitcast.63, bf16[192,3072]{1,0:T(8,128)(2,1)} %collective-permute-done.2, pred[]{:T(512)S(6)} %lt.111, pred[]{:T(512)S(6)} %or.9, pred[]{:T(512)S(6)} %eq.50, bf16[192,768]{1,0:T(8,128)(2,1)} %collective-permute-done.4), kind=kLoop, calls=%fused_computation.48 | loop fusion | flops 442368 | bytes 1179651 | tf_op jit(solution)/shard_map/jit(_where)/select_n | solution.py:188
  72.5 1.3 %collective-permute-start.7 = (bf16[192,384]{1,0:T(8,128)(2,1)}, bf16[192,384]{1,0:T(8,128)(2,1)S(1)}, u32[]{:S(2)}, u32[]{:S(2)}) collective-permute-start(bf16[192,384]{1,0:T(8,128)(2,1)} %get-tuple-element.28), channel_id=1, source_target_pairs={{0,64},{128,192},{448,384},{320,256},{1,65},{129,193},{449,385},{3... | collective-permute-start | bytes 442376 | tf_op jit(solution)/shard_map/ppermute | solution.py:185
  73.8 0.0 collective-permute-done.9
  73.8 0.5 fusion.4
  74.3 1.9 %collective-permute-start.10 = (bf16[192,1024]{1,0:T(8,128)(2,1)S(1)}, bf16[192,1024]{1,0:T(8,128)(2,1)S(1)}, u32[]{:S(2)}, u32[]{:S(2)}) collective-permute-start(bf16[192,1024]{1,0:T(8,128)(2,1)S(1)} %fusion.4), channel_id=1, source_target_pairs={{0,64},{64,128},{128,192},{192,256},{256,320},{320,384},{384,448},... | collective-permute-start | bytes 1179656 | tf_op jit(solution)/shard_map/ppermute | solution.py:18
  76.2 0.0 collective-permute-done.13
  76.3 0.5 fusion.7
  76.8 4.6 %collective-permute-start.14 = (bf16[192,1024]{1,0:T(8,128)(2,1)S(1)}, bf16[192,1024]{1,0:T(8,128)(2,1)}, u32[]{:S(2)}, u32[]{:S(2)}) collective-permute-start(bf16[192,1024]{1,0:T(8,128)(2,1)S(1)} %fusion.7), channel_id=1, source_target_pairs={{0,448},{64,0},{128,64},{192,128},{256,192},{320,256},{384,320},{4... | collective-permute-start | bytes 1179656 | tf_op jit(solution)/shard_map/ppermute | solution.py:18
  81.3 0.0 collective-permute-done.7.handed
  81.4 2.7 %collective-permute-done.10 = bf16[192,1024]{1,0:T(8,128)(2,1)S(1)} collective-permute-done((bf16[192,1024]{1,0:T(8,128)(2,1)S(1)}, bf16[192,1024]{1,0:T(8,128)(2,1)S(1)}, u32[]{:S(2)}, u32[]{:S(2)}) %collective-permute-start.10) | collective-permute-done | bytes 393248 | tf_op jit(solution)/shard_map/ppermute | solution.py:18
  84.0 2.2 %fusion.3 = bf16[192,1024]{1,0:T(8,128)(2,1)} fusion(bf16[768,1024]{1,0:T(8,128)(2,1)S(1)} %shard_map.94, bf16[192,1024]{1,0:T(8,128)(2,1)S(1)} %collective-permute-done.10, bf16[8,192,768]{2,1,0:T(8,128)(2,1)} %bitcast.53, s32[]{:T(128)S(6)} %select_n.249), kind=kOutput, calls=%fused_computation.11 | convolution fusion | flops 302579712 | bytes 2654212 | tf_op jit(solution)/shard_map/dot_general | solution.py:134
  86.2 2.3 %collective-permute-start.11 = (bf16[192,1024]{1,0:T(8,128)(2,1)}, bf16[192,1024]{1,0:T(8,128)(2,1)}, u32[]{:S(2)}, u32[]{:S(2)}) collective-permute-start(bf16[192,1024]{1,0:T(8,128)(2,1)} %fusion.3), channel_id=1, source_target_pairs={{0,64},{64,128},{128,192},{192,256},{256,320},{320,384},{384,448},... | collective-permute-start | bytes 1179656 | tf_op jit(solution)/shard_map/ppermute | solution.py:18
  88.5 0.0 collective-permute-done.14
  88.6 1.6 %fusion.6 = bf16[192,1024]{1,0:T(8,128)(2,1)S(1)} fusion(bf16[768,1024]{1,0:T(8,128)(2,1)S(1)} %shard_map.94, bf16[192,1024]{1,0:T(8,128)(2,1)} %collective-permute-done.14, bf16[8,192,768]{2,1,0:T(8,128)(2,1)} %bitcast.54, s32[]{:T(128)S(6)} %select_n.263), kind=kOutput, calls=%fused_computation.14 | convolution fusion | flops 302579712 | bytes 2654212 | tf_op jit(solution)/shard_map/dot_general | solution.py:134
  90.1 4.3 %collective-permute-start.15 = (bf16[192,1024]{1,0:T(8,128)(2,1)S(1)}, bf16[192,1024]{1,0:T(8,128)(2,1)}, u32[]{:S(2)}, u32[]{:S(2)}) collective-permute-start(bf16[192,1024]{1,0:T(8,128)(2,1)S(1)} %fusion.6), channel_id=1, source_target_pairs={{0,448},{64,0},{128,64},{192,128},{256,192},{320,256},{384,320},{4... | collective-permute-start | bytes 1179656 | tf_op jit(solution)/shard_map/ppermute | solution.py:18
  94.5 0.5 fusion
  95.0 9.7 %collective-permute-start.17 = (f32[192]{0:T(256)S(1)}, f32[192]{0:T(256)S(1)}, u32[]{:S(2)}, u32[]{:S(2)}) collective-permute-start(f32[192]{0:T(256)S(1)} %fusion), channel_id=1, source_target_pairs={{0,1},{1,0},{2,3},{3,2},{4,5},{5,4},{6,7},{7,6},{8,9},{9,8},{10,11... | collective-permute-start | bytes 2312 | tf_op jit(solution)/shard_map/ppermute | solution.py:18
  104.7 0.9 collective-permute-done.17
  105.6 0.0 collective-permute-done.11
  105.6 0.0 collective-permute-done.15
  105.6 1.4 %convolution_add_fusion.6 = bf16[192,512]{1,0:T(8,128)(2,1)S(1)} fusion(bf16[768,1024]{1,0:T(8,128)(2,1)S(1)} %shard_map.94, bf16[8,192,768]{2,1,0:T(8,128)(2,1)} %bitcast.55, s32[]{:T(128)S(6)} %select_n.241, bf16[192,1024]{1,0:T(8,128)(2,1)} %collective-permute-done.15, bf16[192,1024]{1,0:T(8,128)(2,1)} %collective-permute-done.11), kind=kOutput, calls=%fused_computation.17 | convolution fusion | flops 151486464 | bytes 1671172 | tf_op jit(solution)/shard_map/dot_general | solution.py:201
  107.1 8.8 %collective-permute-start.16 = (bf16[192,512]{1,0:T(8,128)(2,1)S(1)}, bf16[192,512]{1,0:T(8,128)(2,1)S(1)}, u32[]{:S(2)}, u32[]{:S(2)}) collective-permute-start(bf16[192,512]{1,0:T(8,128)(2,1)S(1)} %convolution_add_fusion.6), channel_id=1, source_target_pairs={{0,2},{2,0},{1,3},{3,1},{4,6},{6,4},{5,7},{7,5},{8,10},{10,8},{9,1... | collective-permute-start | bytes 589832 | tf_op jit(solution)/shard_map/ppermute | solution.py:18
  115.9 1.5 %fusion.9 = bf16[1,192,3072]{2,1,0:T(8,128)(2,1)} fusion(f32[3072]{0:T(1024)S(1)} %bitcast.65, f32[192]{0:T(256)S(1)} %add_rsqrt_fusion, bf16[192,3072]{1,0:T(8,128)(2,1)S(1)} %copy-done.8, bf16[192,3072]{1,0:T(8,128)(2,1)} %collective-permute-done.2, pred[]{:T(512)S(6)} %eq.50), kind=kLoop, calls=%fused_computation.19 | loop fusion | flops 2949120 | bytes 3552001 | tf_op jit(solution)/shard_map/broadcast_in_dim | solution.py:206
  117.4 1.5 %fusion.10.mine = bf16[192,512]{1,0:T(8,128)(2,1)S(1)} fusion(bf16[768,1024]{1,0:T(8,128)(2,1)S(1)} %shard_map.94, bf16[8,192,768]{2,1,0:T(8,128)(2,1)} %bitcast.56, s32[]{:T(128)S(6)} %select_n.241, bf16[192,1024]{1,0:T(8,128)(2,1)} %collective-permute-done.15, bf16[192,1024]{1,0:T(8,128)(2,1)} %collective-permute-done.11), kind=kOutput, calls=%fused_computation.21 | convolution fusion | flops 151486464 | bytes 1671172 | tf_op jit(solution)/shard_map/dot_general | solution.py:201
  118.9 0.0 collective-permute-done.16.other
  118.9 1.3 %shard_map.97 = (bf16[512,384]{1,0:T(8,128)(2,1)}, f32[192,384]{1,0:T(8,128)}) custom-call(s32[1]{0:T(128)} %bitcast.core, s32[1]{0:T(128)} %bitcast.1.keeps, bf16[192,512]{1,0:T(8,128)(2,1)S(1)} %fusion.10.mine, bf16[192,512]{1,0:T(8,128)(2,1)S(1)} %collective-permute-done.16.other, f32[512,384]{1,0:T(8,128)S(1)} %copy-done.3, ...), custom_call_target="tpu_custom_call" | custom-call | tf_op jit(solution)/shard_map/pallas_call | solution.py:208
  (16 shorter events, 0.1 us)
Async XLA Ops:
  0.6 38.6 %copy-start.7 = (s32[1,12]{1,0:T(1,128)S(1)}, s32[1,12]{1,0:T(1,128)}, u32[]{:S(2)}) copy-start(s32[1,12]{1,0:T(1,128)} %blocks.1) | copy-start | bytes 148
  0.6 38.6 %copy-start.4 = (bf16[512,384]{1,0:T(8,128)(2,1)S(1)}, bf16[512,384]{1,0:T(8,128)(2,1)}, u32[]{:S(2)}) copy-start(bf16[512,384]{1,0:T(8,128)(2,1)} %previous.1) | copy-start | bytes 1179652
  0.7 31.8 %collective-permute-start.2 = (bf16[192,3072]{1,0:T(8,128)(2,1)}, bf16[192,3072]{1,0:T(8,128)(2,1)}, u32[]{:S(2)}, u32[]{:S(2)}) collective-permute-start(bf16[192,3072]{1,0:T(8,128)(2,1)} %bitcast.61), channel_id=1, source_target_pairs={{0,64},{64,128},{128,192},{192,256},{256,320},{320,384},{384,448},... | collective-permute-start | bytes 3538952 | tf_op jit(solution)/shard_map/ppermute | solution.py:18
  4.8 36.7 %collective-permute-start.1 = (bf16[512,768]{1,0:T(8,128)(2,1)}, bf16[512,768]{1,0:T(8,128)(2,1)}, u32[]{:S(2)}, u32[]{:S(2)}) collective-permute-start(bf16[512,768]{1,0:T(8,128)(2,1)} %first.1), channel_id=1, source_target_pairs={{0,2},{2,0},{1,3},{3,1},{4,6},{6,4},{5,7},{7,5},{8,10},{10,8},{9,1... | collective-permute-start | bytes 2359304 | tf_op jit(solution)/shard_map/ppermute | solution.py:18
  25.8 17.4 %collective-permute-start = (bf16[4,96,768]{2,1,0:T(8,128)(2,1)S(1)}, bf16[4,96,768]{2,1,0:T(8,128)(2,1)S(1)}, u32[]{:S(2)}, u32[]{:S(2)}) collective-permute-start(bf16[4,96,768]{2,1,0:T(8,128)(2,1)S(1)} %bitcast.57), channel_id=1, source_target_pairs={{0,12},{4,0},{8,4},{12,8},{1,13},{5,1},{9,5},{13,9},{2,14},{6,2},{... | collective-permute-start | bytes 1769480 | tf_op jit(solution)/shard_map/ppermute | solution.py:18
  30.5 18.2 %collective-permute-start.5 = (bf16[4,96,768]{2,1,0:T(8,128)(2,1)S(1)}, bf16[4,96,768]{2,1,0:T(8,128)(2,1)S(1)}, u32[]{:S(2)}, u32[]{:S(2)}) collective-permute-start(bf16[4,96,768]{2,1,0:T(8,128)(2,1)S(1)} %bitcast.58), channel_id=1, source_target_pairs={{0,4},{4,8},{8,12},{12,0},{1,5},{5,9},{9,13},{13,1},{2,6},{6,10},{... | collective-permute-start | bytes 1769480 | tf_op jit(solution)/shard_map/ppermute | solution.py:18
  32.5 9.1 %copy-start.1 = (bf16[512,768]{1,0:T(8,128)(2,1)S(1)}, bf16[512,768]{1,0:T(8,128)(2,1)}, u32[]{:S(2)}) copy-start(bf16[512,768]{1,0:T(8,128)(2,1)} %first.1) | copy-start | bytes 2359300
  34.4 17.0 %collective-permute-start.4 = (bf16[192,768]{1,0:T(8,128)(2,1)}, bf16[192,768]{1,0:T(8,128)(2,1)}, u32[]{:S(2)}, u32[]{:S(2)}) collective-permute-start(bf16[192,768]{1,0:T(8,128)(2,1)} %slice_select_fusion), channel_id=1, source_target_pairs={{0,128},{448,320},{1,129},{449,321},{2,130},{450,322},{3,131},{451... | collective-permute-start | bytes 884744 | tf_op jit(solution)/shard_map/ppermute | solution.py:127
  40.0 0.9 copy-start.2
  40.9 0.7 copy-start.5
  44.0 12.7 %collective-permute-start.3 = (bf16[3,96,768]{2,1,0:T(8,128)(2,1)}, bf16[3,96,768]{2,1,0:T(8,128)(2,1)}, u32[]{:S(2)}, u32[]{:S(2)}) collective-permute-start(bf16[3,96,768]{2,1,0:T(8,128)(2,1)} %slice.52), channel_id=1, source_target_pairs={{0,12},{4,0},{8,4},{12,8},{1,13},{5,1},{9,5},{13,9},{2,14},{6,2},{... | collective-permute-start | bytes 1327112 | tf_op jit(solution)/shard_map/ppermute | solution.py:18
  49.4 7.3 %collective-permute-start.6 = (bf16[1,96,768]{2,1,0:T(8,128)(2,1)}, bf16[1,96,768]{2,1,0:T(8,128)(2,1)S(1)}, u32[]{:S(2)}, u32[]{:S(2)}) collective-permute-start(bf16[1,96,768]{2,1,0:T(8,128)(2,1)} %slice.53), channel_id=1, source_target_pairs={{0,4},{4,8},{8,12},{12,0},{1,5},{5,9},{9,13},{13,1},{2,6},{6,10},{... | collective-permute-start | bytes 442376 | tf_op jit(solution)/shard_map/ppermute | solution.py:18
  51.8 11.2 %collective-permute-start.8 = (bf16[96,1024]{1,0:T(8,128)(2,1)S(1)}, bf16[96,1024]{1,0:T(8,128)(2,1)S(1)}, u32[]{:S(2)}, u32[]{:S(2)}) collective-permute-start(bf16[96,1024]{1,0:T(8,128)(2,1)S(1)} %convolution_convert_fusion), channel_id=1, source_target_pairs={{0,64},{64,128},{128,192},{192,256},{256,320},{320,384},{384,448},... | collective-permute-start | bytes 589832 | tf_op jit(solution)/shard_map/ppermute | solution.py:18
  58.0 7.4 %collective-permute-start.12 = (bf16[96,1024]{1,0:T(8,128)(2,1)S(1)}, bf16[96,1024]{1,0:T(8,128)(2,1)S(1)}, u32[]{:S(2)}, u32[]{:S(2)}) collective-permute-start(bf16[96,1024]{1,0:T(8,128)(2,1)S(1)} %convolution_convert_fusion.1), channel_id=1, source_target_pairs={{0,448},{64,0},{128,64},{192,128},{256,192},{320,256},{384,320},{4... | collective-permute-start | bytes 589832 | tf_op jit(solution)/shard_map/ppermute | solution.py:18
  62.9 13.3 %copy-start = (bf16[4,4,96,768]{3,2,1,0:T(8,128)(2,1)}, bf16[4,4,96,768]{3,2,1,0:T(8,128)(2,1)S(1)}, u32[]{:S(2)}) copy-start(bf16[4,4,96,768]{3,2,1,0:T(8,128)(2,1)S(1)} %shard_map.96) | copy-start | bytes 7077892
  63.5 10.3 %collective-permute-start.9 = (bf16[192,1024]{1,0:T(8,128)(2,1)S(1)}, bf16[192,1024]{1,0:T(8,128)(2,1)S(1)}, u32[]{:S(2)}, u32[]{:S(2)}) collective-permute-start(bf16[192,1024]{1,0:T(8,128)(2,1)S(1)} %fusion.5), channel_id=1, source_target_pairs={{0,64},{64,128},{128,192},{192,256},{256,320},{320,384},{384,448},... | collective-permute-start | bytes 1179656 | tf_op jit(solution)/shard_map/ppermute | solution.py:18
  66.0 10.3 %collective-permute-start.13 = (bf16[192,1024]{1,0:T(8,128)(2,1)S(1)}, bf16[192,1024]{1,0:T(8,128)(2,1)S(1)}, u32[]{:S(2)}, u32[]{:S(2)}) collective-permute-start(bf16[192,1024]{1,0:T(8,128)(2,1)S(1)} %fusion.8), channel_id=1, source_target_pairs={{0,448},{64,0},{128,64},{192,128},{256,192},{320,256},{384,320},{4... | collective-permute-start | bytes 1179656 | tf_op jit(solution)/shard_map/ppermute | solution.py:18
  72.5 8.8 %collective-permute-start.7 = (bf16[192,384]{1,0:T(8,128)(2,1)}, bf16[192,384]{1,0:T(8,128)(2,1)S(1)}, u32[]{:S(2)}, u32[]{:S(2)}) collective-permute-start(bf16[192,384]{1,0:T(8,128)(2,1)} %get-tuple-element.28), channel_id=1, source_target_pairs={{0,64},{128,192},{448,384},{320,256},{1,65},{129,193},{449,385},{3... | collective-permute-start | bytes 442376 | tf_op jit(solution)/shard_map/ppermute | solution.py:185
  74.3 9.7 %collective-permute-start.10 = (bf16[192,1024]{1,0:T(8,128)(2,1)S(1)}, bf16[192,1024]{1,0:T(8,128)(2,1)S(1)}, u32[]{:S(2)}, u32[]{:S(2)}) collective-permute-start(bf16[192,1024]{1,0:T(8,128)(2,1)S(1)} %fusion.4), channel_id=1, source_target_pairs={{0,64},{64,128},{128,192},{192,256},{256,320},{320,384},{384,448},... | collective-permute-start | bytes 1179656 | tf_op jit(solution)/shard_map/ppermute | solution.py:18
  76.8 11.8 %collective-permute-start.14 = (bf16[192,1024]{1,0:T(8,128)(2,1)S(1)}, bf16[192,1024]{1,0:T(8,128)(2,1)}, u32[]{:S(2)}, u32[]{:S(2)}) collective-permute-start(bf16[192,1024]{1,0:T(8,128)(2,1)S(1)} %fusion.7), channel_id=1, source_target_pairs={{0,448},{64,0},{128,64},{192,128},{256,192},{320,256},{384,320},{4... | collective-permute-start | bytes 1179656 | tf_op jit(solution)/shard_map/ppermute | solution.py:18
  86.2 8.2 %copy-start.8 = (bf16[192,3072]{1,0:T(8,128)(2,1)S(1)}, bf16[192,3072]{1,0:T(8,128)(2,1)}, u32[]{:S(2)}) copy-start(bf16[192,3072]{1,0:T(8,128)(2,1)} %param.11) | copy-start | bytes 3538948
  86.2 19.4 %collective-permute-start.11 = (bf16[192,1024]{1,0:T(8,128)(2,1)}, bf16[192,1024]{1,0:T(8,128)(2,1)}, u32[]{:S(2)}, u32[]{:S(2)}) collective-permute-start(bf16[192,1024]{1,0:T(8,128)(2,1)} %fusion.3), channel_id=1, source_target_pairs={{0,64},{64,128},{128,192},{192,256},{256,320},{320,384},{384,448},... | collective-permute-start | bytes 1179656 | tf_op jit(solution)/shard_map/ppermute | solution.py:18
  90.1 15.5 %collective-permute-start.15 = (bf16[192,1024]{1,0:T(8,128)(2,1)S(1)}, bf16[192,1024]{1,0:T(8,128)(2,1)}, u32[]{:S(2)}, u32[]{:S(2)}) collective-permute-start(bf16[192,1024]{1,0:T(8,128)(2,1)S(1)} %fusion.6), channel_id=1, source_target_pairs={{0,448},{64,0},{128,64},{192,128},{256,192},{320,256},{384,320},{4... | collective-permute-start | bytes 1179656 | tf_op jit(solution)/shard_map/ppermute | solution.py:18
  95.0 20.9 %copy-start.9 = (f32[1,3072]{1,0:T(1,128)S(1)}, f32[1,3072]{1,0:T(1,128)}, u32[]{:S(2)}) copy-start(f32[1,3072]{1,0:T(1,128)} %param.12) | copy-start | bytes 36868
  95.0 10.6 %collective-permute-start.17 = (f32[192]{0:T(256)S(1)}, f32[192]{0:T(256)S(1)}, u32[]{:S(2)}, u32[]{:S(2)}) collective-permute-start(f32[192]{0:T(256)S(1)} %fusion), channel_id=1, source_target_pairs={{0,1},{1,0},{2,3},{3,2},{4,5},{5,4},{6,7},{7,6},{8,9},{9,8},{10,11... | collective-permute-start | bytes 2312 | tf_op jit(solution)/shard_map/ppermute | solution.py:18
  107.1 11.8 %collective-permute-start.16 = (bf16[192,512]{1,0:T(8,128)(2,1)S(1)}, bf16[192,512]{1,0:T(8,128)(2,1)S(1)}, u32[]{:S(2)}, u32[]{:S(2)}) collective-permute-start(bf16[192,512]{1,0:T(8,128)(2,1)S(1)} %convolution_add_fusion.6), channel_id=1, source_target_pairs={{0,2},{2,0},{1,3},{3,1},{4,6},{6,4},{5,7},{7,5},{8,10},{10,8},{9,1... | collective-permute-start | bytes 589832 | tf_op jit(solution)/shard_map/ppermute | solution.py:18
  117.4 1.5 %copy-start.3 = (f32[512,384]{1,0:T(8,128)S(1)}, f32[512,384]{1,0:T(8,128)}, u32[]{:S(2)}) copy-start(f32[512,384]{1,0:T(8,128)} %copy-done.2) | copy-start | bytes 2359300
  117.4 1.5 %copy-start.6 = (bf16[192,256]{1,0:T(8,128)(2,1)S(1)}, bf16[192,256]{1,0:T(8,128)(2,1)}, u32[]{:S(2)}) copy-start(bf16[192,256]{1,0:T(8,128)(2,1)} %copy-done.5) | copy-start | bytes 294916

commit v10 on v8

--- a/solution.py
+++ b/solution.py
@@ -10,7 +10,7 @@
 PATCHES = 256
 AXES = ("section", "zlo", "x", "core", "tensor")
 DP = ("zlo", "x", "core")
-LATE = 3
+LATE = 2
 
 
 def around(value, axis, steps):
@@ -63,9 +63,7 @@
     )(x.astype(jnp.int32).reshape(1), *parts)
 
 
-def ready_kernel(blocks, previous, out, hot):
-    images = previous.shape[0] // PATCHES
-    out[...] = 0.5 * normed(previous[...].astype(jnp.float32), images)
+def ready_kernel(blocks, hot):
     per_side, size = GRID_SIDE // BLOCK_SIDE, BLOCK_SIDE * BLOCK_SIDE
     within = lax.broadcasted_iota(jnp.int32, (size, PATCHES), 0)
     lane = lax.broadcasted_iota(jnp.int32, (size, PATCHES), 1)
@@ -76,7 +74,7 @@
         hot[k * size:(k + 1) * size] = jnp.where(lane == inside + corner, 1.0, 0.0).astype(hot.dtype)
 
 
-def final_kernel(core, keeps, mine, other, old, hot, kept, handed, targets, error):
+def final_kernel(core, keeps, mine, other, previous, hot, kept, handed, targets, error):
     images = targets.shape[0] // PATCHES
     shard = mine.shape[0] // 2
     first = core[0] == 0
@@ -85,7 +83,7 @@
         a, b = (part[pair * shard:(pair + 1) * shard] for part in (mine, other))
         pieces += [jnp.where(first, a, b), jnp.where(first, b, a)]
     ordered = jnp.concatenate(pieces, axis=0).T.astype(jnp.float32)
-    made = (0.5 * normed(ordered, images) + old[...]).astype(targets.dtype)
+    made = (0.5 * (normed(ordered, images) + normed(previous[...].astype(jnp.float32), images))).astype(targets.dtype)
     targets[...] = made
     picked = jnp.dot(hot[...], made[:PATCHES], preferred_element_type=jnp.float32)
     predicted = jnp.where(keeps[0] == 1, kept[...], handed[...])
@@ -109,18 +107,15 @@
 
     smem, vmem = (pl.BlockSpec(memory_space=space) for space in (pltpu.SMEM, pltpu.VMEM))
     masked = mask_blocks.shape[1] * BLOCK_SIDE * BLOCK_SIDE
-    old, hot = pl.pallas_call(
+    hot = pl.pallas_call(
         ready_kernel,
-        in_specs=[smem, vmem],
-        out_specs=(vmem, vmem),
-        out_shape=(
-            jax.ShapeDtypeStruct((rows, width), f32),
-            jax.ShapeDtypeStruct((masked, PATCHES), bf16),
-        ),
+        in_specs=[smem],
+        out_specs=vmem,
+        out_shape=jax.ShapeDtypeStruct((masked, PATCHES), bf16),
         compiler_params=pltpu.CompilerParams(vmem_limit_bytes=8 << 20),
-        cost_estimate=pl.CostEstimate(flops=0, bytes_accessed=8 << 20, transcendentals=0),
-    )(mask_blocks, previous)
-    above = tied(above, both, old)
+        cost_estimate=pl.CostEstimate(flops=0, bytes_accessed=1 << 20, transcendentals=0),
+    )(mask_blocks)
+    above = tied(above, both, hot)
     below, incoming = lax.optimization_barrier((below, incoming))
     opposite = around(above[:LATE], "x", -1)
     opposite_rest = around(below[LATE:], "x", 1)
@@ -143,7 +138,8 @@
     begun = product(jnp.where(dest % 2 == x // 2, plane(held), near)).astype(bf16)
     rising = up(begun)
     beside = jnp.where(x % 2 == 0, plane(above), plane(below))
-    across = jnp.where(dest // 2 < LATE, plane(opposite), opposite_rest[0])
+    later = lax.dynamic_index_in_dim(opposite_rest, jnp.maximum(dest // 2 - LATE, 0), 0, keepdims=False)
+    across = jnp.where(dest // 2 < LATE, plane(opposite), later)
     ended = product(jnp.where(dest % 2 == x // 2, beside, across)).astype(bf16)
     falling = down(ended)
 
@@ -214,7 +210,7 @@
             jax.ShapeDtypeStruct((masked, width), f32),
         ),
         compiler_params=pltpu.CompilerParams(vmem_limit_bytes=12 << 20),
-    )(core.astype(jnp.int32).reshape(1), keeps.astype(jnp.int32).reshape(1), mine.astype(bf16), other, old, hot, kept, handed)
+    )(core.astype(jnp.int32).reshape(1), keeps.astype(jnp.int32).reshape(1), mine.astype(bf16), other, previous, hot, kept, handed)
     return (targets, section_out, target_error)
 
 

time: 117 us -> 125 us (1.068)
  the two profiles are of different devices: /device:TPU:41 before, /device:TPU:1 now
where the time goes in v10:
time: 125 us; the launch traced here: 124 us
  starting transfers between devices  71.6 us (57%)
  waiting for transfers between devices  15.7 us (13%)
  blocking collectives  14.3 us (11%)
  matrix products  6.12 us (5%)
  local copies, waits for them, and re-layouts  5.92 us (5%)
  other arithmetic  5.06 us (4%)
  Pallas kernels  3.78 us (3%)
  between operations  1.34 us (1%)
    ppermute x16, starting transfers between devices, around(): lax.ppermute(value, axis, [(i, (i + steps) % count) for i in range(count)])  68.3 us
    ppermute x16, waiting for transfers between devices, around(): lax.ppermute(value, axis, [(i, (i + steps) % count) for i in range(count)])  15.7 us
    all_gather x1, blocking collectives, on_device(): held = lax.all_gather(out_weight.T, 'zlo', axis=0, tiled=False)  14.3 us
    dot_general x8, matrix products, product(): return jnp.dot(weight, both, preferred_element_type=f32)  5.46 us
    unnamed x16, local copies, waits for them, and re-layouts  4.45 us
  transfers between devices with their start and end apart: 18, of which 5 were waited for; matrix products, arithmetic and copies ran while one was open for 8% of the time, Pallas kernels for 2%

profile of v10, /device:TPU:1, one launch (start us, length us, event | category | flops | bytes accessed | tf_op | source)
XLA Modules:
  0.0 123.8 jit_solution(16561556766892549974)
XLA Ops:
  0.6 4.0 %collective-permute-start.4 = (bf16[192,3072]{1,0:T(8,128)(2,1)}, bf16[192,3072]{1,0:T(8,128)(2,1)}, u32[]{:S(2)}, u32[]{:S(2)}) collective-permute-start(bf16[192,3072]{1,0:T(8,128)(2,1)} %bitcast.61), channel_id=1, source_target_pairs={{0,64},{64,128},{128,192},{192,256},{256,320},{320,384},{384,448},... | collective-permute-start | bytes 3538952 | tf_op jit(solution)/shard_map/ppermute | solution.py:18
  4.7 6.7 %collective-permute-start.1 = (bf16[512,768]{1,0:T(8,128)(2,1)}, bf16[512,768]{1,0:T(8,128)(2,1)S(1)}, u32[]{:S(2)}, u32[]{:S(2)}) collective-permute-start(bf16[512,768]{1,0:T(8,128)(2,1)} %first.1), channel_id=1, source_target_pairs={{0,2},{2,0},{1,3},{3,1},{4,6},{6,4},{5,7},{7,5},{8,10},{10,8},{9,1... | collective-permute-start | bytes 2359304 | tf_op jit(solution)/shard_map/ppermute | solution.py:18
  11.4 14.3 %all-gather = bf16[384,768]{1,0:T(8,128)(2,1)S(1)} all-gather(bf16[96,768]{1,0:T(8,128)(2,1)} %bitcast.64), channel_id=2, replica_groups=mesh['section'=8,'zlo'=4,'x'=4,'core'=2,'tensor'=2] {'zlo'}, dimensions={0}, use_global_device_ids=true | all-gather | bytes 737280 | tf_op jit(solution)/shard_map/all_gather | solution.py:102
  25.7 4.7 %collective-permute-start = (bf16[4,96,768]{2,1,0:T(8,128)(2,1)S(1)}, bf16[4,96,768]{2,1,0:T(8,128)(2,1)S(1)}, u32[]{:S(2)}, u32[]{:S(2)}) collective-permute-start(bf16[4,96,768]{2,1,0:T(8,128)(2,1)S(1)} %bitcast.57), channel_id=1, source_target_pairs={{0,12},{4,0},{8,4},{12,8},{1,13},{5,1},{9,5},{13,9},{2,14},{6,2},{... | collective-permute-start | bytes 1769480 | tf_op jit(solution)/shard_map/ppermute | solution.py:18
  30.4 1.9 %collective-permute-start.3 = (bf16[4,96,768]{2,1,0:T(8,128)(2,1)S(1)}, bf16[4,96,768]{2,1,0:T(8,128)(2,1)S(1)}, u32[]{:S(2)}, u32[]{:S(2)}) collective-permute-start(bf16[4,96,768]{2,1,0:T(8,128)(2,1)S(1)} %bitcast.58), channel_id=1, source_target_pairs={{0,4},{4,8},{8,12},{12,0},{1,5},{5,9},{9,13},{13,1},{2,6},{6,10},{... | collective-permute-start | bytes 1769480 | tf_op jit(solution)/shard_map/ppermute | solution.py:18
  32.4 0.0 copy-start.4
  32.4 0.6 copy-done.4
  33.0 0.6 shard_map.95.hot
  33.7 0.0 collective-permute-done.1.second
  33.7 0.0 copy-start.1
  33.7 0.9 copy-done.1
  34.6 1.1 copy-done
  35.7 1.1 copy-done.2
  36.8 0.5 shard_map.94
  37.3 4.0 %collective-permute-done.above = bf16[4,96,768]{2,1,0:T(8,128)(2,1)S(1)} collective-permute-done((bf16[4,96,768]{2,1,0:T(8,128)(2,1)S(1)}, bf16[4,96,768]{2,1,0:T(8,128)(2,1)S(1)}, u32[]{:S(2)}, u32[]{:S(2)}) %collective-permute-start) | collective-permute-done | bytes 589856 | tf_op jit(solution)/shard_map/ppermute | solution.py:18
  41.3 5.0 %collective-permute-done.3.below = bf16[4,96,768]{2,1,0:T(8,128)(2,1)S(1)} collective-permute-done((bf16[4,96,768]{2,1,0:T(8,128)(2,1)S(1)}, bf16[4,96,768]{2,1,0:T(8,128)(2,1)S(1)}, u32[]{:S(2)}, u32[]{:S(2)}) %collective-permute-start.3) | collective-permute-done | bytes 589856 | tf_op jit(solution)/shard_map/ppermute | solution.py:18
  46.4 0.0 collective-permute-done.4
  46.4 1.1 convolution_convert_fusion
  47.4 2.8 %collective-permute-start.6 = (bf16[96,1024]{1,0:T(8,128)(2,1)}, bf16[96,1024]{1,0:T(8,128)(2,1)}, u32[]{:S(2)}, u32[]{:S(2)}) collective-permute-start(bf16[96,1024]{1,0:T(8,128)(2,1)} %convolution_convert_fusion), channel_id=1, source_target_pairs={{0,64},{64,128},{128,192},{192,256},{256,320},{320,384},{384,448},... | collective-permute-start | bytes 589832 | tf_op jit(solution)/shard_map/ppermute | solution.py:18
  50.3 0.7 slice.50
  51.0 1.9 %collective-permute-start.2 = (bf16[2,96,768]{2,1,0:T(8,128)(2,1)}, bf16[2,96,768]{2,1,0:T(8,128)(2,1)}, u32[]{:S(2)}, u32[]{:S(2)}) collective-permute-start(bf16[2,96,768]{2,1,0:T(8,128)(2,1)} %slice.50), channel_id=1, source_target_pairs={{0,12},{4,0},{8,4},{12,8},{1,13},{5,1},{9,5},{13,9},{2,14},{6,2},{... | collective-permute-start | bytes 884744 | tf_op jit(solution)/shard_map/ppermute | solution.py:18
  52.9 0.7 slice.51
  53.7 3.4 %collective-permute-start.5 = (bf16[2,96,768]{2,1,0:T(8,128)(2,1)}, bf16[2,96,768]{2,1,0:T(8,128)(2,1)}, u32[]{:S(2)}, u32[]{:S(2)}) collective-permute-start(bf16[2,96,768]{2,1,0:T(8,128)(2,1)} %slice.51), channel_id=1, source_target_pairs={{0,4},{4,8},{8,12},{12,0},{1,5},{5,9},{9,13},{13,1},{2,6},{6,10},{... | collective-permute-start | bytes 884744 | tf_op jit(solution)/shard_map/ppermute | solution.py:18
  57.2 0.0 collective-permute-done.6
  57.2 1.0 broadcast_select_fusion.4
  58.2 0.8 collective-permute-done.2.opposite
  59.0 3.7 %collective-permute-done.5.rest = bf16[2,96,768]{2,1,0:T(8,128)(2,1)} collective-permute-done((bf16[2,96,768]{2,1,0:T(8,128)(2,1)}, bf16[2,96,768]{2,1,0:T(8,128)(2,1)}, u32[]{:S(2)}, u32[]{:S(2)}) %collective-permute-start.5) | collective-permute-done | bytes 294944 | tf_op jit(solution)/shard_map/ppermute | solution.py:18
  62.6 1.4 %convolution_convert_fusion.1 = bf16[96,1024]{1,0:T(8,128)(2,1)S(1)} fusion(bf16[768,1024]{1,0:T(8,128)(2,1)S(1)} %shard_map.94, bf16[2,96,768]{2,1,0:T(8,128)(2,1)} %collective-permute-done.5.rest, s32[]{:T(128)S(6)} %max.3, bf16[2,96,768]{2,1,0:T(8,128)(2,1)} %collective-permute-done.2.opposite, s32[]{:T(128)S(6)} %select_n.236, pred[]{:T(512)S(6)} %lt.109, ...), kind=kOutput, calls=%fused_computation.23 | convolution fusion | flops 151314432 | bytes 2359311 | tf_op jit(solution)/shard_map/dot_general | solution.py:124
  64.0 3.6 %collective-permute-start.10 = (bf16[96,1024]{1,0:T(8,128)(2,1)S(1)}, bf16[96,1024]{1,0:T(8,128)(2,1)S(1)}, u32[]{:S(2)}, u32[]{:S(2)}) collective-permute-start(bf16[96,1024]{1,0:T(8,128)(2,1)S(1)} %convolution_convert_fusion.1), channel_id=1, source_target_pairs={{0,448},{64,0},{128,64},{192,128},{256,192},{320,256},{384,320},{4... | collective-permute-start | bytes 589832 | tf_op jit(solution)/shard_map/ppermute | solution.py:18
  67.7 1.2 shard_map.96
  68.9 0.5 fusion.5
  69.4 0.0 copy-start.5
  69.4 2.1 %collective-permute-start.7 = (bf16[192,1024]{1,0:T(8,128)(2,1)S(1)}, bf16[192,1024]{1,0:T(8,128)(2,1)S(1)}, u32[]{:S(2)}, u32[]{:S(2)}) collective-permute-start(bf16[192,1024]{1,0:T(8,128)(2,1)S(1)} %fusion.5), channel_id=1, source_target_pairs={{0,64},{64,128},{128,192},{192,256},{256,320},{320,384},{384,448},... | collective-permute-start | bytes 1179656 | tf_op jit(solution)/shard_map/ppermute | solution.py:18
  71.5 0.0 collective-permute-done.10
  71.5 0.5 fusion.8
  72.0 4.6 %collective-permute-start.11 = (bf16[192,1024]{1,0:T(8,128)(2,1)S(1)}, bf16[192,1024]{1,0:T(8,128)(2,1)S(1)}, u32[]{:S(2)}, u32[]{:S(2)}) collective-permute-start(bf16[192,1024]{1,0:T(8,128)(2,1)S(1)} %fusion.8), channel_id=1, source_target_pairs={{0,448},{64,0},{128,64},{192,128},{256,192},{320,256},{384,320},{4... | collective-permute-start | bytes 1179656 | tf_op jit(solution)/shard_map/ppermute | solution.py:18
  76.6 0.5 fusion
  77.1 2.2 %collective-permute-done.7 = bf16[192,1024]{1,0:T(8,128)(2,1)S(1)} collective-permute-done((bf16[192,1024]{1,0:T(8,128)(2,1)S(1)}, bf16[192,1024]{1,0:T(8,128)(2,1)S(1)}, u32[]{:S(2)}, u32[]{:S(2)}) %collective-permute-start.7) | collective-permute-done | bytes 393248 | tf_op jit(solution)/shard_map/ppermute | solution.py:18
  79.3 0.5 fusion.4
  79.8 0.0 copy-start.6
  79.8 2.1 %collective-permute-start.8 = (bf16[192,1024]{1,0:T(8,128)(2,1)S(1)}, bf16[192,1024]{1,0:T(8,128)(2,1)S(1)}, u32[]{:S(2)}, u32[]{:S(2)}) collective-permute-start(bf16[192,1024]{1,0:T(8,128)(2,1)S(1)} %fusion.4), channel_id=1, source_target_pairs={{0,64},{64,128},{128,192},{192,256},{256,320},{320,384},{384,448},... | collective-permute-start | bytes 1179656 | tf_op jit(solution)/shard_map/ppermute | solution.py:18
  81.8 0.0 collective-permute-done.11
  81.9 0.5 fusion.7
  82.4 4.6 %collective-permute-start.12 = (bf16[192,1024]{1,0:T(8,128)(2,1)S(1)}, bf16[192,1024]{1,0:T(8,128)(2,1)S(1)}, u32[]{:S(2)}, u32[]{:S(2)}) collective-permute-start(bf16[192,1024]{1,0:T(8,128)(2,1)S(1)} %fusion.7), channel_id=1, source_target_pairs={{0,448},{64,0},{128,64},{192,128},{256,192},{320,256},{384,320},{4... | collective-permute-start | bytes 1179656 | tf_op jit(solution)/shard_map/ppermute | solution.py:18
  87.0 1.0 slice_select_fusion
  88.0 2.0 %collective-permute-start.15 = (bf16[192,768]{1,0:T(8,128)(2,1)S(1)}, bf16[192,768]{1,0:T(8,128)(2,1)S(1)}, u32[]{:S(2)}, u32[]{:S(2)}) collective-permute-start(bf16[192,768]{1,0:T(8,128)(2,1)S(1)} %slice_select_fusion), channel_id=1, source_target_pairs={{0,128},{448,320},{1,129},{449,321},{2,130},{450,322},{3,131},{451... | collective-permute-start | bytes 884744 | tf_op jit(solution)/shard_map/ppermute | solution.py:173
  90.0 0.5 fusion.3
  90.5 1.9 %collective-permute-start.9 = (bf16[192,1024]{1,0:T(8,128)(2,1)S(1)}, bf16[192,1024]{1,0:T(8,128)(2,1)S(1)}, u32[]{:S(2)}, u32[]{:S(2)}) collective-permute-start(bf16[192,1024]{1,0:T(8,128)(2,1)S(1)} %fusion.3), channel_id=1, source_target_pairs={{0,64},{64,128},{128,192},{192,256},{256,320},{320,384},{384,448},... | collective-permute-start | bytes 1179656 | tf_op jit(solution)/shard_map/ppermute | solution.py:18
  92.4 0.5 fusion.6
  93.0 0.0 copy-start.7
  93.0 4.6 %collective-permute-start.13 = (bf16[192,1024]{1,0:T(8,128)(2,1)S(1)}, bf16[192,1024]{1,0:T(8,128)(2,1)S(1)}, u32[]{:S(2)}, u32[]{:S(2)}) collective-permute-start(bf16[192,1024]{1,0:T(8,128)(2,1)S(1)} %fusion.6), channel_id=1, source_target_pairs={{0,448},{64,0},{128,64},{192,128},{256,192},{320,256},{384,320},{4... | collective-permute-start | bytes 1179656 | tf_op jit(solution)/shard_map/ppermute | solution.py:18
  97.5 7.9 %collective-permute-start.17 = (f32[192]{0:T(256)S(1)}, f32[192]{0:T(256)S(1)}, u32[]{:S(2)}, u32[]{:S(2)}) collective-permute-start(f32[192]{0:T(256)S(1)} %fusion), channel_id=1, source_target_pairs={{0,1},{1,0},{2,3},{3,2},{4,5},{5,4},{6,7},{7,6},{8,9},{9,8},{10,11... | collective-permute-start | bytes 2312 | tf_op jit(solution)/shard_map/ppermute | solution.py:18
  105.5 0.0 collective-permute-done.15
  105.5 1.1 fusion.29
  106.6 1.3 %collective-permute-start.16 = (bf16[192,384]{1,0:T(8,128)(2,1)S(1)}, bf16[192,384]{1,0:T(8,128)(2,1)S(1)}, u32[]{:S(2)}, u32[]{:S(2)}) collective-permute-start(bf16[192,384]{1,0:T(8,128)(2,1)S(1)} %get-tuple-element.21), channel_id=1, source_target_pairs={{0,64},{128,192},{448,384},{320,256},{1,65},{129,193},{449,385},{3... | collective-permute-start | bytes 442376 | tf_op jit(solution)/shard_map/ppermute | solution.py:184
  107.9 0.0 collective-permute-done.17
  107.9 0.0 collective-permute-done.9
  107.9 0.3 convolution_add_fusion.6
  108.3 11.6 %collective-permute-start.14 = (bf16[192,512]{1,0:T(8,128)(2,1)S(1)}, bf16[192,512]{1,0:T(8,128)(2,1)S(1)}, u32[]{:S(2)}, u32[]{:S(2)}) collective-permute-start(bf16[192,512]{1,0:T(8,128)(2,1)S(1)} %convolution_add_fusion.6), channel_id=1, source_target_pairs={{0,2},{2,0},{1,3},{3,1},{4,6},{6,4},{5,7},{7,5},{8,10},{10,8},{9,1... | collective-permute-start | bytes 589832 | tf_op jit(solution)/shard_map/ppermute | solution.py:18
  119.9 1.5 %fusion.9 = bf16[1,192,3072]{2,1,0:T(8,128)(2,1)} fusion(f32[3072]{0:T(1024)S(1)} %bitcast.65, f32[192]{0:T(256)S(1)} %add_rsqrt_fusion, bf16[192,3072]{1,0:T(8,128)(2,1)S(1)} %copy-done.5, bf16[192,3072]{1,0:T(8,128)(2,1)} %collective-permute-done.4, pred[]{:T(512)S(6)} %eq.50), kind=kLoop, calls=%fused_computation.19 | loop fusion | flops 2949120 | bytes 3552001 | tf_op jit(solution)/shard_map/broadcast_in_dim | solution.py:202
  121.4 0.3 fusion.10.mine
  121.7 0.0 collective-permute-done.14.other
  121.7 0.6 copy-done.3
  122.4 1.5 %shard_map.97 = (bf16[512,384]{1,0:T(8,128)(2,1)}, f32[192,384]{1,0:T(8,128)}) custom-call(s32[1]{0:T(128)} %bitcast.core, s32[1]{0:T(128)} %bitcast.1.keeps, bf16[192,512]{1,0:T(8,128)(2,1)S(1)} %fusion.10.mine, bf16[192,512]{1,0:T(8,128)(2,1)S(1)} %collective-permute-done.14.other, bf16[512,384]{1,0:T(8,128)(2,1)S(1)} %copy-done.3, ...), custom_call_target="tpu_custom_call" | custom-call | tf_op jit(solution)/shard_map/pallas_call | solution.py:204
  (12 shorter events, 0.1 us)
Async XLA Ops:
  0.6 45.7 %collective-permute-start.4 = (bf16[192,3072]{1,0:T(8,128)(2,1)}, bf16[192,3072]{1,0:T(8,128)(2,1)}, u32[]{:S(2)}, u32[]{:S(2)}) collective-permute-start(bf16[192,3072]{1,0:T(8,128)(2,1)} %bitcast.61), channel_id=1, source_target_pairs={{0,64},{64,128},{128,192},{192,256},{256,320},{320,384},{384,448},... | collective-permute-start | bytes 3538952 | tf_op jit(solution)/shard_map/ppermute | solution.py:18
  4.7 29.0 %collective-permute-start.1 = (bf16[512,768]{1,0:T(8,128)(2,1)}, bf16[512,768]{1,0:T(8,128)(2,1)S(1)}, u32[]{:S(2)}, u32[]{:S(2)}) collective-permute-start(bf16[512,768]{1,0:T(8,128)(2,1)} %first.1), channel_id=1, source_target_pairs={{0,2},{2,0},{1,3},{3,1},{4,6},{6,4},{5,7},{7,5},{8,10},{10,8},{9,1... | collective-permute-start | bytes 2359304 | tf_op jit(solution)/shard_map/ppermute | solution.py:18
  25.7 15.6 %collective-permute-start = (bf16[4,96,768]{2,1,0:T(8,128)(2,1)S(1)}, bf16[4,96,768]{2,1,0:T(8,128)(2,1)S(1)}, u32[]{:S(2)}, u32[]{:S(2)}) collective-permute-start(bf16[4,96,768]{2,1,0:T(8,128)(2,1)S(1)} %bitcast.57), channel_id=1, source_target_pairs={{0,12},{4,0},{8,4},{12,8},{1,13},{5,1},{9,5},{13,9},{2,14},{6,2},{... | collective-permute-start | bytes 1769480 | tf_op jit(solution)/shard_map/ppermute | solution.py:18
  30.4 16.0 %collective-permute-start.3 = (bf16[4,96,768]{2,1,0:T(8,128)(2,1)S(1)}, bf16[4,96,768]{2,1,0:T(8,128)(2,1)S(1)}, u32[]{:S(2)}, u32[]{:S(2)}) collective-permute-start(bf16[4,96,768]{2,1,0:T(8,128)(2,1)S(1)} %bitcast.58), channel_id=1, source_target_pairs={{0,4},{4,8},{8,12},{12,0},{1,5},{5,9},{9,13},{13,1},{2,6},{6,10},{... | collective-permute-start | bytes 1769480 | tf_op jit(solution)/shard_map/ppermute | solution.py:18
  32.4 0.7 copy-start.4
  33.7 0.9 copy-start.1
  34.6 1.1 copy-start
  35.7 1.1 copy-start.2
  47.4 9.8 %collective-permute-start.6 = (bf16[96,1024]{1,0:T(8,128)(2,1)}, bf16[96,1024]{1,0:T(8,128)(2,1)}, u32[]{:S(2)}, u32[]{:S(2)}) collective-permute-start(bf16[96,1024]{1,0:T(8,128)(2,1)} %convolution_convert_fusion), channel_id=1, source_target_pairs={{0,64},{64,128},{128,192},{192,256},{256,320},{320,384},{384,448},... | collective-permute-start | bytes 589832 | tf_op jit(solution)/shard_map/ppermute | solution.py:18
  51.0 8.0 %collective-permute-start.2 = (bf16[2,96,768]{2,1,0:T(8,128)(2,1)}, bf16[2,96,768]{2,1,0:T(8,128)(2,1)}, u32[]{:S(2)}, u32[]{:S(2)}) collective-permute-start(bf16[2,96,768]{2,1,0:T(8,128)(2,1)} %slice.50), channel_id=1, source_target_pairs={{0,12},{4,0},{8,4},{12,8},{1,13},{5,1},{9,5},{13,9},{2,14},{6,2},{... | collective-permute-start | bytes 884744 | tf_op jit(solution)/shard_map/ppermute | solution.py:18
  53.7 9.0 %collective-permute-start.5 = (bf16[2,96,768]{2,1,0:T(8,128)(2,1)}, bf16[2,96,768]{2,1,0:T(8,128)(2,1)}, u32[]{:S(2)}, u32[]{:S(2)}) collective-permute-start(bf16[2,96,768]{2,1,0:T(8,128)(2,1)} %slice.51), channel_id=1, source_target_pairs={{0,4},{4,8},{8,12},{12,0},{1,5},{5,9},{9,13},{13,1},{2,6},{6,10},{... | collective-permute-start | bytes 884744 | tf_op jit(solution)/shard_map/ppermute | solution.py:18
  64.0 7.4 %collective-permute-start.10 = (bf16[96,1024]{1,0:T(8,128)(2,1)S(1)}, bf16[96,1024]{1,0:T(8,128)(2,1)S(1)}, u32[]{:S(2)}, u32[]{:S(2)}) collective-permute-start(bf16[96,1024]{1,0:T(8,128)(2,1)S(1)} %convolution_convert_fusion.1), channel_id=1, source_target_pairs={{0,448},{64,0},{128,64},{192,128},{256,192},{320,256},{384,320},{4... | collective-permute-start | bytes 589832 | tf_op jit(solution)/shard_map/ppermute | solution.py:18
  69.4 7.2 %copy-start.5 = (bf16[192,3072]{1,0:T(8,128)(2,1)S(1)}, bf16[192,3072]{1,0:T(8,128)(2,1)}, u32[]{:S(2)}) copy-start(bf16[192,3072]{1,0:T(8,128)(2,1)} %param.11) | copy-start | bytes 3538948
  69.4 9.9 %collective-permute-start.7 = (bf16[192,1024]{1,0:T(8,128)(2,1)S(1)}, bf16[192,1024]{1,0:T(8,128)(2,1)S(1)}, u32[]{:S(2)}, u32[]{:S(2)}) collective-permute-start(bf16[192,1024]{1,0:T(8,128)(2,1)S(1)} %fusion.5), channel_id=1, source_target_pairs={{0,64},{64,128},{128,192},{192,256},{256,320},{320,384},{384,448},... | collective-permute-start | bytes 1179656 | tf_op jit(solution)/shard_map/ppermute | solution.py:18
  72.0 9.8 %collective-permute-start.11 = (bf16[192,1024]{1,0:T(8,128)(2,1)S(1)}, bf16[192,1024]{1,0:T(8,128)(2,1)S(1)}, u32[]{:S(2)}, u32[]{:S(2)}) collective-permute-start(bf16[192,1024]{1,0:T(8,128)(2,1)S(1)} %fusion.8), channel_id=1, source_target_pairs={{0,448},{64,0},{128,64},{192,128},{256,192},{320,256},{384,320},{4... | collective-permute-start | bytes 1179656 | tf_op jit(solution)/shard_map/ppermute | solution.py:18
  79.8 7.2 %copy-start.6 = (bf16[1,192,3072]{2,1,0:T(8,128)(2,1)S(1)}, bf16[1,192,3072]{2,1,0:T(8,128)(2,1)}, u32[]{:S(2)}) copy-start(bf16[1,192,3072]{2,1,0:T(8,128)(2,1)} %param.10) | copy-start | bytes 3538948
  79.8 10.2 %collective-permute-start.8 = (bf16[192,1024]{1,0:T(8,128)(2,1)S(1)}, bf16[192,1024]{1,0:T(8,128)(2,1)S(1)}, u32[]{:S(2)}, u32[]{:S(2)}) collective-permute-start(bf16[192,1024]{1,0:T(8,128)(2,1)S(1)} %fusion.4), channel_id=1, source_target_pairs={{0,64},{64,128},{128,192},{192,256},{256,320},{320,384},{384,448},... | collective-permute-start | bytes 1179656 | tf_op jit(solution)/shard_map/ppermute | solution.py:18
  82.4 10.1 %collective-permute-start.12 = (bf16[192,1024]{1,0:T(8,128)(2,1)S(1)}, bf16[192,1024]{1,0:T(8,128)(2,1)S(1)}, u32[]{:S(2)}, u32[]{:S(2)}) collective-permute-start(bf16[192,1024]{1,0:T(8,128)(2,1)S(1)} %fusion.7), channel_id=1, source_target_pairs={{0,448},{64,0},{128,64},{192,128},{256,192},{320,256},{384,320},{4... | collective-permute-start | bytes 1179656 | tf_op jit(solution)/shard_map/ppermute | solution.py:18
  88.0 17.5 %collective-permute-start.15 = (bf16[192,768]{1,0:T(8,128)(2,1)S(1)}, bf16[192,768]{1,0:T(8,128)(2,1)S(1)}, u32[]{:S(2)}, u32[]{:S(2)}) collective-permute-start(bf16[192,768]{1,0:T(8,128)(2,1)S(1)} %slice_select_fusion), channel_id=1, source_target_pairs={{0,128},{448,320},{1,129},{449,321},{2,130},{450,322},{3,131},{451... | collective-permute-start | bytes 884744 | tf_op jit(solution)/shard_map/ppermute | solution.py:173
  90.5 17.4 %collective-permute-start.9 = (bf16[192,1024]{1,0:T(8,128)(2,1)S(1)}, bf16[192,1024]{1,0:T(8,128)(2,1)S(1)}, u32[]{:S(2)}, u32[]{:S(2)}) collective-permute-start(bf16[192,1024]{1,0:T(8,128)(2,1)S(1)} %fusion.3), channel_id=1, source_target_pairs={{0,64},{64,128},{128,192},{192,256},{256,320},{320,384},{384,448},... | collective-permute-start | bytes 1179656 | tf_op jit(solution)/shard_map/ppermute | solution.py:18
  93.0 26.9 %copy-start.7 = (f32[1,3072]{1,0:T(1,128)S(1)}, f32[1,3072]{1,0:T(1,128)}, u32[]{:S(2)}) copy-start(f32[1,3072]{1,0:T(1,128)} %param.12) | copy-start | bytes 36868
  93.0 14.9 %collective-permute-start.13 = (bf16[192,1024]{1,0:T(8,128)(2,1)S(1)}, bf16[192,1024]{1,0:T(8,128)(2,1)S(1)}, u32[]{:S(2)}, u32[]{:S(2)}) collective-permute-start(bf16[192,1024]{1,0:T(8,128)(2,1)S(1)} %fusion.6), channel_id=1, source_target_pairs={{0,448},{64,0},{128,64},{192,128},{256,192},{320,256},{384,320},{4... | collective-permute-start | bytes 1179656 | tf_op jit(solution)/shard_map/ppermute | solution.py:18
  97.5 10.3 %collective-permute-start.17 = (f32[192]{0:T(256)S(1)}, f32[192]{0:T(256)S(1)}, u32[]{:S(2)}, u32[]{:S(2)}) collective-permute-start(f32[192]{0:T(256)S(1)} %fusion), channel_id=1, source_target_pairs={{0,1},{1,0},{2,3},{3,2},{4,5},{5,4},{6,7},{7,6},{8,9},{9,8},{10,11... | collective-permute-start | bytes 2312 | tf_op jit(solution)/shard_map/ppermute | solution.py:18
  106.6 15.1 %collective-permute-start.16 = (bf16[192,384]{1,0:T(8,128)(2,1)S(1)}, bf16[192,384]{1,0:T(8,128)(2,1)S(1)}, u32[]{:S(2)}, u32[]{:S(2)}) collective-permute-start(bf16[192,384]{1,0:T(8,128)(2,1)S(1)} %get-tuple-element.21), channel_id=1, source_target_pairs={{0,64},{128,192},{448,384},{320,256},{1,65},{129,193},{449,385},{3... | collective-permute-start | bytes 442376 | tf_op jit(solution)/shard_map/ppermute | solution.py:184
  108.3 13.5 %collective-permute-start.14 = (bf16[192,512]{1,0:T(8,128)(2,1)S(1)}, bf16[192,512]{1,0:T(8,128)(2,1)S(1)}, u32[]{:S(2)}, u32[]{:S(2)}) collective-permute-start(bf16[192,512]{1,0:T(8,128)(2,1)S(1)} %convolution_add_fusion.6), channel_id=1, source_target_pairs={{0,2},{2,0},{1,3},{3,1},{4,6},{6,4},{5,7},{7,5},{8,10},{10,8},{9,1... | collective-permute-start | bytes 589832 | tf_op jit(solution)/shard_map/ppermute | solution.py:18
  121.4 1.0 copy-start.3

commit v11 on v10

--- a/solution.py
+++ b/solution.py
@@ -10,7 +10,7 @@
 PATCHES = 256
 AXES = ("section", "zlo", "x", "core", "tensor")
 DP = ("zlo", "x", "core")
-LATE = 2
+LATE = 3
 
 
 def around(value, axis, steps):
@@ -138,8 +138,7 @@
     begun = product(jnp.where(dest % 2 == x // 2, plane(held), near)).astype(bf16)
     rising = up(begun)
     beside = jnp.where(x % 2 == 0, plane(above), plane(below))
-    later = lax.dynamic_index_in_dim(opposite_rest, jnp.maximum(dest // 2 - LATE, 0), 0, keepdims=False)
-    across = jnp.where(dest // 2 < LATE, plane(opposite), later)
+    across = jnp.where(dest // 2 < LATE, plane(opposite), opposite_rest[0])
     ended = product(jnp.where(dest % 2 == x // 2, beside, across)).astype(bf16)
     falling = down(ended)
 

time: 125 us -> 117 us (0.936)
  the two profiles are of different devices: /device:TPU:1 before, /device:TPU:41 now
where the time goes in v11:
time: 117 us; the launch traced here: 116 us
  starting transfers between devices  67.3 us (58%)
  blocking collectives  18.3 us (16%)
  waiting for transfers between devices  9.63 us (8%)
  other arithmetic  6.67 us (6%)
  matrix products  5.38 us (5%)
  Pallas kernels  3.75 us (3%)
  local copies, waits for them, and re-layouts  3.24 us (3%)
  between operations  1.32 us (1%)
    ppermute x16, starting transfers between devices, around(): lax.ppermute(value, axis, [(i, (i + steps) % count) for i in range(count)])  61.5 us
    all_gather x1, blocking collectives, on_device(): held = lax.all_gather(out_weight.T, 'zlo', axis=0, tiled=False)  18.3 us
    ppermute x16, waiting for transfers between devices, around(): lax.ppermute(value, axis, [(i, (i + steps) % count) for i in range(count)])  9.62 us
    dot_general x8, matrix products, product(): return jnp.dot(weight, both, preferred_element_type=f32)  4.72 us
    ppermute x1, starting transfers between devices, on_device(): lax.ppermute(onward, 'section', [(0, 1), (2, 3), (last, last - 1), (last...  4.58 us
    broadcast_in_dim x1, other arithmetic, on_device(): (wide * tied(scaling, theirs) * section_gains).astype(bf16)[None]  2.78 us
    unnamed x12, local copies, waits for them, and re-layouts  2.44 us
  transfers between devices with their start and end apart: 18, of which 5 were waited for; matrix products, arithmetic and copies ran while one was open for 11% of the time, Pallas kernels for 2%

profile of v11, /device:TPU:41, one launch (start us, length us, event | category | flops | bytes accessed | tf_op | source)
XLA Modules:
  0.0 115.6 jit_solution(13323696535810519805)
XLA Ops:
  0.6 2.3 %collective-permute-start.4 = (bf16[192,3072]{1,0:T(8,128)(2,1)}, bf16[192,3072]{1,0:T(8,128)(2,1)}, u32[]{:S(2)}, u32[]{:S(2)}) collective-permute-start(bf16[192,3072]{1,0:T(8,128)(2,1)} %bitcast.61), channel_id=1, source_target_pairs={{0,64},{64,128},{128,192},{192,256},{256,320},{320,384},{384,448},... | collective-permute-start | bytes 3538952 | tf_op jit(solution)/shard_map/ppermute | solution.py:18
  2.9 2.9 %collective-permute-start.1 = (bf16[512,768]{1,0:T(8,128)(2,1)}, bf16[512,768]{1,0:T(8,128)(2,1)S(1)}, u32[]{:S(2)}, u32[]{:S(2)}) collective-permute-start(bf16[512,768]{1,0:T(8,128)(2,1)} %first.1), channel_id=1, source_target_pairs={{0,2},{2,0},{1,3},{3,1},{4,6},{6,4},{5,7},{7,5},{8,10},{10,8},{9,1... | collective-permute-start | bytes 2359304 | tf_op jit(solution)/shard_map/ppermute | solution.py:18
  5.8 18.3 %all-gather = bf16[384,768]{1,0:T(8,128)(2,1)S(1)} all-gather(bf16[96,768]{1,0:T(8,128)(2,1)} %bitcast.64), channel_id=2, replica_groups=mesh['section'=8,'zlo'=4,'x'=4,'core'=2,'tensor'=2] {'zlo'}, dimensions={0}, use_global_device_ids=true | all-gather | bytes 737280 | tf_op jit(solution)/shard_map/all_gather | solution.py:102
  24.2 4.4 %collective-permute-start = (bf16[4,96,768]{2,1,0:T(8,128)(2,1)S(1)}, bf16[4,96,768]{2,1,0:T(8,128)(2,1)S(1)}, u32[]{:S(2)}, u32[]{:S(2)}) collective-permute-start(bf16[4,96,768]{2,1,0:T(8,128)(2,1)S(1)} %bitcast.57), channel_id=1, source_target_pairs={{0,12},{4,0},{8,4},{12,8},{1,13},{5,1},{9,5},{13,9},{2,14},{6,2},{... | collective-permute-start | bytes 1769480 | tf_op jit(solution)/shard_map/ppermute | solution.py:18
  28.5 1.9 %collective-permute-start.3 = (bf16[4,96,768]{2,1,0:T(8,128)(2,1)S(1)}, bf16[4,96,768]{2,1,0:T(8,128)(2,1)S(1)}, u32[]{:S(2)}, u32[]{:S(2)}) collective-permute-start(bf16[4,96,768]{2,1,0:T(8,128)(2,1)S(1)} %bitcast.58), channel_id=1, source_target_pairs={{0,4},{4,8},{8,12},{12,0},{1,5},{5,9},{9,13},{13,1},{2,6},{6,10},{... | collective-permute-start | bytes 1769480 | tf_op jit(solution)/shard_map/ppermute | solution.py:18
  30.5 0.0 copy-start.2
  30.5 0.6 copy-done.2
  31.1 0.6 shard_map.95.hot
  31.7 0.0 collective-permute-done.1.second
  31.8 0.0 copy-start
  31.8 1.1 copy-done
  32.9 0.5 shard_map.94
  33.4 5.8 %collective-permute-done.above = bf16[4,96,768]{2,1,0:T(8,128)(2,1)S(1)} collective-permute-done((bf16[4,96,768]{2,1,0:T(8,128)(2,1)S(1)}, bf16[4,96,768]{2,1,0:T(8,128)(2,1)S(1)}, u32[]{:S(2)}, u32[]{:S(2)}) %collective-permute-start) | collective-permute-done | bytes 589856 | tf_op jit(solution)/shard_map/ppermute | solution.py:18
  39.2 0.8 slice.50
  40.0 5.3 %collective-permute-start.2 = (bf16[3,96,768]{2,1,0:T(8,128)(2,1)}, bf16[3,96,768]{2,1,0:T(8,128)(2,1)}, u32[]{:S(2)}, u32[]{:S(2)}) collective-permute-start(bf16[3,96,768]{2,1,0:T(8,128)(2,1)} %slice.50), channel_id=1, source_target_pairs={{0,12},{4,0},{8,4},{12,8},{1,13},{5,1},{9,5},{13,9},{2,14},{6,2},{... | collective-permute-start | bytes 1327112 | tf_op jit(solution)/shard_map/ppermute | solution.py:18
  45.6 0.0 collective-permute-done.3.below
  45.6 0.0 collective-permute-done.4
  45.6 1.9 %collective-permute-start.5 = (bf16[1,96,768]{2,1,0:T(8,128)(2,1)S(1)}, bf16[1,96,768]{2,1,0:T(8,128)(2,1)S(1)}, u32[]{:S(2)}, u32[]{:S(2)}) collective-permute-start(bf16[1,96,768]{2,1,0:T(8,128)(2,1)S(1)} %slice.51), channel_id=1, source_target_pairs={{0,4},{4,8},{8,12},{12,0},{1,5},{5,9},{9,13},{13,1},{2,6},{6,10},{... | collective-permute-start | bytes 442376 | tf_op jit(solution)/shard_map/ppermute | solution.py:18
  47.6 0.4 convolution_convert_fusion
  48.0 2.3 %collective-permute-start.6 = (bf16[96,1024]{1,0:T(8,128)(2,1)S(1)}, bf16[96,1024]{1,0:T(8,128)(2,1)S(1)}, u32[]{:S(2)}, u32[]{:S(2)}) collective-permute-start(bf16[96,1024]{1,0:T(8,128)(2,1)S(1)} %convolution_convert_fusion), channel_id=1, source_target_pairs={{0,64},{64,128},{128,192},{192,256},{256,320},{320,384},{384,448},... | collective-permute-start | bytes 589832 | tf_op jit(solution)/shard_map/ppermute | solution.py:18
  50.3 2.0 %collective-permute-done.2.opposite = bf16[3,96,768]{2,1,0:T(8,128)(2,1)} collective-permute-done((bf16[3,96,768]{2,1,0:T(8,128)(2,1)}, bf16[3,96,768]{2,1,0:T(8,128)(2,1)}, u32[]{:S(2)}, u32[]{:S(2)}) %collective-permute-start.2) | collective-permute-done | bytes 442400 | tf_op jit(solution)/shard_map/ppermute | solution.py:18
  52.3 0.5 collective-permute-done.5.rest
  52.7 1.3 %convolution_convert_fusion.1 = bf16[96,1024]{1,0:T(8,128)(2,1)S(1)} fusion(bf16[768,1024]{1,0:T(8,128)(2,1)S(1)} %shard_map.94, bf16[1,96,768]{2,1,0:T(8,128)(2,1)S(1)} %collective-permute-done.5.rest, bf16[3,96,768]{2,1,0:T(8,128)(2,1)} %collective-permute-done.2.opposite, s32[]{:T(128)S(6)} %select_n.234, pred[]{:T(512)S(6)} %lt.108, pred[]{:T(512)S(6)} %eq.55, ...), kind=kOutput, calls=%fused_computation.23 | convolution fusion | flops 151314432 | bytes 2359307 | tf_op jit(solution)/shard_map/dot_general | solution.py:124
  54.0 3.3 %collective-permute-start.10 = (bf16[96,1024]{1,0:T(8,128)(2,1)S(1)}, bf16[96,1024]{1,0:T(8,128)(2,1)S(1)}, u32[]{:S(2)}, u32[]{:S(2)}) collective-permute-start(bf16[96,1024]{1,0:T(8,128)(2,1)S(1)} %convolution_convert_fusion.1), channel_id=1, source_target_pairs={{0,448},{64,0},{128,64},{192,128},{256,192},{320,256},{384,320},{4... | collective-permute-start | bytes 589832 | tf_op jit(solution)/shard_map/ppermute | solution.py:18
  57.4 1.2 %shard_map.96 = bf16[4,4,96,768]{3,2,1,0:T(8,128)(2,1)S(1)} custom-call(s32[1]{0:T(128)} %bitcast.2.x, bf16[4,96,768]{2,1,0:T(8,128)(2,1)S(1)} %bitcast.60, bf16[4,96,768]{2,1,0:T(8,128)(2,1)S(1)} %collective-permute-done.above, bf16[3,96,768]{2,1,0:T(8,128)(2,1)} %collective-permute-done.2.opposite, bf16[1,96,768]{2,1,0:T(8,128)(2,1)S(1)} %collective-permute-done.5.rest, ...), custom_call_target="tpu_custom_call" | custom-call | tf_op jit(solution)/shard_map/pallas_call | solution.py:58
  58.6 0.0 collective-permute-done.6
  58.6 0.5 fusion.5
  59.1 0.0 copy-start.3
  59.1 2.1 %collective-permute-start.7 = (bf16[192,1024]{1,0:T(8,128)(2,1)S(1)}, bf16[192,1024]{1,0:T(8,128)(2,1)S(1)}, u32[]{:S(2)}, u32[]{:S(2)}) collective-permute-start(bf16[192,1024]{1,0:T(8,128)(2,1)S(1)} %fusion.5), channel_id=1, source_target_pairs={{0,64},{64,128},{128,192},{192,256},{256,320},{320,384},{384,448},... | collective-permute-start | bytes 1179656 | tf_op jit(solution)/shard_map/ppermute | solution.py:18
  61.2 0.0 collective-permute-done.10
  61.3 0.5 fusion.8
  61.8 3.8 %collective-permute-start.11 = (bf16[192,1024]{1,0:T(8,128)(2,1)S(1)}, bf16[192,1024]{1,0:T(8,128)(2,1)S(1)}, u32[]{:S(2)}, u32[]{:S(2)}) collective-permute-start(bf16[192,1024]{1,0:T(8,128)(2,1)S(1)} %fusion.8), channel_id=1, source_target_pairs={{0,448},{64,0},{128,64},{192,128},{256,192},{320,256},{384,320},{4... | collective-permute-start | bytes 1179656 | tf_op jit(solution)/shard_map/ppermute | solution.py:18
  65.6 1.7 %fusion = f32[192]{0:T(256)S(1)} fusion(bf16[192,3072]{1,0:T(8,128)(2,1)S(1)} %copy-done.3, bf16[192,3072]{1,0:T(8,128)(2,1)} %collective-permute-done.4, pred[]{:T(512)S(6)} %eq.50), kind=kLoop, calls=%fused_computation.2 | loop fusion | flops 2359104 | bytes 2360065 | tf_op jit(solution)/shard_map/reduce_sum | solution.py:190
  67.4 0.9 collective-permute-done.7
  68.3 0.5 fusion.4
  68.8 0.0 copy-start.4
  68.8 2.1 %collective-permute-start.8 = (bf16[192,1024]{1,0:T(8,128)(2,1)S(1)}, bf16[192,1024]{1,0:T(8,128)(2,1)S(1)}, u32[]{:S(2)}, u32[]{:S(2)}) collective-permute-start(bf16[192,1024]{1,0:T(8,128)(2,1)S(1)} %fusion.4), channel_id=1, source_target_pairs={{0,64},{64,128},{128,192},{192,256},{256,320},{320,384},{384,448},... | collective-permute-start | bytes 1179656 | tf_op jit(solution)/shard_map/ppermute | solution.py:18
  70.8 0.0 collective-permute-done.11
  70.9 0.5 fusion.7
  71.4 4.6 %collective-permute-start.12 = (bf16[192,1024]{1,0:T(8,128)(2,1)S(1)}, bf16[192,1024]{1,0:T(8,128)(2,1)S(1)}, u32[]{:S(2)}, u32[]{:S(2)}) collective-permute-start(bf16[192,1024]{1,0:T(8,128)(2,1)S(1)} %fusion.7), channel_id=1, source_target_pairs={{0,448},{64,0},{128,64},{192,128},{256,192},{320,256},{384,320},{4... | collective-permute-start | bytes 1179656 | tf_op jit(solution)/shard_map/ppermute | solution.py:18
  76.0 1.0 slice_select_fusion
  77.0 1.3 %collective-permute-start.15 = (bf16[192,768]{1,0:T(8,128)(2,1)S(1)}, bf16[192,768]{1,0:T(8,128)(2,1)S(1)}, u32[]{:S(2)}, u32[]{:S(2)}) collective-permute-start(bf16[192,768]{1,0:T(8,128)(2,1)S(1)} %slice_select_fusion), channel_id=1, source_target_pairs={{0,128},{448,320},{1,129},{449,321},{2,130},{450,322},{3,131},{451... | collective-permute-start | bytes 884744 | tf_op jit(solution)/shard_map/ppermute | solution.py:172
  78.3 0.4 collective-permute-done.8
  78.7 0.5 fusion.3
  79.2 1.9 %collective-permute-start.9 = (bf16[192,1024]{1,0:T(8,128)(2,1)S(1)}, bf16[192,1024]{1,0:T(8,128)(2,1)S(1)}, u32[]{:S(2)}, u32[]{:S(2)}) collective-permute-start(bf16[192,1024]{1,0:T(8,128)(2,1)S(1)} %fusion.3), channel_id=1, source_target_pairs={{0,64},{64,128},{128,192},{192,256},{256,320},{320,384},{384,448},... | collective-permute-start | bytes 1179656 | tf_op jit(solution)/shard_map/ppermute | solution.py:18
  81.1 0.0 collective-permute-done.12
  81.1 0.5 fusion.6
  81.6 0.0 copy-start.5
  81.6 4.6 %collective-permute-start.13 = (bf16[192,1024]{1,0:T(8,128)(2,1)S(1)}, bf16[192,1024]{1,0:T(8,128)(2,1)S(1)}, u32[]{:S(2)}, u32[]{:S(2)}) collective-permute-start(bf16[192,1024]{1,0:T(8,128)(2,1)S(1)} %fusion.6), channel_id=1, source_target_pairs={{0,448},{64,0},{128,64},{192,128},{256,192},{320,256},{384,320},{4... | collective-permute-start | bytes 1179656 | tf_op jit(solution)/shard_map/ppermute | solution.py:18
  86.2 8.0 %collective-permute-start.17 = (f32[192]{0:T(256)S(1)}, f32[192]{0:T(256)S(1)}, u32[]{:S(2)}, u32[]{:S(2)}) collective-permute-start(f32[192]{0:T(256)S(1)} %fusion), channel_id=1, source_target_pairs={{0,1},{1,0},{2,3},{3,2},{4,5},{5,4},{6,7},{7,6},{8,9},{9,8},{10,11... | collective-permute-start | bytes 2312 | tf_op jit(solution)/shard_map/ppermute | solution.py:18
  94.2 0.0 collective-permute-done.15
  94.2 1.1 fusion.29
  95.2 4.6 %collective-permute-start.16 = (bf16[192,384]{1,0:T(8,128)(2,1)S(1)}, bf16[192,384]{1,0:T(8,128)(2,1)S(1)}, u32[]{:S(2)}, u32[]{:S(2)}) collective-permute-start(bf16[192,384]{1,0:T(8,128)(2,1)S(1)} %get-tuple-element.21), channel_id=1, source_target_pairs={{0,64},{128,192},{448,384},{320,256},{1,65},{129,193},{449,385},{3... | collective-permute-start | bytes 442376 | tf_op jit(solution)/shard_map/ppermute | solution.py:183
  99.8 0.0 collective-permute-done.17
  99.9 0.0 collective-permute-done.9
  99.9 0.0 collective-permute-done.13
  99.9 0.3 convolution_add_fusion.6
  100.2 10.2 %collective-permute-start.14 = (bf16[192,512]{1,0:T(8,128)(2,1)S(1)}, bf16[192,512]{1,0:T(8,128)(2,1)S(1)}, u32[]{:S(2)}, u32[]{:S(2)}) collective-permute-start(bf16[192,512]{1,0:T(8,128)(2,1)S(1)} %convolution_add_fusion.6), channel_id=1, source_target_pairs={{0,2},{2,0},{1,3},{3,1},{4,6},{6,4},{5,7},{7,5},{8,10},{10,8},{9,1... | collective-permute-start | bytes 589832 | tf_op jit(solution)/shard_map/ppermute | solution.py:18
  110.4 2.8 %fusion.9 = bf16[1,192,3072]{2,1,0:T(8,128)(2,1)} fusion(f32[3072]{0:T(1024)S(1)} %bitcast.65, f32[192]{0:T(256)S(1)} %add_rsqrt_fusion, bf16[192,3072]{1,0:T(8,128)(2,1)S(1)} %copy-done.3, bf16[192,3072]{1,0:T(8,128)(2,1)} %collective-permute-done.4, pred[]{:T(512)S(6)} %eq.50), kind=kLoop, calls=%fused_computation.19 | loop fusion | flops 2949120 | bytes 3552001 | tf_op jit(solution)/shard_map/broadcast_in_dim | solution.py:201
  113.2 0.3 fusion.10.mine
  113.5 0.0 collective-permute-done.16.handed
  113.5 0.0 collective-permute-done.14.other
  113.5 0.6 copy-done.1
  114.2 1.5 %shard_map.97 = (bf16[512,384]{1,0:T(8,128)(2,1)}, f32[192,384]{1,0:T(8,128)}) custom-call(s32[1]{0:T(128)} %bitcast.core, s32[1]{0:T(128)} %bitcast.1.keeps, bf16[192,512]{1,0:T(8,128)(2,1)S(1)} %fusion.10.mine, bf16[192,512]{1,0:T(8,128)(2,1)S(1)} %collective-permute-done.14.other, bf16[512,384]{1,0:T(8,128)(2,1)S(1)} %copy-done.1, ...), custom_call_target="tpu_custom_call" | custom-call | tf_op jit(solution)/shard_map/pallas_call | solution.py:203
  (8 shorter events, 0.1 us)
Async XLA Ops:
  0.6 45.0 %collective-permute-start.4 = (bf16[192,3072]{1,0:T(8,128)(2,1)}, bf16[192,3072]{1,0:T(8,128)(2,1)}, u32[]{:S(2)}, u32[]{:S(2)}) collective-permute-start(bf16[192,3072]{1,0:T(8,128)(2,1)} %bitcast.61), channel_id=1, source_target_pairs={{0,64},{64,128},{128,192},{192,256},{256,320},{320,384},{384,448},... | collective-permute-start | bytes 3538952 | tf_op jit(solution)/shard_map/ppermute | solution.py:18
  2.9 28.8 %collective-permute-start.1 = (bf16[512,768]{1,0:T(8,128)(2,1)}, bf16[512,768]{1,0:T(8,128)(2,1)S(1)}, u32[]{:S(2)}, u32[]{:S(2)}) collective-permute-start(bf16[512,768]{1,0:T(8,128)(2,1)} %first.1), channel_id=1, source_target_pairs={{0,2},{2,0},{1,3},{3,1},{4,6},{6,4},{5,7},{7,5},{8,10},{10,8},{9,1... | collective-permute-start | bytes 2359304 | tf_op jit(solution)/shard_map/ppermute | solution.py:18
  24.2 15.1 %collective-permute-start = (bf16[4,96,768]{2,1,0:T(8,128)(2,1)S(1)}, bf16[4,96,768]{2,1,0:T(8,128)(2,1)S(1)}, u32[]{:S(2)}, u32[]{:S(2)}) collective-permute-start(bf16[4,96,768]{2,1,0:T(8,128)(2,1)S(1)} %bitcast.57), channel_id=1, source_target_pairs={{0,12},{4,0},{8,4},{12,8},{1,13},{5,1},{9,5},{13,9},{2,14},{6,2},{... | collective-permute-start | bytes 1769480 | tf_op jit(solution)/shard_map/ppermute | solution.py:18
  28.5 17.1 %collective-permute-start.3 = (bf16[4,96,768]{2,1,0:T(8,128)(2,1)S(1)}, bf16[4,96,768]{2,1,0:T(8,128)(2,1)S(1)}, u32[]{:S(2)}, u32[]{:S(2)}) collective-permute-start(bf16[4,96,768]{2,1,0:T(8,128)(2,1)S(1)} %bitcast.58), channel_id=1, source_target_pairs={{0,4},{4,8},{8,12},{12,0},{1,5},{5,9},{9,13},{13,1},{2,6},{6,10},{... | collective-permute-start | bytes 1769480 | tf_op jit(solution)/shard_map/ppermute | solution.py:18
  30.5 0.7 copy-start.2
  31.8 1.1 copy-start
  40.0 12.2 %collective-permute-start.2 = (bf16[3,96,768]{2,1,0:T(8,128)(2,1)}, bf16[3,96,768]{2,1,0:T(8,128)(2,1)}, u32[]{:S(2)}, u32[]{:S(2)}) collective-permute-start(bf16[3,96,768]{2,1,0:T(8,128)(2,1)} %slice.50), channel_id=1, source_target_pairs={{0,12},{4,0},{8,4},{12,8},{1,13},{5,1},{9,5},{13,9},{2,14},{6,2},{... | collective-permute-start | bytes 1327112 | tf_op jit(solution)/shard_map/ppermute | solution.py:18
  45.6 7.1 %collective-permute-start.5 = (bf16[1,96,768]{2,1,0:T(8,128)(2,1)S(1)}, bf16[1,96,768]{2,1,0:T(8,128)(2,1)S(1)}, u32[]{:S(2)}, u32[]{:S(2)}) collective-permute-start(bf16[1,96,768]{2,1,0:T(8,128)(2,1)S(1)} %slice.51), channel_id=1, source_target_pairs={{0,4},{4,8},{8,12},{12,0},{1,5},{5,9},{9,13},{13,1},{2,6},{6,10},{... | collective-permute-start | bytes 442376 | tf_op jit(solution)/shard_map/ppermute | solution.py:18
  48.0 10.6 %collective-permute-start.6 = (bf16[96,1024]{1,0:T(8,128)(2,1)S(1)}, bf16[96,1024]{1,0:T(8,128)(2,1)S(1)}, u32[]{:S(2)}, u32[]{:S(2)}) collective-permute-start(bf16[96,1024]{1,0:T(8,128)(2,1)S(1)} %convolution_convert_fusion), channel_id=1, source_target_pairs={{0,64},{64,128},{128,192},{192,256},{256,320},{320,384},{384,448},... | collective-permute-start | bytes 589832 | tf_op jit(solution)/shard_map/ppermute | solution.py:18
  54.0 7.2 %collective-permute-start.10 = (bf16[96,1024]{1,0:T(8,128)(2,1)S(1)}, bf16[96,1024]{1,0:T(8,128)(2,1)S(1)}, u32[]{:S(2)}, u32[]{:S(2)}) collective-permute-start(bf16[96,1024]{1,0:T(8,128)(2,1)S(1)} %convolution_convert_fusion.1), channel_id=1, source_target_pairs={{0,448},{64,0},{128,64},{192,128},{256,192},{320,256},{384,320},{4... | collective-permute-start | bytes 589832 | tf_op jit(solution)/shard_map/ppermute | solution.py:18
  59.1 6.5 %copy-start.3 = (bf16[192,3072]{1,0:T(8,128)(2,1)S(1)}, bf16[192,3072]{1,0:T(8,128)(2,1)}, u32[]{:S(2)}) copy-start(bf16[192,3072]{1,0:T(8,128)(2,1)} %param.11) | copy-start | bytes 3538948
  59.1 9.1 %collective-permute-start.7 = (bf16[192,1024]{1,0:T(8,128)(2,1)S(1)}, bf16[192,1024]{1,0:T(8,128)(2,1)S(1)}, u32[]{:S(2)}, u32[]{:S(2)}) collective-permute-start(bf16[192,1024]{1,0:T(8,128)(2,1)S(1)} %fusion.5), channel_id=1, source_target_pairs={{0,64},{64,128},{128,192},{192,256},{256,320},{320,384},{384,448},... | collective-permute-start | bytes 1179656 | tf_op jit(solution)/shard_map/ppermute | solution.py:18
  61.8 9.1 %collective-permute-start.11 = (bf16[192,1024]{1,0:T(8,128)(2,1)S(1)}, bf16[192,1024]{1,0:T(8,128)(2,1)S(1)}, u32[]{:S(2)}, u32[]{:S(2)}) collective-permute-start(bf16[192,1024]{1,0:T(8,128)(2,1)S(1)} %fusion.8), channel_id=1, source_target_pairs={{0,448},{64,0},{128,64},{192,128},{256,192},{320,256},{384,320},{4... | collective-permute-start | bytes 1179656 | tf_op jit(solution)/shard_map/ppermute | solution.py:18
  68.8 7.2 %copy-start.4 = (bf16[1,192,3072]{2,1,0:T(8,128)(2,1)S(1)}, bf16[1,192,3072]{2,1,0:T(8,128)(2,1)}, u32[]{:S(2)}) copy-start(bf16[1,192,3072]{2,1,0:T(8,128)(2,1)} %param.10) | copy-start | bytes 3538948
  68.8 9.9 %collective-permute-start.8 = (bf16[192,1024]{1,0:T(8,128)(2,1)S(1)}, bf16[192,1024]{1,0:T(8,128)(2,1)S(1)}, u32[]{:S(2)}, u32[]{:S(2)}) collective-permute-start(bf16[192,1024]{1,0:T(8,128)(2,1)S(1)} %fusion.4), channel_id=1, source_target_pairs={{0,64},{64,128},{128,192},{192,256},{256,320},{320,384},{384,448},... | collective-permute-start | bytes 1179656 | tf_op jit(solution)/shard_map/ppermute | solution.py:18
  71.4 9.7 %collective-permute-start.12 = (bf16[192,1024]{1,0:T(8,128)(2,1)S(1)}, bf16[192,1024]{1,0:T(8,128)(2,1)S(1)}, u32[]{:S(2)}, u32[]{:S(2)}) collective-permute-start(bf16[192,1024]{1,0:T(8,128)(2,1)S(1)} %fusion.7), channel_id=1, source_target_pairs={{0,448},{64,0},{128,64},{192,128},{256,192},{320,256},{384,320},{4... | collective-permute-start | bytes 1179656 | tf_op jit(solution)/shard_map/ppermute | solution.py:18
  77.0 17.2 %collective-permute-start.15 = (bf16[192,768]{1,0:T(8,128)(2,1)S(1)}, bf16[192,768]{1,0:T(8,128)(2,1)S(1)}, u32[]{:S(2)}, u32[]{:S(2)}) collective-permute-start(bf16[192,768]{1,0:T(8,128)(2,1)S(1)} %slice_select_fusion), channel_id=1, source_target_pairs={{0,128},{448,320},{1,129},{449,321},{2,130},{450,322},{3,131},{451... | collective-permute-start | bytes 884744 | tf_op jit(solution)/shard_map/ppermute | solution.py:172
  79.2 20.7 %collective-permute-start.9 = (bf16[192,1024]{1,0:T(8,128)(2,1)S(1)}, bf16[192,1024]{1,0:T(8,128)(2,1)S(1)}, u32[]{:S(2)}, u32[]{:S(2)}) collective-permute-start(bf16[192,1024]{1,0:T(8,128)(2,1)S(1)} %fusion.3), channel_id=1, source_target_pairs={{0,64},{64,128},{128,192},{192,256},{256,320},{320,384},{384,448},... | collective-permute-start | bytes 1179656 | tf_op jit(solution)/shard_map/ppermute | solution.py:18
  81.6 28.8 %copy-start.5 = (f32[1,3072]{1,0:T(1,128)S(1)}, f32[1,3072]{1,0:T(1,128)}, u32[]{:S(2)}) copy-start(f32[1,3072]{1,0:T(1,128)} %param.12) | copy-start | bytes 36868
  81.6 18.2 %collective-permute-start.13 = (bf16[192,1024]{1,0:T(8,128)(2,1)S(1)}, bf16[192,1024]{1,0:T(8,128)(2,1)S(1)}, u32[]{:S(2)}, u32[]{:S(2)}) collective-permute-start(bf16[192,1024]{1,0:T(8,128)(2,1)S(1)} %fusion.6), channel_id=1, source_target_pairs={{0,448},{64,0},{128,64},{192,128},{256,192},{320,256},{384,320},{4... | collective-permute-start | bytes 1179656 | tf_op jit(solution)/shard_map/ppermute | solution.py:18
  86.2 13.6 %collective-permute-start.17 = (f32[192]{0:T(256)S(1)}, f32[192]{0:T(256)S(1)}, u32[]{:S(2)}, u32[]{:S(2)}) collective-permute-start(f32[192]{0:T(256)S(1)} %fusion), channel_id=1, source_target_pairs={{0,1},{1,0},{2,3},{3,2},{4,5},{5,4},{6,7},{7,6},{8,9},{9,8},{10,11... | collective-permute-start | bytes 2312 | tf_op jit(solution)/shard_map/ppermute | solution.py:18
  95.2 18.3 %collective-permute-start.16 = (bf16[192,384]{1,0:T(8,128)(2,1)S(1)}, bf16[192,384]{1,0:T(8,128)(2,1)S(1)}, u32[]{:S(2)}, u32[]{:S(2)}) collective-permute-start(bf16[192,384]{1,0:T(8,128)(2,1)S(1)} %get-tuple-element.21), channel_id=1, source_target_pairs={{0,64},{128,192},{448,384},{320,256},{1,65},{129,193},{449,385},{3... | collective-permute-start | bytes 442376 | tf_op jit(solution)/shard_map/ppermute | solution.py:183
  100.2 13.3 %collective-permute-start.14 = (bf16[192,512]{1,0:T(8,128)(2,1)S(1)}, bf16[192,512]{1,0:T(8,128)(2,1)S(1)}, u32[]{:S(2)}, u32[]{:S(2)}) collective-permute-start(bf16[192,512]{1,0:T(8,128)(2,1)S(1)} %convolution_add_fusion.6), channel_id=1, source_target_pairs={{0,2},{2,0},{1,3},{3,1},{4,6},{6,4},{5,7},{7,5},{8,10},{10,8},{9,1... | collective-permute-start | bytes 589832 | tf_op jit(solution)/shard_map/ppermute | solution.py:18
  113.2 1.0 copy-start.1
